TPU v7x, 32 devices: a whole 2x2x4 slice. The times are simulated.
32 devices in a mesh: seq: 8 (over y, x, core), mp: 4 (over z).
Axes of the slice: x: 2, y: 2, z: 4, core: 2. Of those that a mesh axis runs over, the one named last changes fastest.
Arguments:
- tokens: bfloat16 [6, 3072, 1024], P(None, 'seq'), may hold values from -6 to 6
- patches: bfloat16 [6, 1536, 768], P(None, 'seq'), may hold values from -6 to 6
- counts: int32 [6], replicated, may hold values from 512 to 1536, as said below
- norm_gains: float32 [3, 1024], replicated, may hold values from 0.5 to 1.5
- norm_shifts: float32 [3, 1024], replicated, may hold values from -1.75 to 1.75
- cross_query: bfloat16 [1024, 1024], P(None, 'mp'), may hold values from -0.1875 to 0.1875
- cross_kv: bfloat16 [768, 2, 1024], P(None, None, 'mp'), may hold values from -0.21875 to 0.21875
- cross_out: bfloat16 [1024, 1024], P('mp'), may hold values from -3.5 to 3.5
- self_qkv: bfloat16 [1024, 3, 1024], P(None, None, 'mp'), may hold values from -0.1875 to 0.1875
- self_out: bfloat16 [1024, 1024], P('mp'), may hold values from -6 to 6
- mlp_up: bfloat16 [1024, 4096], P(None, 'mp'), may hold values from -0.1875 to 0.1875
- mlp_down: bfloat16 [4096, 1024], P('mp'), may hold values from -0.09375 to 0.09375
- decoder: bfloat16 [1024, 80, 4], P(None, 'mp'), may hold values from -0.1875 to 0.1875
- sample_weights: bfloat16 [6, 3, 8, 561, 256], P(None, None, 'seq'), may hold values from 0 to 1
- tokens_cot: bfloat16 [6, 3072, 1024], P(None, 'seq'), may hold values from -6 to 6
- sample_cot: bfloat16 [6, 3, 80, 8, 256], P(None, None, 'mp', 'seq'), may hold values from -6 to 6
Outputs:
- tokens_out: bfloat16 [6, 3072, 1024], P(None, ('seq', 'mp'))
- sampled: bfloat16 [6, 3, 80, 8, 256], P(None, None, 'mp', 'seq')
- grad_tokens: float32 [6, 3072, 1024], P(None, ('seq', 'mp'))
- grad_patches: float32 [6, 1536, 768], P(None, 'seq')
- grad_norm_gains: float32 [3, 1024], P(None, 'seq')
- grad_norm_shifts: float32 [2, 1024], P(None, 'seq')
- grad_mlp_shift: float32 [1024], P('seq')
- grad_cross_query: float32 [1024, 1024], P('seq', 'mp')
- grad_cross_kv: float32 [768, 2, 1024], P('seq', None, 'mp')
- grad_cross_out: float32 [1024, 1024], P('mp', 'seq')
- grad_self_qkv: float32 [1024, 3, 1024], P('seq', None, 'mp')
- grad_self_out: float32 [1024, 1024], P('mp', 'seq')
- grad_mlp_up: float32 [1024, 4096], P('seq', 'mp')
- grad_mlp_down: float32 [4096, 1024], P('mp', 'seq')
- grad_decoder: float32 [1024, 80, 4], P('seq', 'mp')
Inputs may be any that keep to these rules, and one draw needn't show every extreme that they name: `counts`: exactly one object has 1536 foreground patch tokens; every object has 512 or more; slots at or past an object's count hold no patch token of it.
All inputs are finite; a program needn't handle non-finite values.
Results may differ from a plain program's by a relative error of at most 0.029.
Values may be sent and summed in bfloat16 or wider, within the bound.
No kernel may reach another device: no remote copies, remote signals or barrier semaphores. Data moves between devices by JAX's collectives and lax.ppermute only.
A program may use at most 704 MiB of HBM per device.

v0:
```python
import math

import jax
import jax.numpy as jnp
from jax import lax
from jax.sharding import PartitionSpec as P

PLANE = 32
HD = 64


norm_eps = 1e-05
masked_score = -1e30


def from_behind(value, axis, steps):
    count = lax.axis_size(axis)
    initial, last = (max(0, -steps), min(count, count - steps))
    return lax.ppermute(value, axis, [(source, source + steps) for source in range(initial, last)])


def layer_norm(values, gain_row, shift_row):
    center = values - jnp.mean(values, axis=-1, keepdims=True)
    spread = jnp.mean(center * center, axis=-1, keepdims=True)
    return center * lax.rsqrt(spread + norm_eps) * gain_row + shift_row


def norm_back(values, gain_row, shift_row, grad_out):
    normed_value, pullback = jax.vjp(layer_norm, values, gain_row, shift_row)
    return pullback(grad_out)


def split_heads(operand):
    return operand.reshape(operand.shape[:-1] + (operand.shape[-1] // HD, HD))


def head_scores(queries, key_rows, key_mask):
    factor = 1.0 / math.sqrt(HD)
    scores = (
        jnp.einsum("orhd,okhd->ohrk", queries, key_rows, preferred_element_type=jnp.float32)
        * factor
    )
    if key_mask is None:
        return scores
    return jnp.where(key_mask[:, None, None, :], scores, masked_score)


def attend(queries, key_rows, value_rows, key_mask):
    scores = head_scores(queries, key_rows, key_mask)
    row_max = jnp.max(scores, axis=-1, keepdims=True)
    raised = jnp.exp(scores - row_max)
    row_total = jnp.sum(raised, axis=-1, keepdims=True)
    weights = (raised / row_total).astype(jnp.bfloat16)
    mixed_rows = jnp.einsum(
        "ohrk,okhd->orhd", weights, value_rows, preferred_element_type=jnp.float32
    )
    return (mixed_rows, row_max + jnp.log(row_total))


def attend_back(queries, key_rows, value_rows, key_mask, log_total, grad_mixed):
    factor = 1.0 / math.sqrt(HD)
    scores = head_scores(queries, key_rows, key_mask)
    prob_full = jnp.exp(scores - log_total)
    grad_probs = jnp.einsum(
        "orhd,okhd->ohrk", grad_mixed, value_rows, preferred_element_type=jnp.float32
    )
    centred = jnp.sum(grad_probs * prob_full, axis=-1, keepdims=True)
    grad_scores = (prob_full * (grad_probs - centred)).astype(jnp.bfloat16)
    grad_query = (
        jnp.einsum("ohrk,okhd->orhd", grad_scores, key_rows, preferred_element_type=jnp.float32)
        * factor
    )
    grad_key = (
        jnp.einsum("ohrk,orhd->okhd", grad_scores, queries, preferred_element_type=jnp.float32)
        * factor
    )
    grad_value = jnp.einsum(
        "ohrk,orhd->okhd",
        prob_full.astype(jnp.bfloat16),
        grad_mixed,
        preferred_element_type=jnp.float32,
    )
    return (grad_query, grad_key, grad_value)


def own_rows(operand):
    share_rows = operand.shape[1] // lax.axis_size("mp")
    return lax.dynamic_slice_in_dim(operand, lax.axis_index("mp") * share_rows, share_rows, 1)


def settle(operand):
    return lax.psum(operand.astype(jnp.bfloat16), "mp").astype(jnp.float32)


def gather_keys(operand):
    return lax.all_gather(operand, "seq", axis=1, tiled=True)


def return_keys(operand):
    return lax.psum_scatter(
        operand.astype(jnp.bfloat16), "seq", scatter_dimension=1, tiled=True
    ).astype(jnp.float32)


def take_rim(operand, offset):
    return from_behind(operand, "seq", offset)


def give_rim(operand, offset):
    return from_behind(operand, "seq", offset)


def to_planes(tile_pixels, tile_rows, tile_cols):
    objects, channels = (tile_pixels.shape[0], tile_pixels.shape[2])
    cells = tile_pixels.reshape(objects, 3, tile_rows, tile_cols, channels, 2, 2)
    cells = cells.transpose(0, 1, 4, 2, 5, 3, 6)
    return cells.reshape(objects, 3, channels, 2 * tile_rows, 2 * tile_cols)


def from_planes(planes, tile_rows, tile_cols):
    objects, channels = (planes.shape[0], planes.shape[2])
    cells = planes.reshape(objects, 3, channels, tile_rows, 2, tile_cols, 2)
    cells = cells.transpose(0, 1, 3, 5, 2, 4, 6)
    return cells.reshape(objects, 3 * tile_rows * tile_cols, channels, 4)


def per_device(
    tokens,
    patches,
    counts,
    norm_gains,
    norm_shifts,
    cross_query,
    cross_kv,
    cross_out,
    self_qkv,
    self_out,
    mlp_up,
    mlp_down,
    decoder,
    sample_weights,
    tokens_cot,
    sample_cot,
):
    objects, row_count, features = tokens.shape
    tile_count = lax.axis_size("seq")
    slot_total = patches.shape[1] * tile_count
    key_mask = jnp.arange(slot_total, dtype=jnp.int32)[None, :] < counts[:, None]
    inputs = tokens.astype(jnp.float32)
    cot_full = tokens_cot.astype(jnp.float32)
    normed_one = layer_norm(inputs, norm_gains[0], norm_shifts[0]).astype(jnp.bfloat16)
    query_one = jnp.einsum(
        "ord,de->ore", normed_one, cross_query, preferred_element_type=jnp.float32
    ).astype(jnp.bfloat16)
    pair_local = jnp.einsum(
        "osi,ije->osje", patches, cross_kv, preferred_element_type=jnp.float32
    ).astype(jnp.bfloat16)
    pair_one = gather_keys(pair_local)
    heads_one = (
        split_heads(query_one),
        split_heads(pair_one[:, :, 0]),
        split_heads(pair_one[:, :, 1]),
    )
    mixed_one, total_one = attend(heads_one[0], heads_one[1], heads_one[2], key_mask)
    mixed_one = mixed_one.reshape(query_one.shape).astype(jnp.bfloat16)
    after_one = inputs + settle(
        jnp.einsum("ore,ed->ord", mixed_one, cross_out, preferred_element_type=jnp.float32)
    )
    normed_two = layer_norm(after_one, norm_gains[1], norm_shifts[1]).astype(jnp.bfloat16)
    triple = jnp.einsum(
        "ord,dje->orje", normed_two, self_qkv, preferred_element_type=jnp.float32
    ).astype(jnp.bfloat16)
    pair_two = gather_keys(triple[:, :, 1:])
    heads_two = (
        split_heads(triple[:, :, 0]),
        split_heads(pair_two[:, :, 0]),
        split_heads(pair_two[:, :, 1]),
    )
    mixed_two, total_two = attend(heads_two[0], heads_two[1], heads_two[2], None)
    mixed_two = mixed_two.reshape(query_one.shape).astype(jnp.bfloat16)
    after_two = after_one + settle(
        jnp.einsum("ore,ed->ord", mixed_two, self_out, preferred_element_type=jnp.float32)
    )
    normed_three = layer_norm(after_two, norm_gains[2], norm_shifts[2]).astype(jnp.bfloat16)
    hidden = jnp.einsum("ord,df->orf", normed_three, mlp_up, preferred_element_type=jnp.float32)
    activated, gelu_pull = jax.vjp(jax.nn.gelu, hidden)
    activated = activated.astype(jnp.bfloat16)
    after_three = after_two + settle(
        jnp.einsum("orf,fd->ord", activated, mlp_down, preferred_element_type=jnp.float32)
    )
    out_rows = after_three.astype(jnp.bfloat16)
    tokens_out = own_rows(out_rows)
    grid_cols = 4
    tile_rows = PLANE * grid_cols // tile_count
    tile_cols = PLANE // grid_cols
    channels = decoder.shape[1]
    spread_rows = row_count // tile_count
    arrived = lax.all_to_all(
        out_rows.reshape(objects, spread_rows, tile_count, features),
        "seq",
        split_axis=2,
        concat_axis=1,
        tiled=True,
    )
    tile_tokens = arrived.reshape(objects, row_count, features)
    tile_pixels = jnp.einsum(
        "okd,dcu->okcu", tile_tokens, decoder, preferred_element_type=jnp.float32
    ).astype(jnp.bfloat16)
    tile_index = lax.axis_index("seq")
    planes = to_planes(tile_pixels, tile_rows, tile_cols)
    from_right = take_rim(planes[..., 0], -1)
    from_right = jnp.where(
        tile_index % grid_cols == grid_cols - 1, jnp.zeros_like(from_right), from_right
    )
    widened = jnp.concatenate([planes, from_right[..., None]], axis=-1)
    from_below = take_rim(widened[..., 0, :], -grid_cols)
    window = jnp.concatenate([widened, from_below[..., None, :]], axis=-2)
    flat_window = window.reshape(objects, 3, channels, -1)
    sampled = jnp.einsum(
        "opce,opes->opcs", flat_window, sample_weights[:, :, 0], preferred_element_type=jnp.float32
    )
    sampled_out = sampled.astype(jnp.bfloat16)[:, :, :, None, :]
    grad_window = jnp.einsum(
        "opcs,opes->opce",
        sample_cot[:, :, :, 0],
        sample_weights[:, :, 0],
        preferred_element_type=jnp.float32,
    ).reshape(window.shape)
    below_back = give_rim(grad_window[..., -1, :], grid_cols)
    grad_wide = jnp.concatenate(
        [grad_window[..., :1, :] + below_back[..., None, :], grad_window[..., 1:-1, :]], axis=-2
    )
    right_back = give_rim(grad_wide[..., -1], 1)
    right_back = jnp.where(tile_index % grid_cols == 0, jnp.zeros_like(right_back), right_back)
    grad_planes = jnp.concatenate(
        [grad_wide[..., :1] + right_back[..., None], grad_wide[..., 1:-1]], axis=-1
    )
    grad_pixels = from_planes(grad_planes.astype(jnp.bfloat16), tile_rows, tile_cols)
    grad_decoder = jnp.einsum(
        "okd,okcu->dcu", tile_tokens, grad_pixels, preferred_element_type=jnp.float32
    )
    grad_tile = jnp.einsum(
        "okcu,dcu->okd", grad_pixels, decoder, preferred_element_type=jnp.float32
    )
    grad_top = (
        lax.all_to_all(
            grad_tile.reshape(objects, row_count, 1, features).astype(jnp.bfloat16),
            "seq",
            split_axis=1,
            concat_axis=2,
            tiled=True,
        )
        .astype(jnp.float32)
        .reshape(objects, row_count, features)
    )
    grad_three = cot_full + settle(grad_top)
    grad_out_one = grad_three.astype(jnp.bfloat16)
    grad_mlp_down = jnp.einsum(
        "orf,ord->fd", activated, grad_out_one, preferred_element_type=jnp.float32
    )
    grad_act = jnp.einsum("ord,fd->orf", grad_out_one, mlp_down, preferred_element_type=jnp.float32)
    grad_hidden = gelu_pull(grad_act)[0].astype(jnp.bfloat16)
    grad_mlp_up = jnp.einsum(
        "ord,orf->df", normed_three, grad_hidden, preferred_element_type=jnp.float32
    )
    grad_normed = settle(
        jnp.einsum("orf,df->ord", grad_hidden, mlp_up, preferred_element_type=jnp.float32)
    )
    grad_in, gain_three, shift_three = norm_back(
        after_two, norm_gains[2], norm_shifts[2], grad_normed
    )
    grad_two = grad_three + grad_in
    grad_out_two = grad_two.astype(jnp.bfloat16)
    grad_self_out = jnp.einsum(
        "ore,ord->ed", mixed_two, grad_out_two, preferred_element_type=jnp.float32
    )
    grad_mixed = jnp.einsum(
        "ord,ed->ore", grad_out_two, self_out, preferred_element_type=jnp.float32
    ).astype(jnp.bfloat16)
    grad_query, grad_key, grad_value = attend_back(
        heads_two[0], heads_two[1], heads_two[2], None, total_two, split_heads(grad_mixed)
    )
    grad_pair = return_keys(jnp.stack([grad_key, grad_value], axis=2).reshape(pair_two.shape))
    grad_triple = jnp.concatenate(
        [grad_query.reshape(objects, row_count, 1, -1), grad_pair], axis=2
    ).astype(jnp.bfloat16)
    grad_self_qkv = jnp.einsum(
        "ord,orje->dje", normed_two, grad_triple, preferred_element_type=jnp.float32
    )
    grad_normed = settle(
        jnp.einsum("orje,dje->ord", grad_triple, self_qkv, preferred_element_type=jnp.float32)
    )
    grad_in, gain_two, shift_two = norm_back(after_one, norm_gains[1], norm_shifts[1], grad_normed)
    grad_one = grad_two + grad_in
    grad_out_three = grad_one.astype(jnp.bfloat16)
    grad_cross_out = jnp.einsum(
        "ore,ord->ed", mixed_one, grad_out_three, preferred_element_type=jnp.float32
    )
    grad_mixed = jnp.einsum(
        "ord,ed->ore", grad_out_three, cross_out, preferred_element_type=jnp.float32
    ).astype(jnp.bfloat16)
    grad_query, grad_key, grad_value = attend_back(
        heads_one[0], heads_one[1], heads_one[2], key_mask, total_one, split_heads(grad_mixed)
    )
    grad_pair = return_keys(
        jnp.stack([grad_key, grad_value], axis=2).reshape(pair_one.shape)
    ).astype(jnp.bfloat16)
    grad_cross_kv = jnp.einsum(
        "osi,osje->ije", patches, grad_pair, preferred_element_type=jnp.float32
    )
    patch_part = jnp.einsum(
        "osje,ije->osi", grad_pair, cross_kv, preferred_element_type=jnp.float32
    )
    grad_query = grad_query.reshape(query_one.shape).astype(jnp.bfloat16)
    grad_cross_query = jnp.einsum(
        "ord,ore->de", normed_one, grad_query, preferred_element_type=jnp.float32
    )
    grad_normed = settle(
        jnp.einsum("ore,de->ord", grad_query, cross_query, preferred_element_type=jnp.float32)
    )
    grad_in, gain_one, shift_one = norm_back(inputs, norm_gains[0], norm_shifts[0], grad_normed)
    grad_inputs = grad_one + grad_in
    gain_grads = jnp.stack([gain_one, gain_two, gain_three])
    shift_grads = jnp.stack([shift_one, shift_two, shift_three])
    patch_grad = lax.psum(patch_part.astype(jnp.bfloat16), "mp").astype(jnp.float32)
    grad_tokens = own_rows(grad_inputs)
    reduced = (
        lax.psum_scatter(
            gain_grads.astype(jnp.bfloat16), "seq", scatter_dimension=1, tiled=True
        ).astype(jnp.float32),
        lax.psum_scatter(
            shift_grads.astype(jnp.bfloat16), "seq", scatter_dimension=1, tiled=True
        ).astype(jnp.float32),
        lax.psum_scatter(
            grad_cross_query.astype(jnp.bfloat16), "seq", scatter_dimension=0, tiled=True
        ).astype(jnp.float32),
        lax.psum_scatter(
            grad_cross_kv.astype(jnp.bfloat16), "seq", scatter_dimension=0, tiled=True
        ).astype(jnp.float32),
        lax.psum_scatter(
            grad_cross_out.astype(jnp.bfloat16), "seq", scatter_dimension=1, tiled=True
        ).astype(jnp.float32),
        lax.psum_scatter(
            grad_self_qkv.astype(jnp.bfloat16), "seq", scatter_dimension=0, tiled=True
        ).astype(jnp.float32),
        lax.psum_scatter(
            grad_self_out.astype(jnp.bfloat16), "seq", scatter_dimension=1, tiled=True
        ).astype(jnp.float32),
        lax.psum_scatter(
            grad_mlp_up.astype(jnp.bfloat16), "seq", scatter_dimension=0, tiled=True
        ).astype(jnp.float32),
        lax.psum_scatter(
            grad_mlp_down.astype(jnp.bfloat16), "seq", scatter_dimension=1, tiled=True
        ).astype(jnp.float32),
        lax.psum_scatter(
            grad_decoder.astype(jnp.bfloat16), "seq", scatter_dimension=0, tiled=True
        ).astype(jnp.float32),
    )
    return (
        tokens_out,
        sampled_out,
        grad_tokens,
        patch_grad,
        reduced[0],
        reduced[1][:2],
        reduced[1][2],
        reduced[2],
        reduced[3],
        reduced[4],
        reduced[5],
        reduced[6],
        reduced[7],
        reduced[8],
        reduced[9],
    )


def solution(mesh):
    return jax.shard_map(
        per_device,
        mesh=mesh,
        in_specs=(
            P(None, "seq", None),
            P(None, "seq", None),
            P(),
            P(),
            P(),
            P(None, "mp"),
            P(None, None, "mp"),
            P("mp", None),
            P(None, None, "mp"),
            P("mp", None),
            P(None, "mp"),
            P("mp", None),
            P(None, "mp", None),
            P(None, None, "seq", None, None),
            P(None, "seq", None),
            P(None, None, "mp", "seq", None),
        ),
        out_specs=(
            P(None, ("seq", "mp"), None),
            P(None, None, "mp", "seq", None),
            P(None, ("seq", "mp"), None),
            P(None, "seq", None),
            P(None, "seq"),
            P(None, "seq"),
            P("seq"),
            P("seq", "mp"),
            P("seq", None, "mp"),
            P("mp", "seq"),
            P("seq", None, "mp"),
            P("mp", "seq"),
            P("seq", "mp"),
            P("mp", "seq"),
            P("seq", "mp", None),
        ),
        check_vma=False,
    )
```

profile of v0, /device:TPU:0, one launch (start us, length us, event | category | flops | bytes accessed | tf_op | source)
XLA Modules:
  0.0 2914.5 jit_solution(172080898485261352)
XLA Ops:
  22.9 50.0 %all-gather.3.cloned.1.call-done = bf16[6,1536,2,256]{3,1,2,0:T(8,128)(2,1)} async-done(((bf16[6,192,2,256]{3,1,2,0:T(8,128)(2,1)}), bf16[6,1536,2,256]{3,1,2,0:T(8,128)(2,1)}) %all-gather.3.cloned.1.call-update) | async-done | bytes 9437200 | tf_op jit(solution)/shard_map/all_gather | solution.py:96
  94.2 22.9 fusion.162
  117.2 18.3 fusion.7
  135.6 21.5 fusion.95
  161.9 171.8 %all-reduce.10.cloned.1.call-done = bf16[6,384,1024]{2,1,0:T(8,128)(2,1)} async-done(((bf16[6,384,1024]{2,1,0:T(8,128)(2,1)}), bf16[6,384,1024]{2,1,0:T(8,128)(2,1)}) %all-reduce.10.cloned.1.call-update) | async-done | bytes 4718608 | tf_op jit(solution)/shard_map/psum | solution.py:92
  411.8 108.6 %all_to_all.33 = bf16[6,384,1,1024]{3,0,2,1:T(8,128)(2,1)S(1)} all-to-all(bf16[6,384,1,1024]{3,0,2,1:T(8,128)(2,1)S(1)} %copy.219), channel_id=1, replica_groups=mesh['seq'=8,'mp'=4] {'seq'}, dimensions={1} | all-to-all | bytes 9437184 | tf_op jit(solution)/shard_map/all_to_all | solution.py:246
  526.6 15.2 fusion.157
  541.9 41.4 %multiply_reduce_fusion.1 = (f32[6,4,384]{2,1,0:T(4,128)S(1)}, f32[6,4,384,3072]{3,2,1,0:T(8,128)}) fusion(bf16[6,384,4,64]{1,3,2,0:T(8,128)(2,1)S(1)} %bitcast.291, bf16[6,3072,4,64]{1,3,2,0:T(8,128)(2,1)} %bitcast.269), kind=kOutput, calls=%fused_computation.6 | convolution fusion | flops 3680492544 | bytes 123899904 | tf_op jit(solution)/shard_map/orhd,okhd->ohrk/dot_general | solution.py:40
  583.3 34.8 %fusion = f32[6,4,384]{2,1,0:T(4,128)S(1)} fusion(f32[6,4,384,3072]{3,2,1,0:T(8,128)} %get-tuple-element.120, f32[6,4,384]{2,1,0:T(4,128)S(1)} %get-tuple-element.119), kind=kLoop, calls=%fused_computation.5 | loop fusion | flops 84925440 | bytes 113319936 | tf_op jit(solution)/shard_map/reduce_sum | solution.py:52
  618.1 40.5 %fusion.96 = bf16[6,4,64,384]{3,2,1,0:T(8,128)(2,1)S(1)} fusion(bf16[6,3072,4,64]{1,3,2,0:T(8,128)(2,1)} %bitcast.273, f32[6,4,384,3072]{3,2,1,0:T(8,128)} %get-tuple-element.120, f32[6,4,384]{2,1,0:T(4,128)S(1)} %fusion, f32[6,4,384]{2,1,0:T(4,128)S(1)} %get-tuple-element.119), kind=kOutput, calls=%fused_computation.143 | convolution fusion | flops 3737714688 | bytes 123936768 | tf_op jit(solution)/shard_map/ohrk,okhd->orhd/dot_general | solution.py:54
  664.0 324.1 %all-reduce.20.cloned.1.call-done = (bf16[6,384,1024]{2,1,0:T(8,128)(2,1)}, bf16[6,384,1024]{2,1,0:T(8,128)(2,1)}) async-done(((bf16[6,384,1024]{2,1,0:T(8,128)(2,1)}, bf16[6,384,1024]{2,1,0:T(8,128)(2,1)}), (bf16[6,384,1024]{2,1,0:T(8,128)(2,1)}, bf16[6,384,1024]{2,1,0:T(8,128)(2,1)})) %all-reduce.20.cloned.1.call-update) | async-done | bytes 9437200 | tf_op jit(solution)/shard_map/psum | solution.py:92
  988.2 10.6 fusion.156
  1012.9 13.5 fusion.36
  1026.4 9.2 convolution_convert_fusion
  1035.9 170.9 %all-reduce.12.cloned.1.call-done = bf16[6,384,1024]{2,1,0:T(8,128)(2,1)} async-done(((bf16[6,384,1024]{2,1,0:T(8,128)(2,1)}), bf16[6,384,1024]{2,1,0:T(8,128)(2,1)}) %all-reduce.12.cloned.1.call-update) | async-done | bytes 4718608 | tf_op jit(solution)/shard_map/psum | solution.py:92
  1233.7 41.0 %fusion.42 = bf16[6,4,64,3072]{3,2,1,0:T(8,128)(2,1)} fusion(bf16[6,384,4,64]{1,3,2,0:T(8,128)(2,1)S(1)} %bitcast.293, f32[6,4,384,3072]{3,2,1,0:T(8,128)} %get-tuple-element.120, f32[6,4,384]{2,1,0:T(4,128)S(1)} %bitcast.319), kind=kOutput, calls=%fused_computation.82 | convolution fusion | flops 3713531904 | bytes 123899904 | tf_op jit(solution)/shard_map/ohrk,orhd->okhd/dot_general | solution.py:77
  1274.7 82.1 %multiply_reduce_fusion = (f32[6,4,384]{2,1,0:T(4,128)S(1)}, f32[6,4,384,3072]{3,2,1,0:T(8,128)}) fusion(f32[6,4,384,3072]{3,2,1,0:T(8,128)} %get-tuple-element.120, f32[6,4,384]{2,1,0:T(4,128)S(1)} %bitcast.320, bf16[6,384,4,64]{1,3,2,0:T(8,128)(2,1)S(1)} %bitcast.294, bf16[6,3072,4,64]{1,3,2,0:T(8,128)(2,1)} %bitcast.274), kind=kOutput, calls=%fused_computation.1 | convolution fusion | flops 3737115648 | bytes 237182976 | tf_op jit(solution)/shard_map/orhd,okhd->ohrk/dot_general | solution.py:64
  1356.9 12.6 copy.222
  1369.5 88.1 %multiply_convert_fusion = bf16[6,4,384,3072]{3,2,1,0:T(8,128)(2,1)} fusion(f32[6,4,384,3072]{3,2,1,0:T(8,128)} %get-tuple-element.122, f32[6,4,384,3072]{3,2,1,0:T(8,128)} %get-tuple-element.120, f32[6,4,384]{2,1,0:T(4,128)S(1)} %get-tuple-element.121, f32[6,4,384]{2,1,0:T(4,128)S(1)} %bitcast.321), kind=kLoop, calls=%fused_computation | loop fusion | flops 141557760 | bytes 283189248 | tf_op jit(solution)/shard_map/convert_element_type | solution.py:68
  1457.6 25.0 multiply_convert_fusion.2
  1482.6 12.6 copy.221
  1495.2 16.5 pad_maximum_fusion
  1511.8 33.9 %multiply_convert_fusion.6 = bf16[6,4,64,384]{3,2,1,0:T(8,128)(2,1)S(1)} fusion(bf16[6,3072,4,64]{1,3,2,0:T(8,128)(2,1)} %bitcast.270, bf16[6,4,384,3072]{3,2,1,0:T(8,128)(2,1)} %multiply_convert_fusion), kind=kOutput, calls=%fused_computation.120 | convolution fusion | flops 3625058304 | bytes 67239936 | tf_op jit(solution)/shard_map/ohrk,okhd->orhd/dot_general | solution.py:70
  1546.4 90.3 %reduce-scatter.24.cloned.1.call-done = bf16[6,384,2,256]{3,1,2,0:T(8,128)(2,1)} async-done(((bf16[6,3072,2,256]{3,1,2,0:T(8,128)(2,1)}), bf16[6,384,2,256]{3,1,2,0:T(8,128)(2,1)}) %reduce-scatter.24.cloned.1.call-update) | async-done | bytes 2359312 | tf_op jit(solution)/shard_map/reduce_scatter | solution.py:100
  1645.0 172.0 %all-reduce.14.cloned.1.call-done = bf16[6,384,1024]{2,1,0:T(8,128)(2,1)} async-done(((bf16[6,384,1024]{2,1,0:T(8,128)(2,1)}), bf16[6,384,1024]{2,1,0:T(8,128)(2,1)}) %all-reduce.14.cloned.1.call-update) | async-done | bytes 4718608 | tf_op jit(solution)/shard_map/psum | solution.py:92
  1824.2 9.1 fusion.28
  1845.4 22.8 fusion.51
  1868.2 38.3 %multiply_reduce_fusion.2 = (f32[6,4,384]{2,1,0:T(4,128)S(1)}, f32[6,4,384,1536]{3,2,1,0:T(8,128)}) fusion(f32[6,4,384,1536]{3,2,1,0:T(8,128)} %get-tuple-element.118, f32[6,4,384]{2,1,0:T(4,128)S(1)} %bitcast.325, bf16[6,384,4,64]{1,3,2,0:T(8,128)(2,1)S(1)} %bitcast.296, bf16[6,1536,4,64]{1,3,2,0:T(8,128)(2,1)} %bitcast.287), kind=kOutput, calls=%fused_computation.10 | convolution fusion | flops 1854397440 | bytes 119218176 | tf_op jit(solution)/shard_map/orhd,okhd->ohrk/dot_general | solution.py:64
  1913.2 44.6 %multiply_convert_fusion.1 = bf16[6,4,384,1536]{3,2,1,0:T(8,128)(2,1)} fusion(f32[6,4,384,1536]{3,2,1,0:T(8,128)} %get-tuple-element.124, f32[6,4,384,1536]{3,2,1,0:T(8,128)} %get-tuple-element.118, f32[6,4,384]{2,1,0:T(4,128)S(1)} %get-tuple-element.123, f32[6,4,384]{2,1,0:T(4,128)S(1)} %bitcast.326), kind=kLoop, calls=%fused_computation.9 | loop fusion | flops 56623104 | bytes 141631488 | tf_op jit(solution)/shard_map/convert_element_type | solution.py:68
  1957.8 14.2 multiply_convert_fusion.3
  1978.6 8.3 pad_maximum_fusion.1
  1988.5 9.8 convolution_convert_fusion.1
  1998.3 16.1 multiply_convert_fusion.5
  2018.1 44.5 %reduce-scatter.26.cloned.1.call-done = bf16[6,192,2,256]{3,1,0,2:T(8,128)(2,1)} async-done(((bf16[6,1536,2,256]{3,1,0,2:T(8,128)(2,1)}), bf16[6,192,2,256]{3,1,0,2:T(8,128)(2,1)}) %reduce-scatter.26.cloned.1.call-update) | async-done | bytes 1179664 | tf_op jit(solution)/shard_map/reduce_scatter | solution.py:100
  2066.3 15.9 bitcast_convert_fusion.2
  2086.7 12.3 bitcast_convert_fusion.3
  2105.3 10.9 bitcast_convert_fusion.5
  2128.4 321.1 %all-reduce.18.cloned.1.call-done = (bf16[6,384,1024]{2,1,0:T(8,128)(2,1)}, bf16[6,384,1024]{2,1,0:T(8,128)(2,1)}, bf16[6,192,768]{2,1,0:T(8,128)(2,1)}) async-done(((bf16[6,384,1024]{2,1,0:T(8,128)(2,1)}, bf16[6,384,1024]{2,1,0:T(8,128)(2,1)}, bf16[6,192,768]{2,1,0:T(8,128)(2,1)}), (bf16[6,384,1024]{2,1,0:T(8,128)(2,1)}, bf16[6,384,1024]{2,1,0:T(8,128)(2,1)}, ...) | async-done | bytes 11206672 | tf_op jit(solution)/shard_map/psum | solution.py:92
  2477.6 32.2 %reduce-scatter.42.cloned.1.call-done = bf16[128,1024]{1,0:T(8,128)(2,1)} async-done(((bf16[1024,1024]{1,0:T(8,128)(2,1)}), bf16[128,1024]{1,0:T(8,128)(2,1)}) %reduce-scatter.42.cloned.1.call-update) | async-done | bytes 262160
  2511.8 53.3 %reduce-scatter.32.cloned.1.call-done = bf16[128,1024]{1,0:T(8,128)(2,1)} async-done(((bf16[1024,1024]{1,0:T(8,128)(2,1)}), bf16[128,1024]{1,0:T(8,128)(2,1)}) %reduce-scatter.32.cloned.1.call-update) | async-done | bytes 262160 | tf_op jit(solution)/shard_map/reduce_scatter | solution.py:349
  2570.0 32.2 %reduce-scatter.40.cloned.1.call-done = bf16[128,256]{1,0:T(8,128)(2,1)} async-done(((bf16[1024,256]{1,0:T(8,128)(2,1)}), bf16[128,256]{1,0:T(8,128)(2,1)}) %reduce-scatter.40.cloned.1.call-update) | async-done | bytes 65552
  2603.8 40.5 %reduce-scatter.30.cloned.1.call-done = bf16[128,3,256]{2,0,1:T(8,128)(2,1)} async-done(((bf16[1024,3,256]{2,0,1:T(8,128)(2,1)}), bf16[128,3,256]{2,0,1:T(8,128)(2,1)}) %reduce-scatter.30.cloned.1.call-update) | async-done | bytes 196624 | tf_op jit(solution)/shard_map/reduce_scatter | solution.py:343
  2649.3 32.4 %reduce-scatter.38.cloned.1.call-done = bf16[128,256]{1,0:T(8,128)(2,1)} async-done(((bf16[1024,256]{1,0:T(8,128)(2,1)}), bf16[128,256]{1,0:T(8,128)(2,1)}) %reduce-scatter.38.cloned.1.call-update) | async-done | bytes 65552
  2683.4 35.4 %reduce-scatter.28.cloned.1.call-done = bf16[128,256]{1,0:T(8,128)(2,1)} async-done(((bf16[1024,256]{1,0:T(8,128)(2,1)}), bf16[128,256]{1,0:T(8,128)(2,1)}) %reduce-scatter.28.cloned.1.call-update) | async-done | bytes 65552 | tf_op jit(solution)/shard_map/reduce_scatter | solution.py:334
  2720.3 58.0 %all-reduce.16.cloned.1.call-done = bf16[768,2,256]{2,1,0:T(2,128)(2,1)} async-done(((bf16[768,2,256]{2,1,0:T(2,128)(2,1)}), bf16[768,2,256]{2,1,0:T(2,128)(2,1)}) %all-reduce.16.cloned.1.call-update) | async-done | bytes 786448
  2806.1 17.6 reduce-scatter.36.cloned.1.call-done
  2842.8 17.4 reduce-scatter.34.cloned.1.call-done
  2884.3 21.7 reduce-scatter.44.cloned.1.call-done
  (371 shorter events, 361.7 us)
Async XLA Ops:
  7.2 996.6 %copy-start = (bf16[1024,1024]{1,0:T(8,128)(2,1)S(1)}, bf16[1024,1024]{1,0:T(8,128)(2,1)}, u32[]{:S(2)}) copy-start(bf16[1024,1024]{1,0:T(8,128)(2,1)} %param.26) | copy-start | bytes 6291460
  7.2 65.7 %all-gather.3.cloned.1.call-start = ((), (), s32[]{:S(2)}) async-start(), calls=%async_computation.13 | async-start | bytes 10616832 | tf_op jit(solution)/shard_map/all_gather | solution.py:96
  11.2 322.6 %all-reduce.10.cloned.1.call-start = ((), (), s32[]{:S(2)}) async-start(), calls=%async_computation.14 | async-start | bytes 9437184 | tf_op jit(solution)/shard_map/psum | solution.py:92
  18.9 62.1 %copy-start.57 = (f32[1,1024]{1,0:T(1,128)}, f32[1,1024]{1,0:T(1,128)S(1)}, u32[]{:S(2)}) copy-start(f32[1,1024]{1,0:T(1,128)S(1)} %get-tuple-element.112) | copy-start | bytes 12292
  18.9 324.8 %copy-start.52 = (f32[1,1024]{1,0:T(1,128)}, f32[1,1024]{1,0:T(1,128)S(1)}, u32[]{:S(2)}) copy-start(f32[1,1024]{1,0:T(1,128)S(1)} %get-tuple-element.113) | copy-start | bytes 12292
  19.5 61.5 %copy-start.63 = (f32[1,1024]{1,0:T(1,128)}, f32[1,1024]{1,0:T(1,128)S(1)}, u32[]{:S(2)}) copy-start(f32[1,1024]{1,0:T(1,128)S(1)} %get-tuple-element.115) | copy-start | bytes 12292
  19.5 324.2 %copy-start.65 = (f32[1,1024]{1,0:T(1,128)}, f32[1,1024]{1,0:T(1,128)S(1)}, u32[]{:S(2)}) copy-start(f32[1,1024]{1,0:T(1,128)S(1)} %get-tuple-element.116) | copy-start | bytes 12292
  22.9 71.4 %copy-start.18 = (bf16[6,384,256]{1,2,0:T(8,128)(2,1)}, bf16[6,384,256]{1,2,0:T(8,128)(2,1)S(1)}, u32[]{:S(2)}) copy-start(bf16[6,384,256]{1,2,0:T(8,128)(2,1)S(1)} %fusion.92) | copy-start | bytes 3538948
  161.7 182.0 %slice-start = ((s8[4718592]{0:T(1024)(128)(4,1)}), s8[524288]{0:T(1024)(128)(4,1)S(1)}, s32[]{:S(2)}) async-start(s8[4718592]{0:T(1024)(128)(4,1)} %bitcast.261), calls=%async_computation.32 | async-start | bytes 1048576
  161.7 364.9 %all-gather.5.cloned.1.call-start = ((), (), s32[]{:S(2)}) async-start(), calls=%async_computation.15 | async-start | bytes 21233664 | tf_op jit(solution)/shard_map/all_gather | solution.py:96
  352.6 635.6 %all-reduce.20.cloned.1.call-start = ((), (), s32[]{:S(2)}) async-start(), calls=%async_computation.31 | async-start | bytes 18874368 | tf_op jit(solution)/shard_map/psum | solution.py:92
  363.7 20.2 collective-permute-start.2
  394.2 3.3 collective-permute-start.3
  526.6 56.7 %copy-start.11 = (bf16[6,384,1,256]{1,3,2,0:T(8,128)(2,1)}, bf16[6,384,1,256]{1,3,2,0:T(8,128)(2,1)S(1)}, u32[]{:S(2)}) copy-start(bf16[6,384,1,256]{1,3,2,0:T(8,128)(2,1)S(1)} %slice.96) | copy-start | bytes 3538948
  658.6 340.2 %copy-start.16 = (bf16[6,4,64,384]{3,2,1,0:T(8,128)(2,1)}, bf16[6,4,64,384]{3,2,1,0:T(8,128)(2,1)S(1)}, u32[]{:S(2)}) copy-start(bf16[6,4,64,384]{3,2,1,0:T(8,128)(2,1)S(1)} %fusion.96) | copy-start | bytes 3538948
  663.6 543.2 %all-reduce.12.cloned.1.call-start = ((), (), s32[]{:S(2)}) async-start(), calls=%async_computation.16 | async-start | bytes 9437184 | tf_op jit(solution)/shard_map/psum | solution.py:92
  998.8 223.0 %copy-start.34 = (f32[6,384]{1,0:T(8,128)}, f32[6,384]{1,0:T(8,128)S(1)}, u32[]{:S(2)}) copy-start(f32[6,384]{1,0:T(8,128)S(1)} %broadcast_multiply_fusion) | copy-start | bytes 27652
  1003.8 218.1 %copy-start.44 = (f32[6,384]{1,0:T(8,128)}, f32[6,384]{1,0:T(8,128)S(1)}, u32[]{:S(2)}) copy-start(f32[6,384]{1,0:T(8,128)S(1)} %fusion.148) | copy-start | bytes 27652
  1035.6 601.0 %reduce-scatter.24.cloned.1.call-start = ((), (), s32[]{:S(2)}) async-start(), calls=%async_computation.17 | async-start | bytes 21233664 | tf_op jit(solution)/shard_map/reduce_scatter | solution.py:100
  1369.5 88.1 %copy-start.12 = (bf16[6,384,1,256]{1,3,2,0:T(8,128)(2,1)S(1)}, bf16[6,384,1,256]{1,3,2,0:T(8,128)(2,1)}, u32[]{:S(2)}) copy-start(bf16[6,384,1,256]{1,3,2,0:T(8,128)(2,1)} %copy-done.11) | copy-start | bytes 3538948
  1511.8 305.2 %all-reduce.14.cloned.1.call-start = ((), (), s32[]{:S(2)}) async-start(), calls=%async_computation.18 | async-start | bytes 9437184 | tf_op jit(solution)/shard_map/psum | solution.py:92
  1546.3 98.5 %copy-start.26 = (bf16[6,384,1,256]{3,1,2,0:T(8,128)(2,1)}, bf16[6,384,1,256]{3,1,2,0:T(8,128)(2,1)S(1)}, u32[]{:S(2)}) copy-start(bf16[6,384,1,256]{3,1,2,0:T(8,128)(2,1)S(1)} %copy.223) | copy-start | bytes 3538948
  1546.3 98.6 %copy-start.30 = (f32[6,4,384]{2,1,0:T(4,128)S(1)}, f32[6,4,384]{2,1,0:T(4,128)}, u32[]{:S(2)}) copy-start(f32[6,4,384]{2,1,0:T(4,128)} %copy-done.29) | copy-start | bytes 110596
  1546.3 98.6 %copy-start.40 = (f32[6,4,384]{2,1,0:T(4,128)S(1)}, f32[6,4,384]{2,1,0:T(4,128)}, u32[]{:S(2)}) copy-start(f32[6,4,384]{2,1,0:T(4,128)} %copy-done.39) | copy-start | bytes 110596
  1546.4 270.6 %copy-start.32 = (f32[6,384]{1,0:T(8,128)S(1)}, f32[6,384]{1,0:T(8,128)}, u32[]{:S(2)}) copy-start(f32[6,384]{1,0:T(8,128)} %copy-done.31) | copy-start | bytes 27652
  1546.4 270.6 %copy-start.53 = (f32[1,1024]{1,0:T(1,128)S(1)}, f32[1,1024]{1,0:T(1,128)}, u32[]{:S(2)}) copy-start(f32[1,1024]{1,0:T(1,128)} %copy-done.52) | copy-start | bytes 12292
  1644.8 179.3 %copy-start.51 = (f32[6,384]{1,0:T(8,128)S(1)}, f32[6,384]{1,0:T(8,128)}, u32[]{:S(2)}) copy-start(f32[6,384]{1,0:T(8,128)} %copy-done.50) | copy-start | bytes 27652
  1644.8 179.3 %copy-start.42 = (f32[6,384]{1,0:T(8,128)S(1)}, f32[6,384]{1,0:T(8,128)}, u32[]{:S(2)}) copy-start(f32[6,384]{1,0:T(8,128)} %copy-done.41) | copy-start | bytes 27652
  1644.9 417.7 %reduce-scatter.26.cloned.1.call-start = ((), (), s32[]{:S(2)}) async-start(), calls=%async_computation.19 | async-start | bytes 10616832 | tf_op jit(solution)/shard_map/reduce_scatter | solution.py:100
  1913.2 44.6 %copy-start.19 = (bf16[6,384,256]{1,2,0:T(8,128)(2,1)S(1)}, bf16[6,384,256]{1,2,0:T(8,128)(2,1)}, u32[]{:S(2)}) copy-start(bf16[6,384,256]{1,2,0:T(8,128)(2,1)} %copy-done.18) | copy-start | bytes 3538948
  1986.9 462.6 %all-reduce.18.cloned.1.call-start = ((), (), s32[]{:S(2)}) async-start(), calls=%async_computation.30 | async-start | bytes 22413312 | tf_op jit(solution)/shard_map/psum | solution.py:92
  1998.2 64.3 %copy-start.73 = (bf16[768,2,256]{2,1,0:T(2,128)(2,1)S(1)}, bf16[768,2,256]{2,1,0:T(2,128)(2,1)}, u32[]{:S(2)}) copy-start(bf16[768,2,256]{2,1,0:T(2,128)(2,1)} %param.22) | copy-start | bytes 2359300
  2066.2 443.6 %reduce-scatter.42.cloned.1.call-start = ((), (), s32[]{:S(2)}) async-start(), calls=%async_computation.27 | async-start | bytes 2359296
  2086.2 478.9 %reduce-scatter.32.cloned.1.call-start = ((), (), s32[]{:S(2)}) async-start(), calls=%async_computation.22 | async-start | bytes 2359296 | tf_op jit(solution)/shard_map/reduce_scatter | solution.py:349
  2099.0 503.2 %reduce-scatter.40.cloned.1.call-start = ((), (), s32[]{:S(2)}) async-start(), calls=%async_computation.26 | async-start | bytes 589824
  2105.2 539.1 %reduce-scatter.30.cloned.1.call-start = ((), (), s32[]{:S(2)}) async-start(), calls=%async_computation.21 | async-start | bytes 1769472 | tf_op jit(solution)/shard_map/reduce_scatter | solution.py:343
  2116.2 565.5 %reduce-scatter.38.cloned.1.call-start = ((), (), s32[]{:S(2)}) async-start(), calls=%async_computation.25 | async-start | bytes 589824
  2122.7 596.1 %reduce-scatter.28.cloned.1.call-start = ((), (), s32[]{:S(2)}) async-start(), calls=%async_computation.20 | async-start | bytes 589824 | tf_op jit(solution)/shard_map/reduce_scatter | solution.py:334
  2463.2 361.3 %all-to-all-start = ((bf16[6,48,8,1024]{3,1,0,2:T(8,128)(2,1)}), bf16[6,48,8,1024]{3,1,0,2:T(8,128)(2,1)}, u32[]{:S(2)}, u32[]{:S(2)}) async-start(bf16[6,48,8,1024]{3,1,0,2:T(8,128)(2,1)} %copy.200), calls=%async_computation | async-start | bytes 9437184 | tf_op jit(solution)/shard_map/all_to_all | solution.py:198
  2468.0 102.0 %copy-start.61 = (bf16[1024]{0:T(1024)(128)(2,1)S(1)}, bf16[1024]{0:T(1024)(128)(2,1)}, u32[]{:S(2)}) copy-start(bf16[1024]{0:T(1024)(128)(2,1)} %get-tuple-element.92) | copy-start | bytes 6148
  2468.0 310.3 %all-reduce.16.cloned.1.call-start = ((), (), s32[]{:S(2)}) async-start(), calls=%async_computation.29 | async-start | bytes 1572864
  2470.8 178.5 %copy-start.62 = (bf16[1024]{0:T(1024)(128)(2,1)S(1)}, bf16[1024]{0:T(1024)(128)(2,1)}, u32[]{:S(2)}) copy-start(bf16[1024]{0:T(1024)(128)(2,1)} %get-tuple-element.90) | copy-start | bytes 6148
  2472.6 351.1 %reduce-scatter.36.cloned.1.call-start = ((), (), s32[]{:S(2)}) async-start(), calls=%async_computation.24 | async-start | bytes 294912
  2646.0 145.6 %copy-start.24 = (bf16[6,192,768]{2,1,0:T(8,128)(2,1)S(1)}, bf16[6,192,768]{2,1,0:T(8,128)(2,1)}, u32[]{:S(2)}) copy-start(bf16[6,192,768]{2,1,0:T(8,128)(2,1)} %get-tuple-element.98) | copy-start | bytes 5308420
  2790.7 69.5 %reduce-scatter.34.cloned.1.call-start = ((), (), s32[]{:S(2)}) async-start(), calls=%async_computation.23 | async-start | bytes 294912
  2793.8 112.2 %reduce-scatter.44.cloned.1.call-start = ((), (), s32[]{:S(2)}) async-start(), calls=%async_computation.28 | async-start | bytes 294912
  2840.4 21.2 collective-permute-start
  2862.8 7.4 collective-permute-start.1
  (68 other events, 662.4 us)
Sparse Core Ops, SparseCore 0:
  11.3 61.5 all-gather.2
  161.8 171.9 all-reduce.9
  352.7 161.5 all-gather.4
  663.7 324.4 all-reduce.19
  1035.7 170.9 all-reduce.11
  1511.9 124.7 reduce-scatter.23
  1645.0 171.9 all-reduce.13
  1987.0 75.4 reduce-scatter.25
  2066.3 383.1 all-reduce.17
  2453.2 56.5 reduce-scatter.41
  2514.0 51.0 reduce-scatter.31
  2568.0 34.1 reduce-scatter.39
  2605.8 38.4 reduce-scatter.29
  2647.6 34.1 reduce-scatter.37
  2684.7 34.0 reduce-scatter.27
  2722.7 55.5 all-reduce.15
  2790.8 32.8 reduce-scatter.35
  2826.6 33.5 reduce-scatter.33
  2870.3 35.6 reduce-scatter.43
where the time goes:
time: 2930 us; the launch traced here: 2910 us
  waiting for transfers between devices  1690 us (58%)
  matrix products  553 us (19%)
  other arithmetic  345 us (12%)
  local copies, waits for them, and re-layouts  191 us (7%)
  blocking collectives  109 us (4%)
    psum x5, waiting for transfers between devices, settle(): return lax.psum(operand.astype(jnp.bfloat16), 'mp').astype(jnp.float32)  1160 us
    unnamed x26, waiting for transfers between devices  212 us
    reduce_scatter x2, waiting for transfers between devices, return_keys(): lax.psum_scatter(operand.astype(jnp.bfloat16), 'seq', scatter_dimension=1...  135 us
    convert_element_type x2, other arithmetic, attend_back(): grad_scores = (prob_full * (grad_probs - centred)).astype(jnp.bfloat16)  133 us
    dot_general x2, matrix products, attend_back(): jnp.einsum('orhd,okhd->ohrk', grad_mixed, value_rows, preferred_element_t...  120 us
    all_to_all x1, blocking collectives, per_device(): lax.all_to_all(grad_tile.reshape(objects, row_count, 1, features).astype(...  109 us
    dot_general x2, matrix products, head_scores(): jnp.einsum('orhd,okhd->ohrk', queries, key_rows, preferred_element_type=j...  64.4 us
    dot_general x2, matrix products, attend_back(): jnp.einsum('ohrk,orhd->okhd', prob_full.astype(jnp.bfloat16), grad_mixed,...  63.8 us
  transfers between devices with their start and end apart: 24, of which 18 were waited for; matrix products, arithmetic and copies ran while one was open for 10% of the time, Pallas kernels for 0%

commit v1 on v0

v1 whole, which is shorter than its diff:
```python
import functools
import math

import jax
import jax.numpy as jnp
from jax import lax
from jax.experimental import pallas as pl
from jax.experimental.pallas import tpu as pltpu
from jax.sharding import PartitionSpec as P


PLANE = 32
HD = 64
LANES = 128
norm_eps = 1e-05
f32 = jnp.float32
bf16 = jnp.bfloat16

NT = (((1,), (1,)), ((), ()))
NN = (((1,), (0,)), ((), ()))
TN = (((0,), (0,)), ((), ()))


def dot(a, b, dims):
    return lax.dot_general(a, b, dims, preferred_element_type=f32)


def mm(a, b):
    return jnp.dot(a, b, preferred_element_type=f32)


def split3(v):
    hi = v.astype(bf16).astype(f32)
    rest = v - hi
    mid = rest.astype(bf16).astype(f32)
    return hi, mid, rest - mid


def spread(base, cols):
    lane = lax.broadcasted_iota(jnp.int32, (base.shape[0], HD), 1)
    tail = jnp.zeros((base.shape[0], HD), f32)
    for at, col in cols.items():
        tail = jnp.where(lane == at, col, tail)
    return jnp.concatenate([base, tail], axis=1).astype(bf16)


def load_keys(n_ref, kv_specs, refs, ka, va, hpd, blocks):
    for ref_at, rows, k_at, v_at, base in kv_specs:
        src = refs[ref_at]

        def build(i, _):
            natural = base + (i ^ n_ref[1]) * rows
            dst = pl.ds(pl.multiple_of(natural, 16), rows)
            slot = natural + lax.broadcasted_iota(jnp.int32, (rows, 1), 0)
            mask = jnp.where(slot < n_ref[0], 0.0, -1e30).astype(f32)
            for h in range(hpd):
                k = src[i, k_at[0] : k_at[0] + rows, k_at[1] + h * HD : k_at[1] + (h + 1) * HD]
                v = src[i, v_at[0] : v_at[0] + rows, v_at[1] + h * HD : v_at[1] + (h + 1) * HD]
                ka[h, dst, :] = spread(k.astype(f32), {0: 1.0, 1: 1.0, 2: 1.0, 3: mask})
                va[h, dst, :] = spread(v.astype(f32), {0: 1.0, 1: 1.0, 2: 1.0})
            return 0

        lax.fori_loop(0, blocks, build, 0)


def fwd_kernel(n_ref, *refs, n_in, blocks, q_spec, kv_specs, hpd, bq, kc, fixed):
    ins, (o_ref, qa_ref, ka, va) = refs[:n_in], refs[n_in:]
    load_keys(n_ref, kv_specs, ins, ka, va, hpd, blocks)
    q_at, rows_q, q_off, q_lane = q_spec

    def build(i, _):
        dst = pl.ds(pl.multiple_of((i ^ n_ref[1]) * rows_q, 16), rows_q)
        for h in range(hpd):
            q = ins[q_at][i, q_off : q_off + rows_q, q_lane + h * HD : q_lane + (h + 1) * HD]
            qa_ref[h, dst, :] = spread(q.astype(f32) * (1.0 / math.sqrt(HD)), {3: 1.0})
        return 0

    lax.fori_loop(0, blocks, build, 0)
    total = ka.shape[1]

    def block(b, _):
        rows = pl.ds(pl.multiple_of(b * bq, bq), bq)

        def chunk(c, carry):
            cols = pl.ds(pl.multiple_of(c * kc, kc), kc)
            out = []
            for h in range(hpd):
                m, acc = carry[h]
                s = dot(qa_ref[h, rows, :], ka[h, cols, :], NT)
                top = jnp.maximum(m, jnp.max(s, axis=1, keepdims=True))
                p = jnp.exp(s - top).astype(bf16)
                out.append((top, acc * jnp.exp(m - top) + dot(p, va[h, cols, :], NN)))
            return tuple(out)

        carry = ((jnp.full((bq, 1), -1e30, f32), jnp.zeros((bq, LANES), f32)),) * hpd
        if fixed:
            for c in range(total // kc):
                carry = chunk(c, carry)
        else:
            carry = lax.fori_loop(0, (n_ref[0] + kc - 1) // kc, chunk, carry)
        outs = []
        for h in range(hpd):
            m, acc = carry[h]
            norm = acc[:, HD : HD + 1]
            outs.append(acc[:, :HD] / norm)
            hi, mid, lo = split3(-(m + jnp.log(norm)))
            qa_ref[h, rows, :] = spread(
                qa_ref[h, rows, :HD].astype(f32), {0: hi, 1: mid, 2: lo, 3: 1.0}
            )
        o_ref[rows, :] = jnp.concatenate(outs, axis=1).astype(bf16)
        return 0

    lax.fori_loop(0, qa_ref.shape[1] // bq, block, 0)


def bwd_kernel(n_ref, *refs, n_in, blocks, do_spec, kv_specs, hpd, bq, kc, fixed):
    ins, (dq_ref, dkv_ref, ka, va, da, dk, dv) = refs[:n_in], refs[n_in:]
    qa_ref, do_ref, o_ref = ins[:3]
    load_keys(n_ref, kv_specs, ins, ka, va, hpd, blocks)
    rows_q, do_off = do_spec

    def build(i, _):
        rows = pl.ds(pl.multiple_of(i * rows_q, 16), rows_q)
        for h in range(hpd):
            d = do_ref[i, do_off : do_off + rows_q, h * HD : (h + 1) * HD].astype(f32)
            o = o_ref[rows, h * HD : (h + 1) * HD].astype(f32)
            hi, mid, lo = split3(-jnp.sum(d * o, axis=1, keepdims=True))
            da[h, rows, :] = spread(d, {0: hi, 1: mid, 2: lo})
        return 0

    lax.fori_loop(0, blocks, build, 0)
    dk[...] = jnp.zeros_like(dk)
    dv[...] = jnp.zeros_like(dv)
    total = ka.shape[1]
    steps = total // kc if fixed else (n_ref[0] + kc - 1) // kc

    def block(b, _):
        rows = pl.ds(pl.multiple_of(b * bq, bq), bq)

        def chunk(c, dqs):
            cols = pl.ds(pl.multiple_of(c * kc, kc), kc)
            out = []
            for h in range(hpd):
                k, q, d = ka[h, cols, :], qa_ref[h, rows, :], da[h, rows, :]
                p = jnp.exp(dot(k, q, NT))
                dp = dot(va[h, cols, :], d, NT)
                dv[h, cols, :] += dot(p.astype(bf16), d, NN)
                g = (p * dp).astype(bf16)
                dk[h, cols, :] += dot(g, q, NN)
                out.append(dqs[h] + dot(k, g, TN))
            return tuple(out)

        dqs = lax.fori_loop(0, steps, chunk, (jnp.zeros((LANES, bq), f32),) * hpd)
        dq = jnp.concatenate([v[:HD, :] for v in dqs], axis=0).T
        dq_ref[rows, :] = (dq * (1.0 / math.sqrt(HD))).astype(bf16)
        return 0

    lax.fori_loop(0, qa_ref.shape[1] // bq, block, 0)
    step = total // blocks

    def finish(i, _):
        rows = pl.ds(pl.multiple_of(i * step, 16), step)
        parts = [dk[h, rows, :HD] for h in range(hpd)] + [dv[h, rows, :HD] for h in range(hpd)]
        dkv_ref[rows, :] = jnp.concatenate(parts, axis=1).astype(bf16)
        return 0

    lax.fori_loop(0, blocks, finish, 0)


VM = pl.BlockSpec(memory_space=pltpu.VMEM)
SM = pl.BlockSpec(memory_space=pltpu.SMEM)


def fit(rows, most):
    return math.gcd(rows, most)


def attend(limits, ins, blocks, q_spec, kv_specs, total, hpd, fixed):
    queries = blocks * q_spec[1]
    kc = fit(total, 1024 if fixed else 512)
    body = functools.partial(
        fwd_kernel,
        n_in=len(ins),
        blocks=blocks,
        q_spec=q_spec,
        kv_specs=kv_specs,
        hpd=hpd,
        bq=fit(queries, 512),
        kc=kc,
        fixed=fixed,
    )
    work = hpd * queries * total
    return pl.pallas_call(
        body,
        out_shape=(
            jax.ShapeDtypeStruct((queries, hpd * HD), bf16),
            jax.ShapeDtypeStruct((hpd, queries, LANES), bf16),
        ),
        in_specs=[SM] + [VM] * len(ins),
        out_specs=(VM, VM),
        scratch_shapes=[pltpu.VMEM((hpd, total, LANES), bf16)] * 2,
        compiler_params=pltpu.CompilerParams(vmem_limit_bytes=44 * 2**20),
        cost_estimate=pl.CostEstimate(
            flops=1024 * work, bytes_accessed=16 * queries * hpd * HD, transcendentals=work
        ),
    )(limits, *ins)


def attend_back(limits, ins, blocks, do_spec, kv_specs, total, hpd, fixed):
    queries = blocks * do_spec[0]
    body = functools.partial(
        bwd_kernel,
        n_in=len(ins),
        blocks=blocks,
        do_spec=do_spec,
        kv_specs=kv_specs,
        hpd=hpd,
        bq=fit(queries, 512),
        kc=fit(total, 512),
        fixed=fixed,
    )
    work = hpd * queries * total
    return pl.pallas_call(
        body,
        out_shape=(
            jax.ShapeDtypeStruct((queries, hpd * HD), bf16),
            jax.ShapeDtypeStruct((total, 2 * hpd * HD), bf16),
        ),
        in_specs=[SM] + [VM] * len(ins),
        out_specs=(VM, VM),
        scratch_shapes=[pltpu.VMEM((hpd, total, LANES), bf16)] * 2
        + [pltpu.VMEM((hpd, queries, LANES), bf16)]
        + [pltpu.VMEM((hpd, total, LANES), f32)] * 2,
        compiler_params=pltpu.CompilerParams(vmem_limit_bytes=52 * 2**20),
        cost_estimate=pl.CostEstimate(
            flops=2560 * work, bytes_accessed=24 * queries * hpd * HD, transcendentals=work
        ),
    )(limits, *ins)


def norm_parts(values):
    center = values - jnp.mean(values, axis=-1, keepdims=True)
    scale = lax.rsqrt(jnp.mean(center * center, axis=-1, keepdims=True) + norm_eps)
    return center * scale, scale


def layer_norm(values, gain_row, shift_row):
    return (norm_parts(values)[0] * gain_row + shift_row).astype(bf16)


def norm_back(values, gain_row, grad_out):
    unit, scale = norm_parts(values)
    lifted = grad_out * gain_row
    grad_in = scale * (
        lifted
        - jnp.mean(lifted, axis=-1, keepdims=True)
        - unit * jnp.mean(lifted * unit, axis=-1, keepdims=True)
    )
    return grad_in, jnp.sum(grad_out * unit, axis=0), jnp.sum(grad_out, axis=0)


def swap_seq(value):
    return lax.all_to_all(value, "seq", split_axis=0, concat_axis=0, tiled=True)


def swap_all(value):
    return lax.all_to_all(value, ("seq", "mp"), split_axis=0, concat_axis=0, tiled=True)


def swap_pair(value):
    count = lax.axis_size("mp")
    return lax.ppermute(value, "mp", [(i, i ^ 1) for i in range(count)])


def gather_rows(piece):
    return lax.all_gather(piece, ("mp", "seq"), axis=0, tiled=True)


def reduce_rows(value):
    return lax.psum_scatter(value.astype(bf16), "seq", scatter_dimension=0, tiled=True)


def reduce_cols(value):
    return lax.psum_scatter(value, "mp", scatter_dimension=1, tiled=True).astype(f32)


def from_behind(value, axis, steps):
    count = lax.axis_size(axis)
    initial, last = (max(0, -steps), min(count, count - steps))
    return lax.ppermute(value, axis, [(source, source + steps) for source in range(initial, last)])


def to_owner(value, rank, seq_rows):
    ranks = lax.axis_size("mp")
    pairs = ranks // 2
    pair, half = rank // 2, rank % 2
    own = seq_rows // ranks
    whole = lax.all_to_all(
        value[:seq_rows].reshape(ranks, own, -1), "mp", split_axis=0, concat_axis=0, tiled=True
    )
    blocks = value[seq_rows:].reshape(pairs, own, -1)
    arrived = []
    for step in range(pairs):
        moves = [(2 * p + h, pairs * h + (p ^ step)) for p in range(pairs) for h in range(2)]
        block = lax.dynamic_index_in_dim(blocks, pair ^ step, 0, keepdims=False)
        arrived.append(lax.ppermute(block, "mp", moves))
    arrived = jnp.stack(arrived)
    place = rank % pairs
    rows = []
    for p in range(pairs):
        rows += [
            whole[2 * p],
            lax.dynamic_index_in_dim(arrived, place ^ p, 0, keepdims=False),
            whole[2 * p + 1],
        ]
    return jnp.stack(rows)


def to_planes(tile_pixels, tile_rows, tile_cols):
    objects, channels = (tile_pixels.shape[0], tile_pixels.shape[2])
    cells = tile_pixels.reshape(objects, 3, tile_rows, tile_cols, channels, 2, 2)
    cells = cells.transpose(0, 1, 4, 2, 5, 3, 6)
    return cells.reshape(objects, 3, channels, 2 * tile_rows, 2 * tile_cols)


def from_planes(planes, tile_rows, tile_cols):
    objects, channels = (planes.shape[0], planes.shape[2])
    cells = planes.reshape(objects, 3, channels, tile_rows, 2, tile_cols, 2)
    cells = cells.transpose(0, 1, 3, 5, 2, 4, 6)
    return cells.reshape(objects, 3 * tile_rows * tile_cols, channels * 4)


def per_device(
    tokens,
    patches,
    counts,
    norm_gains,
    norm_shifts,
    cross_query,
    cross_kv,
    cross_out,
    self_qkv,
    self_out,
    mlp_up,
    mlp_down,
    decoder,
    sample_weights,
    tokens_cot,
    sample_cot,
):
    objects, R, D = tokens.shape
    S, M = lax.axis_size("seq"), lax.axis_size("mp")
    s, m = lax.axis_index("seq"), lax.axis_index("mp")
    pairs = M // 2
    if objects != 3 * pairs or S != 2 * M or D != 1024:
        raise ValueError("unexpected sizes")
    pair, half = m // 2, m % 2
    at_a, at_b = 3 * pair + 2 * half, 3 * pair + 1
    RB = R // 2
    RS = R + RB
    W = D // S
    hpd = W // HD
    slots, width = patches.shape[1], patches.shape[2]
    slot_total = slots * S
    row_total = R * S

    def pick(arr, a, b, h):
        first = lax.dynamic_index_in_dim(arr, a, 0, keepdims=False)
        second = lax.dynamic_slice_in_dim(
            lax.dynamic_index_in_dim(arr, b, 0, keepdims=False), h * RB, RB, 0
        )
        return jnp.concatenate([first, second], axis=0)

    def mine(arr, axis):
        share = arr.shape[axis] // S
        return lax.dynamic_slice_in_dim(arr, s * share, share, axis)

    w_cross_out = gather_rows(mine(cross_out, 0))
    qkv_piece = mine(self_qkv, 2).transpose(1, 2, 0)
    w_qkv = gather_rows(qkv_piece.reshape(-1, D)).reshape(S, M, 3, D // (M * S), D)
    w_qkv = w_qkv.transpose(0, 2, 1, 3, 4).reshape(3 * D, D)
    w_self_out = gather_rows(mine(self_out, 0))
    w_up = gather_rows(mine(mlp_up, 1).T)
    w_down = gather_rows(mine(mlp_down, 0))
    channels = decoder.shape[1]
    cu = 4 * channels
    dec = lax.all_gather(mine(decoder.reshape(D, cu), 0), ("seq", "mp"), axis=0, tiled=False)
    w_dec = dec.reshape(S, M, D // S, cu).transpose(0, 2, 1, 3).reshape(D, M * cu)
    w_query = gather_rows(mine(cross_query, 1).T)
    kv_piece = mine(cross_kv, 2).transpose(1, 2, 0)
    w_kv = gather_rows(kv_piece.reshape(-1, width)).reshape(S, M, 2, D // (M * S), width)
    w_kv = w_kv.transpose(0, 2, 1, 3, 4).reshape(2 * D, width)

    grid_cols = 4
    tile_rows, tile_cols = PLANE * grid_cols // S, PLANE // grid_cols
    ext_rows, ext_cols = 2 * tile_rows + 1, 2 * tile_cols + 1
    weights_in = sample_weights[:, :, 0]
    grad_window = jnp.einsum(
        "opcs,opes->opce", sample_cot[:, :, :, 0], weights_in, preferred_element_type=f32
    ).reshape(objects, 3, channels, ext_rows, ext_cols)
    below_back = from_behind(grad_window[..., -1, :], "seq", grid_cols)
    grad_wide = jnp.concatenate(
        [grad_window[..., :1, :] + below_back[..., None, :], grad_window[..., 1:-1, :]], axis=-2
    )
    right_back = from_behind(grad_wide[..., -1], "seq", 1)
    right_back = jnp.where(s % grid_cols == 0, jnp.zeros_like(right_back), right_back)
    grad_planes = jnp.concatenate(
        [grad_wide[..., :1] + right_back[..., None], grad_wide[..., 1:-1]], axis=-1
    )
    KA, KB = R // S, RB // S
    grad_pix = from_planes(grad_planes.astype(bf16), tile_rows, tile_cols)
    grad_pix = grad_pix.reshape(pairs, 3, S, KA, cu)
    gp_a = jnp.stack([grad_pix[:, 0], grad_pix[:, 2]], axis=1).transpose(2, 0, 1, 3, 4)
    gp_b = grad_pix[:, 1].reshape(pairs, S, 2, KB, cu).transpose(1, 0, 2, 3, 4)
    sent = jnp.concatenate([gp_a, gp_b], axis=3).reshape(S * M, KA + KB, cu)
    back = swap_all(sent).reshape(S, M, KA + KB, cu).transpose(2, 0, 1, 3)
    d_pix = back.reshape(RS, M * cu)

    n1_all = layer_norm(tokens.astype(f32), norm_gains[0], norm_shifts[0])
    q1 = jnp.einsum("ord,de->ore", n1_all, cross_query, preferred_element_type=f32).astype(bf16)
    kv1 = jnp.einsum("osi,ije->osje", patches, cross_kv, preferred_element_type=f32).astype(bf16)
    kv1 = kv1.reshape(objects, slots, 2, -1)
    arrived = []
    for step in range(S):
        to = s ^ step
        lane, rank = to % 2, to // 2
        a, b, h = 3 * (rank // 2) + 2 * (rank % 2), 3 * (rank // 2) + 1, rank % 2
        part = lax.dynamic_slice_in_dim(pick(q1, a, b, h), lane * W, W, 1)
        kv = []
        for o in (a, b):
            one = lax.dynamic_index_in_dim(kv1, o, 0, keepdims=False)
            one = lax.dynamic_slice_in_dim(one, lane * W, W, 2)
            kv += [one[:, 0], one[:, 1]]
        moves = []
        for i in range(S):
            for j in range(M):
                t = i ^ step
                moves.append((i * M + j, (2 * j + t % 2) * M + t // 2))
        arrived.append(lax.ppermute(jnp.concatenate([part] + kv, axis=0), ("seq", "mp"), moves))
    heads_one = jnp.stack(arrived)
    order = 2 * m + s % 2
    n_a = lax.dynamic_index_in_dim(counts, at_a, 0, keepdims=False)
    n_b = lax.dynamic_index_in_dim(counts, at_b, 0, keepdims=False)
    lim_a, lim_b = jnp.stack([n_a, order]), jnp.stack([n_b, order])
    q_a1, q_b1 = (0, R, 0, 0), (0, RB, R, 0)
    kv_a1 = (RS, 0), (RS + slots, 0)
    kv_b1 = (RS + 2 * slots, 0), (RS + 3 * slots, 0)
    o_a1, res_a1 = attend(
        lim_a, [heads_one], S, q_a1, [(0, slots) + kv_a1 + (0,)], slot_total, hpd, False
    )
    o_b1, res_b1 = attend(
        lim_b, [heads_one], S, q_b1, [(0, slots) + kv_b1 + (0,)], slot_total, hpd, False
    )

    def join(a, b):
        return jnp.concatenate([a.reshape(S, R, -1), b.reshape(S, RB, -1)], axis=1)

    def to_rows(value):
        return swap_seq(value).transpose(1, 0, 2).reshape(value.shape[1], -1)

    def to_heads(value):
        return swap_seq(value.reshape(value.shape[0], S, -1).transpose(1, 0, 2))

    x0 = pick(tokens, at_a, at_b, half).astype(f32)
    a1 = to_rows(join(o_a1, o_b1))
    x1 = x0 + mm(a1, w_cross_out)
    n2 = layer_norm(x1, norm_gains[1], norm_shifts[1])

    t2 = dot(n2, w_qkv, NT).astype(bf16)
    heads_two = to_heads(t2)
    pair_kv = swap_pair(heads_two[:, R:, W:])
    open_a = jnp.array([row_total, 0], jnp.int32)
    o_a2, res_a2 = attend(
        open_a, [heads_two], S, (0, R, 0, 0), [(0, R, (0, W), (0, 2 * W), 0)], row_total, hpd, True
    )
    kv_b2 = [(0, RB, (R, W), (R, 2 * W), 0), (1, RB, (0, 0), (0, W), row_total // 2)]
    o_b2, res_b2 = attend(
        open_a, [heads_two, pair_kv], S, (0, RB, R, 0), kv_b2, row_total, hpd, True
    )
    a2 = to_rows(join(o_a2, o_b2))
    x2 = x1 + mm(a2, w_self_out)
    n3 = layer_norm(x2, norm_gains[2], norm_shifts[2])

    u = dot(n3, w_up, NT)
    slope = math.sqrt(2.0 / math.pi)
    bend = jnp.tanh(slope * (u + 0.044715 * u * u * u))
    g = (0.5 * u * (1.0 + bend)).astype(bf16)
    rise = 0.5 * (1.0 + bend) + 0.5 * u * (1.0 - bend * bend) * slope * (1.0 + 0.134145 * u * u)
    rise = rise.astype(bf16)
    x3 = x2 + mm(g, w_down)
    x3b = x3.astype(bf16)
    tokens_out = to_owner(x3b, m, R)

    pix = mm(x3b, w_dec).astype(bf16).reshape(KA + KB, S, M, cu).transpose(1, 2, 0, 3)
    got = swap_all(pix.reshape(S * M, KA + KB, cu)).reshape(S, pairs, 2, KA + KB, cu)
    px_a = got[:, :, :, :KA].transpose(1, 2, 0, 3, 4).reshape(pairs, 2, S * KA, cu)
    px_b = got[:, :, :, KA:].transpose(1, 0, 2, 3, 4).reshape(pairs, S * KA, cu)
    tile = jnp.stack([px_a[:, 0], px_b, px_a[:, 1]], axis=1)
    planes = to_planes(tile.reshape(objects, S * KA, channels, 4), tile_rows, tile_cols)
    from_right = from_behind(planes[..., 0], "seq", -1)
    from_right = jnp.where(s % grid_cols == grid_cols - 1, jnp.zeros_like(from_right), from_right)
    widened = jnp.concatenate([planes, from_right[..., None]], axis=-1)
    from_below = from_behind(widened[..., 0, :], "seq", -grid_cols)
    window = jnp.concatenate([widened, from_below[..., None, :]], axis=-2)
    sampled = jnp.einsum(
        "opce,opes->opcs",
        window.reshape(objects, 3, channels, -1),
        weights_in,
        preferred_element_type=f32,
    ).astype(bf16)[:, :, :, None, :]

    d3 = pick(tokens_cot, at_a, at_b, half).astype(f32) + dot(d_pix, w_dec, NT)
    e3 = d3.astype(bf16)
    du = (dot(e3, w_down, NT) * rise.astype(f32)).astype(bf16)
    grad_decoder = reduce_rows(dot(x3b, d_pix, TN))
    grad_mlp_down = reduce_rows(dot(e3, g, TN))
    grad_mlp_up = reduce_rows(dot(n3, du, TN))
    grad_in, gain_three, shift_three = norm_back(x2, norm_gains[2], mm(du, w_up))
    d2 = d3 + grad_in
    e2 = d2.astype(bf16)

    da2 = to_heads(dot(e2, w_self_out, NT).astype(bf16))
    grad_self_out = reduce_rows(dot(e2, a2, TN))
    dq_a2, dkv_a2 = attend_back(
        open_a,
        [res_a2, da2, o_a2, heads_two],
        S,
        (R, 0),
        [(3, R, (0, W), (0, 2 * W), 0)],
        row_total,
        hpd,
        True,
    )
    kv_b2 = [(3, RB, (R, W), (R, 2 * W), 0), (4, RB, (0, 0), (0, W), row_total // 2)]
    dq_b2, dkv_b2 = attend_back(
        open_a,
        [res_b2, da2, o_b2, heads_two, pair_kv],
        S,
        (RB, R),
        kv_b2,
        row_total,
        hpd,
        True,
    )
    kept, given = dkv_b2[: row_total // 2], dkv_b2[row_total // 2 :]
    dkv_b2 = (kept.astype(f32) + swap_pair(given).astype(f32)).astype(bf16)
    dt2 = to_rows(
        join(
            jnp.concatenate([dq_a2, dkv_a2], axis=1),
            jnp.concatenate([dq_b2, dkv_b2], axis=1),
        )
    )
    grad_self_qkv = reduce_rows(dot(n2, dt2, TN))
    grad_in, gain_two, shift_two = norm_back(x1, norm_gains[1], mm(dt2, w_qkv))
    d1 = d2 + grad_in
    e1 = d1.astype(bf16)

    da1 = to_heads(dot(e1, w_cross_out, NT).astype(bf16))
    grad_cross_out = reduce_rows(dot(e1, a1, TN))
    dq_a1, dkv_a1 = attend_back(
        lim_a,
        [res_a1, da1, o_a1, heads_one],
        S,
        (R, 0),
        [(3, slots) + kv_a1 + (0,)],
        slot_total,
        hpd,
        False,
    )
    dq_b1, dkv_b1 = attend_back(
        lim_b,
        [res_b1, da1, o_b1, heads_one],
        S,
        (RB, R),
        [(3, slots) + kv_b1 + (0,)],
        slot_total,
        hpd,
        False,
    )
    dkv1 = to_rows(
        jnp.concatenate([dkv_a1.reshape(S, slots, -1), dkv_b1.reshape(S, slots, -1)], axis=1)
    )
    both = [lax.dynamic_index_in_dim(patches, o, 0, keepdims=False) for o in (at_a, at_b)]
    grad_cross_kv = reduce_rows(dot(jnp.concatenate(both, axis=0), dkv1, TN))
    patch_part = mm(dkv1, w_kv).astype(bf16)
    patch_all = lax.all_gather(patch_part, "mp", axis=0).astype(f32)
    patch_all = patch_all.reshape(pairs, 2, 2, slots, width)
    patch_grad = jnp.stack(
        [patch_all[:, 0, 0], patch_all[:, 0, 1] + patch_all[:, 1, 1], patch_all[:, 1, 0]], axis=1
    ).reshape(objects, slots, width)

    dq1 = to_rows(join(dq_a1, dq_b1))
    n1 = layer_norm(x0, norm_gains[0], norm_shifts[0])
    grad_cross_query = reduce_rows(dot(n1, dq1, TN))
    grad_in, gain_one, shift_one = norm_back(x0, norm_gains[0], mm(dq1, w_query))
    grad_tokens = to_owner((d1 + grad_in).astype(bf16), m, R).astype(f32)

    rows = jnp.stack([gain_one, gain_two, gain_three, shift_one, shift_two, shift_three])
    rows = jnp.sum(swap_seq(rows.reshape(6, S, D // S).transpose(1, 0, 2)), axis=0)
    rows = lax.all_to_all(
        jnp.broadcast_to(rows, (M,) + rows.shape), "mp", split_axis=0, concat_axis=0, tiled=True
    )
    rows = jnp.sum(rows, axis=0)

    grad_self_qkv = grad_self_qkv.reshape(D // S, M, 2, 3, W)
    grad_self_qkv = reduce_cols(grad_self_qkv.reshape(D // S, -1)).reshape(D // S, 2, 3, W)
    grad_cross_kv = reduce_cols(grad_cross_kv).reshape(width // S, 2, 2, W)
    return (
        tokens_out,
        sampled,
        grad_tokens,
        patch_grad,
        rows[:3],
        rows[3:5],
        rows[5],
        reduce_cols(grad_cross_query),
        grad_cross_kv.transpose(0, 2, 1, 3).reshape(width // S, 2, -1),
        reduce_cols(grad_cross_out).T,
        grad_self_qkv.transpose(0, 2, 1, 3).reshape(D // S, 3, -1),
        reduce_cols(grad_self_out).T,
        reduce_cols(grad_mlp_up),
        reduce_cols(grad_mlp_down).T,
        reduce_cols(grad_decoder).reshape(D // S, channels, 4),
    )


def solution(mesh):
    return jax.shard_map(
        per_device,
        mesh=mesh,
        in_specs=(
            P(None, "seq", None),
            P(None, "seq", None),
            P(),
            P(),
            P(),
            P(None, "mp"),
            P(None, None, "mp"),
            P("mp", None),
            P(None, None, "mp"),
            P("mp", None),
            P(None, "mp"),
            P("mp", None),
            P(None, "mp", None),
            P(None, None, "seq", None, None),
            P(None, "seq", None),
            P(None, None, "mp", "seq", None),
        ),
        out_specs=(
            P(None, ("seq", "mp"), None),
            P(None, None, "mp", "seq", None),
            P(None, ("seq", "mp"), None),
            P(None, "seq", None),
            P(None, "seq"),
            P(None, "seq"),
            P("seq"),
            P("seq", "mp"),
            P("seq", None, "mp"),
            P("mp", "seq"),
            P("seq", None, "mp"),
            P("mp", "seq"),
            P("seq", "mp"),
            P("mp", "seq"),
            P("seq", "mp", None),
        ),
        check_vma=False,
    )
```

time: 2930 us -> 1520 us (0.52)
  waiting for transfers between devices: 1690 us -> 601 us
  matrix products: 553 us -> 143 us
  other arithmetic: 345 us -> 57.9 us
  Pallas kernels: 0 us -> 216 us
  starting transfers between devices: 15.1 us -> 167 us
    psum x5 -> x0, waiting for transfers between devices: 1160 us -> none  [settle(): return lax.psum(operand.astype(jnp.bfloat16), 'mp').astype(jnp.float32)]
    dot_general x38 -> x26, matrix products: 553 us -> 143 us  [the longest x14 88.6 us: dot(): return lax.dot_general(a, b, dims, preferred_element_type=f32)]
    pallas_call x0 -> x8, Pallas kernels: none -> 216 us  [the longest x4 139 us: attend_back(): pl.pallas_call(body, out_shape=(jax.ShapeDtypeStruct((queries, hpd * HD),...]
    unnamed x26 -> x25, waiting for transfers between devices: 212 us -> 2.03 us
    convert_element_type x13 -> x5, other arithmetic: 151 us -> 7.75 us  [the longest x2 4.25 us: per_device(): grad_tokens = to_owner((d1 + grad_in).astype(bf16), m, R).astype(f32)]
    reduce_sum x17 -> x8, other arithmetic: 138 us -> 6.08 us  [the longest x2 3.42 us: norm_parts(): center = values - jnp.mean(values, axis=-1, keepdims=True)]
    all_to_all x1 -> x13, starting transfers between devices: 4.75 us -> 98.1 us  [the longest x8 71.7 us: swap_seq(): return lax.all_to_all(value, 'seq', split_axis=0, concat_axis=0, tiled=True)]
    all_to_all x1 -> x13, waiting for transfers between devices: 0.01 us -> 92.7 us  [the longest x8 92.2 us: swap_seq(): return lax.all_to_all(value, 'seq', split_axis=0, concat_axis=0, tiled=True)]
  transfers between devices with their start and end apart: 24 -> 55, of which waited for: 18 -> 28; matrix products, arithmetic and copies ran while one was open for 10% -> 23% of each run, Pallas kernels for 0% -> 12%
where the time goes in v1:
time: 1520 us; the launch traced here: 1500 us
  waiting for transfers between devices  601 us (40%)
  Pallas kernels  216 us (14%)
  local copies, waits for them, and re-layouts  200 us (13%)
  starting transfers between devices  167 us (11%)
  matrix products  143 us (9%)
  blocking collectives  97 us (6%)
  other arithmetic  57.9 us (4%)
  between operations  17.4 us (1%)
    reduce_scatter x7, waiting for transfers between devices, reduce_rows(): lax.psum_scatter(value.astype(bf16), 'seq', scatter_dimension=0, tiled=True)  189 us
    reduce_scatter x8, waiting for transfers between devices, reduce_cols(): lax.psum_scatter(value, 'mp', scatter_dimension=1, tiled=True).astype(f32)  142 us
    pallas_call x4, Pallas kernels, attend_back(): pl.pallas_call(body, out_shape=(jax.ShapeDtypeStruct((queries, hpd * HD),...  139 us
    all_gather x7, waiting for transfers between devices, gather_rows(): return lax.all_gather(piece, ('mp', 'seq'), axis=0, tiled=True)  93 us
    all_to_all x8, waiting for transfers between devices, swap_seq(): return lax.all_to_all(value, 'seq', split_axis=0, concat_axis=0, tiled=True)  92.2 us
    dot_general x14, matrix products, dot(): return lax.dot_general(a, b, dims, preferred_element_type=f32)  88.6 us
    pallas_call x4, Pallas kernels, attend(): pl.pallas_call(body, out_shape=(jax.ShapeDtypeStruct((queries, hpd * HD),...  77.7 us
    all_gather x1, blocking collectives, per_device(): lax.all_gather(mine(decoder.reshape(D, cu), 0), ('seq', 'mp'), axis=0, ti...  76.8 us
  transfers between devices with their start and end apart: 55, of which 28 were waited for; matrix products, arithmetic and copies ran while one was open for 23% of the time, Pallas kernels for 12%

profile of v1, /device:TPU:0, one launch (start us, length us, event | category | flops | bytes accessed | tf_op | source)
XLA Modules:
  0.0 1499.1 jit_solution(15057799887770871336)
XLA Ops:
  58.6 35.8 %collective-permute-start.6 = (bf16[1344,128]{1,0:T(8,128)(2,1)S(1)}, bf16[1344,128]{1,0:T(8,128)(2,1)S(1)}, u32[]{:S(2)}, u32[]{:S(2)}) collective-permute-start(bf16[1344,128]{1,0:T(8,128)(2,1)S(1)} %constant_dynamic-update-slice_fusion.24), channel_id=1, source_target_pairs={{0,3},{1,11},{2,19},{3,27},{4,7},{5,15},{6,23},{7,31},{8,2},{9,10}... | collective-permute-start | bytes 1032200 | tf_op jit(solution)/shard_map/ppermute | solution.py:439
  97.2 7.5 collective-permute-done.6
  110.5 11.1 shard_map.281
  122.5 20.1 %shard_map.280 = (bf16[3072,128]{1,0:T(8,128)(2,1)S(1)}, bf16[2,3072,128]{2,1,0:T(8,128)(2,1)S(1)}) custom-call(s32[2]{0:T(128)S(1)} %get-tuple-element.241.n_ref, bf16[8,1344,128]{2,1,0:T(8,128)(2,1)S(1)} %bitcast_dynamic-update-slice_fusion.refs_0_.refs_3_), custom_call_target="tpu_custom_call" | custom-call | flops 9663676416 | bytes 6291456 | tf_op jit(solution)/shard_map/pallas_call | solution.py:193
  145.9 44.2 %all-to-all-start = ((bf16[8,576,128]{2,1,0:T(8,128)(2,1)}), bf16[8,576,128]{2,1,0:T(8,128)(2,1)S(1)}, u32[]{:S(2)}, u32[]{:S(2)}) async-start(bf16[8,576,128]{2,1,0:T(8,128)(2,1)} %pad_maximum_fusion.8), calls=%async_computation | async-start | bytes 2359296 | tf_op jit(solution)/shard_map/all_to_all | solution.py:263
  192.5 14.8 all-to-all-done
  246.4 6.4 slice.347
  252.9 6.5 copy.404
  264.0 12.5 collective-permute-done.13
  301.5 14.3 copy.370
  315.8 7.6 reshape_reshape.7
  335.4 10.1 all-to-all-start.5
  347.6 29.7 %shard_map.282 = (bf16[3072,128]{1,0:T(8,128)(2,1)S(1)}, bf16[2,3072,128]{2,1,0:T(8,128)(2,1)S(1)}) custom-call(s32[2]{0:T(128)S(1)} %copy-done.16, bf16[8,576,384]{2,1,0:T(8,128)(2,1)S(1)} %all-to-all-done.1.refs_0_.refs_3_), custom_call_target="tpu_custom_call" | custom-call | flops 19327352832 | bytes 6291456 | tf_op jit(solution)/shard_map/pallas_call | solution.py:193
  379.1 16.7 %shard_map.283 = (bf16[1536,128]{1,0:T(8,128)(2,1)S(1)}, bf16[2,1536,128]{2,1,0:T(8,128)(2,1)S(1)}) custom-call(s32[2]{0:T(128)S(1)} %copy-done.16, bf16[8,576,384]{2,1,0:T(8,128)(2,1)S(1)} %all-to-all-done.1.refs_0_.refs_3_, bf16[8,192,256]{2,1,0:T(8,128)(2,1)S(1)} %collective-permute-done.8.refs_1_.refs_4_), custom_call_target="tpu_custom_call" | custom-call | flops 9663676416 | bytes 3145728 | tf_op jit(solution)/shard_map/pallas_call | solution.py:193
  403.2 76.8 %all-gather = bf16[4096,80]{0,1:T(8,128)(2,1)S(1)} all-gather(bf16[128,80]{0,1:T(8,128)(2,1)S(1)} %constant_dynamic-slice_fusion.2), channel_id=2, replica_groups=mesh['seq'=8,'mp'=4] {'seq','mp'}, dimensions={0}, use_global_device_ids=true | all-gather | bytes 675840 | tf_op jit(solution)/shard_map/all_gather | solution.py:387
  494.9 11.6 fusion.120
  506.5 14.3 multiply_convert_fusion
  520.9 6.1 multiply_reduce_fusion
  530.3 20.2 %all_to_all.70.refs_1_ = bf16[8,576,128]{2,1,0:T(8,128)(2,1)} all-to-all(bf16[8,576,128]{2,1,0:T(8,128)(2,1)S(1)} %bitcast.528), channel_id=1, replica_groups=mesh['seq'=8,'mp'=4] {'seq'}, dimensions={0} | all-to-all | bytes 2359296 | tf_op jit(solution)/shard_map/all_to_all | solution.py:263
  550.6 35.6 %shard_map.285 = (bf16[1536,128]{1,0:T(8,128)(2,1)S(1)}, bf16[3072,256]{1,0:T(8,128)(2,1)}) custom-call(s32[2]{0:T(128)S(1)} %copy-done.16, bf16[2,1536,128]{2,1,0:T(8,128)(2,1)S(1)} %copy-done.20, bf16[8,576,128]{2,1,0:T(8,128)(2,1)} %all_to_all.70.refs_1_, bf16[1536,128]{1,0:T(8,128)(2,1)S(1)} %copy-done.9, bf16[8,576,384]{2,1,0:T(8,128)(2,1)} %copy-done.2, ...), custom_call_target="tpu_custom_call" | custom-call | flops 24159191040 | bytes 4718592 | tf_op jit(solution)/shard_map/pallas_call | solution.py:223
  587.5 61.3 %shard_map.284 = (bf16[3072,128]{1,0:T(8,128)(2,1)S(1)}, bf16[3072,256]{1,0:T(8,128)(2,1)}) custom-call(s32[2]{0:T(128)S(1)} %copy-done.16, bf16[2,3072,128]{2,1,0:T(8,128)(2,1)} %copy-done.21, bf16[8,576,128]{2,1,0:T(8,128)(2,1)} %all_to_all.70.refs_1_, bf16[3072,128]{1,0:T(8,128)(2,1)S(1)} %copy-done.5, bf16[8,576,384]{2,1,0:T(8,128)(2,1)} %copy-done.2), custom_call_target="tpu_custom_call" | custom-call | flops 48318382080 | bytes 9437184 | tf_op jit(solution)/shard_map/pallas_call | solution.py:223
  656.9 11.4 add_convert_fusion
  678.5 22.5 %all-to-all-done.7 = bf16[8,576,384]{2,1,0:T(8,128)(2,1)S(1)} async-done(((bf16[8,576,384]{2,1,0:T(8,128)(2,1)}), bf16[8,576,384]{2,1,0:T(8,128)(2,1)S(1)}, u32[]{:S(2)}, u32[]{:S(2)}) %all-to-all-start.7) | async-done | bytes 3538976 | tf_op jit(solution)/shard_map/all_to_all | solution.py:263
  702.8 7.6 multiply_reduce_fusion.1
  723.6 12.3 all-to-all-done.8.refs_1_
  735.9 26.0 %shard_map.286 = (bf16[3072,128]{1,0:T(8,128)(2,1)S(1)}, bf16[1536,256]{1,0:T(8,128)(2,1)S(1)}) custom-call(s32[2]{0:T(128)S(1)} %copy-done.14, bf16[2,3072,128]{2,1,0:T(8,128)(2,1)} %copy-done.18, bf16[8,576,128]{2,1,0:T(8,128)(2,1)} %all-to-all-done.8.refs_1_, bf16[3072,128]{1,0:T(8,128)(2,1)} %copy-done.3, bf16[8,1344,128]{2,1,0:T(8,128)(2,1)} %copy-done.10), custom_call_target="tpu_custom_call" | custom-call | flops 24159191040 | bytes 9437184 | tf_op jit(solution)/shard_map/pallas_call | solution.py:223
  761.9 15.9 %shard_map.287 = (bf16[1536,128]{1,0:T(8,128)(2,1)S(1)}, bf16[1536,256]{1,0:T(8,128)(2,1)S(1)}) custom-call(s32[2]{0:T(128)S(1)} %copy-done.12, bf16[2,1536,128]{2,1,0:T(8,128)(2,1)} %copy-done.17, bf16[8,576,128]{2,1,0:T(8,128)(2,1)} %all-to-all-done.8.refs_1_, bf16[1536,128]{1,0:T(8,128)(2,1)S(1)} %copy-done.7, bf16[8,1344,128]{2,1,0:T(8,128)(2,1)} %copy-done.10), custom_call_target="tpu_custom_call" | custom-call | flops 12079595520 | bytes 4718592 | tf_op jit(solution)/shard_map/pallas_call | solution.py:223
  784.3 16.8 %all-to-all-done.9 = bf16[8,576,128]{2,1,0:T(8,128)(2,1)} async-done(((bf16[8,576,128]{2,1,0:T(8,128)(2,1)}), bf16[8,576,128]{2,1,0:T(8,128)(2,1)}, u32[]{:S(2)}, u32[]{:S(2)}) %all-to-all-start.9) | async-done | bytes 1179680 | tf_op jit(solution)/shard_map/all_to_all | solution.py:263
  818.9 21.0 %all-to-all-done.11 = bf16[8,384,256]{1,2,0:T(8,128)(2,1)S(1)} async-done(((bf16[8,384,256]{1,2,0:T(8,128)(2,1)}), bf16[8,384,256]{1,2,0:T(8,128)(2,1)S(1)}, u32[]{:S(2)}, u32[]{:S(2)}) %all-to-all-start.11) | async-done | bytes 1572896 | tf_op jit(solution)/shard_map/all_to_all | solution.py:263
  846.3 11.6 convolution_convert_fusion
  863.7 11.6 convolution_convert_fusion.1
  877.0 9.3 convolution_convert_fusion.2
  887.7 38.1 %all-gather.23.cloned.1.call-done = bf16[2048,768]{1,0:T(8,128)(2,1)} async-done(((bf16[64,768]{1,0:T(8,128)(2,1)}), bf16[2048,768]{1,0:T(8,128)(2,1)}) %all-gather.23.cloned.1.call-update) | async-done | bytes 3145744 | tf_op jit(solution)/shard_map/all_gather | solution.py:276
  937.5 37.3 %reduce-scatter.23.cloned.1.call-done = bf16[96,2048]{1,0:T(8,128)(2,1)} async-done(((bf16[768,2048]{1,0:T(8,128)(2,1)}), bf16[96,2048]{1,0:T(8,128)(2,1)}) %reduce-scatter.23.cloned.1.call-update) | async-done | bytes 393232 | tf_op jit(solution)/shard_map/reduce_scatter | solution.py:280
  975.5 7.9 reshape_reshape.6
  983.4 11.6 copy.358
  1007.9 41.6 %reduce-scatter.43.cloned.1.call-done = bf16[128,4096]{1,0:T(8,128)(2,1)} async-done(((bf16[1024,4096]{1,0:T(8,128)(2,1)}), bf16[128,4096]{1,0:T(8,128)(2,1)}) %reduce-scatter.43.cloned.1.call-update) | async-done | bytes 1048592 | tf_op jit(solution)/shard_map/reduce_scatter | solution.py:280
  1074.6 54.9 %all-gather.21.cloned.1.call-done = bf16[1024,1024]{1,0:T(8,128)(2,1)} async-done(((bf16[32,1024]{1,0:T(8,128)(2,1)}), bf16[1024,1024]{1,0:T(8,128)(2,1)}) %all-gather.21.cloned.1.call-update) | async-done | bytes 2097168 | tf_op jit(solution)/shard_map/all_gather | solution.py:276
  1147.6 55.3 %reduce-scatter.39.cloned.1.call-done = bf16[128,4096]{1,0:T(8,128)(2,1)} async-done(((bf16[1024,4096]{1,0:T(8,128)(2,1)}), bf16[128,4096]{1,0:T(8,128)(2,1)}) %reduce-scatter.39.cloned.1.call-update) | async-done | bytes 1048592 | tf_op jit(solution)/shard_map/reduce_scatter | solution.py:280
  1217.3 9.4 reduce-scatter.37.cloned.1.call-done
  1240.6 55.1 %reduce-scatter.31.cloned.1.call-done = bf16[128,3072]{1,0:T(8,128)(2,1)} async-done(((bf16[1024,3072]{1,0:T(8,128)(2,1)}), bf16[128,3072]{1,0:T(8,128)(2,1)}) %reduce-scatter.31.cloned.1.call-update) | async-done | bytes 786448 | tf_op jit(solution)/shard_map/reduce_scatter | solution.py:280
  1297.5 20.0 %reduce-scatter.29.cloned.1.call-done = bf16[128,256]{1,0:T(8,128)(2,1)} async-done(((bf16[128,1024]{1,0:T(8,128)(2,1)}), bf16[128,256]{1,0:T(8,128)(2,1)}) %reduce-scatter.29.cloned.1.call-update) | async-done | bytes 65552 | tf_op jit(solution)/shard_map/reduce_scatter | solution.py:284
  1319.2 18.5 %reduce-scatter.21.cloned.1.call-done = bf16[128,256]{1,0:T(8,128)(2,1)} async-done(((bf16[128,1024]{1,0:T(8,128)(2,1)}), bf16[128,256]{1,0:T(8,128)(2,1)}) %reduce-scatter.21.cloned.1.call-update) | async-done | bytes 65552 | tf_op jit(solution)/shard_map/reduce_scatter | solution.py:284
  1339.2 48.7 %all-gather.25.cloned.1.call-done = bf16[1536,768]{1,0:T(8,128)(2,1)} async-done(((bf16[384,768]{1,0:T(8,128)(2,1)}), bf16[1536,768]{1,0:T(8,128)(2,1)}) %all-gather.25.cloned.1.call-update) | async-done | bytes 2359312 | tf_op jit(solution)/shard_map/all_gather | solution.py:586
  1392.8 17.0 %reduce-scatter.25.cloned.1.call-done = bf16[96,512]{1,0:T(8,128)(2,1)} async-done(((bf16[96,2048]{1,0:T(8,128)(2,1)}), bf16[96,512]{1,0:T(8,128)(2,1)}) %reduce-scatter.25.cloned.1.call-update) | async-done | bytes 98320 | tf_op jit(solution)/shard_map/reduce_scatter | solution.py:284
  1411.6 25.9 %reduce-scatter.45.cloned.1.call-done = bf16[128,1024]{1,0:T(8,128)(2,1)} async-done(((bf16[128,4096]{1,0:T(8,128)(2,1)}), bf16[128,1024]{1,0:T(8,128)(2,1)}) %reduce-scatter.45.cloned.1.call-update) | async-done | bytes 262160 | tf_op jit(solution)/shard_map/reduce_scatter | solution.py:284
  1439.5 26.2 %reduce-scatter.41.cloned.1.call-done = bf16[128,1024]{1,0:T(8,128)(2,1)} async-done(((bf16[128,4096]{1,0:T(8,128)(2,1)}), bf16[128,1024]{1,0:T(8,128)(2,1)}) %reduce-scatter.41.cloned.1.call-update) | async-done | bytes 262160 | tf_op jit(solution)/shard_map/reduce_scatter | solution.py:284
  1467.5 22.3 %reduce-scatter.33.cloned.1.call-done = bf16[128,768]{1,0:T(8,128)(2,1)} async-done(((bf16[128,3072]{1,0:T(8,128)(2,1)}), bf16[128,768]{1,0:T(8,128)(2,1)}) %reduce-scatter.33.cloned.1.call-update) | async-done | bytes 196624 | tf_op jit(solution)/shard_map/reduce_scatter | solution.py:284
  (502 shorter events, 362.6 us)
Async XLA Ops:
  7.2 201.2 %all-gather.11.cloned.1.call-start = ((), (), s32[]{:S(2)}) async-start(), calls=%async_computation.30 | async-start | bytes 2162688 | tf_op jit(solution)/shard_map/all_gather | solution.py:276
  8.9 203.4 %all-gather.13.cloned.1.call-start = ((), (), s32[]{:S(2)}) async-start(), calls=%async_computation.31 | async-start | bytes 6488064 | tf_op jit(solution)/shard_map/all_gather | solution.py:276
  11.3 478.3 %all-gather.15.cloned.1.call-start = ((), (), s32[]{:S(2)}) async-start(), calls=%async_computation.32 | async-start | bytes 2162688 | tf_op jit(solution)/shard_map/all_gather | solution.py:276
  12.9 482.0 %all-gather.17.cloned.1.call-start = ((), (), s32[]{:S(2)}) async-start(), calls=%async_computation.33 | async-start | bytes 8650752 | tf_op jit(solution)/shard_map/all_gather | solution.py:276
  13.7 492.8 %all-gather.19.cloned.1.call-start = ((), (), s32[]{:S(2)}) async-start(), calls=%async_computation.34 | async-start | bytes 8650752 | tf_op jit(solution)/shard_map/all_gather | solution.py:276
  28.5 66.0 %collective-permute-start.2 = (bf16[1344,128]{1,0:T(8,128)(2,1)}, bf16[1344,128]{1,0:T(8,128)(2,1)S(1)}, u32[]{:S(2)}, u32[]{:S(2)}) collective-permute-start(bf16[1344,128]{1,0:T(8,128)(2,1)} %constant_dynamic-update-slice_fusion.8), channel_id=1, source_target_pairs={{0,1},{1,9},{2,17},{3,25},{4,5},{5,13},{6,21},{7,29},{8,0},{9,8},{... | collective-permute-start | bytes 1032200 | tf_op jit(solution)/shard_map/ppermute | solution.py:439
  34.0 61.1 %collective-permute-start.3 = (bf16[1344,128]{1,0:T(8,128)(2,1)}, bf16[1344,128]{1,0:T(8,128)(2,1)S(1)}, u32[]{:S(2)}, u32[]{:S(2)}) collective-permute-start(bf16[1344,128]{1,0:T(8,128)(2,1)} %constant_dynamic-update-slice_fusion.12), channel_id=1, source_target_pairs={{0,5},{1,13},{2,21},{3,29},{4,1},{5,9},{6,17},{7,25},{8,4},{9,12},... | collective-permute-start | bytes 1032200 | tf_op jit(solution)/shard_map/ppermute | solution.py:439
  37.9 57.3 %collective-permute-start.4 = (bf16[1344,128]{1,0:T(8,128)(2,1)}, bf16[1344,128]{1,0:T(8,128)(2,1)}, u32[]{:S(2)}, u32[]{:S(2)}) collective-permute-start(bf16[1344,128]{1,0:T(8,128)(2,1)} %constant_dynamic-update-slice_fusion.16), channel_id=1, source_target_pairs={{0,2},{1,10},{2,18},{3,26},{4,6},{5,14},{6,22},{7,30},{8,3},{9,11}... | collective-permute-start | bytes 1032200 | tf_op jit(solution)/shard_map/ppermute | solution.py:439
  44.7 51.4 %collective-permute-start.5 = (bf16[1344,128]{1,0:T(8,128)(2,1)}, bf16[1344,128]{1,0:T(8,128)(2,1)}, u32[]{:S(2)}, u32[]{:S(2)}) collective-permute-start(bf16[1344,128]{1,0:T(8,128)(2,1)} %constant_dynamic-update-slice_fusion.20), channel_id=1, source_target_pairs={{0,6},{1,14},{2,22},{3,30},{4,2},{5,10},{6,18},{7,26},{8,7},{9,15}... | collective-permute-start | bytes 1032200 | tf_op jit(solution)/shard_map/ppermute | solution.py:439
  58.6 46.1 %collective-permute-start.6 = (bf16[1344,128]{1,0:T(8,128)(2,1)S(1)}, bf16[1344,128]{1,0:T(8,128)(2,1)S(1)}, u32[]{:S(2)}, u32[]{:S(2)}) collective-permute-start(bf16[1344,128]{1,0:T(8,128)(2,1)S(1)} %constant_dynamic-update-slice_fusion.24), channel_id=1, source_target_pairs={{0,3},{1,11},{2,19},{3,27},{4,7},{5,15},{6,23},{7,31},{8,2},{9,10}... | collective-permute-start | bytes 1032200 | tf_op jit(solution)/shard_map/ppermute | solution.py:439
  94.5 16.0 %collective-permute-start.7 = (bf16[1344,128]{1,0:T(8,128)(2,1)S(1)}, bf16[1344,128]{1,0:T(8,128)(2,1)S(1)}, u32[]{:S(2)}, u32[]{:S(2)}) collective-permute-start(bf16[1344,128]{1,0:T(8,128)(2,1)S(1)} %constant_dynamic-update-slice_fusion.28), channel_id=1, source_target_pairs={{0,7},{1,15},{2,23},{3,31},{4,3},{5,11},{6,19},{7,27},{8,6},{9,14}... | collective-permute-start | bytes 1032200 | tf_op jit(solution)/shard_map/ppermute | solution.py:439
  145.9 61.5 %all-to-all-start = ((bf16[8,576,128]{2,1,0:T(8,128)(2,1)}), bf16[8,576,128]{2,1,0:T(8,128)(2,1)S(1)}, u32[]{:S(2)}, u32[]{:S(2)}) async-start(bf16[8,576,128]{2,1,0:T(8,128)(2,1)} %pad_maximum_fusion.8), calls=%async_computation | async-start | bytes 2359296 | tf_op jit(solution)/shard_map/all_to_all | solution.py:263
  222.9 112.6 %all-to-all-start.1 = ((bf16[8,576,384]{2,1,0:T(8,128)(2,1)}), bf16[8,576,384]{2,1,0:T(8,128)(2,1)S(1)}, u32[]{:S(2)}, u32[]{:S(2)}) async-start(bf16[8,576,384]{2,1,0:T(8,128)(2,1)} %bitcast.519), calls=%async_computation.1 | async-start | bytes 7077888 | tf_op jit(solution)/shard_map/all_to_all | solution.py:263
  241.7 34.8 %collective-permute-start.13 = (f32[6,3,20,17]{2,0,3,1:T(8,128)}, f32[6,3,20,17]{2,0,3,1:T(8,128)}, u32[]{:S(2)}, u32[]{:S(2)}) collective-permute-start(f32[6,3,20,17]{2,0,3,1:T(8,128)} %bitcast.563), channel_id=1, source_target_pairs={{0,16},{4,20},{8,24},{12,28},{1,17},{5,21},{9,25},{13,29},{2,18},{... | collective-permute-start | bytes 73448 | tf_op jit(solution)/shard_map/ppermute | solution.py:290
  335.4 63.2 %all-to-all-start.5 = ((bf16[32,72,80]{2,1,0:T(8,128)(2,1)}), bf16[32,72,80]{2,1,0:T(8,128)(2,1)}, u32[]{:S(2)}, u32[]{:S(2)}) async-start(bf16[32,72,80]{2,1,0:T(8,128)(2,1)} %bitcast.542), calls=%async_computation.5 | async-start | bytes 1179648 | tf_op jit(solution)/shard_map/all_to_all | solution.py:267
  345.6 33.5 %collective-permute-start.8 = (bf16[8,192,256]{2,1,0:T(8,128)(2,1)S(1)}, bf16[8,192,256]{2,1,0:T(8,128)(2,1)S(1)}, u32[]{:S(2)}, u32[]{:S(2)}) collective-permute-start(bf16[8,192,256]{2,1,0:T(8,128)(2,1)S(1)} %slice.334), channel_id=1, source_target_pairs={{0,1},{1,0},{2,3},{3,2},{4,5},{5,4},{6,7},{7,6},{8,9},{9,8},{10,11... | collective-permute-start | bytes 2359304 | tf_op jit(solution)/shard_map/ppermute | solution.py:272
  398.6 91.0 %all-to-all-start.2 = ((bf16[8,576,128]{2,1,0:T(8,128)(2,1)}), bf16[8,576,128]{2,1,0:T(8,128)(2,1)}, u32[]{:S(2)}, u32[]{:S(2)}) async-start(bf16[8,576,128]{2,1,0:T(8,128)(2,1)} %pad_maximum_fusion.9), calls=%async_computation.2 | async-start | bytes 2359296 | tf_op jit(solution)/shard_map/all_to_all | solution.py:263
  587.4 63.3 %collective-permute-start.15 = (bf16[1536,256]{1,0:T(8,128)(2,1)S(1)}, bf16[1536,256]{1,0:T(8,128)(2,1)S(1)}, u32[]{:S(2)}, u32[]{:S(2)}) collective-permute-start(bf16[1536,256]{1,0:T(8,128)(2,1)S(1)} %slice.289), channel_id=1, source_target_pairs={{0,1},{1,0},{2,3},{3,2},{4,5},{5,4},{6,7},{7,6},{8,9},{9,8},{10,11... | collective-permute-start | bytes 2359304 | tf_op jit(solution)/shard_map/ppermute | solution.py:272
  653.2 47.8 %all-to-all-start.7 = ((bf16[8,576,384]{2,1,0:T(8,128)(2,1)}), bf16[8,576,384]{2,1,0:T(8,128)(2,1)S(1)}, u32[]{:S(2)}, u32[]{:S(2)}) async-start(bf16[8,576,384]{2,1,0:T(8,128)(2,1)} %pad_maximum_fusion.1), calls=%async_computation.7 | async-start | bytes 7077888 | tf_op jit(solution)/shard_map/all_to_all | solution.py:263
  656.9 201.1 %reduce-scatter.49.cloned.1.call-start = ((), (), s32[]{:S(2)}) async-start(), calls=%async_computation.53 | async-start | bytes 884736
  673.2 202.2 %reduce-scatter.35.cloned.1.call-start = ((), (), s32[]{:S(2)}) async-start(), calls=%async_computation.45 | async-start | bytes 2359296 | tf_op jit(solution)/shard_map/reduce_scatter | solution.py:280
  714.7 21.2 %all-to-all-start.8 = ((bf16[8,576,128]{2,1,0:T(8,128)(2,1)}), bf16[8,576,128]{2,1,0:T(8,128)(2,1)}, u32[]{:S(2)}, u32[]{:S(2)}) async-start(bf16[8,576,128]{2,1,0:T(8,128)(2,1)} %bitcast.527), calls=%async_computation.8 | async-start | bytes 2359296 | tf_op jit(solution)/shard_map/all_to_all | solution.py:263
  719.0 167.3 %reduce-scatter.27.cloned.1.call-start = ((), (), s32[]{:S(2)}) async-start(), calls=%async_computation.41 | async-start | bytes 2359296 | tf_op jit(solution)/shard_map/reduce_scatter | solution.py:280
  778.9 22.2 %all-to-all-start.9 = ((bf16[8,576,128]{2,1,0:T(8,128)(2,1)}), bf16[8,576,128]{2,1,0:T(8,128)(2,1)}, u32[]{:S(2)}, u32[]{:S(2)}) async-start(bf16[8,576,128]{2,1,0:T(8,128)(2,1)} %pad_maximum_fusion.11), calls=%async_computation.9 | async-start | bytes 2359296 | tf_op jit(solution)/shard_map/all_to_all | solution.py:263
  783.3 103.6 %reduce-scatter.19.cloned.1.call-start = ((), (), s32[]{:S(2)}) async-start(), calls=%async_computation.37 | async-start | bytes 2359296 | tf_op jit(solution)/shard_map/reduce_scatter | solution.py:280
  805.7 120.0 %all-gather.23.cloned.1.call-start = ((), (), s32[]{:S(2)}) async-start(), calls=%async_computation.36 | async-start | bytes 3244032 | tf_op jit(solution)/shard_map/all_gather | solution.py:276
  814.2 25.7 %all-to-all-start.11 = ((bf16[8,384,256]{1,2,0:T(8,128)(2,1)}), bf16[8,384,256]{1,2,0:T(8,128)(2,1)S(1)}, u32[]{:S(2)}, u32[]{:S(2)}) async-start(bf16[8,384,256]{1,2,0:T(8,128)(2,1)} %pad_maximum_fusion.5), calls=%async_computation.11 | async-start | bytes 3145728 | tf_op jit(solution)/shard_map/all_to_all | solution.py:263
  817.8 157.1 %reduce-scatter.23.cloned.1.call-start = ((), (), s32[]{:S(2)}) async-start(), calls=%async_computation.39 | async-start | bytes 3538944 | tf_op jit(solution)/shard_map/reduce_scatter | solution.py:280
  844.6 204.8 %reduce-scatter.43.cloned.1.call-start = ((), (), s32[]{:S(2)}) async-start(), calls=%async_computation.49 | async-start | bytes 9437184 | tf_op jit(solution)/shard_map/reduce_scatter | solution.py:280
  857.9 213.7 %reduce-scatter.47.cloned.1.call-start = ((), (), s32[]{:S(2)}) async-start(), calls=%async_computation.51 | async-start | bytes 102400 | tf_op jit(solution)/shard_map/reduce_scatter | solution.py:284
  859.8 269.7 %all-gather.21.cloned.1.call-start = ((), (), s32[]{:S(2)}) async-start(), calls=%async_computation.35 | async-start | bytes 2162688 | tf_op jit(solution)/shard_map/all_gather | solution.py:276
  863.4 339.6 %reduce-scatter.39.cloned.1.call-start = ((), (), s32[]{:S(2)}) async-start(), calls=%async_computation.47 | async-start | bytes 9437184 | tf_op jit(solution)/shard_map/reduce_scatter | solution.py:280
  875.3 351.3 %reduce-scatter.37.cloned.1.call-start = ((), (), s32[]{:S(2)}) async-start(), calls=%async_computation.46 | async-start | bytes 327680 | tf_op jit(solution)/shard_map/reduce_scatter | solution.py:284
  875.9 419.7 %reduce-scatter.31.cloned.1.call-start = ((), (), s32[]{:S(2)}) async-start(), calls=%async_computation.43 | async-start | bytes 7077888 | tf_op jit(solution)/shard_map/reduce_scatter | solution.py:280
  886.3 431.2 %reduce-scatter.29.cloned.1.call-start = ((), (), s32[]{:S(2)}) async-start(), calls=%async_computation.42 | async-start | bytes 327680 | tf_op jit(solution)/shard_map/reduce_scatter | solution.py:284
  886.9 450.8 %reduce-scatter.21.cloned.1.call-start = ((), (), s32[]{:S(2)}) async-start(), calls=%async_computation.38 | async-start | bytes 327680 | tf_op jit(solution)/shard_map/reduce_scatter | solution.py:284
  887.6 500.3 %all-gather.25.cloned.1.call-start = ((), (), s32[]{:S(2)}) async-start(), calls=%async_computation.52 | async-start | bytes 2949120 | tf_op jit(solution)/shard_map/all_gather | solution.py:586
  934.0 40.9 %all-to-all-start.4 = ((bf16[32,72,80]{2,1,0:T(8,128)(2,1)}), bf16[32,72,80]{2,1,0:T(8,128)(2,1)S(1)}, u32[]{:S(2)}, u32[]{:S(2)}) async-start(bf16[32,72,80]{2,1,0:T(8,128)(2,1)} %bitcast.106), calls=%async_computation.4 | async-start | bytes 1179648 | tf_op jit(solution)/shard_map/all_to_all | solution.py:267
  937.4 472.3 %reduce-scatter.25.cloned.1.call-start = ((), (), s32[]{:S(2)}) async-start(), calls=%async_computation.40 | async-start | bytes 491520 | tf_op jit(solution)/shard_map/reduce_scatter | solution.py:284
  1002.2 70.8 %all-to-all-start.3 = ((bf16[4,96,1024]{2,1,0:T(8,128)(2,1)}), bf16[4,96,1024]{2,1,0:T(8,128)(2,1)}, u32[]{:S(2)}, u32[]{:S(2)}) async-start(bf16[4,96,1024]{2,1,0:T(8,128)(2,1)} %bitcast.536), calls=%async_computation.3 | async-start | bytes 1572864 | tf_op jit(solution)/shard_map/all_to_all | solution.py:298
  1006.9 430.6 %reduce-scatter.45.cloned.1.call-start = ((), (), s32[]{:S(2)}) async-start(), calls=%async_computation.50 | async-start | bytes 1310720 | tf_op jit(solution)/shard_map/reduce_scatter | solution.py:284
  1053.4 158.8 %collective-permute-start.10 = (bf16[96,1024]{1,0:T(8,128)(2,1)}, bf16[96,1024]{1,0:T(8,128)(2,1)}, u32[]{:S(2)}, u32[]{:S(2)}) collective-permute-start(bf16[96,1024]{1,0:T(8,128)(2,1)} %get-tuple-element.224), channel_id=1, source_target_pairs={{0,1},{1,3},{2,0},{3,2},{4,5},{5,7},{6,4},{7,6},{8,9},{9,11},{10,8... | collective-permute-start | bytes 589832 | tf_op jit(solution)/shard_map/ppermute | solution.py:306
  1055.1 157.1 %collective-permute-start.9 = (bf16[96,1024]{1,0:T(8,128)(2,1)}, bf16[96,1024]{1,0:T(8,128)(2,1)}, u32[]{:S(2)}, u32[]{:S(2)}) collective-permute-start(bf16[96,1024]{1,0:T(8,128)(2,1)} %get-tuple-element.225), channel_id=1, source_target_pairs={{0,0},{1,2},{2,1},{3,3},{4,4},{5,6},{6,5},{7,7},{8,8},{9,10},{10,9... | collective-permute-start | bytes 589832 | tf_op jit(solution)/shard_map/ppermute | solution.py:306
  1144.2 63.4 %all-to-all-start.13 = ((f32[4,6,128]{2,1,0:T(8,128)}), f32[4,6,128]{2,1,0:T(8,128)S(1)}, u32[]{:S(2)}, u32[]{:S(2)}) async-start(f32[4,6,128]{2,1,0:T(8,128)} %broadcast_in_dim.23), calls=%async_computation.13 | async-start | bytes 32768 | tf_op jit(solution)/shard_map/all_to_all | solution.py:600
  1147.6 318.1 %reduce-scatter.41.cloned.1.call-start = ((), (), s32[]{:S(2)}) async-start(), calls=%async_computation.48 | async-start | bytes 1310720 | tf_op jit(solution)/shard_map/reduce_scatter | solution.py:284
  1207.5 28.1 %all-to-all-start.10 = ((bf16[4,96,1024]{2,1,0:T(8,128)(2,1)}), bf16[4,96,1024]{2,1,0:T(8,128)(2,1)S(1)}, u32[]{:S(2)}, u32[]{:S(2)}) async-start(bf16[4,96,1024]{2,1,0:T(8,128)(2,1)} %bitcast.147), calls=%async_computation.10 | async-start | bytes 1572864 | tf_op jit(solution)/shard_map/all_to_all | solution.py:298
  1212.2 277.6 %reduce-scatter.33.cloned.1.call-start = ((), (), s32[]{:S(2)}) async-start(), calls=%async_computation.44 | async-start | bytes 983040 | tf_op jit(solution)/shard_map/reduce_scatter | solution.py:284
  1228.3 12.1 collective-permute-start.17
  (96 other events, 2503.8 us)
Sparse Core Ops, SparseCore 0:
  11.5 96.2 all-gather.10
  111.2 73.8 all-gather.12
  188.6 58.0 all-gather.14
  249.4 118.0 all-gather.16
  370.2 78.8 all-gather.18
  673.4 35.3 reduce-scatter.48
  712.1 41.1 reduce-scatter.34
  756.9 46.9 reduce-scatter.26
  807.2 55.8 reduce-scatter.18
  866.8 58.8 all-gather.22
  929.5 45.3 reduce-scatter.22
  978.2 71.2 reduce-scatter.42
  1052.3 19.2 reduce-scatter.46
  1074.9 54.5 all-gather.20
  1132.8 70.1 reduce-scatter.38
  1205.2 21.4 reduce-scatter.36
  1229.9 65.7 reduce-scatter.30
  1297.9 19.6 reduce-scatter.28
  1319.8 17.8 reduce-scatter.20
  1339.2 48.7 all-gather.24
  1390.3 19.3 reduce-scatter.24
  1412.0 25.3 reduce-scatter.44
  1439.9 25.7 reduce-scatter.40
  1467.9 21.9 reduce-scatter.32

commit v2 on v1

v2 whole, which is shorter than its diff:
```python
import functools
import math

import jax
import jax.numpy as jnp
from jax import lax
from jax.experimental import pallas as pl
from jax.experimental.pallas import tpu as pltpu
from jax.sharding import PartitionSpec as P


PLANE = 32
HD = 64
LANES = 128
norm_eps = 1e-05
f32 = jnp.float32
bf16 = jnp.bfloat16

NT = (((1,), (1,)), ((), ()))
NN = (((1,), (0,)), ((), ()))
TN = (((0,), (0,)), ((), ()))


def dot(a, b, dims):
    return lax.dot_general(a, b, dims, preferred_element_type=f32)


def mm(a, b):
    return jnp.dot(a, b, preferred_element_type=f32)


def split3(v):
    hi = v.astype(bf16).astype(f32)
    rest = v - hi
    mid = rest.astype(bf16).astype(f32)
    return hi, mid, rest - mid


def spread(base, cols):
    lane = lax.broadcasted_iota(jnp.int32, (base.shape[0], HD), 1)
    tail = jnp.zeros((base.shape[0], HD), f32)
    for at, col in cols.items():
        tail = jnp.where(lane == at, col, tail)
    return jnp.concatenate([base, tail], axis=1).astype(bf16)


def load_keys(n_ref, kv_specs, refs, ka, va, hpd, blocks):
    for ref_at, rows, k_at, v_at, base in kv_specs:
        src = refs[ref_at]

        def build(i, _):
            natural = base + (i ^ n_ref[1]) * rows
            dst = pl.ds(pl.multiple_of(natural, 16), rows)
            slot = natural + lax.broadcasted_iota(jnp.int32, (rows, 1), 0)
            mask = jnp.where(slot < n_ref[0], 0.0, -1e30).astype(f32)
            for h in range(hpd):
                k = src[i, k_at[0] : k_at[0] + rows, k_at[1] + h * HD : k_at[1] + (h + 1) * HD]
                v = src[i, v_at[0] : v_at[0] + rows, v_at[1] + h * HD : v_at[1] + (h + 1) * HD]
                ka[h, dst, :] = spread(k.astype(f32), {0: 1.0, 1: 1.0, 2: 1.0, 3: mask})
                va[h, dst, :] = spread(v.astype(f32), {0: 1.0, 1: 1.0, 2: 1.0})
            return 0

        lax.fori_loop(0, blocks, build, 0)


def fwd_kernel(n_ref, *refs, n_in, blocks, q_spec, kv_specs, hpd, bq, kc, fixed):
    ins, (o_ref, qa_ref, ka, va) = refs[:n_in], refs[n_in:]
    load_keys(n_ref, kv_specs, ins, ka, va, hpd, blocks)
    q_at, rows_q, q_off, q_lane = q_spec

    def build(i, _):
        dst = pl.ds(pl.multiple_of((i ^ n_ref[1]) * rows_q, 16), rows_q)
        for h in range(hpd):
            q = ins[q_at][i, q_off : q_off + rows_q, q_lane + h * HD : q_lane + (h + 1) * HD]
            qa_ref[h, dst, :] = spread(q.astype(f32) * (1.0 / math.sqrt(HD)), {3: 1.0})
        return 0

    lax.fori_loop(0, blocks, build, 0)
    total = ka.shape[1]

    def block(b, _):
        rows = pl.ds(pl.multiple_of(b * bq, bq), bq)

        def chunk(c, carry):
            cols = pl.ds(pl.multiple_of(c * kc, kc), kc)
            out = []
            for h in range(hpd):
                m, acc = carry[h]
                s = dot(qa_ref[h, rows, :], ka[h, cols, :], NT)
                top = jnp.maximum(m, jnp.max(s, axis=1, keepdims=True))
                p = jnp.exp(s - top).astype(bf16)
                out.append((top, acc * jnp.exp(m - top) + dot(p, va[h, cols, :], NN)))
            return tuple(out)

        carry = ((jnp.full((bq, 1), -1e30, f32), jnp.zeros((bq, LANES), f32)),) * hpd
        if fixed:
            for c in range(total // kc):
                carry = chunk(c, carry)
        else:
            carry = lax.fori_loop(0, (n_ref[0] + kc - 1) // kc, chunk, carry)
        outs = []
        for h in range(hpd):
            m, acc = carry[h]
            norm = acc[:, HD : HD + 1]
            outs.append(acc[:, :HD] / norm)
            hi, mid, lo = split3(-(m + jnp.log(norm)))
            qa_ref[h, rows, :] = spread(
                qa_ref[h, rows, :HD].astype(f32), {0: hi, 1: mid, 2: lo, 3: 1.0}
            )
        o_ref[rows, :] = jnp.concatenate(outs, axis=1).astype(bf16)
        return 0

    lax.fori_loop(0, qa_ref.shape[1] // bq, block, 0)


def bwd_kernel(n_ref, *refs, n_in, blocks, do_spec, kv_specs, hpd, bq, kc, fixed):
    ins, (dq_ref, dkv_ref, ka, va, da, dk, dv) = refs[:n_in], refs[n_in:]
    qa_ref, do_ref, o_ref = ins[:3]
    load_keys(n_ref, kv_specs, ins, ka, va, hpd, blocks)
    rows_q, do_off = do_spec

    def build(i, _):
        rows = pl.ds(pl.multiple_of(i * rows_q, 16), rows_q)
        for h in range(hpd):
            d = do_ref[i, do_off : do_off + rows_q, h * HD : (h + 1) * HD].astype(f32)
            o = o_ref[rows, h * HD : (h + 1) * HD].astype(f32)
            hi, mid, lo = split3(-jnp.sum(d * o, axis=1, keepdims=True))
            da[h, rows, :] = spread(d, {0: hi, 1: mid, 2: lo})
        return 0

    lax.fori_loop(0, blocks, build, 0)
    dk[...] = jnp.zeros_like(dk)
    dv[...] = jnp.zeros_like(dv)
    total = ka.shape[1]
    steps = total // kc if fixed else (n_ref[0] + kc - 1) // kc

    def block(b, _):
        rows = pl.ds(pl.multiple_of(b * bq, bq), bq)

        def chunk(c, dqs):
            cols = pl.ds(pl.multiple_of(c * kc, kc), kc)
            out = []
            for h in range(hpd):
                k, q, d = ka[h, cols, :], qa_ref[h, rows, :], da[h, rows, :]
                p = jnp.exp(dot(k, q, NT))
                dp = dot(va[h, cols, :], d, NT)
                dv[h, cols, :] += dot(p.astype(bf16), d, NN)
                g = (p * dp).astype(bf16)
                dk[h, cols, :] += dot(g, q, NN)
                out.append(dqs[h] + dot(k, g, TN))
            return tuple(out)

        dqs = lax.fori_loop(0, steps, chunk, (jnp.zeros((LANES, bq), f32),) * hpd)
        dq = jnp.concatenate([v[:HD, :] for v in dqs], axis=0).T
        dq_ref[rows, :] = (dq * (1.0 / math.sqrt(HD))).astype(bf16)
        return 0

    lax.fori_loop(0, qa_ref.shape[1] // bq, block, 0)
    step = total // blocks

    def finish(i, _):
        rows = pl.ds(pl.multiple_of(i * step, 16), step)
        parts = [dk[h, rows, :HD] for h in range(hpd)] + [dv[h, rows, :HD] for h in range(hpd)]
        dkv_ref[rows, :] = jnp.concatenate(parts, axis=1).astype(bf16)
        return 0

    lax.fori_loop(0, blocks, finish, 0)


VM = pl.BlockSpec(memory_space=pltpu.VMEM)
SM = pl.BlockSpec(memory_space=pltpu.SMEM)


def fit(rows, most):
    return math.gcd(rows, most)


def attend(limits, ins, blocks, q_spec, kv_specs, total, hpd, fixed):
    queries = blocks * q_spec[1]
    kc = fit(total, 1024 if fixed else 512)
    body = functools.partial(
        fwd_kernel,
        n_in=len(ins),
        blocks=blocks,
        q_spec=q_spec,
        kv_specs=kv_specs,
        hpd=hpd,
        bq=fit(queries, 512),
        kc=kc,
        fixed=fixed,
    )
    work = hpd * queries * total
    return pl.pallas_call(
        body,
        out_shape=(
            jax.ShapeDtypeStruct((queries, hpd * HD), bf16),
            jax.ShapeDtypeStruct((hpd, queries, LANES), bf16),
        ),
        in_specs=[SM] + [VM] * len(ins),
        out_specs=(VM, VM),
        scratch_shapes=[pltpu.VMEM((hpd, total, LANES), bf16)] * 2,
        compiler_params=pltpu.CompilerParams(vmem_limit_bytes=44 * 2**20),
        cost_estimate=pl.CostEstimate(
            flops=1024 * work, bytes_accessed=16 * queries * hpd * HD, transcendentals=work
        ),
    )(limits, *ins)


def attend_back(limits, ins, blocks, do_spec, kv_specs, total, hpd, fixed):
    queries = blocks * do_spec[0]
    body = functools.partial(
        bwd_kernel,
        n_in=len(ins),
        blocks=blocks,
        do_spec=do_spec,
        kv_specs=kv_specs,
        hpd=hpd,
        bq=fit(queries, 512),
        kc=fit(total, 512),
        fixed=fixed,
    )
    work = hpd * queries * total
    return pl.pallas_call(
        body,
        out_shape=(
            jax.ShapeDtypeStruct((queries, hpd * HD), bf16),
            jax.ShapeDtypeStruct((total, 2 * hpd * HD), bf16),
        ),
        in_specs=[SM] + [VM] * len(ins),
        out_specs=(VM, VM),
        scratch_shapes=[pltpu.VMEM((hpd, total, LANES), bf16)] * 2
        + [pltpu.VMEM((hpd, queries, LANES), bf16)]
        + [pltpu.VMEM((hpd, total, LANES), f32)] * 2,
        compiler_params=pltpu.CompilerParams(vmem_limit_bytes=52 * 2**20),
        cost_estimate=pl.CostEstimate(
            flops=2560 * work, bytes_accessed=24 * queries * hpd * HD, transcendentals=work
        ),
    )(limits, *ins)


def norm_parts(values):
    center = values - jnp.mean(values, axis=-1, keepdims=True)
    scale = lax.rsqrt(jnp.mean(center * center, axis=-1, keepdims=True) + norm_eps)
    return center * scale, scale


def layer_norm(values, gain_row, shift_row):
    return (norm_parts(values)[0] * gain_row + shift_row).astype(bf16)


def norm_back(values, gain_row, grad_out):
    unit, scale = norm_parts(values)
    lifted = grad_out * gain_row
    grad_in = scale * (
        lifted
        - jnp.mean(lifted, axis=-1, keepdims=True)
        - unit * jnp.mean(lifted * unit, axis=-1, keepdims=True)
    )
    gain = jnp.sum(grad_out * unit, axis=0, keepdims=True)
    return grad_in, gain, jnp.sum(grad_out, axis=0, keepdims=True)


def flat(ref):
    return ref[...].reshape(-1, ref.shape[-1])


def joined(ref):
    return jnp.concatenate([ref[i] for i in range(ref.shape[0])], axis=1)


def once(shape, index=None):
    at = (0,) * len(shape) if index is None else index
    return pl.BlockSpec(shape, lambda i: at, pipeline_mode=pl.Buffered(1))


def held(shape):
    return pl.BlockSpec(shape, lambda i: (0,) * len(shape))


def mid_kernel(a_ref, x_ref, norm_ref, wo_ref, wt_ref, x1_ref, n_ref, ac_ref, t_ref):
    @pl.when(pl.program_id(0) == 0)
    def _():
        a = joined(a_ref)
        ac_ref[...] = a
        x1 = x_ref[...].astype(f32) + dot(a, flat(wo_ref), NN)
        x1_ref[...] = x1
        n_ref[...] = layer_norm(x1, norm_ref[0:1, :], norm_ref[1:2, :])

    t_ref[0] = dot(n_ref[...], flat(wt_ref), NT).astype(bf16)


def middle(a, x, norm, w_out, w_triple):
    S, rows, W = a.shape
    D = S * W
    return pl.pallas_call(
        mid_kernel,
        grid=(S,),
        out_shape=(
            jax.ShapeDtypeStruct((rows, D), f32),
            jax.ShapeDtypeStruct((rows, D), bf16),
            jax.ShapeDtypeStruct((rows, D), bf16),
            jax.ShapeDtypeStruct((S, rows, 3 * W), bf16),
        ),
        in_specs=[
            once((S, rows, W)),
            once((rows, D)),
            once((2, D)),
            w_out[1],
            w_triple[1],
        ],
        out_specs=(
            held((rows, D)),
            held((rows, D)),
            held((rows, D)),
            pl.BlockSpec((1, rows, 3 * W), lambda i: (i, 0, 0)),
        ),
        compiler_params=pltpu.CompilerParams(vmem_limit_bytes=40 * 2**20),
        cost_estimate=pl.CostEstimate(
            flops=8 * rows * D * D, bytes_accessed=8 * D * D + 14 * rows * D, transcendentals=0
        ),
    )(a, x, norm, w_out[0], w_triple[0])


def mlp_kernel(
    aa_ref,
    ab_ref,
    xa_ref,
    xb_ref,
    ca_ref,
    cb_ref,
    dp_ref,
    norm_ref,
    ws_ref,
    wd_ref,
    up_ref,
    down_ref,
    n_ref,
    ac_ref,
    g_ref,
    du_ref,
    x3_ref,
    pix_ref,
    e3_ref,
    d2_ref,
    e2_ref,
    da_ref,
    db_ref,
    sum_ref,
    x2,
    d3,
    acc,
    back,
    *,
    steps,
):
    step = pl.program_id(0)
    R = xa_ref.shape[0]
    S, _, W = aa_ref.shape

    @pl.when(step == 0)
    def _():
        for rows, a_ref, x_ref, c_ref in (
            (slice(0, R), aa_ref, xa_ref, ca_ref),
            (slice(R, x2.shape[0]), ab_ref, xb_ref, cb_ref),
        ):
            a = joined(a_ref)
            ac_ref[rows, :] = a
            x = x_ref[...] + dot(a, flat(ws_ref), NN)
            x2[rows, :] = x
            n_ref[rows, :] = layer_norm(x, norm_ref[0:1, :], norm_ref[1:2, :])
            d = c_ref[...].astype(f32) + dot(dp_ref[rows, :], flat(wd_ref), NN)
            d3[rows, :] = d
            e3_ref[rows, :] = d.astype(bf16)
        acc[...] = jnp.zeros_like(acc)
        back[...] = jnp.zeros_like(back)

    up = flat(up_ref)
    u = dot(n_ref[...], up, NT)
    slope = math.sqrt(2.0 / math.pi)
    square = u * u
    bend = jnp.tanh(slope * u * (1.0 + 0.044715 * square))
    half = 0.5 * (1.0 + bend)
    g = (u * half).astype(bf16)
    rise = half + 0.5 * slope * u * (1.0 - bend * bend) * (1.0 + 0.134145 * square)
    du = (dot(e3_ref[...], down_ref[...], NT) * rise).astype(bf16)
    g_ref[...] = g
    du_ref[...] = du
    acc[...] += dot(g, down_ref[...], NN)
    back[...] += dot(du, up, NN)

    @pl.when(step == steps - 1)
    def _():
        x3 = (x2[...] + acc[...]).astype(bf16)
        x3_ref[...] = x3
        pix_ref[...] = dot(x3, flat(wd_ref), NT).astype(bf16)
        grad_in, gain, shift = norm_back(x2[...], norm_ref[0:1, :], back[...])
        d2 = d3[...] + grad_in
        d2_ref[...] = d2
        e2 = d2.astype(bf16)
        e2_ref[...] = e2
        sum_ref[...] = jnp.concatenate([gain, shift], axis=0)
        da = dot(e2, flat(ws_ref), NT).astype(bf16)
        for i in range(S):
            da_ref[i] = da[:R, i * W : (i + 1) * W]
            db_ref[i] = da[R:, i * W : (i + 1) * W]


def feed_forward(a, x1, cot, d_pix, norm, w_out, w_dec, w_up, w_down, steps):
    S, R, W = a[0].shape
    RB = a[1].shape[1]
    D, total, pixels = S * W, R + RB, d_pix.shape[1]
    hidden = w_down.shape[0]
    part = hidden // steps
    row = jax.ShapeDtypeStruct((total, D), bf16)
    wide = jax.ShapeDtypeStruct((total, hidden), bf16)
    blocked = pl.BlockSpec((total, part), lambda i: (0, i))
    full = held((total, D))
    return pl.pallas_call(
        functools.partial(mlp_kernel, steps=steps),
        grid=(steps,),
        out_shape=(
            row,
            row,
            wide,
            wide,
            row,
            jax.ShapeDtypeStruct((total, pixels), bf16),
            row,
            jax.ShapeDtypeStruct((total, D), f32),
            row,
            jax.ShapeDtypeStruct((S, R, W), bf16),
            jax.ShapeDtypeStruct((S, RB, W), bf16),
            jax.ShapeDtypeStruct((2, D), f32),
        ),
        in_specs=[
            once((S, R, W)),
            once((S, RB, W)),
            once((R, D)),
            once((RB, D)),
            once((R, D)),
            once((RB, D)),
            once((total, pixels)),
            once((2, D)),
            w_out[1],
            w_dec[1],
            w_up[1],
            pl.BlockSpec((part, D), lambda i: (i, 0)),
        ],
        out_specs=(
            full,
            full,
            blocked,
            blocked,
            full,
            held((total, pixels)),
            full,
            full,
            full,
            held((S, R, W)),
            held((S, RB, W)),
            held((2, D)),
        ),
        scratch_shapes=[pltpu.VMEM((total, D), f32)] * 4,
        compiler_params=pltpu.CompilerParams(vmem_limit_bytes=60 * 2**20),
        cost_estimate=pl.CostEstimate(
            flops=8 * total * D * hidden + 8 * total * D * D,
            bytes_accessed=4 * D * hidden + 30 * total * D,
            transcendentals=total * hidden,
        ),
    )(*a, *x1, *cot, d_pix, norm, w_out[0], w_dec[0], w_up[0], w_down)


def back_kernel(
    t_ref, x_ref, d_ref, norm_ref, wo_ref, wt_ref, d1_ref, e_ref, da_ref, sum_ref, acc, *, steps
):
    step = pl.program_id(0)
    part = dot(t_ref[0], flat(wt_ref), NN)

    @pl.when(step == 0)
    def _():
        acc[...] = part

    @pl.when(step > 0)
    def _():
        acc[...] += part

    @pl.when(step == steps - 1)
    def _():
        grad_in, gain, shift = norm_back(x_ref[...], norm_ref[0:1, :], acc[...])
        d1 = d_ref[...] + grad_in
        d1_ref[...] = d1
        e = d1.astype(bf16)
        e_ref[...] = e
        sum_ref[...] = jnp.concatenate([gain, shift], axis=0)
        da = dot(e, flat(wo_ref), NT).astype(bf16)
        W = da_ref.shape[2]
        for i in range(steps):
            da_ref[i] = da[:, i * W : (i + 1) * W]


def middle_back(t, x1, d2, at, norm, w_out, w_triple):
    S, rows, wide = t.shape
    D = x1.shape[1]
    W = wide // 3
    return pl.pallas_call(
        functools.partial(back_kernel, steps=S),
        grid=(S,),
        out_shape=(
            jax.ShapeDtypeStruct((rows, D), f32),
            jax.ShapeDtypeStruct((rows, D), bf16),
            jax.ShapeDtypeStruct((S, rows, W), bf16),
            jax.ShapeDtypeStruct((2, D), f32),
        ),
        in_specs=[
            pl.BlockSpec((1, rows, wide), lambda i: (i, 0, 0)),
            once((rows, D)),
            once((rows, D), (at, 0)),
            once((2, D)),
            w_out[1],
            w_triple[1],
        ],
        out_specs=(
            held((rows, D)),
            held((rows, D)),
            held((S, rows, W)),
            held((2, D)),
        ),
        scratch_shapes=[pltpu.VMEM((rows, D), f32)],
        compiler_params=pltpu.CompilerParams(vmem_limit_bytes=40 * 2**20),
        cost_estimate=pl.CostEstimate(
            flops=8 * rows * D * D, bytes_accessed=8 * D * D + 24 * rows * D, transcendentals=0
        ),
    )(t, x1, d2, norm, w_out[0], w_triple[0])


def grads_kernel(*refs, shape, widths):
    count = sum(shape)
    lefts, rights = refs[:count], refs[count : 2 * count]
    out_ref, turned = refs[2 * count], refs[2 * count + 1 :]

    @pl.when(pl.program_id(0) == 0)
    def _():
        for left, t in zip(lefts, turned):
            t[...] = left[...].T

    at = n = 0
    for pieces, width in zip(shape, widths):
        total = 0.0
        for i in range(n, n + pieces):
            right = joined(rights[i]) if len(rights[i].shape) == 3 else rights[i][...]
            total += dot(turned[i][...], right, NN)
        out_ref[:, at : at + width] = total.astype(bf16)
        at, n = at + width, n + pieces


def weight_grads(terms, ranks):
    pieces = [p for term in terms for p in term]
    shape = [len(term) for term in terms]
    widths = [term[0][1].size // term[0][0].shape[0] // ranks for term in terms]
    D, per = pieces[0][0].shape[1], sum(widths)
    lefts = [p[0] for p in pieces]
    rights = [p[1] for p in pieces]
    work = sum(p[0].shape[0] for p in pieces) * D * per * ranks // len(pieces)
    return pl.pallas_call(
        functools.partial(grads_kernel, shape=shape, widths=widths),
        grid=(ranks,),
        out_shape=jax.ShapeDtypeStruct((D, per * ranks), bf16),
        in_specs=[once(v.shape) for v in lefts]
        + [
            pl.BlockSpec((v.shape[0] // ranks,) + v.shape[1:], lambda i: (i, 0, 0))
            if v.ndim == 3
            else pl.BlockSpec((v.shape[0], v.shape[1] // ranks), lambda i: (0, i))
            for v in rights
        ],
        out_specs=pl.BlockSpec((D, per), lambda i: (0, i)),
        scratch_shapes=[pltpu.VMEM(v.shape[::-1], bf16) for v in lefts],
        compiler_params=pltpu.CompilerParams(vmem_limit_bytes=56 * 2**20),
        cost_estimate=pl.CostEstimate(
            flops=2 * work, bytes_accessed=4 * D * per * ranks, transcendentals=0
        ),
    )(*lefts, *rights)


CP = 32


def place(perm, toks, TR, TC):
    own, ext = TR * TC, perm.shape[2]
    tok = lax.broadcasted_iota(jnp.int32, (toks, 1), 0)
    row = jnp.where(tok < own, tok // TC, jnp.where(tok < own + TR, tok - own, TR))
    col = jnp.where(
        tok < own, tok % TC, jnp.where(tok < own + TR, TC, tok - own - TR)
    )
    real = tok <= own + TR + TC
    pixel = lax.broadcasted_iota(jnp.int32, (toks, ext), 1)
    for a in range(2):
        for b in range(2):
            ok = real & ((row < TR) | (a == 0)) & ((col < TC) | (b == 0))
            at = jnp.where(ok, (2 * row + a) * (2 * TC + 1) + 2 * col + b, -1)
            perm[2 * a + b] = jnp.where(pixel == at, 1.0, 0.0).astype(bf16)


def pixel_grad_kernel(cot_ref, w_ref, out_ref, perm, *, TR, TC):
    @pl.when(pl.program_id(0) == 0)
    def _():
        place(perm, out_ref.shape[1], TR, TC)

    grad = dot(cot_ref[0], w_ref[0], NT)
    hi = grad.astype(bf16)
    lo = (grad - hi.astype(f32)).astype(bf16)
    parts = [dot(perm[i], hi, NT) + dot(perm[i], lo, NT) for i in range(4)]
    out_ref[0] = jnp.concatenate(parts, axis=1)


def pixel_sample_kernel(x_ref, w_ref, out_ref, perm, *, TR, TC):
    @pl.when(pl.program_id(0) == 0)
    def _():
        place(perm, x_ref.shape[1], TR, TC)

    x = x_ref[0]
    window = sum(dot(x[:, i * CP : (i + 1) * CP], perm[i], TN) for i in range(4))
    out_ref[0] = dot(window.astype(bf16), w_ref[0], NN).astype(bf16)


def per_plane(body, first, weights, out_rows, out_lanes, out_type, toks, TR, TC):
    planes, ext, samples = weights.shape

    def whole(shape):
        return pl.BlockSpec((1,) + shape, lambda i: (i, 0, 0))

    return pl.pallas_call(
        functools.partial(body, TR=TR, TC=TC),
        grid=(planes,),
        out_shape=jax.ShapeDtypeStruct((planes, out_rows, out_lanes), out_type),
        in_specs=[whole(first.shape[1:]), whole((ext, samples))],
        out_specs=whole((out_rows, out_lanes)),
        scratch_shapes=[pltpu.VMEM((4, toks, ext), bf16)],
        compiler_params=pltpu.CompilerParams(vmem_limit_bytes=24 * 2**20),
        cost_estimate=pl.CostEstimate(
            flops=6 * 10**8, bytes_accessed=7 * 10**6, transcendentals=0
        ),
    )(first, weights)


def swap_seq(value):
    return lax.all_to_all(value, "seq", split_axis=0, concat_axis=0, tiled=True)


def swap_mp(value):
    return lax.all_to_all(value, "mp", split_axis=0, concat_axis=0, tiled=True)


def swap_all(value):
    return lax.all_to_all(value, ("seq", "mp"), split_axis=0, concat_axis=0, tiled=True)


def swap_pair(value):
    count = lax.axis_size("mp")
    return lax.ppermute(value, "mp", [(i, i ^ 1) for i in range(count)])


def gather_rows(piece):
    return lax.all_gather(piece, ("mp", "seq"), axis=0, tiled=False)


def bundle_part(bundle, at, rows, per_step=None):
    pieces, _, D = bundle.shape
    if rows % 16 == 0 and at % rows == 0:
        place = at // rows
        if per_step is None:
            return bundle, once((pieces, rows, D), (0, place, 0))
        return bundle, pl.BlockSpec((per_step, rows, D), lambda i: (i, place, 0))
    value = bundle[:, at : at + rows].reshape(1, -1, D)
    if per_step is None:
        return value, once(value.shape)
    return value, pl.BlockSpec((1, per_step * rows, D), lambda i: (0, i, 0))


def reduce_rows(value):
    return lax.psum_scatter(value, "seq", scatter_dimension=0, tiled=True)


def from_ranks(blocks):
    ranks, rank = lax.axis_size("mp"), lax.axis_index("mp")
    got = []
    for step in range(ranks):
        block = lax.dynamic_index_in_dim(blocks, rank ^ step, 0, keepdims=False)
        if step > 0:
            block = lax.ppermute(block, "mp", [(i, i ^ step) for i in range(ranks)])
        got.append(block)
    return got


def in_order(got, at):
    got = jnp.stack(got)
    return [lax.dynamic_index_in_dim(got, at ^ i, 0, keepdims=False) for i in range(got.shape[0])]


def sum_ranks(value):
    ranks = lax.axis_size("mp")
    parts = value.reshape(value.shape[0], ranks, -1).transpose(1, 0, 2)
    return sum(v.astype(f32) for v in from_ranks(parts))


def gather_seq(value):
    shares, me = lax.axis_size("seq"), lax.axis_index("seq")
    got = [value]
    for step in range(1, shares // 2):
        moves = [(i, i ^ (2 * step)) for i in range(shares)]
        got.append(lax.ppermute(value, "seq", moves))
    got = jnp.stack(got)
    other = lax.ppermute(got, "seq", [(i, i ^ 1) for i in range(shares)])
    both = jnp.stack([got, other], axis=1).reshape((shares,) + value.shape)
    return jnp.stack(
        [lax.dynamic_index_in_dim(both, me ^ i, 0, keepdims=False) for i in range(shares)]
    )


def own_blocks(whole, blocks):
    ranks, rank = lax.axis_size("mp"), lax.axis_index("mp")
    pairs = ranks // 2
    pair = rank // 2
    own = whole.shape[0] // ranks
    whole = in_order(from_ranks(whole.reshape(ranks, own, -1)), rank)
    blocks = blocks.reshape(pairs, own, -1)
    arrived = []
    for step in range(pairs):
        moves = [(2 * p + h, pairs * h + (p ^ step)) for p in range(pairs) for h in range(2)]
        block = lax.dynamic_index_in_dim(blocks, pair ^ step, 0, keepdims=False)
        arrived.append(lax.ppermute(block, "mp", moves))
    arrived = in_order(arrived, rank % pairs)
    rows = []
    for p in range(pairs):
        rows += [whole[2 * p], arrived[p], whole[2 * p + 1]]
    return jnp.stack(rows)


def to_rows(value):
    return swap_seq(value).transpose(1, 0, 2).reshape(value.shape[1], -1)


def after(values, others):
    return lax.optimization_barrier((values, others))[0]


def per_device(
    tokens,
    patches,
    counts,
    norm_gains,
    norm_shifts,
    cross_query,
    cross_kv,
    cross_out,
    self_qkv,
    self_out,
    mlp_up,
    mlp_down,
    decoder,
    sample_weights,
    tokens_cot,
    sample_cot,
):
    objects, R, D = tokens.shape
    S, M = lax.axis_size("seq"), lax.axis_size("mp")
    s, m = lax.axis_index("seq"), lax.axis_index("mp")
    pairs = M // 2
    if objects != 3 * pairs or S != 2 * M or D % (HD * S) != 0:
        raise ValueError("unexpected sizes")
    pair, half = m // 2, m % 2
    at_a, at_b = 3 * pair + 2 * half, 3 * pair + 1
    RB = R // 2
    RS = R + RB
    rows = [R, RB]
    W = D // S
    hpd = W // HD
    slots, width = patches.shape[1], patches.shape[2]
    slot_total = slots * S
    row_total = R * S

    def pick(arr):
        whole = lax.dynamic_index_in_dim(arr, at_b, 0, keepdims=False)
        return [
            lax.dynamic_index_in_dim(arr, at_a, 0, keepdims=False),
            lax.dynamic_slice_in_dim(whole, half * RB, RB, 0),
        ]

    def mine(arr, axis):
        share = arr.shape[axis] // S
        return lax.dynamic_slice_in_dim(arr, s * share, share, axis)

    channels = decoder.shape[1]
    local_dec = jnp.pad(decoder.transpose(2, 1, 0), ((0, 0), (0, CP - channels), (0, 0)))
    local_qkv = self_qkv.reshape(D, 3, 2, W).transpose(2, 1, 3, 0).reshape(-1, D)
    local_kv = cross_kv.reshape(width, 2, 2, W).transpose(2, 1, 3, 0).reshape(-1, width)
    per = D // (S * M)
    up_rows = mlp_up.shape[1] // S
    dec_rows = 4 * CP // S
    lead = jnp.concatenate([mine(cross_query, 1).T, mine(local_kv, 0).reshape(-1, D)], axis=0)
    lead = gather_rows(lead)
    w_query = lead[:, :per].reshape(-1, D)
    w_kv = lead[:, per:].reshape(-1, width)
    first = gather_rows(jnp.concatenate([mine(local_qkv, 0), mine(cross_out, 0)], axis=0))
    w_triple = bundle_part(first, 0, 3 * per, M)
    w_cross_out = bundle_part(first, 3 * per, per)
    second = gather_rows(
        jnp.concatenate(
            [mine(mlp_up, 1).T, mine(self_out, 0), mine(local_dec.reshape(-1, D), 0)], axis=0
        )
    )
    steps = 8
    w_up = bundle_part(second, 0, up_rows, S * M // steps)
    w_self_out = bundle_part(second, up_rows, per)
    w_dec = bundle_part(second, up_rows + per, dec_rows)
    w_down = gather_rows(mine(mlp_down, 0)).reshape(-1, D)

    x0 = pick(tokens)
    both = [lax.dynamic_index_in_dim(patches, o, 0, keepdims=False) for o in (at_a, at_b)]
    patch_all = gather_seq(jnp.concatenate(both, axis=0)).reshape(-1, width)
    x0_all = jnp.concatenate(x0, axis=0)
    n1 = layer_norm(x0_all.astype(f32), norm_gains[0], norm_shifts[0])
    q1 = dot(n1, w_query, NT).astype(bf16)
    heads_one = swap_seq(q1.reshape(RS, S, W).transpose(1, 0, 2))
    own_kv = lax.dynamic_slice_in_dim(w_kv, s * 2 * W, 2 * W, 0)
    keys_one = dot(patch_all, own_kv, NT).astype(bf16).reshape(S, 2 * slots, 2 * W)

    TC = PLANE // 4
    TR = PLANE * 4 // S
    own, rim = TR * TC, TR * TC + TR
    toks = -(-(rim + TC + 1) // 32) * 32
    planes = objects * 3
    weights_in = sample_weights.reshape(planes, *sample_weights.shape[3:])
    cot_in = sample_cot.reshape(planes, channels, -1)
    cot_in = jnp.pad(cot_in, ((0, 0), (0, CP - channels), (0, 0)))
    ext = per_plane(pixel_grad_kernel, cot_in, weights_in, toks, 4 * CP, f32, toks, TR, TC)
    ways = {
        1: [i for i in range(S) if i % 4 != 3],
        4: [i for i in range(S) if i + 4 < S],
        5: [i for i in range(S) if i % 4 != 3 and i + 4 < S],
    }
    rights = lax.ppermute(ext[:, own:rim], "seq", [(i, i + 1) for i in ways[1]])
    belows = lax.ppermute(ext[:, rim : rim + TC], "seq", [(i, i + 4) for i in ways[4]])
    corner = lax.ppermute(ext[:, rim + TC : rim + TC + 1], "seq", [(i, i + 5) for i in ways[5]])
    grid = ext[:, :own].reshape(planes, TR, TC, -1)
    belows = jnp.concatenate([belows[:, :1] + corner, belows[:, 1:]], axis=1)
    grid = grid + jnp.pad(rights[:, :, None], ((0, 0), (0, 0), (0, TC - 1), (0, 0)))
    grid = grid + jnp.pad(belows[:, None], ((0, 0), (0, TR - 1), (0, 0), (0, 0)))
    KA, KB = R // S, RB // S
    cu = 4 * CP
    grad_pix = grid.astype(bf16).reshape(pairs, 3, S, KA, cu)
    gp_a = jnp.stack([grad_pix[:, 0], grad_pix[:, 2]], axis=1).transpose(2, 0, 1, 3, 4)
    gp_b = grad_pix[:, 1].reshape(pairs, S, 2, KB, cu).transpose(1, 0, 2, 3, 4)
    sent = jnp.concatenate([gp_a, gp_b], axis=3).reshape(S * M, KA + KB, cu)
    back = swap_all(sent).reshape(S, M, KA + KB, cu).transpose(2, 0, 1, 3)
    d_pix = back.reshape(RS, M * cu)

    limits = [
        jnp.stack([lax.dynamic_index_in_dim(counts, o, 0, keepdims=False), jnp.int32(0)])
        for o in (at_a, at_b)
    ]
    kv_one = [(slots, (i * slots, 0), (i * slots, W), 0) for i in range(2)]
    o1, res1 = [], []
    for i in range(2):
        out, res = attend(
            limits[i],
            [heads_one, keys_one],
            S,
            (0, rows[i], i * R, 0),
            [(1,) + kv_one[i]],
            slot_total,
            hpd,
            False,
        )
        o1.append(out)
        res1.append(res)

    norms = [jnp.stack([norm_gains[i], norm_shifts[i]]) for i in range(3)]
    mids = [
        middle(swap_seq(o1[i].reshape(S, rows[i], W)), x0[i], norms[1], w_cross_out, w_triple)
        for i in range(2)
    ]
    x1, n2, a1, t2 = zip(*mids)

    heads_two = [swap_seq(v) for v in t2]
    pair_kv = swap_pair(heads_two[1][:, :, W:])
    wide = jnp.array([row_total, 0], jnp.int32)
    kv_a2 = (R, (0, W), (0, 2 * W), 0)
    kv_b2 = (RB, (0, W), (0, 2 * W), 0)
    kv_p2 = (RB, (0, 0), (0, W), row_total // 2)
    o_a2, res_a2 = attend(
        wide, [heads_two[0]], S, (0, R, 0, 0), [(0,) + kv_a2], row_total, hpd, True
    )
    o_b2, res_b2 = attend(
        wide,
        [heads_two[1], pair_kv],
        S,
        (0, RB, 0, 0),
        [(0,) + kv_b2, (1,) + kv_p2],
        row_total,
        hpd,
        True,
    )
    a2 = [swap_seq(o_a2.reshape(S, R, W)), swap_seq(o_b2.reshape(S, RB, W))]

    n3, a2, g, du, x3b, pix, e3, d2, e2, da2_a, da2_b, sums_three = feed_forward(
        a2, x1, pick(tokens_cot), d_pix, norms[2], w_self_out, w_dec, w_up, w_down, steps
    )

    da2 = [swap_seq(da2_a), swap_seq(da2_b)]
    grads_one = weight_grads([[(n3, du)], [(e3, g)], [(e2, a2)], [(x3b, d_pix)]], M)
    da2[0] = after(da2[0], grads_one)
    grads_one = reduce_rows(grads_one)
    dq_a2, dkv_a2 = attend_back(
        wide,
        [res_a2, da2[0], o_a2, heads_two[0]],
        S,
        (R, 0),
        [(3,) + kv_a2],
        row_total,
        hpd,
        True,
    )
    tokens_out = own_blocks(x3b[:R], x3b[R:])
    pix = pix.reshape(KA + KB, S, M, cu).transpose(1, 2, 0, 3)
    got = swap_all(pix.reshape(S * M, KA + KB, cu)).reshape(S, pairs, 2, KA + KB, cu)
    da2[1] = after(da2[1], (tokens_out, got, dkv_a2))
    dq_b2, dkv_b2 = attend_back(
        wide,
        [res_b2, da2[1], o_b2, heads_two[1], pair_kv],
        S,
        (RB, 0),
        [(3,) + kv_b2, (4,) + kv_p2],
        row_total,
        hpd,
        True,
    )
    kept, given = dkv_b2[: row_total // 2], dkv_b2[row_total // 2 :]
    dkv_b2 = (kept.astype(f32) + swap_pair(given).astype(f32)).astype(bf16)
    dt2 = [
        swap_seq(jnp.concatenate([dq_a2, dkv_a2], axis=1).reshape(S, R, 3 * W)),
        swap_seq(jnp.concatenate([dq_b2, dkv_b2], axis=1).reshape(S, RB, 3 * W)),
    ]
    outs = [
        middle_back(dt2[i], x1[i], d2, (0, R // RB)[i], norms[1], w_cross_out, w_triple)
        for i in range(2)
    ]
    d1, e1, da1, sums_two = zip(*outs)
    da1 = [swap_seq(v) for v in da1]

    px_a = got[:, :, :, :KA].transpose(1, 2, 0, 3, 4).reshape(pairs, 2, S * KA, cu)
    px_b = got[:, :, :, KA:].transpose(1, 0, 2, 3, 4).reshape(pairs, S * KA, cu)
    tile = jnp.stack([px_a[:, 0], px_b, px_a[:, 1]], axis=1).reshape(planes, TR, TC, cu)
    rights = lax.ppermute(tile[:, :, 0], "seq", [(i + 1, i) for i in ways[1]])
    belows = lax.ppermute(tile[:, 0], "seq", [(i + 4, i) for i in ways[4]])
    corner = lax.ppermute(tile[:, 0, :1], "seq", [(i + 5, i) for i in ways[5]])
    fill = jnp.zeros((planes, toks - rim - TC - 1, cu), bf16)
    ext = jnp.concatenate([tile.reshape(planes, own, cu), rights, belows, corner, fill], axis=1)
    sampled = per_plane(
        pixel_sample_kernel, ext, weights_in, CP, weights_in.shape[2], bf16, toks, TR, TC
    )
    sampled = sampled[:, :channels].reshape(objects, 3, channels, 1, -1)

    grads_two = weight_grads(
        [[(n2[i], dt2[i]) for i in range(2)], [(e1[i], a1[i]) for i in range(2)]], M
    )
    n1_all = gather_seq(n1).reshape(-1, D)
    da1[1] = after(da1[1], (grads_two, sampled, n1_all))
    grads_two = reduce_rows(grads_two)
    dq1, dkv1 = [], []
    for i in range(2):
        dq, dkv = attend_back(
            limits[i],
            [res1[i], da1[i], o1[i], keys_one],
            S,
            (rows[i], 0),
            [(3,) + kv_one[i]],
            slot_total,
            hpd,
            False,
        )
        dq1.append(dq.reshape(S, rows[i], W))
        dkv1.append(dkv.reshape(S, slots, 2 * W))

    parts = [mm(to_rows(v), w_kv).astype(bf16) for v in dkv1]
    every = [[p] for p in parts]
    for step in range(1, M):
        moves = [(i, i ^ step) for i in range(M)]
        for i in range(2):
            every[i].append(lax.ppermute(parts[i], "mp", moves))
    from_a, from_b = [in_order(v, m) for v in every]
    patch_grad = []
    for p in range(pairs):
        shared = from_b[2 * p].astype(f32) + from_b[2 * p + 1].astype(f32)
        patch_grad += [from_a[2 * p].astype(f32), shared, from_a[2 * p + 1].astype(f32)]
    patch_grad = jnp.stack(patch_grad)

    grads = [mm(to_rows(v), w_query) for v in dq1]
    back_one = [norm_back(x0[i].astype(f32), norm_gains[0], grads[i]) for i in range(2)]
    d0 = [(d1[i] + back_one[i][0]).astype(bf16) for i in range(2)]
    grad_tokens = own_blocks(d0[0], d0[1]).astype(f32)

    order = 2 * m + s % 2
    dq_all = jnp.concatenate(dq1, axis=1).reshape(-1, W)
    dkv_all = jnp.concatenate(dkv1, axis=1).reshape(-1, 2 * W)
    grad_q = dot(n1_all, dq_all, TN).astype(bf16).reshape(S, D // S, W)
    grad_kv = dot(patch_all, dkv_all, TN).astype(bf16)
    grad_kv = grad_kv.reshape(S, width // S, 2 * W)
    grad_kv = jnp.concatenate([grad_kv[..., :W], grad_kv[..., W:]], axis=1)
    by_head = jnp.concatenate([grad_q, grad_kv], axis=1)
    sums = [0.0, 0.0]
    for step in range(S):
        moves = []
        for i in range(S):
            for j in range(M):
                t = i ^ step
                moves.append(((2 * j + t % 2) * M + t // 2, i * M + j))
        piece = lax.dynamic_index_in_dim(by_head, order ^ step, 0, keepdims=False)
        sums[step % 2] += lax.ppermute(piece, ("seq", "mp"), moves).astype(f32)
    swap = s % 2 == 1
    owned = jnp.concatenate(
        [jnp.where(swap, sums[1], sums[0]), jnp.where(swap, sums[0], sums[1])], axis=1
    )
    grad_cross_query = owned[: D // S]
    grad_cross_kv = owned[D // S :].reshape(2, width // S, 2 * W).transpose(1, 0, 2)

    grads_one, grads_two = sum_ranks(grads_one), sum_ranks(grads_two)
    ff = g.shape[1] // M
    grad_mlp_up, grad_mlp_down = grads_one[:, :ff], grads_one[:, ff : 2 * ff].T
    grad_self_out = grads_one[:, 2 * ff : 2 * ff + D // M].T
    grad_decoder = grads_one[:, 2 * ff + D // M :]
    grad_decoder = grad_decoder.reshape(D // S, 4, CP)[:, :, :channels].transpose(0, 2, 1)
    grad_self_qkv = grads_two[:, : 3 * D // M].reshape(D // S, 2, 3, W).transpose(0, 2, 1, 3)
    grad_cross_out = grads_two[:, 3 * D // M :].T

    one = [back_one[0][i] + back_one[1][i] for i in (1, 2)]
    two = sums_two[0] + sums_two[1]
    small = jnp.concatenate(
        [one[0], two[:1], sums_three[:1], one[1], two[1:], sums_three[1:]], axis=0
    )
    small = jnp.sum(swap_seq(small.reshape(6, S, D // S).transpose(1, 0, 2)), axis=0)
    small = sum(from_ranks(jnp.broadcast_to(small, (M,) + small.shape)))

    return (
        tokens_out,
        sampled,
        grad_tokens,
        patch_grad,
        small[:3],
        small[3:5],
        small[5],
        grad_cross_query,
        grad_cross_kv,
        grad_cross_out,
        grad_self_qkv.reshape(D // S, 3, -1),
        grad_self_out,
        grad_mlp_up,
        grad_mlp_down,
        grad_decoder,
    )


def solution(mesh):
    return jax.shard_map(
        per_device,
        mesh=mesh,
        in_specs=(
            P(None, "seq", None),
            P(None, "seq", None),
            P(),
            P(),
            P(),
            P(None, "mp"),
            P(None, None, "mp"),
            P("mp", None),
            P(None, None, "mp"),
            P("mp", None),
            P(None, "mp"),
            P("mp", None),
            P(None, "mp", None),
            P(None, None, "seq", None, None),
            P(None, "seq", None),
            P(None, None, "mp", "seq", None),
        ),
        out_specs=(
            P(None, ("seq", "mp"), None),
            P(None, None, "mp", "seq", None),
            P(None, ("seq", "mp"), None),
            P(None, "seq", None),
            P(None, "seq"),
            P(None, "seq"),
            P("seq"),
            P("seq", "mp"),
            P("seq", None, "mp"),
            P("mp", "seq"),
            P("seq", None, "mp"),
            P("mp", "seq"),
            P("seq", "mp"),
            P("mp", "seq"),
            P("seq", "mp", None),
        ),
        check_vma=False,
    )
```

time: 1520 us -> 1150 us (0.76)
  waiting for transfers between devices: 601 us -> 293 us
  Pallas kernels: 216 us -> 376 us
  matrix products: 143 us -> 26.3 us
  blocking collectives: 97 us -> 0 us
    reduce_scatter x15 -> x2, waiting for transfers between devices: 332 us -> 0.01 us  [reduce_rows(): return lax.psum_scatter(value, 'seq', scatter_dimension=0, tiled=True)]
    pallas_call x0 -> x9, Pallas kernels: none -> 135 us  [the longest x1 36.8 us: feed_forward(): pl.pallas_call(functools.partial(mlp_kernel, steps=steps), grid=(steps,),...]
    ppermute x16 -> x47, waiting for transfers between devices: 32.2 us -> 150 us  [the longest x6 73.3 us: gather_seq(): got.append(lax.ppermute(value, 'seq', moves))]
    all_gather x8 -> x4, waiting for transfers between devices: 142 us -> 29.2 us  [gather_rows(): return lax.all_gather(piece, ('mp', 'seq'), axis=0, tiled=False)]
    all_gather x1 -> x0, blocking collectives: 76.8 us -> none  [per_device(): lax.all_gather(mine(decoder.reshape(D, cu), 0), ('seq', 'mp'), axis=0, ti...]
    dot_general x14 -> x4, matrix products: 88.6 us -> 16.2 us  [dot(): return lax.dot_general(a, b, dims, preferred_element_type=f32)]
    ppermute x2, waiting for transfers between devices: 0.71 us -> 46.8 us  [swap_pair(): return lax.ppermute(value, 'mp', [(i, i ^ 1) for i in range(count)])]
    dot_general x8 -> x4, matrix products: 41.4 us -> 10.1 us  [mm(): return jnp.dot(a, b, preferred_element_type=f32)]
  transfers between devices with their start and end apart: 55 -> 75, of which waited for: 28 -> 24; matrix products, arithmetic and copies ran while one was open for 23% -> 19% of each run, Pallas kernels for 12% -> 28%
where the time goes in v2:
time: 1150 us; the launch traced here: 1140 us
  Pallas kernels  376 us (33%)
  waiting for transfers between devices  293 us (25%)
  local copies, waits for them, and re-layouts  187 us (16%)
  starting transfers between devices  180 us (16%)
  other arithmetic  60.8 us (5%)
  matrix products  26.3 us (2%)
  between operations  15.9 us (1%)
    pallas_call x4, Pallas kernels, attend_back(): pl.pallas_call(body, out_shape=(jax.ShapeDtypeStruct((queries, hpd * HD),...  151 us
    pallas_call x4, Pallas kernels, attend(): pl.pallas_call(body, out_shape=(jax.ShapeDtypeStruct((queries, hpd * HD),...  90.4 us
    unnamed x199, local copies, waits for them, and re-layouts  77.8 us
    all_to_all x18, starting transfers between devices, swap_seq(): return lax.all_to_all(value, 'seq', split_axis=0, concat_axis=0, tiled=True)  74.4 us
    ppermute x6, waiting for transfers between devices, gather_seq(): got.append(lax.ppermute(value, 'seq', moves))  73.3 us
    all_to_all x18, waiting for transfers between devices, swap_seq(): return lax.all_to_all(value, 'seq', split_axis=0, concat_axis=0, tiled=True)  66.4 us
    ppermute x2, waiting for transfers between devices, swap_pair(): return lax.ppermute(value, 'mp', [(i, i ^ 1) for i in range(count)])  46.8 us
    ppermute x15, waiting for transfers between devices, from_ranks(): block = lax.ppermute(block, 'mp', [(i, i ^ step) for i in range(ranks)])  36.9 us
  transfers between devices with their start and end apart: 75, of which 24 were waited for; matrix products, arithmetic and copies ran while one was open for 19% of the time, Pallas kernels for 28%

profile of v2, /device:TPU:0, one launch (start us, length us, event | category | flops | bytes accessed | tf_op | source)
XLA Modules:
  0.0 1138.5 jit_solution(11906886912207247001)
XLA Ops:
  17.0 4.9 copy.138
  37.3 15.2 %shard_map.286 = f32[18,160,128]{2,1,0:T(8,128)S(1)} custom-call(bf16[18,32,256]{2,1,0:T(8,128)(2,1)S(1)} %pad.16.cot_ref, bf16[18,561,256]{2,1,0:T(8,128)(2,1)S(1)} %bitcast.289), custom_call_target="tpu_custom_call" | custom-call | flops 600000000 | bytes 7000000 | tf_op jit(solution)/shard_map/pallas_call | solution.py:631
  77.8 7.5 all-gather.9.cloned.1.call-done
  100.4 6.7 copy.136
  116.9 5.4 all-to-all-start.7
  128.1 6.7 copy.137
  138.8 6.2 reshape.448
  148.9 15.0 %shard_map.283 = (bf16[1536,128]{1,0:T(8,128)(2,1)}, bf16[2,1536,128]{2,1,0:T(8,128)(2,1)S(1)}) custom-call(s32[2]{0:T(128)S(1)} %get-tuple-element.242.n_ref, bf16[8,576,128]{2,1,0:T(8,128)(2,1)S(1)} %all-to-all-done.refs_0_, bf16[8,384,256]{2,1,0:T(8,128)(2,1)S(1)} %bitcast.292), custom_call_target="tpu_custom_call" | custom-call | flops 4831838208 | bytes 3145728 | tf_op jit(solution)/shard_map/pallas_call | solution.py:193
  171.4 26.3 %shard_map.280 = (bf16[3072,128]{1,0:T(8,128)(2,1)S(1)}, bf16[2,3072,128]{2,1,0:T(8,128)(2,1)S(1)}) custom-call(s32[2]{0:T(128)S(1)} %get-tuple-element.243.n_ref, bf16[8,576,128]{2,1,0:T(8,128)(2,1)S(1)} %all-to-all-done.refs_0_, bf16[8,384,256]{2,1,0:T(8,128)(2,1)S(1)} %bitcast.295), custom_call_target="tpu_custom_call" | custom-call | flops 9663676416 | bytes 6291456 | tf_op jit(solution)/shard_map/pallas_call | solution.py:193
  207.9 5.1 shard_map.284
  216.4 7.8 all-to-all-done.1.a_ref
  227.8 10.1 shard_map.281
  242.2 10.7 all-to-all-done.5.refs_0_.refs_3_
  257.8 28.3 %collective-permute-done.4.refs_1_.refs_4_ = bf16[8,192,256]{2,1,0:T(8,128)(2,1)S(1)} collective-permute-done((bf16[8,192,256]{2,1,0:T(8,128)(2,1)S(1)}, bf16[8,192,256]{2,1,0:T(8,128)(2,1)S(1)}, u32[]{:S(2)}, u32[]{:S(2)}) %collective-permute-start.4) | collective-permute-done | bytes 786464 | tf_op jit(solution)/shard_map/ppermute | solution.py:659
  286.1 17.4 %shard_map.285 = (bf16[1536,128]{1,0:T(8,128)(2,1)}, bf16[2,1536,128]{2,1,0:T(8,128)(2,1)S(1)}) custom-call(s32[2]{0:T(128)S(1)} %copy-done.36, bf16[8,192,384]{2,1,0:T(8,128)(2,1)S(1)} %all-to-all-done.5.refs_0_.refs_3_, bf16[8,192,256]{2,1,0:T(8,128)(2,1)S(1)} %collective-permute-done.4.refs_1_.refs_4_), custom_call_target="tpu_custom_call" | custom-call | flops 9663676416 | bytes 3145728 | tf_op jit(solution)/shard_map/pallas_call | solution.py:193
  305.4 4.8 all-to-all-start.6
  310.2 31.7 %shard_map.282 = (bf16[3072,128]{1,0:T(8,128)(2,1)}, bf16[2,3072,128]{2,1,0:T(8,128)(2,1)S(1)}) custom-call(s32[2]{0:T(128)S(1)} %copy-done.36, bf16[8,384,384]{2,1,0:T(8,128)(2,1)} %all-to-all-done.2.refs_0_.refs_3_), custom_call_target="tpu_custom_call" | custom-call | flops 19327352832 | bytes 6291456 | tf_op jit(solution)/shard_map/pallas_call | solution.py:193
  352.1 15.6 %all-to-all-done.3.aa_ref = bf16[8,384,128]{2,1,0:T(8,128)(2,1)} async-done(((bf16[8,384,128]{2,1,0:T(8,128)(2,1)}), bf16[8,384,128]{2,1,0:T(8,128)(2,1)}, u32[]{:S(2)}, u32[]{:S(2)}) %all-to-all-start.3) | async-done | bytes 786464 | tf_op jit(solution)/shard_map/all_to_all | solution.py:646
  367.7 21.8 %all-gather.13.cloned.1.call-done = bf16[5632,1024]{1,0:T(8,128)(2,1)} async-done(((bf16[176,1024]{1,0:T(8,128)(2,1)}), bf16[5632,1024]{1,0:T(8,128)(2,1)}) %all-gather.13.cloned.1.call-update) | async-done | bytes 11534352 | tf_op jit(solution)/shard_map/all_gather | solution.py:663
  389.5 36.8 %shard_map.287 = (bf16[576,1024]{1,0:T(8,128)(2,1)}, bf16[576,1024]{1,0:T(8,128)(2,1)}, bf16[576,4096]{1,0:T(8,128)(2,1)}, bf16[576,4096]{1,0:T(8,128)(2,1)}, bf...) custom-call(bf16[8,384,128]{2,1,0:T(8,128)(2,1)} %all-to-all-done.3., ...), custom_call_target="tpu_custom_call" | custom-call | flops 24159191040 | bytes 34471936 | tf_op jit(solution)/shard_map/pallas_call | solution.py:418
  444.0 24.1 %shard_map.289 = bf16[1024,9728]{1,0:T(8,128)(2,1)} custom-call(bf16[576,1024]{1,0:T(8,128)(2,1)} %get-tuple-element.74.refs_0_, bf16[576,1024]{1,0:T(8,128)(2,1)} %get-tuple-element.75.refs_1_, bf16[576,1024]{1,0:T(8,128)(2,1)} %get-tuple-element.76.refs_2_, bf16[576,1024]{1,0:T(8,128)(2,1)} %get-tuple-element.70.refs_3_, ...), custom_call_target="tpu_custom_call" | custom-call | flops 11475615744 | bytes 39845888 | tf_op jit(solution)/shard_map/pallas_call | solution.py:564
  479.8 5.3 all-to-all-done.13.refs_1_
  487.7 60.9 %shard_map.290 = (bf16[3072,128]{1,0:T(8,128)(2,1)S(1)}, bf16[3072,256]{1,0:T(8,128)(2,1)}) custom-call(s32[2]{0:T(128)S(1)} %copy-done.36, bf16[2,3072,128]{2,1,0:T(8,128)(2,1)} %copy-done.41, bf16[8,384,128]{2,1,0:T(8,128)(2,1)S(1)} %all-to-all-done.9.refs_1_, bf16[3072,128]{1,0:T(8,128)(2,1)} %get-tuple-element.64.refs_2_, ...), custom_call_target="tpu_custom_call" | custom-call | flops 48318382080 | bytes 9437184 | tf_op jit(solution)/shard_map/pallas_call | solution.py:223
  558.5 34.6 %shard_map.293 = (bf16[1536,128]{1,0:T(8,128)(2,1)S(1)}, bf16[3072,256]{1,0:T(8,128)(2,1)}) custom-call(s32[2]{0:T(128)S(1)} %copy-done.36, bf16[2,1536,128]{2,1,0:T(8,128)(2,1)S(1)} %copy-done.40, bf16[8,192,128]{2,1,0:T(8,128)(2,1)S(1)} %copy-done.23, bf16[1536,128]{1,0:T(8,128)(2,1)} %get-tuple-element.67.refs_2_, bf16[8,192,384]{2,1,0:T(8,128)(2,1)} %copy-done.9, ...), custom_call_target="tpu_custom_call" | custom-call | flops 24159191040 | bytes 4718592 | tf_op jit(solution)/shard_map/pallas_call | solution.py:223
  596.0 18.4 %collective-permute-done.19 = bf16[1536,256]{1,0:T(8,128)(2,1)S(1)} collective-permute-done((bf16[1536,256]{1,0:T(8,128)(2,1)S(1)}, bf16[1536,256]{1,0:T(8,128)(2,1)S(1)}, u32[]{:S(2)}, u32[]{:S(2)}) %collective-permute-start.19) | collective-permute-done | bytes 786464 | tf_op jit(solution)/shard_map/ppermute | solution.py:659
  623.4 11.9 %shard_map.291 = (f32[384,1024]{1,0:T(8,128)S(1)}, bf16[384,1024]{1,0:T(8,128)(2,1)S(1)}, bf16[8,384,128]{2,1,0:T(8,128)(2,1)}, f32[2,1024]{1,0:T(2,128)S(1)}) custom-call(bf16[8,384,384]{2,1,0:T(8,128)(2,1)S(1)} %all-to-all-done.10.t_ref.refs_4_, f32[384,1024]{1,0:T(8,128)S(1)} %copy-done.14, f32[576,1024]{1,0:T(8,128)S(1)} %copy-done.7, ...), custom_call_target="tpu_custom_call" | custom-call | flops 3221225472 | bytes 17825792 | tf_op jit(solution)/shard_map/pallas_call | solution.py:505
  643.6 8.1 shard_map.294
  652.4 11.6 %shard_map.295 = bf16[1024,4096]{1,0:T(8,128)(2,1)} custom-call(bf16[384,1024]{1,0:T(8,128)(2,1)} %copy-done.19, bf16[192,1024]{1,0:T(8,128)(2,1)} %copy-done.24, bf16[384,1024]{1,0:T(8,128)(2,1)} %copy-done.21, bf16[192,1024]{1,0:T(8,128)(2,1)} %copy-done.26, bf16[8,384,384]{2,1,0:T(8,128)(2,1)} %copy-done.4, ...), custom_call_target="tpu_custom_call" | custom-call | flops 2415919104 | bytes 16777216 | tf_op jit(solution)/shard_map/pallas_call | solution.py:564
  668.7 26.9 %collective-permute-done.31 = bf16[576,1024]{1,0:T(8,128)(2,1)S(1)} collective-permute-done((bf16[576,1024]{1,0:T(8,128)(2,1)}, bf16[576,1024]{1,0:T(8,128)(2,1)S(1)}, u32[]{:S(2)}, u32[]{:S(2)}) %collective-permute-start.31) | collective-permute-done | bytes 1179680 | tf_op jit(solution)/shard_map/ppermute | solution.py:710
  695.6 6.1 collective-permute-done.32
  701.8 40.3 %collective-permute-done.33 = bf16[576,1024]{1,0:T(8,128)(2,1)S(1)} collective-permute-done((bf16[576,1024]{1,0:T(8,128)(2,1)}, bf16[576,1024]{1,0:T(8,128)(2,1)S(1)}, u32[]{:S(2)}, u32[]{:S(2)}) %collective-permute-start.33) | collective-permute-done | bytes 1179680 | tf_op jit(solution)/shard_map/ppermute | solution.py:710
  747.7 6.5 collective-permute-done.34
  754.1 8.3 pad_maximum_fusion
  762.5 8.6 copy.162
  803.5 20.3 %shard_map.296 = (bf16[1536,128]{1,0:T(8,128)(2,1)}, bf16[1536,256]{1,0:T(8,128)(2,1)}) custom-call(s32[2]{0:T(128)S(1)} %copy-done.32, bf16[2,1536,128]{2,1,0:T(8,128)(2,1)} %copy-done.37, bf16[8,192,128]{2,1,0:T(8,128)(2,1)S(1)} %all-to-all-done.15.refs_1_, bf16[1536,128]{1,0:T(8,128)(2,1)} %get-tuple-element.65.refs_2_, bf16[8,384,256]{2,1,0:T(8,128)(2,1)} %bitcast.293), custom_call_target="tpu_custom_call" | custom-call | flops 12079595520 | bytes 4718592 | tf_op jit(solution)/shard_map/pallas_call | solution.py:223
  828.0 35.1 %shard_map.292 = (bf16[3072,128]{1,0:T(8,128)(2,1)}, bf16[1536,256]{1,0:T(8,128)(2,1)}) custom-call(s32[2]{0:T(128)S(1)} %copy-done.30, bf16[2,3072,128]{2,1,0:T(8,128)(2,1)} %copy-done.38, bf16[8,384,128]{2,1,0:T(8,128)(2,1)} %all-to-all-done.11.refs_1_, bf16[3072,128]{1,0:T(8,128)(2,1)} %copy-done.18, bf16[8,384,256]{2,1,0:T(8,128)(2,1)} %bitcast.294), custom_call_target="tpu_custom_call" | custom-call | flops 24159191040 | bytes 9437184 | tf_op jit(solution)/shard_map/pallas_call | solution.py:223
  867.4 6.7 fusion.31
  882.8 11.7 %shard_map.288 = bf16[18,32,256]{2,1,0:T(8,128)(2,1)S(1)} custom-call(bf16[18,160,128]{2,1,0:T(8,128)(2,1)S(1)} %concatenate.70.x_ref, bf16[18,561,256]{2,1,0:T(8,128)(2,1)S(1)} %bitcast.290), custom_call_target="tpu_custom_call" | custom-call | flops 600000000 | bytes 7000000 | tf_op jit(solution)/shard_map/pallas_call | solution.py:631
  913.0 10.4 collective-permute-done.40
  928.7 10.6 all-to-all-done.18
  945.8 10.3 all-to-all-done.12
  998.6 11.1 collective-permute-start.21
  1017.6 10.5 collective-permute-start.23
  1028.2 11.5 %collective-permute-done.21 = bf16[96,1024]{1,0:T(8,128)(2,1)S(1)} collective-permute-done((bf16[96,1024]{1,0:T(8,128)(2,1)S(1)}, bf16[96,1024]{1,0:T(8,128)(2,1)S(1)}, u32[]{:S(2)}, u32[]{:S(2)}) %collective-permute-start.21) | collective-permute-done | bytes 196640 | tf_op jit(solution)/shard_map/ppermute | solution.py:730
  1041.7 8.9 collective-permute-done.23
  1067.6 6.5 constant_dynamic-slice_fusion.3
  1095.7 5.0 collective-permute-done.46
  1100.7 25.7 %collective-permute-done.47 = bf16[128,2432]{0,1:T(8,128)(2,1)} collective-permute-done((bf16[128,2432]{0,1:T(8,128)(2,1)}, bf16[128,2432]{0,1:T(8,128)(2,1)}, u32[]{:S(2)}, u32[]{:S(2)}) %collective-permute-start.47) | collective-permute-done | bytes 622624 | tf_op jit(solution)/shard_map/ppermute | solution.py:689
  (488 shorter events, 383.0 us)
Async XLA Ops:
  7.2 78.0 %all-gather.9.cloned.1.call-start = ((), (), s32[]{:S(2)}) async-start(), calls=%async_computation.24 | async-start | bytes 5406720 | tf_op jit(solution)/shard_map/all_gather | solution.py:663
  13.5 190.8 %all-gather.11.cloned.1.call-start = ((), (), s32[]{:S(2)}) async-start(), calls=%async_computation.25 | async-start | bytes 8650752 | tf_op jit(solution)/shard_map/all_gather | solution.py:663
  24.5 327.6 %all-gather.15.cloned.1.call-start = ((), (), s32[]{:S(2)}) async-start(), calls=%async_computation.27 | async-start | bytes 8650752 | tf_op jit(solution)/shard_map/all_gather | solution.py:663
  25.3 364.2 %all-gather.13.cloned.1.call-start = ((), (), s32[]{:S(2)}) async-start(), calls=%async_computation.26 | async-start | bytes 11894784 | tf_op jit(solution)/shard_map/all_gather | solution.py:663
  30.3 33.8 %collective-permute-start = (bf16[384,768]{1,0:T(8,128)(2,1)}, bf16[384,768]{1,0:T(8,128)(2,1)}, u32[]{:S(2)}, u32[]{:S(2)}) collective-permute-start(bf16[384,768]{1,0:T(8,128)(2,1)} %get-tuple-element.219), channel_id=1, source_target_pairs={{0,8},{4,12},{8,0},{12,4},{16,24},{20,28},{24,16},{28,20},{1,9},{5... | collective-permute-start | bytes 1769480 | tf_op jit(solution)/shard_map/ppermute | solution.py:710
  33.3 33.2 %collective-permute-start.1 = (bf16[384,768]{1,0:T(8,128)(2,1)}, bf16[384,768]{1,0:T(8,128)(2,1)}, u32[]{:S(2)}, u32[]{:S(2)}) collective-permute-start(bf16[384,768]{1,0:T(8,128)(2,1)} %get-tuple-element.219), channel_id=1, source_target_pairs={{0,16},{4,20},{8,24},{12,28},{16,0},{20,4},{24,8},{28,12},{1,17},{... | collective-permute-start | bytes 1769480 | tf_op jit(solution)/shard_map/ppermute | solution.py:710
  34.8 31.7 %collective-permute-start.2 = (bf16[384,768]{1,0:T(8,128)(2,1)}, bf16[384,768]{1,0:T(8,128)(2,1)}, u32[]{:S(2)}, u32[]{:S(2)}) collective-permute-start(bf16[384,768]{1,0:T(8,128)(2,1)} %get-tuple-element.219), channel_id=1, source_target_pairs={{0,24},{4,28},{8,16},{12,20},{16,8},{20,12},{24,0},{28,4},{1,25},{... | collective-permute-start | bytes 1769480 | tf_op jit(solution)/shard_map/ppermute | solution.py:710
  89.8 27.1 %all-to-all-start = ((bf16[8,576,128]{2,1,0:T(8,128)(2,1)}), bf16[8,576,128]{2,1,0:T(8,128)(2,1)S(1)}, u32[]{:S(2)}, u32[]{:S(2)}) async-start(bf16[8,576,128]{2,1,0:T(8,128)(2,1)} %bitcast.317), calls=%async_computation | async-start | bytes 2359296 | tf_op jit(solution)/shard_map/all_to_all | solution.py:646
  116.9 49.0 %all-to-all-start.7 = ((bf16[32,72,128]{2,1,0:T(8,128)(2,1)}), bf16[32,72,128]{2,1,0:T(8,128)(2,1)S(1)}, u32[]{:S(2)}, u32[]{:S(2)}) async-start(bf16[32,72,128]{2,1,0:T(8,128)(2,1)} %bitcast.334), calls=%async_computation.7 | async-start | bytes 1179648 | tf_op jit(solution)/shard_map/all_to_all | solution.py:654
  166.0 34.0 %all-to-all-start.4 = ((bf16[8,192,128]{2,1,0:T(8,128)(2,1)}), bf16[8,192,128]{2,1,0:T(8,128)(2,1)S(1)}, u32[]{:S(2)}, u32[]{:S(2)}) async-start(bf16[8,192,128]{2,1,0:T(8,128)(2,1)} %bitcast.27), calls=%async_computation.4 | async-start | bytes 786432 | tf_op jit(solution)/shard_map/all_to_all | solution.py:646
  224.2 28.7 %all-to-all-start.5 = ((bf16[8,192,384]{2,1,0:T(8,128)(2,1)}), bf16[8,192,384]{2,1,0:T(8,128)(2,1)S(1)}, u32[]{:S(2)}, u32[]{:S(2)}) async-start(bf16[8,192,384]{2,1,0:T(8,128)(2,1)} %copy-done.15), calls=%async_computation.5 | async-start | bytes 2359296 | tf_op jit(solution)/shard_map/all_to_all | solution.py:646
  252.9 52.4 %all-to-all-start.2 = ((bf16[8,384,384]{2,1,0:T(8,128)(2,1)}), bf16[8,384,384]{2,1,0:T(8,128)(2,1)}, u32[]{:S(2)}, u32[]{:S(2)}) async-start(bf16[8,384,384]{2,1,0:T(8,128)(2,1)} %copy-done.10), calls=%async_computation.2 | async-start | bytes 4718592 | tf_op jit(solution)/shard_map/all_to_all | solution.py:646
  257.7 28.4 %collective-permute-start.4 = (bf16[8,192,256]{2,1,0:T(8,128)(2,1)S(1)}, bf16[8,192,256]{2,1,0:T(8,128)(2,1)S(1)}, u32[]{:S(2)}, u32[]{:S(2)}) collective-permute-start(bf16[8,192,256]{2,1,0:T(8,128)(2,1)S(1)} %slice.196), channel_id=1, source_target_pairs={{0,1},{1,0},{2,3},{3,2},{4,5},{5,4},{6,7},{7,6},{8,9},{9,8},{10,11... | collective-permute-start | bytes 2359304 | tf_op jit(solution)/shard_map/ppermute | solution.py:659
  305.4 36.5 %all-to-all-start.6 = ((bf16[8,192,128]{2,1,0:T(8,128)(2,1)}), bf16[8,192,128]{2,1,0:T(8,128)(2,1)}, u32[]{:S(2)}, u32[]{:S(2)}) async-start(bf16[8,192,128]{2,1,0:T(8,128)(2,1)} %bitcast.28), calls=%async_computation.6 | async-start | bytes 786432 | tf_op jit(solution)/shard_map/all_to_all | solution.py:646
  341.8 25.9 %all-to-all-start.3 = ((bf16[8,384,128]{2,1,0:T(8,128)(2,1)}), bf16[8,384,128]{2,1,0:T(8,128)(2,1)}, u32[]{:S(2)}, u32[]{:S(2)}) async-start(bf16[8,384,128]{2,1,0:T(8,128)(2,1)} %bitcast.26), calls=%async_computation.3 | async-start | bytes 1572864 | tf_op jit(solution)/shard_map/all_to_all | solution.py:646
  428.6 44.0 %all-to-all-start.9 = ((bf16[8,384,128]{2,1,0:T(8,128)(2,1)}), bf16[8,384,128]{2,1,0:T(8,128)(2,1)S(1)}, u32[]{:S(2)}, u32[]{:S(2)}) async-start(bf16[8,384,128]{2,1,0:T(8,128)(2,1)} %get-tuple-element.73), calls=%async_computation.9 | async-start | bytes 1572864 | tf_op jit(solution)/shard_map/all_to_all | solution.py:646
  433.0 36.2 %collective-permute-start.8 = (bf16[96,1024]{1,0:T(8,128)(2,1)}, bf16[96,1024]{1,0:T(8,128)(2,1)}, u32[]{:S(2)}, u32[]{:S(2)}) collective-permute-start(bf16[96,1024]{1,0:T(8,128)(2,1)} %get-tuple-element.204), channel_id=1, source_target_pairs={{0,1},{1,0},{2,3},{3,2},{4,5},{5,4},{6,7},{7,6},{8,9},{9,8},{10,11... | collective-permute-start | bytes 589832 | tf_op jit(solution)/shard_map/ppermute | solution.py:689
  436.5 32.7 %collective-permute-start.9 = (bf16[96,1024]{1,0:T(8,128)(2,1)}, bf16[96,1024]{1,0:T(8,128)(2,1)}, u32[]{:S(2)}, u32[]{:S(2)}) collective-permute-start(bf16[96,1024]{1,0:T(8,128)(2,1)} %get-tuple-element.203), channel_id=1, source_target_pairs={{0,2},{1,3},{2,0},{3,1},{4,6},{5,7},{6,4},{7,5},{8,10},{9,11},{10,... | collective-permute-start | bytes 589832 | tf_op jit(solution)/shard_map/ppermute | solution.py:689
  438.7 30.5 %collective-permute-start.10 = (bf16[96,1024]{1,0:T(8,128)(2,1)}, bf16[96,1024]{1,0:T(8,128)(2,1)}, u32[]{:S(2)}, u32[]{:S(2)}) collective-permute-start(bf16[96,1024]{1,0:T(8,128)(2,1)} %get-tuple-element.202), channel_id=1, source_target_pairs={{0,3},{1,2},{2,1},{3,0},{4,7},{5,6},{6,5},{7,4},{8,11},{9,10},{10,... | collective-permute-start | bytes 589832 | tf_op jit(solution)/shard_map/ppermute | solution.py:689
  439.6 31.5 %collective-permute-start.11 = (bf16[96,1024]{1,0:T(8,128)(2,1)}, bf16[96,1024]{1,0:T(8,128)(2,1)S(1)}, u32[]{:S(2)}, u32[]{:S(2)}) collective-permute-start(bf16[96,1024]{1,0:T(8,128)(2,1)} %get-tuple-element.227), channel_id=1, source_target_pairs={{0,0},{1,2},{2,1},{3,3},{4,4},{5,6},{6,5},{7,7},{8,8},{9,10},{10,9... | collective-permute-start | bytes 589832 | tf_op jit(solution)/shard_map/ppermute | solution.py:730
  441.2 29.9 %collective-permute-start.12 = (bf16[96,1024]{1,0:T(8,128)(2,1)}, bf16[96,1024]{1,0:T(8,128)(2,1)S(1)}, u32[]{:S(2)}, u32[]{:S(2)}) collective-permute-start(bf16[96,1024]{1,0:T(8,128)(2,1)} %get-tuple-element.226), channel_id=1, source_target_pairs={{0,1},{1,3},{2,0},{3,2},{4,5},{5,7},{6,4},{7,6},{8,9},{9,11},{10,8... | collective-permute-start | bytes 589832 | tf_op jit(solution)/shard_map/ppermute | solution.py:730
  485.0 66.7 %all-to-all-start.8 = ((bf16[32,72,128]{2,1,0:T(8,128)(2,1)}), bf16[32,72,128]{2,1,0:T(8,128)(2,1)S(1)}, u32[]{:S(2)}, u32[]{:S(2)}) async-start(bf16[32,72,128]{2,1,0:T(8,128)(2,1)} %bitcast.333), calls=%async_computation.8 | async-start | bytes 1179648 | tf_op jit(solution)/shard_map/all_to_all | solution.py:654
  552.6 63.3 %all-to-all-start.10 = ((bf16[8,384,384]{2,1,0:T(8,128)(2,1)}), bf16[8,384,384]{2,1,0:T(8,128)(2,1)S(1)}, u32[]{:S(2)}, u32[]{:S(2)}) async-start(bf16[8,384,384]{2,1,0:T(8,128)(2,1)} %bitcast.312), calls=%async_computation.10 | async-start | bytes 4718592 | tf_op jit(solution)/shard_map/all_to_all | solution.py:646
  620.1 434.2 %reduce-scatter.3.cloned.1.call-start = ((), (), s32[]{:S(2)}) async-start(), calls=%async_computation.22 | async-start | bytes 9437184 | tf_op jit(solution)/shard_map/reduce_scatter | solution.py:680
  664.1 400.7 %reduce-scatter.5.cloned.1.call-start = ((), (), s32[]{:S(2)}) async-start(), calls=%async_computation.23 | async-start | bytes 22413312 | tf_op jit(solution)/shard_map/reduce_scatter | solution.py:680
  664.7 31.0 %collective-permute-start.31 = (bf16[576,1024]{1,0:T(8,128)(2,1)}, bf16[576,1024]{1,0:T(8,128)(2,1)S(1)}, u32[]{:S(2)}, u32[]{:S(2)}) collective-permute-start(bf16[576,1024]{1,0:T(8,128)(2,1)} %fusion.5), channel_id=1, source_target_pairs={{0,8},{4,12},{8,0},{12,4},{16,24},{20,28},{24,16},{28,20},{1,9},{5... | collective-permute-start | bytes 3538952 | tf_op jit(solution)/shard_map/ppermute | solution.py:710
  666.6 35.2 %collective-permute-start.32 = (bf16[576,1024]{1,0:T(8,128)(2,1)}, bf16[576,1024]{1,0:T(8,128)(2,1)S(1)}, u32[]{:S(2)}, u32[]{:S(2)}) collective-permute-start(bf16[576,1024]{1,0:T(8,128)(2,1)} %fusion.5), channel_id=1, source_target_pairs={{0,16},{4,20},{8,24},{12,28},{16,0},{20,4},{24,8},{28,12},{1,17},{... | collective-permute-start | bytes 3538952 | tf_op jit(solution)/shard_map/ppermute | solution.py:710
  668.1 74.0 %collective-permute-start.33 = (bf16[576,1024]{1,0:T(8,128)(2,1)}, bf16[576,1024]{1,0:T(8,128)(2,1)S(1)}, u32[]{:S(2)}, u32[]{:S(2)}) collective-permute-start(bf16[576,1024]{1,0:T(8,128)(2,1)} %fusion.5), channel_id=1, source_target_pairs={{0,24},{4,28},{8,16},{12,20},{16,8},{20,12},{24,0},{28,4},{1,25},{... | collective-permute-start | bytes 3538952 | tf_op jit(solution)/shard_map/ppermute | solution.py:710
  785.5 91.4 %collective-permute-start.13 = (bf16[18,16,128]{2,1,0:T(8,128)(2,1)}, bf16[18,16,128]{2,1,0:T(8,128)(2,1)S(1)}, u32[]{:S(2)}, u32[]{:S(2)}) collective-permute-start(bf16[18,16,128]{2,1,0:T(8,128)(2,1)} %bitcast.272), channel_id=1, source_target_pairs={{4,0},{8,4},{12,8},{20,16},{24,20},{28,24},{5,1},{9,5},{13,9},{21,... | collective-permute-start | bytes 221192 | tf_op jit(solution)/shard_map/ppermute | solution.py:953
  791.1 85.8 %collective-permute-start.14 = (bf16[18,8,128]{2,1,0:T(8,128)(2,1)}, bf16[18,8,128]{2,1,0:T(8,128)(2,1)S(1)}, u32[]{:S(2)}, u32[]{:S(2)}) collective-permute-start(bf16[18,8,128]{2,1,0:T(8,128)(2,1)} %slice_bitcast_fusion.7), channel_id=1, source_target_pairs={{16,0},{20,4},{24,8},{28,12},{17,1},{21,5},{25,9},{29,13},{18,2},{... | collective-permute-start | bytes 110600 | tf_op jit(solution)/shard_map/ppermute | solution.py:954
  793.0 83.8 %collective-permute-start.15 = (bf16[18,1,128]{2,1,0:T(2,128)(2,1)}, bf16[18,1,128]{2,1,0:T(2,128)(2,1)}, u32[]{:S(2)}, u32[]{:S(2)}) collective-permute-start(bf16[18,1,128]{2,1,0:T(2,128)(2,1)} %slice_bitcast_fusion.8), channel_id=1, source_target_pairs={{20,0},{24,4},{28,8},{21,1},{25,5},{29,9},{22,2},{26,6},{30,10},{2... | collective-permute-start | bytes 13832 | tf_op jit(solution)/shard_map/ppermute | solution.py:955
  823.8 85.4 %all-to-all-start.16 = ((bf16[8,192,128]{2,1,0:T(8,128)(2,1)}), bf16[8,192,128]{2,1,0:T(8,128)(2,1)}, u32[]{:S(2)}, u32[]{:S(2)}) async-start(bf16[8,192,128]{2,1,0:T(8,128)(2,1)} %bitcast.88), calls=%async_computation.16 | async-start | bytes 786432 | tf_op jit(solution)/shard_map/all_to_all | solution.py:646
  875.6 28.5 %collective-permute-start.36 = (bf16[320,128]{1,0:T(8,128)(2,1)}, bf16[320,128]{1,0:T(8,128)(2,1)}, u32[]{:S(2)}, u32[]{:S(2)}) collective-permute-start(bf16[320,128]{1,0:T(8,128)(2,1)} %get-tuple-element.213), channel_id=1, source_target_pairs={{5,0},{13,1},{21,2},{29,3},{1,4},{9,5},{17,6},{25,7},{4,8},{12,9},... | collective-permute-start | bytes 245768 | tf_op jit(solution)/shard_map/ppermute | solution.py:1018
  876.8 30.7 %collective-permute-start.37 = (bf16[320,128]{1,0:T(8,128)(2,1)}, bf16[320,128]{1,0:T(8,128)(2,1)}, u32[]{:S(2)}, u32[]{:S(2)}) collective-permute-start(bf16[320,128]{1,0:T(8,128)(2,1)} %get-tuple-element.212), channel_id=1, source_target_pairs={{6,0},{14,1},{22,2},{30,3},{2,4},{10,5},{18,6},{26,7},{7,8},{15,9}... | collective-permute-start | bytes 245768 | tf_op jit(solution)/shard_map/ppermute | solution.py:1018
  909.2 30.1 %all-to-all-start.18 = ((bf16[8,192,256]{2,1,0:T(8,128)(2,1)}), bf16[8,192,256]{2,1,0:T(8,128)(2,1)S(1)}, u32[]{:S(2)}, u32[]{:S(2)}) async-start(bf16[8,192,256]{2,1,0:T(8,128)(2,1)} %bitcast.101), calls=%async_computation.18 | async-start | bytes 1572864 | tf_op jit(solution)/shard_map/all_to_all | solution.py:646
  962.5 28.8 %collective-permute-start.25 = (bf16[192,768]{1,0:T(8,128)(2,1)S(1)}, bf16[192,768]{1,0:T(8,128)(2,1)}, u32[]{:S(2)}, u32[]{:S(2)}) collective-permute-start(bf16[192,768]{1,0:T(8,128)(2,1)S(1)} %convolution_convert_fusion.2), channel_id=1, source_target_pairs={{0,1},{1,0},{2,3},{3,2},{4,5},{5,4},{6,7},{7,6},{8,9},{9,8},{10,11... | collective-permute-start | bytes 884744 | tf_op jit(solution)/shard_map/ppermute | solution.py:989
  963.3 31.8 %collective-permute-start.26 = (bf16[192,768]{1,0:T(8,128)(2,1)S(1)}, bf16[192,768]{1,0:T(8,128)(2,1)}, u32[]{:S(2)}, u32[]{:S(2)}) collective-permute-start(bf16[192,768]{1,0:T(8,128)(2,1)S(1)} %convolution_convert_fusion.2), channel_id=1, source_target_pairs={{0,2},{1,3},{2,0},{3,1},{4,6},{5,7},{6,4},{7,5},{8,10},{9,11},{10,... | collective-permute-start | bytes 884744 | tf_op jit(solution)/shard_map/ppermute | solution.py:989
  990.7 26.9 %collective-permute-start.17 = (bf16[96,1024]{1,0:T(8,128)(2,1)S(1)}, bf16[96,1024]{1,0:T(8,128)(2,1)S(1)}, u32[]{:S(2)}, u32[]{:S(2)}) collective-permute-start(bf16[96,1024]{1,0:T(8,128)(2,1)S(1)} %get-tuple-element.199), channel_id=1, source_target_pairs={{0,2},{1,3},{2,0},{3,1},{4,6},{5,7},{6,4},{7,5},{8,10},{9,11},{10,... | collective-permute-start | bytes 589832 | tf_op jit(solution)/shard_map/ppermute | solution.py:689
  991.3 26.3 %collective-permute-start.18 = (bf16[96,1024]{1,0:T(8,128)(2,1)S(1)}, bf16[96,1024]{1,0:T(8,128)(2,1)S(1)}, u32[]{:S(2)}, u32[]{:S(2)}) collective-permute-start(bf16[96,1024]{1,0:T(8,128)(2,1)S(1)} %get-tuple-element.198), channel_id=1, source_target_pairs={{0,3},{1,2},{2,1},{3,0},{4,7},{5,6},{6,5},{7,4},{8,11},{9,10},{10,... | collective-permute-start | bytes 589832 | tf_op jit(solution)/shard_map/ppermute | solution.py:689
  995.1 33.1 %collective-permute-start.20 = (bf16[96,1024]{1,0:T(8,128)(2,1)S(1)}, bf16[96,1024]{1,0:T(8,128)(2,1)S(1)}, u32[]{:S(2)}, u32[]{:S(2)}) collective-permute-start(bf16[96,1024]{1,0:T(8,128)(2,1)S(1)} %copy-done.62), channel_id=1, source_target_pairs={{0,0},{1,2},{2,1},{3,3},{4,4},{5,6},{6,5},{7,7},{8,8},{9,10},{10,9... | collective-permute-start | bytes 589832 | tf_op jit(solution)/shard_map/ppermute | solution.py:730
  998.6 41.1 %collective-permute-start.21 = (bf16[96,1024]{1,0:T(8,128)(2,1)S(1)}, bf16[96,1024]{1,0:T(8,128)(2,1)S(1)}, u32[]{:S(2)}, u32[]{:S(2)}) collective-permute-start(bf16[96,1024]{1,0:T(8,128)(2,1)S(1)} %copy-done.61), channel_id=1, source_target_pairs={{0,1},{1,3},{2,0},{3,2},{4,5},{5,7},{6,4},{7,6},{8,9},{9,11},{10,8... | collective-permute-start | bytes 589832 | tf_op jit(solution)/shard_map/ppermute | solution.py:730
  1011.0 30.8 %collective-permute-start.24 = (bf16[192,768]{1,0:T(8,128)(2,1)S(1)}, bf16[192,768]{1,0:T(8,128)(2,1)S(1)}, u32[]{:S(2)}, u32[]{:S(2)}) collective-permute-start(bf16[192,768]{1,0:T(8,128)(2,1)S(1)} %convolution_convert_fusion.3), channel_id=1, source_target_pairs={{0,3},{1,2},{2,1},{3,0},{4,7},{5,6},{6,5},{7,4},{8,11},{9,10},{10,... | collective-permute-start | bytes 884744 | tf_op jit(solution)/shard_map/ppermute | solution.py:989
  1017.6 33.0 %collective-permute-start.23 = (bf16[192,768]{1,0:T(8,128)(2,1)S(1)}, bf16[192,768]{1,0:T(8,128)(2,1)S(1)}, u32[]{:S(2)}, u32[]{:S(2)}) collective-permute-start(bf16[192,768]{1,0:T(8,128)(2,1)S(1)} %convolution_convert_fusion.3), channel_id=1, source_target_pairs={{0,2},{1,3},{2,0},{3,1},{4,6},{5,7},{6,4},{7,5},{8,10},{9,11},{10,... | collective-permute-start | bytes 884744 | tf_op jit(solution)/shard_map/ppermute | solution.py:989
  1059.4 26.7 %collective-permute-start.43 = (bf16[128,1024]{0,1:T(8,128)(2,1)}, bf16[128,1024]{0,1:T(8,128)(2,1)}, u32[]{:S(2)}, u32[]{:S(2)}) collective-permute-start(bf16[128,1024]{0,1:T(8,128)(2,1)} %bitcast.140), channel_id=1, source_target_pairs={{0,1},{1,0},{2,3},{3,2},{4,5},{5,4},{6,7},{7,6},{8,9},{9,8},{10,11... | collective-permute-start | bytes 786440 | tf_op jit(solution)/shard_map/ppermute | solution.py:689
  1059.8 31.1 %collective-permute-start.44 = (bf16[128,1024]{0,1:T(8,128)(2,1)S(1)}, bf16[128,1024]{0,1:T(8,128)(2,1)}, u32[]{:S(2)}, u32[]{:S(2)}) collective-permute-start(bf16[128,1024]{0,1:T(8,128)(2,1)S(1)} %bitcast.378), channel_id=1, source_target_pairs={{0,2},{1,3},{2,0},{3,1},{4,6},{5,7},{6,4},{7,5},{8,10},{9,11},{10,... | collective-permute-start | bytes 786440 | tf_op jit(solution)/shard_map/ppermute | solution.py:689
  1063.0 27.9 %collective-permute-start.45 = (bf16[128,1024]{0,1:T(8,128)(2,1)S(1)}, bf16[128,1024]{0,1:T(8,128)(2,1)}, u32[]{:S(2)}, u32[]{:S(2)}) collective-permute-start(bf16[128,1024]{0,1:T(8,128)(2,1)S(1)} %bitcast.379), channel_id=1, source_target_pairs={{0,3},{1,2},{2,1},{3,0},{4,7},{5,6},{6,5},{7,4},{8,11},{9,10},{10,... | collective-permute-start | bytes 786440 | tf_op jit(solution)/shard_map/ppermute | solution.py:689
  1081.5 44.9 %collective-permute-start.47 = (bf16[128,2432]{0,1:T(8,128)(2,1)}, bf16[128,2432]{0,1:T(8,128)(2,1)}, u32[]{:S(2)}, u32[]{:S(2)}) collective-permute-start(bf16[128,2432]{0,1:T(8,128)(2,1)} %bitcast.367), channel_id=1, source_target_pairs={{0,2},{1,3},{2,0},{3,1},{4,6},{5,7},{6,4},{7,5},{8,10},{9,11},{10,... | collective-permute-start | bytes 1867784 | tf_op jit(solution)/shard_map/ppermute | solution.py:689
  1086.1 40.3 %collective-permute-start.48 = (bf16[128,2432]{0,1:T(8,128)(2,1)}, bf16[128,2432]{0,1:T(8,128)(2,1)}, u32[]{:S(2)}, u32[]{:S(2)}) collective-permute-start(bf16[128,2432]{0,1:T(8,128)(2,1)} %bitcast.368), channel_id=1, source_target_pairs={{0,3},{1,2},{2,1},{3,0},{4,7},{5,6},{6,5},{7,4},{8,11},{9,10},{10,... | collective-permute-start | bytes 1867784 | tf_op jit(solution)/shard_map/ppermute | solution.py:689
  (112 other events, 1326.9 us)
Sparse Core Ops, SparseCore 0:
  13.6 71.5 all-gather.8
  88.7 89.5 all-gather.10
  181.1 102.2 all-gather.14
  286.1 103.3 all-gather.12
  664.1 99.8 reduce-scatter.2
  768.0 173.1 reduce-scatter.4

commit v3 on v2

--- a/solution.py
+++ b/solution.py
@@ -64,7 +64,7 @@
 
 
 def fwd_kernel(n_ref, *refs, n_in, blocks, q_spec, kv_specs, hpd, bq, kc, fixed):
-    ins, (o_ref, qa_ref, ka, va) = refs[:n_in], refs[n_in:]
+    ins, (o_ref, qa_ref, ka, va) = refs[:n_in], refs[-4:]
     load_keys(n_ref, kv_specs, ins, ka, va, hpd, blocks)
     q_at, rows_q, q_off, q_lane = q_spec
 
@@ -114,7 +114,7 @@
 
 
 def bwd_kernel(n_ref, *refs, n_in, blocks, do_spec, kv_specs, hpd, bq, kc, fixed):
-    ins, (dq_ref, dkv_ref, ka, va, da, dk, dv) = refs[:n_in], refs[n_in:]
+    ins, (dq_ref, dkv_ref, ka, va, da, dk, dv) = refs[:n_in], refs[-7:]
     qa_ref, do_ref, o_ref = ins[:3]
     load_keys(n_ref, kv_specs, ins, ka, va, hpd, blocks)
     rows_q, do_off = do_spec
@@ -169,13 +169,14 @@
 
 VM = pl.BlockSpec(memory_space=pltpu.VMEM)
 SM = pl.BlockSpec(memory_space=pltpu.SMEM)
+AN = pl.BlockSpec(memory_space=pl.ANY)
 
 
 def fit(rows, most):
     return math.gcd(rows, most)
 
 
-def attend(limits, ins, blocks, q_spec, kv_specs, total, hpd, fixed):
+def attend(limits, ins, blocks, q_spec, kv_specs, total, hpd, fixed, deps=()):
     queries = blocks * q_spec[1]
     kc = fit(total, 1024 if fixed else 512)
     body = functools.partial(
@@ -196,17 +197,17 @@
             jax.ShapeDtypeStruct((queries, hpd * HD), bf16),
             jax.ShapeDtypeStruct((hpd, queries, LANES), bf16),
         ),
-        in_specs=[SM] + [VM] * len(ins),
+        in_specs=[SM] + [VM] * len(ins) + [AN] * len(deps),
         out_specs=(VM, VM),
         scratch_shapes=[pltpu.VMEM((hpd, total, LANES), bf16)] * 2,
         compiler_params=pltpu.CompilerParams(vmem_limit_bytes=44 * 2**20),
         cost_estimate=pl.CostEstimate(
             flops=1024 * work, bytes_accessed=16 * queries * hpd * HD, transcendentals=work
         ),
-    )(limits, *ins)
-
-
-def attend_back(limits, ins, blocks, do_spec, kv_specs, total, hpd, fixed):
+    )(limits, *ins, *deps)
+
+
+def attend_back(limits, ins, blocks, do_spec, kv_specs, total, hpd, fixed, deps=()):
     queries = blocks * do_spec[0]
     body = functools.partial(
         bwd_kernel,
@@ -226,7 +227,7 @@
             jax.ShapeDtypeStruct((queries, hpd * HD), bf16),
             jax.ShapeDtypeStruct((total, 2 * hpd * HD), bf16),
         ),
-        in_specs=[SM] + [VM] * len(ins),
+        in_specs=[SM] + [VM] * len(ins) + [AN] * len(deps),
         out_specs=(VM, VM),
         scratch_shapes=[pltpu.VMEM((hpd, total, LANES), bf16)] * 2
         + [pltpu.VMEM((hpd, queries, LANES), bf16)]
@@ -235,7 +236,7 @@
         cost_estimate=pl.CostEstimate(
             flops=2560 * work, bytes_accessed=24 * queries * hpd * HD, transcendentals=work
         ),
-    )(limits, *ins)
+    )(limits, *ins, *deps)
 
 
 def norm_parts(values):
@@ -471,8 +472,9 @@
 
 
 def back_kernel(
-    t_ref, x_ref, d_ref, norm_ref, wo_ref, wt_ref, d1_ref, e_ref, da_ref, sum_ref, acc, *, steps
+    t_ref, x_ref, d_ref, norm_ref, wo_ref, wt_ref, *refs, steps
 ):
+    d1_ref, e_ref, da_ref, sum_ref, acc = refs[-5:]
     step = pl.program_id(0)
     part = dot(t_ref[0], flat(wt_ref), NN)
 
@@ -498,7 +500,7 @@
             da_ref[i] = da[:, i * W : (i + 1) * W]
 
 
-def middle_back(t, x1, d2, at, norm, w_out, w_triple):
+def middle_back(t, x1, d2, at, norm, w_out, w_triple, deps=()):
     S, rows, wide = t.shape
     D = x1.shape[1]
     W = wide // 3
@@ -518,7 +520,8 @@
             once((2, D)),
             w_out[1],
             w_triple[1],
-        ],
+        ]
+        + [AN] * len(deps),
         out_specs=(
             held((rows, D)),
             held((rows, D)),
@@ -530,7 +533,7 @@
         cost_estimate=pl.CostEstimate(
             flops=8 * rows * D * D, bytes_accessed=8 * D * D + 24 * rows * D, transcendentals=0
         ),
-    )(t, x1, d2, norm, w_out[0], w_triple[0])
+    )(t, x1, d2, norm, w_out[0], w_triple[0], *deps)
 
 
 def grads_kernel(*refs, shape, widths):
@@ -581,6 +584,90 @@
     )(*lefts, *rights)
 
 
+def start_kernel(at_ref, xa_ref, xb_ref, norm_ref, *refs, pieces, weights, parts, rows):
+    w_in, refs = refs[:weights], refs[weights:]
+    p_in, kv_in, (q_ref, k_ref, n_ref, wq_ref) = refs[:pieces], refs[pieces:-4], refs[-4:]
+    seq, rank = at_ref[0], at_ref[1]
+    R = xa_ref.shape[0]
+    for i in range(weights):
+        for j in range(w_in[i].shape[0]):
+            at = 0 if weights == 1 else ((rank ^ j) * pieces + (seq ^ i)) * rows
+            wq_ref[pl.ds(pl.multiple_of(at, 16), w_in[i].shape[1]), :] = w_in[i][j]
+    for block, x_ref in ((slice(0, R), xa_ref), (slice(R, n_ref.shape[0]), xb_ref)):
+        n_ref[block, :] = layer_norm(x_ref[...].astype(f32), norm_ref[0:1, :], norm_ref[1:2, :])
+    W = q_ref.shape[2]
+    for i in range(pieces):
+        q_ref[i] = dot(n_ref[...], wq_ref[i * W : (i + 1) * W, :], NT).astype(bf16)
+    w_kv = sum(v[...] for v in kv_in)
+    for i in range(pieces):
+        k_ref[seq ^ i] = dot(p_in[i][...], w_kv, NT).astype(bf16)
+
+
+def start(at, x0, norm, w_pieces, patch_pieces, kv_parts, W):
+    S, D = len(patch_pieces), x0[0].shape[1]
+    total = x0[0].shape[0] + x0[1].shape[0]
+    slots = patch_pieces[0].shape[0]
+    body = functools.partial(
+        start_kernel,
+        pieces=S,
+        weights=len(w_pieces),
+        parts=len(kv_parts),
+        rows=w_pieces[0].shape[1],
+    )
+    return pl.pallas_call(
+        body,
+        out_shape=(
+            jax.ShapeDtypeStruct((S, total, W), bf16),
+            jax.ShapeDtypeStruct((S, slots, 2 * W), bf16),
+            jax.ShapeDtypeStruct((total, D), bf16),
+            jax.ShapeDtypeStruct((D, D), bf16),
+        ),
+        in_specs=[SM] + [VM] * (3 + len(w_pieces) + S + len(kv_parts)),
+        out_specs=(VM,) * 4,
+        compiler_params=pltpu.CompilerParams(vmem_limit_bytes=44 * 2**20),
+        cost_estimate=pl.CostEstimate(
+            flops=2 * total * D * D + 4 * S * slots * 768 * W,
+            bytes_accessed=6 * D * D + 12 * total * D,
+            transcendentals=0,
+        ),
+    )(at, *x0, norm, *w_pieces, *patch_pieces, *kv_parts)
+
+
+def finish_kernel(at_ref, qa_ref, qb_ref, ka_ref, kb_ref, *refs, pieces):
+    n_in, p_in, out_ref = refs[:pieces], refs[pieces:-1], refs[-1]
+    seq = at_ref[0]
+    R, slots, W = qa_ref.shape[1], ka_ref.shape[1], qa_ref.shape[2]
+    by_q, by_kv = 0.0, 0.0
+    for i in range(pieces):
+        j = seq ^ i
+        by_q += dot(qa_ref[j], n_in[i][:R, :], TN) + dot(qb_ref[j], n_in[i][R:, :], TN)
+        by_kv += dot(ka_ref[j], p_in[i][:slots, :], TN) + dot(kb_ref[j], p_in[i][slots:, :], TN)
+    grad = by_q.T.astype(bf16)
+    rows = grad.shape[0] // pieces
+    wide = by_kv.shape[1] // pieces
+    grad_k, grad_v = by_kv[:W].T.astype(bf16), by_kv[W:].T.astype(bf16)
+    for i in range(pieces):
+        out_ref[i, :rows, :] = grad[i * rows : (i + 1) * rows, :]
+        out_ref[i, rows : rows + wide, :] = grad_k[i * wide : (i + 1) * wide, :]
+        out_ref[i, rows + wide :, :] = grad_v[i * wide : (i + 1) * wide, :]
+
+
+def finish(at, dq, dkv, n_pieces, patch_pieces):
+    S, _, W = dq[0].shape
+    D, width = n_pieces[0].shape[1], patch_pieces[0].shape[1]
+    rows = D // S + 2 * width // S
+    return pl.pallas_call(
+        functools.partial(finish_kernel, pieces=S),
+        out_shape=jax.ShapeDtypeStruct((S, rows, W), bf16),
+        in_specs=[SM] + [VM] * (4 + 2 * S),
+        out_specs=VM,
+        compiler_params=pltpu.CompilerParams(vmem_limit_bytes=48 * 2**20),
+        cost_estimate=pl.CostEstimate(
+            flops=3 * 10**9, bytes_accessed=18 * 10**6, transcendentals=0
+        ),
+    )(at, *dq, *dkv, *n_pieces, *patch_pieces)
+
+
 CP = 32
 
 
@@ -697,23 +784,17 @@
 
 
 def sum_ranks(value):
-    ranks = lax.axis_size("mp")
-    parts = value.reshape(value.shape[0], ranks, -1).transpose(1, 0, 2)
-    return sum(v.astype(f32) for v in from_ranks(parts))
-
-
-def gather_seq(value):
-    shares, me = lax.axis_size("seq"), lax.axis_index("seq")
-    got = [value]
-    for step in range(1, shares // 2):
-        moves = [(i, i ^ (2 * step)) for i in range(shares)]
-        got.append(lax.ppermute(value, "seq", moves))
-    got = jnp.stack(got)
-    other = lax.ppermute(got, "seq", [(i, i ^ 1) for i in range(shares)])
-    both = jnp.stack([got, other], axis=1).reshape((shares,) + value.shape)
-    return jnp.stack(
-        [lax.dynamic_index_in_dim(both, me ^ i, 0, keepdims=False) for i in range(shares)]
-    )
+    return lax.psum_scatter(value, "mp", scatter_dimension=1, tiled=True).astype(f32)
+
+
+def gather_pieces(value):
+    shares = lax.axis_size("seq")
+    pieces = []
+    for step in range(0, shares, 2):
+        moves = [(i, i ^ step) for i in range(shares)]
+        pieces.append(value if step == 0 else lax.ppermute(value, "seq", moves))
+    cores = [(i, i ^ 1) for i in range(shares)]
+    return [p for piece in pieces for p in (piece, lax.ppermute(piece, "seq", cores))]
 
 
 def own_blocks(whole, blocks):
@@ -737,10 +818,6 @@
 
 def to_rows(value):
     return swap_seq(value).transpose(1, 0, 2).reshape(value.shape[1], -1)
-
-
-def after(values, others):
-    return lax.optimization_barrier((values, others))[0]
 
 
 def per_device(
@@ -796,10 +873,6 @@
     per = D // (S * M)
     up_rows = mlp_up.shape[1] // S
     dec_rows = 4 * CP // S
-    lead = jnp.concatenate([mine(cross_query, 1).T, mine(local_kv, 0).reshape(-1, D)], axis=0)
-    lead = gather_rows(lead)
-    w_query = lead[:, :per].reshape(-1, D)
-    w_kv = lead[:, per:].reshape(-1, width)
     first = gather_rows(jnp.concatenate([mine(local_qkv, 0), mine(cross_out, 0)], axis=0))
     w_triple = bundle_part(first, 0, 3 * per, M)
     w_cross_out = bundle_part(first, 3 * per, per)
@@ -813,16 +886,35 @@
     w_self_out = bundle_part(second, up_rows, per)
     w_dec = bundle_part(second, up_rows + per, dec_rows)
     w_down = gather_rows(mine(mlp_down, 0)).reshape(-1, D)
+    w_kv = gather_rows(mine(local_kv, 0)).reshape(-1, width)
 
     x0 = pick(tokens)
+    norms = [jnp.stack([norm_gains[i], norm_shifts[i]]) for i in range(3)]
+    at = jnp.stack([s, m])
     both = [lax.dynamic_index_in_dim(patches, o, 0, keepdims=False) for o in (at_a, at_b)]
-    patch_all = gather_seq(jnp.concatenate(both, axis=0)).reshape(-1, width)
-    x0_all = jnp.concatenate(x0, axis=0)
-    n1 = layer_norm(x0_all.astype(f32), norm_gains[0], norm_shifts[0])
-    q1 = dot(n1, w_query, NT).astype(bf16)
-    heads_one = swap_seq(q1.reshape(RS, S, W).transpose(1, 0, 2))
-    own_kv = lax.dynamic_slice_in_dim(w_kv, s * 2 * W, 2 * W, 0)
-    keys_one = dot(patch_all, own_kv, NT).astype(bf16).reshape(S, 2 * slots, 2 * W)
+    patch_pieces = gather_pieces(jnp.concatenate(both, axis=0))
+    piece = mine(cross_query, 1).T
+    ranks = [piece]
+    for step in range(1, M):
+        ranks.append(lax.ppermute(piece, "mp", [(i, i ^ step) for i in range(M)]))
+    w_pieces = gather_pieces(jnp.stack(ranks))
+    if per % 16 != 0:
+        w_pieces = jnp.stack(w_pieces)
+        w_pieces = [
+            lax.dynamic_index_in_dim(w_pieces, s ^ i, 0, keepdims=False) for i in range(S)
+        ]
+        w_pieces = jnp.stack(w_pieces, axis=1)
+        w_pieces = [
+            lax.dynamic_index_in_dim(w_pieces, m ^ i, 0, keepdims=False) for i in range(M)
+        ]
+        w_pieces = [jnp.stack(w_pieces).reshape(1, D, D)]
+    own_kv = lax.dynamic_slice_in_dim(local_kv, (s % 2) * 2 * W, 2 * W, 0)
+    kv_parts = [jnp.where(m == s // 2, own_kv, jnp.zeros_like(own_kv))]
+    for step in range(1, M):
+        moves = [(i * M + i // 2, i * M + ((i // 2) ^ step)) for i in range(S)]
+        kv_parts.append(lax.ppermute(own_kv, ("seq", "mp"), moves))
+    q1, keys_one, n1, w_query = start(at, x0, norms[0], w_pieces, patch_pieces, kv_parts, W)
+    heads_one = swap_seq(q1)
 
     TC = PLANE // 4
     TR = PLANE * 4 // S
@@ -874,7 +966,6 @@
         o1.append(out)
         res1.append(res)
 
-    norms = [jnp.stack([norm_gains[i], norm_shifts[i]]) for i in range(3)]
     mids = [
         middle(swap_seq(o1[i].reshape(S, rows[i], W)), x0[i], norms[1], w_cross_out, w_triple)
         for i in range(2)
@@ -908,8 +999,6 @@
 
     da2 = [swap_seq(da2_a), swap_seq(da2_b)]
     grads_one = weight_grads([[(n3, du)], [(e3, g)], [(e2, a2)], [(x3b, d_pix)]], M)
-    da2[0] = after(da2[0], grads_one)
-    grads_one = reduce_rows(grads_one)
     dq_a2, dkv_a2 = attend_back(
         wide,
         [res_a2, da2[0], o_a2, heads_two[0]],
@@ -919,11 +1008,13 @@
         row_total,
         hpd,
         True,
-    )
+        [grads_one],
+    )
+    grads_one = reduce_rows(grads_one)
+    n_pieces = gather_pieces(n1)
     tokens_out = own_blocks(x3b[:R], x3b[R:])
     pix = pix.reshape(KA + KB, S, M, cu).transpose(1, 2, 0, 3)
     got = swap_all(pix.reshape(S * M, KA + KB, cu)).reshape(S, pairs, 2, KA + KB, cu)
-    da2[1] = after(da2[1], (tokens_out, got, dkv_a2))
     dq_b2, dkv_b2 = attend_back(
         wide,
         [res_b2, da2[1], o_b2, heads_two[1], pair_kv],
@@ -933,6 +1024,7 @@
         row_total,
         hpd,
         True,
+        [dq_a2, tokens_out, got] + n_pieces[::2],
     )
     kept, given = dkv_b2[: row_total // 2], dkv_b2[row_total // 2 :]
     dkv_b2 = (kept.astype(f32) + swap_pair(given).astype(f32)).astype(bf16)
@@ -940,12 +1032,29 @@
         swap_seq(jnp.concatenate([dq_a2, dkv_a2], axis=1).reshape(S, R, 3 * W)),
         swap_seq(jnp.concatenate([dq_b2, dkv_b2], axis=1).reshape(S, RB, 3 * W)),
     ]
-    outs = [
-        middle_back(dt2[i], x1[i], d2, (0, R // RB)[i], norms[1], w_cross_out, w_triple)
-        for i in range(2)
-    ]
-    d1, e1, da1, sums_two = zip(*outs)
-    da1 = [swap_seq(v) for v in da1]
+    def below(i, deps):
+        return middle_back(
+            dt2[i], x1[i], d2, (0, R // RB)[i], norms[1], w_cross_out, w_triple, deps
+        )
+
+    def cross_back(i, da1, deps):
+        dq, dkv = attend_back(
+            limits[i],
+            [res1[i], da1, o1[i], keys_one],
+            S,
+            (rows[i], 0),
+            [(3,) + kv_one[i]],
+            slot_total,
+            hpd,
+            False,
+            deps,
+        )
+        return dq.reshape(S, rows[i], W), dkv.reshape(S, slots, 2 * W)
+
+    low_a = below(0, [])
+    cross_a = cross_back(0, swap_seq(low_a[2]), [grads_one] + n_pieces[1::2])
+    low_b = below(1, [cross_a[0]])
+    d1, e1, da1, sums_two = zip(low_a, low_b)
 
     px_a = got[:, :, :, :KA].transpose(1, 2, 0, 3, 4).reshape(pairs, 2, S * KA, cu)
     px_b = got[:, :, :, KA:].transpose(1, 0, 2, 3, 4).reshape(pairs, S * KA, cu)
@@ -963,23 +1072,9 @@
     grads_two = weight_grads(
         [[(n2[i], dt2[i]) for i in range(2)], [(e1[i], a1[i]) for i in range(2)]], M
     )
-    n1_all = gather_seq(n1).reshape(-1, D)
-    da1[1] = after(da1[1], (grads_two, sampled, n1_all))
+    cross_b = cross_back(1, swap_seq(da1[1]), [grads_two, sampled])
+    dq1, dkv1 = zip(cross_a, cross_b)
     grads_two = reduce_rows(grads_two)
-    dq1, dkv1 = [], []
-    for i in range(2):
-        dq, dkv = attend_back(
-            limits[i],
-            [res1[i], da1[i], o1[i], keys_one],
-            S,
-            (rows[i], 0),
-            [(3,) + kv_one[i]],
-            slot_total,
-            hpd,
-            False,
-        )
-        dq1.append(dq.reshape(S, rows[i], W))
-        dkv1.append(dkv.reshape(S, slots, 2 * W))
 
     parts = [mm(to_rows(v), w_kv).astype(bf16) for v in dkv1]
     every = [[p] for p in parts]
@@ -1000,13 +1095,7 @@
     grad_tokens = own_blocks(d0[0], d0[1]).astype(f32)
 
     order = 2 * m + s % 2
-    dq_all = jnp.concatenate(dq1, axis=1).reshape(-1, W)
-    dkv_all = jnp.concatenate(dkv1, axis=1).reshape(-1, 2 * W)
-    grad_q = dot(n1_all, dq_all, TN).astype(bf16).reshape(S, D // S, W)
-    grad_kv = dot(patch_all, dkv_all, TN).astype(bf16)
-    grad_kv = grad_kv.reshape(S, width // S, 2 * W)
-    grad_kv = jnp.concatenate([grad_kv[..., :W], grad_kv[..., W:]], axis=1)
-    by_head = jnp.concatenate([grad_q, grad_kv], axis=1)
+    by_head = finish(at, dq1, dkv1, n_pieces, patch_pieces)
     sums = [0.0, 0.0]
     for step in range(S):
         moves = []

time: 1150 us -> 1060 us (0.922)
  local copies, waits for them, and re-layouts: 187 us -> 111 us
  starting transfers between devices: 180 us -> 208 us
  other arithmetic: 60.8 us -> 39.4 us
  matrix products: 26.3 us -> 11.3 us
    all_to_all x18, waiting for transfers between devices: 66.4 us -> 120 us  [swap_seq(): return lax.all_to_all(value, 'seq', split_axis=0, concat_axis=0, tiled=True)]
    ppermute x8 -> x27, waiting for transfers between devices: 79.8 us -> 33.8 us  [the longest x3 27.3 us: per_device(): kv_parts.append(lax.ppermute(own_kv, ('seq', 'mp'), moves))]
    another operation x13 -> x0, local copies, waits for them, and re-layouts: 44 us -> none
    all_gather x4, waiting for transfers between devices: 29.2 us -> 0.04 us  [gather_rows(): return lax.all_gather(piece, ('mp', 'seq'), axis=0, tiled=False)]
    another operation x5 -> x2, other arithmetic: 20.9 us -> 0.11 us  [the longest x1 0.08 us: per_device(): at = jnp.stack([s, m])]
    ppermute x8 -> x27, starting transfers between devices: 9.24 us -> 27.5 us  [the longest x9 10.7 us: gather_pieces(): pieces.append(value if step == 0 else lax.ppermute(value, 'seq', moves))]
    pallas_call x0 -> x2, Pallas kernels: none -> 17.9 us  [the longest x1 9.48 us: finish(): pl.pallas_call(functools.partial(finish_kernel, pieces=S), out_shape=jax....]
    ppermute x8, starting transfers between devices: 15.9 us -> 32.8 us  [per_device(): sums[step % 2] += lax.ppermute(piece, ('seq', 'mp'), moves).astype(f32)]
  transfers between devices with their start and end apart: 75 -> 90, of which waited for: 24 -> 30; matrix products, arithmetic and copies ran while one was open for 19% -> 9% of each run, Pallas kernels for 28% -> 30%
where the time goes in v3:
time: 1060 us; the launch traced here: 1040 us
  Pallas kernels  374 us (35%)
  waiting for transfers between devices  283 us (27%)
  starting transfers between devices  208 us (20%)
  local copies, waits for them, and re-layouts  111 us (10%)
  other arithmetic  39.4 us (4%)
  between operations  16.1 us (2%)
  matrix products  11.3 us (1%)
    pallas_call x4, Pallas kernels, attend_back(): pl.pallas_call(body, out_shape=(jax.ShapeDtypeStruct((queries, hpd * HD),...  138 us
    all_to_all x18, waiting for transfers between devices, swap_seq(): return lax.all_to_all(value, 'seq', split_axis=0, concat_axis=0, tiled=True)  120 us
    pallas_call x4, Pallas kernels, attend(): pl.pallas_call(body, out_shape=(jax.ShapeDtypeStruct((queries, hpd * HD),...  81.5 us
    all_to_all x18, starting transfers between devices, swap_seq(): return lax.all_to_all(value, 'seq', split_axis=0, concat_axis=0, tiled=True)  76.4 us
    unnamed x222, local copies, waits for them, and re-layouts  63.9 us
    ppermute x2, waiting for transfers between devices, swap_pair(): return lax.ppermute(value, 'mp', [(i, i ^ 1) for i in range(count)])  39 us
    pallas_call x1, Pallas kernels, feed_forward(): pl.pallas_call(functools.partial(mlp_kernel, steps=steps), grid=(steps,),...  36.8 us
    pallas_call x2, Pallas kernels, weight_grads(): pl.pallas_call(functools.partial(grads_kernel, shape=shape, widths=widths...  35.8 us
  transfers between devices with their start and end apart: 90, of which 30 were waited for; matrix products, arithmetic and copies ran while one was open for 9% of the time, Pallas kernels for 30%

profile of v3, /device:TPU:0, one launch (start us, length us, event | category | flops | bytes accessed | tf_op | source)
XLA Modules:
  0.0 1042.2 jit_solution(6930313225264772206)
XLA Ops:
  10.9 4.9 copy.118
  28.2 4.7 collective-permute-done.1
  53.0 5.3 collective-permute-done.17.refs_17_
  59.6 13.1 %collective-permute-done.18.refs_18_ = bf16[256,768]{1,0:T(8,128)(2,1)S(1)} collective-permute-done((bf16[256,768]{1,0:T(8,128)(2,1)}, bf16[256,768]{1,0:T(8,128)(2,1)S(1)}, u32[]{:S(2)}, u32[]{:S(2)}) %collective-permute-start.18) | collective-permute-done | bytes 393248 | tf_op jit(solution)/shard_map/ppermute | solution.py:915
  72.7 8.9 collective-permute-done.19.refs_19_
  89.6 15.2 %shard_map.287 = f32[18,160,128]{2,1,0:T(8,128)S(1)} custom-call(bf16[18,32,256]{2,1,0:T(8,128)(2,1)S(1)} %pad.16.cot_ref, bf16[18,561,256]{2,1,0:T(8,128)(2,1)S(1)} %bitcast.227), custom_call_target="tpu_custom_call" | custom-call | flops 600000000 | bytes 7000000 | tf_op jit(solution)/shard_map/pallas_call | solution.py:718
  115.0 7.6 collective-permute-start.21
  128.4 8.4 shard_map.280
  145.8 16.3 %all-to-all-done.refs_0_ = bf16[8,576,128]{2,1,0:T(8,128)(2,1)} async-done(((bf16[8,576,128]{2,1,0:T(8,128)(2,1)}), bf16[8,576,128]{2,1,0:T(8,128)(2,1)}, u32[]{:S(2)}, u32[]{:S(2)}) %all-to-all-start) | async-done | bytes 1179680 | tf_op jit(solution)/shard_map/all_to_all | solution.py:733
  168.4 12.6 %shard_map.284 = (bf16[1536,128]{1,0:T(8,128)(2,1)}, bf16[2,1536,128]{2,1,0:T(8,128)(2,1)S(1)}) custom-call(s32[2]{0:T(128)S(1)} %pad_add_fusion.n_ref, bf16[8,576,128]{2,1,0:T(8,128)(2,1)} %all-to-all-done.refs_0_, bf16[8,384,256]{2,1,0:T(8,128)(2,1)S(1)} %copy-done.61), custom_call_target="tpu_custom_call" | custom-call | flops 4831838208 | bytes 3145728 | tf_op jit(solution)/shard_map/pallas_call | solution.py:194
  181.9 11.5 %all-to-all-done.7 = bf16[32,72,128]{2,1,0:T(8,128)(2,1)S(1)} async-done(((bf16[32,72,128]{2,1,0:T(8,128)(2,1)}), bf16[32,72,128]{2,1,0:T(8,128)(2,1)S(1)}, u32[]{:S(2)}, u32[]{:S(2)}) %all-to-all-start.7) | async-done | bytes 589856 | tf_op jit(solution)/shard_map/all_to_all | solution.py:741
  193.4 6.7 all-to-all-start.4
  201.5 21.6 %shard_map.281 = (bf16[3072,128]{1,0:T(8,128)(2,1)}, bf16[2,3072,128]{2,1,0:T(8,128)(2,1)S(1)}) custom-call(s32[2]{0:T(128)S(1)} %pad_add_fusion.1.n_ref, bf16[8,576,128]{2,1,0:T(8,128)(2,1)} %all-to-all-done.refs_0_, bf16[8,384,256]{2,1,0:T(8,128)(2,1)S(1)} %copy-done.62), custom_call_target="tpu_custom_call" | custom-call | flops 9663676416 | bytes 6291456 | tf_op jit(solution)/shard_map/pallas_call | solution.py:194
  224.3 4.3 all-to-all-start.1
  232.1 5.1 shard_map.285
  246.8 9.9 shard_map.282
  269.2 38.3 %collective-permute-done.20.refs_1_.refs_4_ = bf16[8,192,256]{2,1,0:T(8,128)(2,1)S(1)} collective-permute-done((bf16[8,192,256]{2,1,0:T(8,128)(2,1)S(1)}, bf16[8,192,256]{2,1,0:T(8,128)(2,1)S(1)}, u32[]{:S(2)}, u32[]{:S(2)}) %collective-permute-start.20) | collective-permute-done | bytes 786464 | tf_op jit(solution)/shard_map/ppermute | solution.py:746
  307.5 16.7 %shard_map.286 = (bf16[1536,128]{1,0:T(8,128)(2,1)S(1)}, bf16[2,1536,128]{2,1,0:T(8,128)(2,1)S(1)}) custom-call(s32[2]{0:T(128)S(1)} %copy-done.68, bf16[8,192,384]{2,1,0:T(8,128)(2,1)S(1)} %all-to-all-done.5.refs_0_.refs_3_, bf16[8,192,256]{2,1,0:T(8,128)(2,1)S(1)} %collective-permute-done.20.refs_1_.refs_4_), custom_call_target="tpu_custom_call" | custom-call | flops 9663676416 | bytes 3145728 | tf_op jit(solution)/shard_map/pallas_call | solution.py:194
  330.4 30.6 %shard_map.283 = (bf16[3072,128]{1,0:T(8,128)(2,1)}, bf16[2,3072,128]{2,1,0:T(8,128)(2,1)S(1)}) custom-call(s32[2]{0:T(128)S(1)} %copy-done.68, bf16[8,384,384]{2,1,0:T(8,128)(2,1)S(1)} %all-to-all-done.2.refs_0_.refs_3_), custom_call_target="tpu_custom_call" | custom-call | flops 19327352832 | bytes 6291456 | tf_op jit(solution)/shard_map/pallas_call | solution.py:194
  362.1 4.3 all-to-all-start.3
  372.3 6.7 all-to-all-done.3.aa_ref
  379.9 36.8 %shard_map.288 = (bf16[576,1024]{1,0:T(8,128)(2,1)}, bf16[576,1024]{1,0:T(8,128)(2,1)}, bf16[576,4096]{1,0:T(8,128)(2,1)}, bf16[576,4096]{1,0:T(8,128)(2,1)}, bf...) custom-call(bf16[8,384,128]{2,1,0:T(8,128)(2,1)} %copy-done.85, ...), custom_call_target="tpu_custom_call" | custom-call | flops 24159191040 | bytes 34471936 | tf_op jit(solution)/shard_map/pallas_call | solution.py:419
  416.8 24.2 %shard_map.290.refs_4_ = bf16[1024,9728]{1,0:T(8,128)(2,1)} custom-call(bf16[576,1024]{1,0:T(8,128)(2,1)} %get-tuple-element.77.refs_0_, bf16[576,1024]{1,0:T(8,128)(2,1)} %get-tuple-element.78.refs_1_, bf16[576,1024]{1,0:T(8,128)(2,1)} %get-tuple-element.79.refs_2_, bf16[576,1024]{1,0:T(8,128)(2,1)} %get-tuple-element.73.refs_3_, ...), custom_call_target="tpu_custom_call" | custom-call | flops 11475615744 | bytes 39845888 | tf_op jit(solution)/shard_map/pallas_call | solution.py:567
  463.7 5.5 all-to-all-start.9
  474.6 82.2 %all-to-all-done.9.refs_1_ = bf16[8,384,128]{2,1,0:T(8,128)(2,1)S(1)} async-done(((bf16[8,384,128]{2,1,0:T(8,128)(2,1)}), bf16[8,384,128]{2,1,0:T(8,128)(2,1)S(1)}, u32[]{:S(2)}, u32[]{:S(2)}) %all-to-all-start.9) | async-done | bytes 786464 | tf_op jit(solution)/shard_map/all_to_all | solution.py:733
  559.5 61.0 %shard_map.291 = (bf16[3072,128]{1,0:T(8,128)(2,1)S(1)}, bf16[3072,256]{1,0:T(8,128)(2,1)}) custom-call(s32[2]{0:T(128)S(1)} %copy-done.68, bf16[2,3072,128]{2,1,0:T(8,128)(2,1)} %copy-done.72, bf16[8,384,128]{2,1,0:T(8,128)(2,1)S(1)} %all-to-all-done.9.refs_1_, bf16[3072,128]{1,0:T(8,128)(2,1)} %get-tuple-element.67.refs_2_, ...), custom_call_target="tpu_custom_call" | custom-call | flops 48318382080 | bytes 9437184 | tf_op jit(solution)/shard_map/pallas_call | solution.py:224
  630.7 34.4 %shard_map.294 = (bf16[1536,128]{1,0:T(8,128)(2,1)S(1)}, bf16[3072,256]{1,0:T(8,128)(2,1)}) custom-call(s32[2]{0:T(128)S(1)} %copy-done.68, bf16[2,1536,128]{2,1,0:T(8,128)(2,1)} %copy-done.71, bf16[8,192,128]{2,1,0:T(8,128)(2,1)S(1)} %copy-done.43, bf16[1536,128]{1,0:T(8,128)(2,1)S(1)} %copy-done.41, bf16[8,192,384]{2,1,0:T(8,128)(2,1)} %copy-done.15, ...), custom_call_target="tpu_custom_call" | custom-call | flops 24159191040 | bytes 4718592 | tf_op jit(solution)/shard_map/pallas_call | solution.py:224
  673.8 12.0 %shard_map.292 = (f32[384,1024]{1,0:T(8,128)S(1)}, bf16[384,1024]{1,0:T(8,128)(2,1)S(1)}, bf16[8,384,128]{2,1,0:T(8,128)(2,1)}, f32[2,1024]{1,0:T(2,128)S(1)}) custom-call(bf16[8,384,384]{2,1,0:T(8,128)(2,1)S(1)} %all-to-all-done.10.t_ref.refs_4_, f32[384,1024]{1,0:T(8,128)S(1)} %copy-done.24, f32[576,1024]{1,0:T(8,128)S(1)} %copy-done.11, ...), custom_call_target="tpu_custom_call" | custom-call | flops 3221225472 | bytes 17825792 | tf_op jit(solution)/shard_map/pallas_call | solution.py:507
  695.5 9.3 all-to-all-done.11.refs_1_
  709.1 26.9 %shard_map.293 = (bf16[3072,128]{1,0:T(8,128)(2,1)}, bf16[1536,256]{1,0:T(8,128)(2,1)}) custom-call(s32[2]{0:T(128)S(1)} %copy-done.67, bf16[2,3072,128]{2,1,0:T(8,128)(2,1)} %copy-done.70, bf16[8,384,128]{2,1,0:T(8,128)(2,1)} %copy-done.84, bf16[3072,128]{1,0:T(8,128)(2,1)} %get-tuple-element.65.refs_2_, ...), custom_call_target="tpu_custom_call" | custom-call | flops 24159191040 | bytes 9437184 | tf_op jit(solution)/shard_map/pallas_call | solution.py:224
  737.6 9.7 shard_map.295
  749.6 11.6 %shard_map.296.refs_4_ = bf16[1024,4096]{1,0:T(8,128)(2,1)} custom-call(bf16[384,1024]{1,0:T(8,128)(2,1)} %copy-done.31, bf16[192,1024]{1,0:T(8,128)(2,1)} %copy-done.44, bf16[384,1024]{1,0:T(8,128)(2,1)} %copy-done.33, bf16[192,1024]{1,0:T(8,128)(2,1)} %copy-done.46, bf16[8,384,384]{2,1,0:T(8,128)(2,1)} %copy-done.3, bf16[8,192,384]{2,1,0:T(8,128)(2,1)} %copy-done.8, ...), custom_call_target="tpu_custom_call" | custom-call | flops 2415919104 | bytes 16777216 | tf_op jit(solution)/shard_map/pallas_call | solution.py:567
  771.9 4.7 collective-permute-done.31
  780.9 11.7 %shard_map.289 = bf16[18,32,256]{2,1,0:T(8,128)(2,1)S(1)} custom-call(bf16[18,160,128]{2,1,0:T(8,128)(2,1)S(1)} %concatenate.44.x_ref, bf16[18,561,256]{2,1,0:T(8,128)(2,1)S(1)} %bitcast.228), custom_call_target="tpu_custom_call" | custom-call | flops 600000000 | bytes 7000000 | tf_op jit(solution)/shard_map/pallas_call | solution.py:718
  796.7 16.2 %shard_map.297 = (bf16[1536,128]{1,0:T(8,128)(2,1)}, bf16[1536,256]{1,0:T(8,128)(2,1)}) custom-call(s32[2]{0:T(128)S(1)} %copy-done.65, bf16[2,1536,128]{2,1,0:T(8,128)(2,1)} %copy-done.69, bf16[8,192,128]{2,1,0:T(8,128)(2,1)S(1)} %all-to-all-done.15.refs_1_, bf16[1536,128]{1,0:T(8,128)(2,1)} %get-tuple-element.68.refs_2_, ...), custom_call_target="tpu_custom_call" | custom-call | flops 12079595520 | bytes 4718592 | tf_op jit(solution)/shard_map/pallas_call | solution.py:224
  812.9 9.5 shard_map.298
  825.1 10.5 %collective-permute-start.56 = (bf16[320,128]{1,0:T(8,128)(2,1)S(1)}, bf16[320,128]{1,0:T(8,128)(2,1)S(1)}, u32[]{:S(2)}, u32[]{:S(2)}) collective-permute-start(bf16[320,128]{1,0:T(8,128)(2,1)S(1)} %get-tuple-element.204), channel_id=1, source_target_pairs={{6,0},{14,1},{22,2},{30,3},{2,4},{10,5},{18,6},{26,7},{7,8},{15,9}... | collective-permute-start | bytes 245768 | tf_op jit(solution)/shard_map/ppermute | solution.py:1107
  851.0 9.5 collective-permute-start.61
  861.0 4.3 copy.152
  865.4 9.5 collective-permute-done.57
  879.6 4.6 all-to-all-start.16
  892.3 6.4 collective-permute-start.46
  934.9 12.0 %collective-permute-done.39 = bf16[96,1024]{1,0:T(8,128)(2,1)S(1)} collective-permute-done((bf16[96,1024]{1,0:T(8,128)(2,1)S(1)}, bf16[96,1024]{1,0:T(8,128)(2,1)S(1)}, u32[]{:S(2)}, u32[]{:S(2)}) %collective-permute-start.39) | collective-permute-done | bytes 196640 | tf_op jit(solution)/shard_map/ppermute | solution.py:776
  948.7 4.4 collective-permute-done.40
  956.4 12.5 %collective-permute-start.44 = (bf16[96,1024]{1,0:T(8,128)(2,1)S(1)}, bf16[96,1024]{1,0:T(8,128)(2,1)S(1)}, u32[]{:S(2)}, u32[]{:S(2)}) collective-permute-start(bf16[96,1024]{1,0:T(8,128)(2,1)S(1)} %get-tuple-element.210), channel_id=1, source_target_pairs={{0,1},{1,3},{2,0},{3,2},{4,5},{5,7},{6,4},{7,6},{8,9},{9,11},{10,8... | collective-permute-start | bytes 589832 | tf_op jit(solution)/shard_map/ppermute | solution.py:811
  969.8 12.8 %collective-permute-done.44 = bf16[96,1024]{1,0:T(8,128)(2,1)S(1)} collective-permute-done((bf16[96,1024]{1,0:T(8,128)(2,1)S(1)}, bf16[96,1024]{1,0:T(8,128)(2,1)S(1)}, u32[]{:S(2)}, u32[]{:S(2)}) %collective-permute-start.44) | collective-permute-done | bytes 196640 | tf_op jit(solution)/shard_map/ppermute | solution.py:811
  1001.2 17.2 %collective-permute-done.49 = bf16[192,768]{1,0:T(8,128)(2,1)S(1)} collective-permute-done((bf16[192,768]{1,0:T(8,128)(2,1)S(1)}, bf16[192,768]{1,0:T(8,128)(2,1)S(1)}, u32[]{:S(2)}, u32[]{:S(2)}) %collective-permute-start.49) | collective-permute-done | bytes 294944 | tf_op jit(solution)/shard_map/ppermute | solution.py:1084
  1027.3 4.8 reduce-scatter.11.cloned.1.call-done
  (514 shorter events, 309.1 us)
Async XLA Ops:
  7.2 221.5 %all-gather.9.cloned.1.call-start = ((), (), s32[]{:S(2)}) async-start(), calls=%async_computation.27 | async-start | bytes 8650752 | tf_op jit(solution)/shard_map/all_gather | solution.py:750
  18.4 354.0 %all-gather.13.cloned.1.call-start = ((), (), s32[]{:S(2)}) async-start(), calls=%async_computation.29 | async-start | bytes 8650752 | tf_op jit(solution)/shard_map/all_gather | solution.py:750
  19.2 359.9 %all-gather.11.cloned.1.call-start = ((), (), s32[]{:S(2)}) async-start(), calls=%async_computation.28 | async-start | bytes 11894784 | tf_op jit(solution)/shard_map/all_gather | solution.py:750
  44.7 28.0 %collective-permute-start.18 = (bf16[256,768]{1,0:T(8,128)(2,1)}, bf16[256,768]{1,0:T(8,128)(2,1)S(1)}, u32[]{:S(2)}, u32[]{:S(2)}) collective-permute-start(bf16[256,768]{1,0:T(8,128)(2,1)} %get-tuple-element.184), channel_id=1, source_target_pairs={{0,2},{4,6},{9,11},{13,15},{18,16},{22,20},{27,25},{31,29}} | collective-permute-start | bytes 1179656 | tf_op jit(solution)/shard_map/ppermute | solution.py:915
  48.8 34.8 %collective-permute-start.11 = (bf16[384,768]{1,0:T(8,128)(2,1)S(1)}, bf16[384,768]{1,0:T(8,128)(2,1)}, u32[]{:S(2)}, u32[]{:S(2)}) collective-permute-start(bf16[384,768]{1,0:T(8,128)(2,1)S(1)} %pad_maximum_fusion.6.refs_8_), channel_id=1, source_target_pairs={{0,8},{4,12},{8,0},{12,4},{16,24},{20,28},{24,16},{28,20},{1,9},{5... | collective-permute-start | bytes 1769480 | tf_op jit(solution)/shard_map/ppermute | solution.py:795
  49.3 34.3 %collective-permute-start.13 = (bf16[384,768]{1,0:T(8,128)(2,1)S(1)}, bf16[384,768]{1,0:T(8,128)(2,1)}, u32[]{:S(2)}, u32[]{:S(2)}) collective-permute-start(bf16[384,768]{1,0:T(8,128)(2,1)S(1)} %pad_maximum_fusion.6.refs_8_), channel_id=1, source_target_pairs={{0,16},{4,20},{8,24},{12,28},{16,0},{20,4},{24,8},{28,12},{1,17},{... | collective-permute-start | bytes 1769480 | tf_op jit(solution)/shard_map/ppermute | solution.py:795
  51.6 32.5 %collective-permute-start.15 = (bf16[384,768]{1,0:T(8,128)(2,1)S(1)}, bf16[384,768]{1,0:T(8,128)(2,1)}, u32[]{:S(2)}, u32[]{:S(2)}) collective-permute-start(bf16[384,768]{1,0:T(8,128)(2,1)S(1)} %pad_maximum_fusion.6.refs_8_), channel_id=1, source_target_pairs={{0,24},{4,28},{8,16},{12,20},{16,8},{20,12},{24,0},{28,4},{1,25},{... | collective-permute-start | bytes 1769480 | tf_op jit(solution)/shard_map/ppermute | solution.py:795
  81.7 32.1 %collective-permute-start.10 = (bf16[384,768]{1,0:T(8,128)(2,1)S(1)}, bf16[384,768]{1,0:T(8,128)(2,1)}, u32[]{:S(2)}, u32[]{:S(2)}) collective-permute-start(bf16[384,768]{1,0:T(8,128)(2,1)S(1)} %pad_maximum_fusion.6.refs_8_), channel_id=1, source_target_pairs={{0,4},{4,0},{8,12},{12,8},{16,20},{20,16},{24,28},{28,24},{1,5},{5... | collective-permute-start | bytes 1769480 | tf_op jit(solution)/shard_map/ppermute | solution.py:797
  83.6 31.4 %collective-permute-start.12 = (bf16[384,768]{1,0:T(8,128)(2,1)}, bf16[384,768]{1,0:T(8,128)(2,1)}, u32[]{:S(2)}, u32[]{:S(2)}) collective-permute-start(bf16[384,768]{1,0:T(8,128)(2,1)} %collective-permute-done.11.refs_10_), channel_id=1, source_target_pairs={{0,4},{4,0},{8,12},{12,8},{16,20},{20,16},{24,28},{28,24},{1,5},{5... | collective-permute-start | bytes 1769480 | tf_op jit(solution)/shard_map/ppermute | solution.py:797
  83.6 38.9 %collective-permute-start.14 = (bf16[384,768]{1,0:T(8,128)(2,1)}, bf16[384,768]{1,0:T(8,128)(2,1)}, u32[]{:S(2)}, u32[]{:S(2)}) collective-permute-start(bf16[384,768]{1,0:T(8,128)(2,1)} %collective-permute-done.13.refs_12_), channel_id=1, source_target_pairs={{0,4},{4,0},{8,12},{12,8},{16,20},{20,16},{24,28},{28,24},{1,5},{5... | collective-permute-start | bytes 1769480 | tf_op jit(solution)/shard_map/ppermute | solution.py:797
  84.1 38.5 %collective-permute-start.16 = (bf16[384,768]{1,0:T(8,128)(2,1)}, bf16[384,768]{1,0:T(8,128)(2,1)}, u32[]{:S(2)}, u32[]{:S(2)}) collective-permute-start(bf16[384,768]{1,0:T(8,128)(2,1)} %collective-permute-done.15.refs_14_), channel_id=1, source_target_pairs={{0,4},{4,0},{8,12},{12,8},{16,20},{20,16},{24,28},{28,24},{1,5},{5... | collective-permute-start | bytes 1769480 | tf_op jit(solution)/shard_map/ppermute | solution.py:797
  110.1 31.5 %collective-permute-start.22 = (f32[18,8,128]{2,1,0:T(8,128)}, f32[18,8,128]{2,1,0:T(8,128)}, u32[]{:S(2)}, u32[]{:S(2)}) collective-permute-start(f32[18,8,128]{2,1,0:T(8,128)} %slice.181), channel_id=1, source_target_pairs={{0,16},{4,20},{8,24},{12,28},{1,17},{5,21},{9,25},{13,29},{2,18},{... | collective-permute-start | bytes 221192 | tf_op jit(solution)/shard_map/ppermute | solution.py:934
  113.7 27.8 %collective-permute-start.23 = (f32[18,1,128]{2,1,0:T(1,128)S(1)}, f32[18,1,128]{2,1,0:T(1,128)S(1)}, u32[]{:S(2)}, u32[]{:S(2)}) collective-permute-start(f32[18,1,128]{2,1,0:T(1,128)S(1)} %slice.183), channel_id=1, source_target_pairs={{0,20},{4,24},{8,28},{1,21},{5,25},{9,29},{2,22},{6,26},{10,30},{3... | collective-permute-start | bytes 27656 | tf_op jit(solution)/shard_map/ppermute | solution.py:935
  115.0 28.3 %collective-permute-start.21 = (f32[18,16,128]{2,1,0:T(8,128)}, f32[18,16,128]{2,1,0:T(8,128)}, u32[]{:S(2)}, u32[]{:S(2)}) collective-permute-start(f32[18,16,128]{2,1,0:T(8,128)} %slice.180), channel_id=1, source_target_pairs={{0,4},{4,8},{8,12},{16,20},{20,24},{24,28},{1,5},{5,9},{9,13},{17,... | collective-permute-start | bytes 442376 | tf_op jit(solution)/shard_map/ppermute | solution.py:933
  162.1 31.2 %all-to-all-start.7 = ((bf16[32,72,128]{2,1,0:T(8,128)(2,1)}), bf16[32,72,128]{2,1,0:T(8,128)(2,1)S(1)}, u32[]{:S(2)}, u32[]{:S(2)}) async-start(bf16[32,72,128]{2,1,0:T(8,128)(2,1)} %bitcast.247), calls=%async_computation.7 | async-start | bytes 1179648 | tf_op jit(solution)/shard_map/all_to_all | solution.py:741
  193.4 31.0 %all-to-all-start.4 = ((bf16[8,192,128]{2,1,0:T(8,128)(2,1)}), bf16[8,192,128]{2,1,0:T(8,128)(2,1)S(1)}, u32[]{:S(2)}, u32[]{:S(2)}) async-start(bf16[8,192,128]{2,1,0:T(8,128)(2,1)} %bitcast.18), calls=%async_computation.4 | async-start | bytes 786432 | tf_op jit(solution)/shard_map/all_to_all | solution.py:733
  264.2 62.5 %all-to-all-start.2 = ((bf16[8,384,384]{2,1,0:T(8,128)(2,1)}), bf16[8,384,384]{2,1,0:T(8,128)(2,1)S(1)}, u32[]{:S(2)}, u32[]{:S(2)}) async-start(bf16[8,384,384]{2,1,0:T(8,128)(2,1)} %copy-done.17), calls=%async_computation.2 | async-start | bytes 4718592 | tf_op jit(solution)/shard_map/all_to_all | solution.py:733
  268.1 39.4 %collective-permute-start.20 = (bf16[8,192,256]{2,1,0:T(8,128)(2,1)S(1)}, bf16[8,192,256]{2,1,0:T(8,128)(2,1)S(1)}, u32[]{:S(2)}, u32[]{:S(2)}) collective-permute-start(bf16[8,192,256]{2,1,0:T(8,128)(2,1)S(1)} %slice.178), channel_id=1, source_target_pairs={{0,1},{1,0},{2,3},{3,2},{4,5},{5,4},{6,7},{7,6},{8,9},{9,8},{10,11... | collective-permute-start | bytes 2359304 | tf_op jit(solution)/shard_map/ppermute | solution.py:746
  326.7 35.4 %all-to-all-start.6 = ((bf16[8,192,128]{2,1,0:T(8,128)(2,1)}), bf16[8,192,128]{2,1,0:T(8,128)(2,1)S(1)}, u32[]{:S(2)}, u32[]{:S(2)}) async-start(bf16[8,192,128]{2,1,0:T(8,128)(2,1)} %bitcast.232), calls=%async_computation.6 | async-start | bytes 786432 | tf_op jit(solution)/shard_map/all_to_all | solution.py:733
  366.5 342.0 %reduce-scatter.7.cloned.1.call-start = ((), (), s32[]{:S(2)}) async-start(), calls=%async_computation.24 | async-start | bytes 22413312 | tf_op jit(solution)/shard_map/reduce_scatter | solution.py:767
  451.8 435.1 %all-gather.15.cloned.1.call-start = ((), (), s32[]{:S(2)}) async-start(), calls=%async_computation.30 | async-start | bytes 3244032 | tf_op jit(solution)/shard_map/all_gather | solution.py:750
  453.5 175.2 %collective-permute-start.33 = (bf16[576,1024]{1,0:T(8,128)(2,1)}, bf16[576,1024]{1,0:T(8,128)(2,1)}, u32[]{:S(2)}, u32[]{:S(2)}) collective-permute-start(bf16[576,1024]{1,0:T(8,128)(2,1)} %get-tuple-element.89.refs_8_.refs_0_), channel_id=1, source_target_pairs={{0,8},{4,12},{8,0},{12,4},{16,24},{20,28},{24,16},{28,20},{1,9},{5... | collective-permute-start | bytes 3538952 | tf_op jit(solution)/shard_map/ppermute | solution.py:795
  455.4 173.3 %collective-permute-start.35 = (bf16[576,1024]{1,0:T(8,128)(2,1)}, bf16[576,1024]{1,0:T(8,128)(2,1)}, u32[]{:S(2)}, u32[]{:S(2)}) collective-permute-start(bf16[576,1024]{1,0:T(8,128)(2,1)} %get-tuple-element.89.refs_8_.refs_0_), channel_id=1, source_target_pairs={{0,16},{4,20},{8,24},{12,28},{16,0},{20,4},{24,8},{28,12},{1,17},{... | collective-permute-start | bytes 3538952 | tf_op jit(solution)/shard_map/ppermute | solution.py:795
  458.1 170.7 %collective-permute-start.37 = (bf16[576,1024]{1,0:T(8,128)(2,1)}, bf16[576,1024]{1,0:T(8,128)(2,1)}, u32[]{:S(2)}, u32[]{:S(2)}) collective-permute-start(bf16[576,1024]{1,0:T(8,128)(2,1)} %get-tuple-element.89.refs_8_.refs_0_), channel_id=1, source_target_pairs={{0,24},{4,28},{8,16},{12,20},{16,8},{20,12},{24,0},{28,4},{1,25},{... | collective-permute-start | bytes 3538952 | tf_op jit(solution)/shard_map/ppermute | solution.py:795
  463.7 93.2 %all-to-all-start.9 = ((bf16[8,384,128]{2,1,0:T(8,128)(2,1)}), bf16[8,384,128]{2,1,0:T(8,128)(2,1)S(1)}, u32[]{:S(2)}, u32[]{:S(2)}) async-start(bf16[8,384,128]{2,1,0:T(8,128)(2,1)} %get-tuple-element.76), calls=%async_computation.9 | async-start | bytes 1572864 | tf_op jit(solution)/shard_map/all_to_all | solution.py:733
  556.9 67.6 %all-to-all-start.8 = ((bf16[32,72,128]{2,1,0:T(8,128)(2,1)}), bf16[32,72,128]{2,1,0:T(8,128)(2,1)S(1)}, u32[]{:S(2)}, u32[]{:S(2)}) async-start(bf16[32,72,128]{2,1,0:T(8,128)(2,1)} %bitcast.53), calls=%async_computation.8 | async-start | bytes 1179648 | tf_op jit(solution)/shard_map/all_to_all | solution.py:741
  624.5 45.4 %all-to-all-start.10 = ((bf16[8,384,384]{2,1,0:T(8,128)(2,1)}), bf16[8,384,384]{2,1,0:T(8,128)(2,1)S(1)}, u32[]{:S(2)}, u32[]{:S(2)}) async-start(bf16[8,384,384]{2,1,0:T(8,128)(2,1)} %bitcast.234), calls=%async_computation.10 | async-start | bytes 4718592 | tf_op jit(solution)/shard_map/all_to_all | solution.py:733
  668.9 39.5 %collective-permute-start.32 = (bf16[576,1024]{1,0:T(8,128)(2,1)}, bf16[576,1024]{1,0:T(8,128)(2,1)}, u32[]{:S(2)}, u32[]{:S(2)}) collective-permute-start(bf16[576,1024]{1,0:T(8,128)(2,1)} %get-tuple-element.89.refs_8_.refs_0_), channel_id=1, source_target_pairs={{0,4},{4,0},{8,12},{12,8},{16,20},{20,16},{24,28},{28,24},{1,5},{5... | collective-permute-start | bytes 3538952 | tf_op jit(solution)/shard_map/ppermute | solution.py:797
  669.1 39.3 %collective-permute-start.34 = (bf16[576,1024]{1,0:T(8,128)(2,1)}, bf16[576,1024]{1,0:T(8,128)(2,1)}, u32[]{:S(2)}, u32[]{:S(2)}) collective-permute-start(bf16[576,1024]{1,0:T(8,128)(2,1)} %collective-permute-done.33.refs_9_.refs_2_), channel_id=1, source_target_pairs={{0,4},{4,0},{8,12},{12,8},{16,20},{20,16},{24,28},{28,24},{1,5},{5... | collective-permute-start | bytes 3538952 | tf_op jit(solution)/shard_map/ppermute | solution.py:797
  669.4 39.1 %collective-permute-start.36 = (bf16[576,1024]{1,0:T(8,128)(2,1)}, bf16[576,1024]{1,0:T(8,128)(2,1)}, u32[]{:S(2)}, u32[]{:S(2)}) collective-permute-start(bf16[576,1024]{1,0:T(8,128)(2,1)} %collective-permute-done.35.refs_10_.refs_4_), channel_id=1, source_target_pairs={{0,4},{4,0},{8,12},{12,8},{16,20},{20,16},{24,28},{28,24},{1,5},{5... | collective-permute-start | bytes 3538952 | tf_op jit(solution)/shard_map/ppermute | solution.py:797
  669.6 38.8 %collective-permute-start.38 = (bf16[576,1024]{1,0:T(8,128)(2,1)}, bf16[576,1024]{1,0:T(8,128)(2,1)}, u32[]{:S(2)}, u32[]{:S(2)}) collective-permute-start(bf16[576,1024]{1,0:T(8,128)(2,1)} %collective-permute-done.37.refs_11_.refs_6_), channel_id=1, source_target_pairs={{0,4},{4,0},{8,12},{12,8},{16,20},{20,16},{24,28},{28,24},{1,5},{5... | collective-permute-start | bytes 3538952 | tf_op jit(solution)/shard_map/ppermute | solution.py:797
  704.8 31.2 %all-to-all-start.14 = ((bf16[8,192,384]{2,1,0:T(8,128)(2,1)}), bf16[8,192,384]{2,1,0:T(8,128)(2,1)S(1)}, u32[]{:S(2)}, u32[]{:S(2)}) async-start(bf16[8,192,384]{2,1,0:T(8,128)(2,1)} %bitcast.79), calls=%async_computation.15 | async-start | bytes 2359296 | tf_op jit(solution)/shard_map/all_to_all | solution.py:733
  708.3 290.5 %reduce-scatter.9.cloned.1.call-start = ((), (), s32[]{:S(2)}) async-start(), calls=%async_computation.25 | async-start | bytes 9437184 | tf_op jit(solution)/shard_map/reduce_scatter | solution.py:767
  763.7 29.2 %all-to-all-start.15 = ((bf16[8,192,128]{2,1,0:T(8,128)(2,1)}), bf16[8,192,128]{2,1,0:T(8,128)(2,1)S(1)}, u32[]{:S(2)}, u32[]{:S(2)}) async-start(bf16[8,192,128]{2,1,0:T(8,128)(2,1)} %get-tuple-element.98), calls=%async_computation.16 | async-start | bytes 786432 | tf_op jit(solution)/shard_map/all_to_all | solution.py:733
  792.9 42.7 %all-to-all-start.12 = ((bf16[8,384,128]{2,1,0:T(8,128)(2,1)}), bf16[8,384,128]{2,1,0:T(8,128)(2,1)S(1)}, u32[]{:S(2)}, u32[]{:S(2)}) async-start(bf16[8,384,128]{2,1,0:T(8,128)(2,1)} %bitcast.68.refs_0_.qa_ref), calls=%async_computation.13 | async-start | bytes 1572864 | tf_op jit(solution)/shard_map/all_to_all | solution.py:733
  835.6 44.0 %all-to-all-start.17 = ((bf16[8,192,256]{2,1,0:T(8,128)(2,1)}), bf16[8,192,256]{2,1,0:T(8,128)(2,1)S(1)}, u32[]{:S(2)}, u32[]{:S(2)}) async-start(bf16[8,192,256]{2,1,0:T(8,128)(2,1)} %bitcast.87.ka_ref), calls=%async_computation.18 | async-start | bytes 1572864 | tf_op jit(solution)/shard_map/all_to_all | solution.py:733
  839.4 183.6 %reduce-scatter.13.cloned.1.call-start = ((), (), s32[]{:S(2)}) async-start(), calls=%async_computation.31 | async-start | bytes 3112960
  840.0 34.9 %collective-permute-start.57 = (bf16[320,128]{1,0:T(8,128)(2,1)S(1)}, bf16[320,128]{1,0:T(8,128)(2,1)}, u32[]{:S(2)}, u32[]{:S(2)}) collective-permute-start(bf16[320,128]{1,0:T(8,128)(2,1)S(1)} %get-tuple-element.203), channel_id=1, source_target_pairs={{7,0},{15,1},{23,2},{31,3},{3,4},{11,5},{19,6},{27,7},{6,8},{14,9}... | collective-permute-start | bytes 245768 | tf_op jit(solution)/shard_map/ppermute | solution.py:1107
  842.7 32.2 %collective-permute-start.58 = (bf16[320,128]{1,0:T(8,128)(2,1)S(1)}, bf16[320,128]{1,0:T(8,128)(2,1)}, u32[]{:S(2)}, u32[]{:S(2)}) collective-permute-start(bf16[320,128]{1,0:T(8,128)(2,1)S(1)} %get-tuple-element.199), channel_id=1, source_target_pairs={{0,0},{8,1},{16,2},{24,3},{4,4},{12,5},{20,6},{28,7},{1,8},{9,9},{... | collective-permute-start | bytes 245768 | tf_op jit(solution)/shard_map/ppermute | solution.py:1107
  844.0 32.7 %collective-permute-start.59 = (bf16[320,128]{1,0:T(8,128)(2,1)S(1)}, bf16[320,128]{1,0:T(8,128)(2,1)}, u32[]{:S(2)}, u32[]{:S(2)}) collective-permute-start(bf16[320,128]{1,0:T(8,128)(2,1)S(1)} %get-tuple-element.202), channel_id=1, source_target_pairs={{1,0},{9,1},{17,2},{25,3},{5,4},{13,5},{21,6},{29,7},{0,8},{8,9},{... | collective-permute-start | bytes 245768 | tf_op jit(solution)/shard_map/ppermute | solution.py:1107
  846.7 29.9 %collective-permute-start.60 = (bf16[320,128]{1,0:T(8,128)(2,1)S(1)}, bf16[320,128]{1,0:T(8,128)(2,1)}, u32[]{:S(2)}, u32[]{:S(2)}) collective-permute-start(bf16[320,128]{1,0:T(8,128)(2,1)S(1)} %get-tuple-element.201), channel_id=1, source_target_pairs={{2,0},{10,1},{18,2},{26,3},{6,4},{14,5},{22,6},{30,7},{3,8},{11,9}... | collective-permute-start | bytes 245768 | tf_op jit(solution)/shard_map/ppermute | solution.py:1107
  890.5 99.2 %collective-permute-start.45 = (bf16[192,768]{1,0:T(8,128)(2,1)}, bf16[192,768]{1,0:T(8,128)(2,1)}, u32[]{:S(2)}, u32[]{:S(2)}) collective-permute-start(bf16[192,768]{1,0:T(8,128)(2,1)} %convolution_convert_fusion.1), channel_id=1, source_target_pairs={{0,1},{1,0},{2,3},{3,2},{4,5},{5,4},{6,7},{7,6},{8,9},{9,8},{10,11... | collective-permute-start | bytes 884744 | tf_op jit(solution)/shard_map/ppermute | solution.py:1084
  892.3 104.3 %collective-permute-start.46 = (bf16[192,768]{1,0:T(8,128)(2,1)}, bf16[192,768]{1,0:T(8,128)(2,1)}, u32[]{:S(2)}, u32[]{:S(2)}) collective-permute-start(bf16[192,768]{1,0:T(8,128)(2,1)} %convolution_convert_fusion.1), channel_id=1, source_target_pairs={{0,2},{1,3},{2,0},{3,1},{4,6},{5,7},{6,4},{7,5},{8,10},{9,11},{10,... | collective-permute-start | bytes 884744 | tf_op jit(solution)/shard_map/ppermute | solution.py:1084
  917.9 67.6 %all-to-all-start.18 = ((bf16[8,192,256]{2,1,0:T(8,128)(2,1)}), bf16[8,192,256]{2,1,0:T(8,128)(2,1)}, u32[]{:S(2)}, u32[]{:S(2)}) async-start(bf16[8,192,256]{2,1,0:T(8,128)(2,1)} %bitcast.94.kb_ref), calls=%async_computation.19 | async-start | bytes 1572864 | tf_op jit(solution)/shard_map/all_to_all | solution.py:733
  922.2 109.9 %reduce-scatter.11.cloned.1.call-start = ((), (), s32[]{:S(2)}) async-start(), calls=%async_computation.26 | async-start | bytes 1310720 | tf_op jit(solution)/shard_map/reduce_scatter | solution.py:787
  946.9 49.8 %collective-permute-start.47 = (bf16[192,768]{1,0:T(8,128)(2,1)}, bf16[192,768]{1,0:T(8,128)(2,1)}, u32[]{:S(2)}, u32[]{:S(2)}) collective-permute-start(bf16[192,768]{1,0:T(8,128)(2,1)} %convolution_convert_fusion.1), channel_id=1, source_target_pairs={{0,3},{1,2},{2,1},{3,0},{4,7},{5,6},{6,5},{7,4},{8,11},{9,10},{10,... | collective-permute-start | bytes 884744 | tf_op jit(solution)/shard_map/ppermute | solution.py:1084
  987.6 30.8 %collective-permute-start.49 = (bf16[192,768]{1,0:T(8,128)(2,1)S(1)}, bf16[192,768]{1,0:T(8,128)(2,1)S(1)}, u32[]{:S(2)}, u32[]{:S(2)}) collective-permute-start(bf16[192,768]{1,0:T(8,128)(2,1)S(1)} %convolution_convert_fusion), channel_id=1, source_target_pairs={{0,2},{1,3},{2,0},{3,1},{4,6},{5,7},{6,4},{7,5},{8,10},{9,11},{10,... | collective-permute-start | bytes 884744 | tf_op jit(solution)/shard_map/ppermute | solution.py:1084
  989.6 28.9 %collective-permute-start.50 = (bf16[192,768]{1,0:T(8,128)(2,1)S(1)}, bf16[192,768]{1,0:T(8,128)(2,1)S(1)}, u32[]{:S(2)}, u32[]{:S(2)}) collective-permute-start(bf16[192,768]{1,0:T(8,128)(2,1)S(1)} %convolution_convert_fusion), channel_id=1, source_target_pairs={{0,3},{1,2},{2,1},{3,0},{4,7},{5,6},{6,5},{7,4},{8,11},{9,10},{10,... | collective-permute-start | bytes 884744 | tf_op jit(solution)/shard_map/ppermute | solution.py:1084
  (145 other events, 2101.4 us)
Sparse Core Ops, SparseCore 0:
  18.5 93.5 all-gather.8
  114.9 92.4 all-gather.12
  210.3 117.6 all-gather.10
  441.2 172.9 reduce-scatter.6
  617.4 64.7 all-gather.14
  761.4 111.3 reduce-scatter.8
  875.2 83.3 reduce-scatter.12
  999.0 33.0 reduce-scatter.10

commit v4 on v3

--- a/solution.py
+++ b/solution.py
@@ -306,7 +306,7 @@
             once((S, rows, W)),
             once((rows, D)),
             once((2, D)),
-            w_out[1],
+            once(*w_out[1]),
             w_triple[1],
         ],
         out_specs=(
@@ -323,6 +323,7 @@
 
 
 def mlp_kernel(
+    at_ref,
     aa_ref,
     ab_ref,
     xa_ref,
@@ -333,33 +334,22 @@
     norm_ref,
     ws_ref,
     wd_ref,
-    up_ref,
-    down_ref,
-    n_ref,
-    ac_ref,
-    g_ref,
-    du_ref,
-    x3_ref,
-    pix_ref,
-    e3_ref,
-    d2_ref,
-    e2_ref,
-    da_ref,
-    db_ref,
-    sum_ref,
-    x2,
-    d3,
-    acc,
-    back,
-    *,
+    *refs,
     steps,
 ):
+    pieces, refs = refs[:steps], refs[steps:]
+    n_ref, ac_ref, g_ref, du_ref, x3_ref, pix_ref, e3_ref, d2_ref, e2_ref = refs[:9]
+    da_ref, db_ref, sum_ref, x2, d3, acc, back, held_w, sems = refs[9:]
     step = pl.program_id(0)
     R = xa_ref.shape[0]
     S, _, W = aa_ref.shape
 
+    def fetch(i):
+        return pltpu.make_async_copy(pieces[i], held_w.at[i % 2], sems.at[i % 2])
+
     @pl.when(step == 0)
     def _():
+        fetch(0).start()
         for rows, a_ref, x_ref, c_ref in (
             (slice(0, R), aa_ref, xa_ref, ca_ref),
             (slice(R, x2.shape[0]), ab_ref, xb_ref, cb_ref),
@@ -375,7 +365,17 @@
         acc[...] = jnp.zeros_like(acc)
         back[...] = jnp.zeros_like(back)
 
-    up = flat(up_ref)
+    for i in range(steps):
+
+        @pl.when(step == i)
+        def _():
+            fetch(i).wait()
+            if i + 1 < steps:
+                fetch(i + 1).start()
+
+    part = held_w.shape[1] // 2
+    up = held_w[step % 2, :part, :]
+    down = held_w[step % 2, part:, :]
     u = dot(n_ref[...], up, NT)
     slope = math.sqrt(2.0 / math.pi)
     square = u * u
@@ -383,10 +383,10 @@
     half = 0.5 * (1.0 + bend)
     g = (u * half).astype(bf16)
     rise = half + 0.5 * slope * u * (1.0 - bend * bend) * (1.0 + 0.134145 * square)
-    du = (dot(e3_ref[...], down_ref[...], NT) * rise).astype(bf16)
+    du = (dot(e3_ref[...], down, NT) * rise).astype(bf16)
     g_ref[...] = g
     du_ref[...] = du
-    acc[...] += dot(g, down_ref[...], NN)
+    acc[...] += dot(g, down, NN)
     back[...] += dot(du, up, NN)
 
     @pl.when(step == steps - 1)
@@ -406,19 +406,62 @@
             db_ref[i] = da[R:, i * W : (i + 1) * W]
 
 
-def feed_forward(a, x1, cot, d_pix, norm, w_out, w_dec, w_up, w_down, steps):
+def feed_forward(at, a, x1, cot, d_pix, norm, w_out, w_dec, pieces):
     S, R, W = a[0].shape
     RB = a[1].shape[1]
     D, total, pixels = S * W, R + RB, d_pix.shape[1]
-    hidden = w_down.shape[0]
-    part = hidden // steps
+    steps = len(pieces)
+    part = pieces[0].shape[0] // 2
+    hidden = steps * part
     row = jax.ShapeDtypeStruct((total, D), bf16)
     wide = jax.ShapeDtypeStruct((total, hidden), bf16)
-    blocked = pl.BlockSpec((total, part), lambda i: (0, i))
-    full = held((total, D))
+
+    def const(shape, index=None):
+        place = (0,) * len(shape) if index is None else index
+        return pl.BlockSpec(shape, lambda i, at: place, pipeline_mode=pl.Buffered(1))
+
+    def keep(shape):
+        return pl.BlockSpec(shape, lambda i, at: (0,) * len(shape))
+
+    blocked = pl.BlockSpec(
+        (total, part), lambda i, at: (0, (at[0] ^ (i // 2)) * 2 + (at[1] ^ (i % 2)))
+    )
+    full = keep((total, D))
     return pl.pallas_call(
         functools.partial(mlp_kernel, steps=steps),
-        grid=(steps,),
+        grid_spec=pltpu.PrefetchScalarGridSpec(
+            num_scalar_prefetch=1,
+            grid=(steps,),
+            in_specs=[
+                const((S, R, W)),
+                const((S, RB, W)),
+                const((R, D)),
+                const((RB, D)),
+                const((R, D)),
+                const((RB, D)),
+                const((total, pixels)),
+                const((2, D)),
+                const(*w_out[1]),
+                const(*w_dec[1]),
+            ]
+            + [AN] * steps,
+            out_specs=(
+                full,
+                full,
+                blocked,
+                blocked,
+                full,
+                keep((total, pixels)),
+                full,
+                full,
+                full,
+                keep((S, R, W)),
+                keep((S, RB, W)),
+                keep((2, D)),
+            ),
+            scratch_shapes=[pltpu.VMEM((total, D), f32)] * 4
+            + [pltpu.VMEM((2,) + pieces[0].shape, bf16), pltpu.SemaphoreType.DMA((2,))],
+        ),
         out_shape=(
             row,
             row,
@@ -433,42 +476,88 @@
             jax.ShapeDtypeStruct((S, RB, W), bf16),
             jax.ShapeDtypeStruct((2, D), f32),
         ),
-        in_specs=[
-            once((S, R, W)),
-            once((S, RB, W)),
-            once((R, D)),
-            once((RB, D)),
-            once((R, D)),
-            once((RB, D)),
-            once((total, pixels)),
-            once((2, D)),
-            w_out[1],
-            w_dec[1],
-            w_up[1],
-            pl.BlockSpec((part, D), lambda i: (i, 0)),
-        ],
-        out_specs=(
-            full,
-            full,
-            blocked,
-            blocked,
-            full,
-            held((total, pixels)),
-            full,
-            full,
-            full,
-            held((S, R, W)),
-            held((S, RB, W)),
-            held((2, D)),
-        ),
-        scratch_shapes=[pltpu.VMEM((total, D), f32)] * 4,
         compiler_params=pltpu.CompilerParams(vmem_limit_bytes=60 * 2**20),
         cost_estimate=pl.CostEstimate(
             flops=8 * total * D * hidden + 8 * total * D * D,
             bytes_accessed=4 * D * hidden + 30 * total * D,
             transcendentals=total * hidden,
         ),
-    )(*a, *x1, *cot, d_pix, norm, w_out[0], w_dec[0], w_up[0], w_down)
+    )(at, *a, *x1, *cot, d_pix, norm, w_out[0], w_dec[0], *pieces)
+
+
+def pack_kernel(at_ref, up_ref, down_ref, *refs):
+    out_ref = refs[-1]
+    half = out_ref.shape[0] // 2
+    odd = at_ref[0] == 1
+    up = jnp.where(odd, up_ref[:, half:], up_ref[:, :half])
+    out_ref[:half, :] = up.T
+    out_ref[half:, :] = down_ref[pl.ds(pl.multiple_of(at_ref[0] * half, 16), half), :]
+
+
+def pack(core, up, down, deps):
+    return pl.pallas_call(
+        pack_kernel,
+        out_shape=jax.ShapeDtypeStruct(down.shape, bf16),
+        in_specs=[SM, VM, VM] + [AN] * len(deps),
+        out_specs=VM,
+        compiler_params=pltpu.CompilerParams(vmem_limit_bytes=24 * 2**20),
+        cost_estimate=pl.CostEstimate(
+            flops=0, bytes_accessed=6 * down.size, transcendentals=0
+        ),
+    )(core.reshape(1), up, down, *deps)
+
+
+def hold_kernel(x_ref, *refs):
+    refs[-1][...] = x_ref[...]
+
+
+def hold(value, deps):
+    return pl.pallas_call(
+        hold_kernel,
+        out_shape=jax.ShapeDtypeStruct(value.shape, value.dtype),
+        in_specs=[VM] + [AN] * len(deps),
+        out_specs=VM,
+        cost_estimate=pl.CostEstimate(
+            flops=0, bytes_accessed=2 * value.size * value.dtype.itemsize, transcendentals=0
+        ),
+        compiler_params=pltpu.CompilerParams(vmem_limit_bytes=16 * 2**20),
+    )(value, *deps)
+
+
+def mlp_grads_kernel(at_ref, n_ref, e_ref, g_ref, du_ref, *refs, ranks, cores, shares):
+    more, (outs, n_t, e_t) = refs[: -ranks - 2], (refs[-ranks - 2 : -2], refs[-2], refs[-1])
+    odd = (at_ref[1] ^ cores) == 1
+    W = n_ref.shape[1] // shares
+    for src, dst in ((n_ref, n_t), (e_ref, e_t)):
+        for i in range(shares // 2):
+            both = src[:, 2 * i * W : (2 * i + 2) * W]
+            dst[i * W : (i + 1) * W, :] = jnp.where(odd, both[:, W:], both[:, :W]).T
+    part = g_ref.shape[1] // ranks
+    for step in range(ranks):
+        cols = pl.ds(pl.multiple_of((at_ref[0] ^ step) * part, 128), part)
+        up, down = dot(n_t[...], du_ref[:, cols], NN), dot(e_t[...], g_ref[:, cols], NN)
+        if more:
+            up += more[step][:, :part].astype(f32)
+            down += more[step][:, part:].astype(f32)
+        outs[step][:, :part] = up.astype(bf16)
+        outs[step][:, part:] = down.astype(bf16)
+
+
+def mlp_grads(at, n3, e3, g, du, ranks, shares, cores, more=()):
+    total, D = n3.shape
+    hidden = g.shape[1]
+    shape = (D // 2, 2 * hidden // ranks)
+    return pl.pallas_call(
+        functools.partial(mlp_grads_kernel, ranks=ranks, cores=cores, shares=shares),
+        out_shape=(jax.ShapeDtypeStruct(shape, bf16),) * ranks,
+        in_specs=[SM] + [VM] * (4 + len(more)),
+        out_specs=(VM,) * ranks,
+        scratch_shapes=[pltpu.VMEM((D // 2, total), bf16)] * 2,
+        compiler_params=pltpu.CompilerParams(vmem_limit_bytes=56 * 2**20),
+        cost_estimate=pl.CostEstimate(
+            flops=2 * total * D * hidden, bytes_accessed=4 * total * hidden + 2 * D * hidden, transcendentals=0
+        ),
+    )(at, n3, e3, g, du, *more)
 
 
 def back_kernel(
@@ -518,7 +607,7 @@
             once((rows, D)),
             once((rows, D), (at, 0)),
             once((2, D)),
-            w_out[1],
+            once(*w_out[1]),
             w_triple[1],
         ]
         + [AN] * len(deps),
@@ -584,53 +673,44 @@
     )(*lefts, *rights)
 
 
-def start_kernel(at_ref, xa_ref, xb_ref, norm_ref, *refs, pieces, weights, parts, rows):
-    w_in, refs = refs[:weights], refs[weights:]
-    p_in, kv_in, (q_ref, k_ref, n_ref, wq_ref) = refs[:pieces], refs[pieces:-4], refs[-4:]
-    seq, rank = at_ref[0], at_ref[1]
+def start_kernel(at_ref, xa_ref, xb_ref, norm_ref, wk_ref, wq_in, *refs, pieces, width):
+    p_in, (q_ref, k_ref, n_ref, wq_ref, wkv_ref) = refs[:pieces], refs[pieces:]
+    seq = at_ref[0]
     R = xa_ref.shape[0]
-    for i in range(weights):
-        for j in range(w_in[i].shape[0]):
-            at = 0 if weights == 1 else ((rank ^ j) * pieces + (seq ^ i)) * rows
-            wq_ref[pl.ds(pl.multiple_of(at, 16), w_in[i].shape[1]), :] = w_in[i][j]
+    W = q_ref.shape[2]
+    wq_ref[...] = flat(wq_in)
+    wkv_ref[...] = flat(wk_ref)[:, :width]
     for block, x_ref in ((slice(0, R), xa_ref), (slice(R, n_ref.shape[0]), xb_ref)):
         n_ref[block, :] = layer_norm(x_ref[...].astype(f32), norm_ref[0:1, :], norm_ref[1:2, :])
-    W = q_ref.shape[2]
     for i in range(pieces):
         q_ref[i] = dot(n_ref[...], wq_ref[i * W : (i + 1) * W, :], NT).astype(bf16)
-    w_kv = sum(v[...] for v in kv_in)
+    own = wkv_ref[pl.ds(pl.multiple_of(seq * 2 * W, 16), 2 * W), :]
     for i in range(pieces):
-        k_ref[seq ^ i] = dot(p_in[i][...], w_kv, NT).astype(bf16)
-
-
-def start(at, x0, norm, w_pieces, patch_pieces, kv_parts, W):
+        k_ref[seq ^ i] = dot(p_in[i][...], own, NT).astype(bf16)
+
+
+def start(at, x0, norm, w_kv, w_query, patch_pieces, W):
     S, D = len(patch_pieces), x0[0].shape[1]
     total = x0[0].shape[0] + x0[1].shape[0]
-    slots = patch_pieces[0].shape[0]
-    body = functools.partial(
-        start_kernel,
-        pieces=S,
-        weights=len(w_pieces),
-        parts=len(kv_parts),
-        rows=w_pieces[0].shape[1],
-    )
+    slots, width = patch_pieces[0].shape
+    whole = [x0[0].shape, x0[1].shape, norm.shape]
+    outs = [(S, total, W), (S, slots, 2 * W), (total, D), (D, D), (2 * D, width)]
     return pl.pallas_call(
-        body,
-        out_shape=(
-            jax.ShapeDtypeStruct((S, total, W), bf16),
-            jax.ShapeDtypeStruct((S, slots, 2 * W), bf16),
-            jax.ShapeDtypeStruct((total, D), bf16),
-            jax.ShapeDtypeStruct((D, D), bf16),
-        ),
-        in_specs=[SM] + [VM] * (3 + len(w_pieces) + S + len(kv_parts)),
-        out_specs=(VM,) * 4,
-        compiler_params=pltpu.CompilerParams(vmem_limit_bytes=44 * 2**20),
+        functools.partial(start_kernel, pieces=S, width=width),
+        grid=(1,),
+        out_shape=tuple(jax.ShapeDtypeStruct(v, bf16) for v in outs),
+        in_specs=[SM]
+        + [once(v) for v in whole]
+        + [once(*w_kv[1]), once(*w_query[1])]
+        + [once((slots, width))] * S,
+        out_specs=tuple(held(v) for v in outs),
+        compiler_params=pltpu.CompilerParams(vmem_limit_bytes=56 * 2**20),
         cost_estimate=pl.CostEstimate(
-            flops=2 * total * D * D + 4 * S * slots * 768 * W,
+            flops=2 * total * D * D + 4 * S * slots * width * W,
             bytes_accessed=6 * D * D + 12 * total * D,
             transcendentals=0,
         ),
-    )(at, *x0, norm, *w_pieces, *patch_pieces, *kv_parts)
+    )(at, *x0, norm, w_kv[0], w_query[0], *patch_pieces)
 
 
 def finish_kernel(at_ref, qa_ref, qb_ref, ka_ref, kb_ref, *refs, pieces):
@@ -750,17 +830,19 @@
     return lax.all_gather(piece, ("mp", "seq"), axis=0, tiled=False)
 
 
-def bundle_part(bundle, at, rows, per_step=None):
+def bundle_part(bundle, at, rows):
     pieces, _, D = bundle.shape
     if rows % 16 == 0 and at % rows == 0:
-        place = at // rows
-        if per_step is None:
-            return bundle, once((pieces, rows, D), (0, place, 0))
-        return bundle, pl.BlockSpec((per_step, rows, D), lambda i: (i, place, 0))
+        return bundle, ((pieces, rows, D), (0, at // rows, 0))
     value = bundle[:, at : at + rows].reshape(1, -1, D)
-    if per_step is None:
-        return value, once(value.shape)
-    return value, pl.BlockSpec((1, per_step * rows, D), lambda i: (0, i, 0))
+    return value, (value.shape, None)
+
+
+def by_step(part, steps):
+    (pieces, rows, D), at = part[1]
+    if pieces > 1:
+        return part[0], pl.BlockSpec((pieces // steps, rows, D), lambda i: (i, at[1], 0))
+    return part[0], pl.BlockSpec((1, rows // steps, D), lambda i: (0, i, 0))
 
 
 def reduce_rows(value):
@@ -871,50 +953,42 @@
     local_qkv = self_qkv.reshape(D, 3, 2, W).transpose(2, 1, 3, 0).reshape(-1, D)
     local_kv = cross_kv.reshape(width, 2, 2, W).transpose(2, 1, 3, 0).reshape(-1, width)
     per = D // (S * M)
-    up_rows = mlp_up.shape[1] // S
     dec_rows = 4 * CP // S
-    first = gather_rows(jnp.concatenate([mine(local_qkv, 0), mine(cross_out, 0)], axis=0))
-    w_triple = bundle_part(first, 0, 3 * per, M)
+    kv_rows = 2 * per
+    local_kv = jnp.pad(local_kv, ((0, 0), (0, D - width)))
+    lead = gather_rows(jnp.concatenate([mine(local_kv, 0), mine(cross_query, 1).T], axis=0))
+    w_kv, w_query = bundle_part(lead, 0, kv_rows), bundle_part(lead, kv_rows, per)
+    first = gather_rows(
+        jnp.concatenate(
+            [
+                mine(local_qkv, 0),
+                mine(cross_out, 0),
+                mine(self_out, 0),
+                mine(local_dec.reshape(-1, D), 0),
+            ],
+            axis=0,
+        )
+    )
+    w_triple = by_step(bundle_part(first, 0, 3 * per), S)
     w_cross_out = bundle_part(first, 3 * per, per)
-    second = gather_rows(
-        jnp.concatenate(
-            [mine(mlp_up, 1).T, mine(self_out, 0), mine(local_dec.reshape(-1, D), 0)], axis=0
-        )
-    )
-    steps = 8
-    w_up = bundle_part(second, 0, up_rows, S * M // steps)
-    w_self_out = bundle_part(second, up_rows, per)
-    w_dec = bundle_part(second, up_rows + per, dec_rows)
-    w_down = gather_rows(mine(mlp_down, 0)).reshape(-1, D)
-    w_kv = gather_rows(mine(local_kv, 0)).reshape(-1, width)
+    w_self_out = bundle_part(first, 4 * per, per)
+    w_dec = bundle_part(first, 5 * per, dec_rows)
 
     x0 = pick(tokens)
     norms = [jnp.stack([norm_gains[i], norm_shifts[i]]) for i in range(3)]
     at = jnp.stack([s, m])
     both = [lax.dynamic_index_in_dim(patches, o, 0, keepdims=False) for o in (at_a, at_b)]
     patch_pieces = gather_pieces(jnp.concatenate(both, axis=0))
-    piece = mine(cross_query, 1).T
-    ranks = [piece]
-    for step in range(1, M):
-        ranks.append(lax.ppermute(piece, "mp", [(i, i ^ step) for i in range(M)]))
-    w_pieces = gather_pieces(jnp.stack(ranks))
-    if per % 16 != 0:
-        w_pieces = jnp.stack(w_pieces)
-        w_pieces = [
-            lax.dynamic_index_in_dim(w_pieces, s ^ i, 0, keepdims=False) for i in range(S)
-        ]
-        w_pieces = jnp.stack(w_pieces, axis=1)
-        w_pieces = [
-            lax.dynamic_index_in_dim(w_pieces, m ^ i, 0, keepdims=False) for i in range(M)
-        ]
-        w_pieces = [jnp.stack(w_pieces).reshape(1, D, D)]
-    own_kv = lax.dynamic_slice_in_dim(local_kv, (s % 2) * 2 * W, 2 * W, 0)
-    kv_parts = [jnp.where(m == s // 2, own_kv, jnp.zeros_like(own_kv))]
-    for step in range(1, M):
-        moves = [(i * M + i // 2, i * M + ((i // 2) ^ step)) for i in range(S)]
-        kv_parts.append(lax.ppermute(own_kv, ("seq", "mp"), moves))
-    q1, keys_one, n1, w_query = start(at, x0, norms[0], w_pieces, patch_pieces, kv_parts, W)
+    q1, keys_one, n1, w_query, w_kv = start(at, x0, norms[0], w_kv, w_query, patch_pieces, W)
     heads_one = swap_seq(q1)
+    core = s % 2
+    cores = [(i, i ^ 1) for i in range(S)]
+    mlp = pack(core, mlp_up, mlp_down, [q1])
+    mlp_pieces = []
+    for step in range(M):
+        moves = [(i, i ^ step) for i in range(M)]
+        one = mlp if step == 0 else lax.ppermute(mlp, "mp", moves)
+        mlp_pieces += [one, lax.ppermute(one, "seq", cores)]
 
     TC = PLANE // 4
     TR = PLANE * 4 // S
@@ -990,15 +1064,23 @@
         row_total,
         hpd,
         True,
+        [o_a2],
     )
     a2 = [swap_seq(o_a2.reshape(S, R, W)), swap_seq(o_b2.reshape(S, RB, W))]
 
+    place = jnp.stack([m, core])
     n3, a2, g, du, x3b, pix, e3, d2, e2, da2_a, da2_b, sums_three = feed_forward(
-        a2, x1, pick(tokens_cot), d_pix, norms[2], w_self_out, w_dec, w_up, w_down, steps
+        place, a2, x1, pick(tokens_cot), d_pix, norms[2], w_self_out, w_dec, mlp_pieces
     )
 
     da2 = [swap_seq(da2_a), swap_seq(da2_b)]
-    grads_one = weight_grads([[(n3, du)], [(e3, g)], [(e2, a2)], [(x3b, d_pix)]], M)
+    given = mlp_grads(place, n3, e3, g, du, M, S, 1)
+    given = [lax.ppermute(v, "seq", cores) for v in given]
+    n1_late = hold(n1, da2)
+    sent = mlp_grads(place, n3, e3, g, du, M, S, 0, given)
+    by_rank = [sent[0]]
+    for step in range(1, M):
+        by_rank.append(lax.ppermute(sent[step], "mp", [(i, i ^ step) for i in range(M)]))
     dq_a2, dkv_a2 = attend_back(
         wide,
         [res_a2, da2[0], o_a2, heads_two[0]],
@@ -1008,10 +1090,11 @@
         row_total,
         hpd,
         True,
-        [grads_one],
-    )
+        [sent[0]],
+    )
+    grads_one = weight_grads([[(e2, a2)], [(x3b, d_pix)]], M)
     grads_one = reduce_rows(grads_one)
-    n_pieces = gather_pieces(n1)
+    n_pieces = gather_pieces(n1_late)
     tokens_out = own_blocks(x3b[:R], x3b[R:])
     pix = pix.reshape(KA + KB, S, M, cu).transpose(1, 2, 0, 3)
     got = swap_all(pix.reshape(S * M, KA + KB, cu)).reshape(S, pairs, 2, KA + KB, cu)
@@ -1052,7 +1135,15 @@
         return dq.reshape(S, rows[i], W), dkv.reshape(S, slots, 2 * W)
 
     low_a = below(0, [])
-    cross_a = cross_back(0, swap_seq(low_a[2]), [grads_one] + n_pieces[1::2])
+    mlp_sum = sum(v.astype(f32) for v in by_rank).astype(bf16).reshape(S // 2, D // S, -1)
+    cross_a = cross_back(0, swap_seq(low_a[2]), [grads_one, mlp_sum] + n_pieces[1::2])
+    by_chip = []
+    for step in range(0, S, 2):
+        block = lax.dynamic_index_in_dim(mlp_sum, (s ^ step) // 2, 0, keepdims=False)
+        if step > 0:
+            block = lax.ppermute(block, "seq", [(i, i ^ step) for i in range(S)])
+        by_chip.append(block)
+    mlp_sum = sum(v.astype(f32) for v in by_chip)
     low_b = below(1, [cross_a[0]])
     d1, e1, da1, sums_two = zip(low_a, low_b)
 
@@ -1114,9 +1205,9 @@
 
     grads_one, grads_two = sum_ranks(grads_one), sum_ranks(grads_two)
     ff = g.shape[1] // M
-    grad_mlp_up, grad_mlp_down = grads_one[:, :ff], grads_one[:, ff : 2 * ff].T
-    grad_self_out = grads_one[:, 2 * ff : 2 * ff + D // M].T
-    grad_decoder = grads_one[:, 2 * ff + D // M :]
+    grad_mlp_up, grad_mlp_down = mlp_sum[:, :ff], mlp_sum[:, ff:].T
+    grad_self_out = grads_one[:, : D // M].T
+    grad_decoder = grads_one[:, D // M :]
     grad_decoder = grad_decoder.reshape(D // S, 4, CP)[:, :, :channels].transpose(0, 2, 1)
     grad_self_qkv = grads_two[:, : 3 * D // M].reshape(D // S, 2, 3, W).transpose(0, 2, 1, 3)
     grad_cross_out = grads_two[:, 3 * D // M :].T

time: 1060 us -> 1170 us (1.10)
  waiting for transfers between devices: 283 us -> 359 us
  Pallas kernels: 374 us -> 398 us
  local copies, waits for them, and re-layouts: 111 us -> 87 us
  starting transfers between devices: 208 us -> 231 us
  blocking collectives: 0 us -> 12.3 us
    all_to_all x18 -> x17, waiting for transfers between devices: 120 us -> 58.1 us  [swap_seq(): return lax.all_to_all(value, 'seq', split_axis=0, concat_axis=0, tiled=True)]
    ppermute x6 -> x17, waiting for transfers between devices: 33.6 us -> 82.9 us  [the longest x3 82.8 us: per_device(): one = mlp if step == 0 else lax.ppermute(mlp, 'mp', moves)]
    all_gather x4 -> x2, waiting for transfers between devices: 0.04 us -> 44.3 us  [gather_rows(): return lax.all_gather(piece, ('mp', 'seq'), axis=0, tiled=False)]
    ppermute x2, starting transfers between devices: 2.76 us -> 44.8 us  [swap_pair(): return lax.ppermute(value, 'mp', [(i, i ^ 1) for i in range(count)])]
    pallas_call x2 -> x6, Pallas kernels: 45.2 us -> 78.5 us  [the longest x1 37.4 us: feed_forward(): pl.pallas_call(functools.partial(mlp_kernel, steps=steps), grid_spec=pltp...]
    ppermute x9 -> x6, waiting for transfers between devices: 0.18 us -> 31 us  [gather_pieces(): pieces.append(value if step == 0 else lax.ppermute(value, 'seq', moves))]
    ppermute x9, waiting for transfers between devices: 21.7 us -> 39 us  [from_ranks(): block = lax.ppermute(block, 'mp', [(i, i ^ step) for i in range(ranks)])]
    pallas_call x2, Pallas kernels: 35.8 us -> 19.2 us  [weight_grads(): pl.pallas_call(functools.partial(grads_kernel, shape=shape, widths=widths...]
  transfers between devices with their start and end apart: 90 -> 91, of which waited for: 30 -> 33; matrix products, arithmetic and copies ran while one was open for 9% -> 8% of each run, Pallas kernels for 30% -> 30%
where the time goes in v4:
time: 1170 us; the launch traced here: 1160 us
  Pallas kernels  398 us (34%)
  waiting for transfers between devices  359 us (31%)
  starting transfers between devices  231 us (20%)
  local copies, waits for them, and re-layouts  87 us (7%)
  other arithmetic  44.2 us (4%)
  between operations  16.6 us (1%)
  blocking collectives  12.3 us (1%)
    pallas_call x4, Pallas kernels, attend_back(): pl.pallas_call(body, out_shape=(jax.ShapeDtypeStruct((queries, hpd * HD),...  143 us
    pallas_call x4, Pallas kernels, attend(): pl.pallas_call(body, out_shape=(jax.ShapeDtypeStruct((queries, hpd * HD),...  83.4 us
    ppermute x3, waiting for transfers between devices, per_device(): one = mlp if step == 0 else lax.ppermute(mlp, 'mp', moves)  82.8 us
    all_to_all x17, starting transfers between devices, swap_seq(): return lax.all_to_all(value, 'seq', split_axis=0, concat_axis=0, tiled=True)  78.8 us
    all_to_all x17, waiting for transfers between devices, swap_seq(): return lax.all_to_all(value, 'seq', split_axis=0, concat_axis=0, tiled=True)  58.1 us
    unnamed x224, local copies, waits for them, and re-layouts  54.9 us
    ppermute x2, starting transfers between devices, swap_pair(): return lax.ppermute(value, 'mp', [(i, i ^ 1) for i in range(count)])  44.8 us
    all_gather x2, waiting for transfers between devices, gather_rows(): return lax.all_gather(piece, ('mp', 'seq'), axis=0, tiled=False)  44.3 us
  transfers between devices with their start and end apart: 91, of which 33 were waited for; matrix products, arithmetic and copies ran while one was open for 8% of the time, Pallas kernels for 30%

profile of v4, /device:TPU:0, one launch (start us, length us, event | category | flops | bytes accessed | tf_op | source)
XLA Modules:
  0.0 1157.3 jit_solution(4427899248098257191)
XLA Ops:
  22.7 13.4 %collective-permute-done.1.refs_2_.refs_10_ = bf16[384,768]{1,0:T(8,128)(2,1)S(1)} collective-permute-done((bf16[384,768]{1,0:T(8,128)(2,1)S(1)}, bf16[384,768]{1,0:T(8,128)(2,1)S(1)}, u32[]{:S(2)}, u32[]{:S(2)}) %collective-permute-start.1) | collective-permute-done | bytes 589856 | tf_op jit(solution)/shard_map/ppermute | solution.py:877
  36.0 14.5 %collective-permute-done.3.refs_4_.refs_12_ = bf16[384,768]{1,0:T(8,128)(2,1)S(1)} collective-permute-done((bf16[384,768]{1,0:T(8,128)(2,1)S(1)}, bf16[384,768]{1,0:T(8,128)(2,1)S(1)}, u32[]{:S(2)}, u32[]{:S(2)}) %collective-permute-start.3) | collective-permute-done | bytes 589856 | tf_op jit(solution)/shard_map/ppermute | solution.py:877
  61.9 28.1 %all-gather.5.cloned.1.call-done = bf16[3072,1024]{1,0:T(8,128)(2,1)} async-done(((bf16[96,1024]{1,0:T(8,128)(2,1)}), bf16[3072,1024]{1,0:T(8,128)(2,1)}) %all-gather.5.cloned.1.call-update) | async-done | bytes 6291472 | tf_op jit(solution)/shard_map/all_gather | solution.py:830
  90.0 11.8 %shard_map.280 = (bf16[8,576,128]{2,1,0:T(8,128)(2,1)}, bf16[8,384,256]{2,1,0:T(8,128)(2,1)}, bf16[576,1024]{1,0:T(8,128)(2,1)}, bf16[1024,1024]{1,0:T(8,128)(2,1)}, bf16[2048,768]{1,0:T(8,128)(2,1)}) custom-call(s32[2]{0:T(128)} %pad_add_fusion.3.at_ref, bf16[384,1024]{1,0:T(8,128)(2,1)} %get-tuple-element.200.xa_ref.x_ref, ...), custom_call_target="tpu_custom_call" | custom-call | flops 2415919104 | bytes 13369344 | tf_op jit(solution)/shard_map/pallas_call | solution.py:698
  107.6 14.9 %all-to-all-done.refs_0_ = bf16[8,576,128]{2,1,0:T(8,128)(2,1)S(1)} async-done(((bf16[8,576,128]{2,1,0:T(8,128)(2,1)}), bf16[8,576,128]{2,1,0:T(8,128)(2,1)S(1)}, u32[]{:S(2)}, u32[]{:S(2)}) %all-to-all-start) | async-done | bytes 1179680 | tf_op jit(solution)/shard_map/all_to_all | solution.py:813
  122.5 15.0 %shard_map.284 = (bf16[1536,128]{1,0:T(8,128)(2,1)}, bf16[2,1536,128]{2,1,0:T(8,128)(2,1)S(1)}) custom-call(s32[2]{0:T(128)S(1)} %get-tuple-element.249.n_ref, bf16[8,576,128]{2,1,0:T(8,128)(2,1)S(1)} %all-to-all-done.refs_0_, bf16[8,384,256]{2,1,0:T(8,128)(2,1)S(1)} %copy-done.69), custom_call_target="tpu_custom_call" | custom-call | flops 4831838208 | bytes 3145728 | tf_op jit(solution)/shard_map/pallas_call | solution.py:194
  142.4 20.0 %shard_map.281 = (bf16[3072,128]{1,0:T(8,128)(2,1)S(1)}, bf16[2,3072,128]{2,1,0:T(8,128)(2,1)S(1)}) custom-call(s32[2]{0:T(128)S(1)} %get-tuple-element.250.n_ref, bf16[8,576,128]{2,1,0:T(8,128)(2,1)S(1)} %all-to-all-done.refs_0_, bf16[8,384,256]{2,1,0:T(8,128)(2,1)S(1)} %copy-done.69), custom_call_target="tpu_custom_call" | custom-call | flops 9663676416 | bytes 6291456 | tf_op jit(solution)/shard_map/pallas_call | solution.py:194
  168.8 16.2 %all-gather.7.cloned.1.call-done = bf16[5632,1024]{1,0:T(8,128)(2,1)} async-done(((bf16[176,1024]{1,0:T(8,128)(2,1)}), bf16[5632,1024]{1,0:T(8,128)(2,1)}) %all-gather.7.cloned.1.call-update) | async-done | bytes 11534352 | tf_op jit(solution)/shard_map/all_gather | solution.py:830
  184.9 8.6 shard_map.285
  210.1 9.9 shard_map.282
  231.4 15.2 %shard_map.287 = f32[18,160,128]{2,1,0:T(8,128)S(1)} custom-call(bf16[18,32,256]{2,1,0:T(8,128)(2,1)S(1)} %pad.22.cot_ref, bf16[18,561,256]{2,1,0:T(8,128)(2,1)S(1)} %bitcast.224), custom_call_target="tpu_custom_call" | custom-call | flops 600000000 | bytes 7000000 | tf_op jit(solution)/shard_map/pallas_call | solution.py:798
  251.8 6.1 collective-permute-done.10
  264.0 34.2 %collective-permute-done.12.refs_2_ = bf16[1024,1024]{1,0:T(8,128)(2,1)} collective-permute-done((bf16[1024,1024]{1,0:T(8,128)(2,1)}, bf16[1024,1024]{1,0:T(8,128)(2,1)}, u32[]{:S(2)}, u32[]{:S(2)}) %collective-permute-start.12) | collective-permute-done | bytes 2097184 | tf_op jit(solution)/shard_map/ppermute | solution.py:990
  298.2 48.6 %collective-permute-done.14.refs_4_ = bf16[1024,1024]{1,0:T(8,128)(2,1)} collective-permute-done((bf16[1024,1024]{1,0:T(8,128)(2,1)}, bf16[1024,1024]{1,0:T(8,128)(2,1)}, u32[]{:S(2)}, u32[]{:S(2)}) %collective-permute-start.14) | collective-permute-done | bytes 2097184 | tf_op jit(solution)/shard_map/ppermute | solution.py:990
  347.4 44.2 %collective-permute-start.7 = (bf16[8,192,256]{2,1,0:T(8,128)(2,1)S(1)}, bf16[8,192,256]{2,1,0:T(8,128)(2,1)S(1)}, u32[]{:S(2)}, u32[]{:S(2)}) collective-permute-start(bf16[8,192,256]{2,1,0:T(8,128)(2,1)S(1)} %slice.178), channel_id=1, source_target_pairs={{0,1},{1,0},{2,3},{3,2},{4,5},{5,4},{6,7},{7,6},{8,9},{9,8},{10,11... | collective-permute-start | bytes 2359304 | tf_op jit(solution)/shard_map/ppermute | solution.py:826
  396.4 31.8 %shard_map.283 = (bf16[3072,128]{1,0:T(8,128)(2,1)}, bf16[2,3072,128]{2,1,0:T(8,128)(2,1)S(1)}) custom-call(s32[2]{0:T(128)S(1)} %copy-done.71, bf16[8,384,384]{2,1,0:T(8,128)(2,1)} %all-to-all-done.2.refs_0_.refs_3_), custom_call_target="tpu_custom_call" | custom-call | flops 19327352832 | bytes 6291456 | tf_op jit(solution)/shard_map/pallas_call | solution.py:194
  429.3 16.6 %shard_map.286 = (bf16[1536,128]{1,0:T(8,128)(2,1)S(1)}, bf16[2,1536,128]{2,1,0:T(8,128)(2,1)S(1)}) custom-call(s32[2]{0:T(128)S(1)} %copy-done.71, bf16[8,192,384]{2,1,0:T(8,128)(2,1)S(1)} %all-to-all-done.5.refs_0_.refs_3_, bf16[8,192,256]{2,1,0:T(8,128)(2,1)S(1)} %collective-permute-done.7.refs_1_.refs_4_, bf16[3072,128]{1,0:T(8,128)(2,1)} %get-tuple-element.76.refs_2_), custom_call_target="tpu_custom_call" | custom-call | flops 9663676416 | bytes 3145728 | tf_op jit(solution)/shard_map/pallas_call | solution.py:194
  446.0 12.3 %all_to_all.100.ab_ref = bf16[8,192,128]{2,1,0:T(8,128)(2,1)} all-to-all(bf16[8,192,128]{2,1,0:T(8,128)(2,1)S(1)} %bitcast.230), channel_id=1, replica_groups=mesh['seq'=8,'mp'=4] {'seq'}, dimensions={0} | all-to-all | bytes 786432 | tf_op jit(solution)/shard_map/all_to_all | solution.py:813
  475.5 37.4 %shard_map.289 = (bf16[576,1024]{1,0:T(8,128)(2,1)}, bf16[576,1024]{1,0:T(8,128)(2,1)}, bf16[576,4096]{1,0:T(8,128)(2,1)}, bf16[576,4096]{1,0:T(8,128)(2,1)}, bf...) custom-call(s32[2]{0:T(128)} %pad_add_fusion.2.at_ref, ...), custom_call_target="tpu_custom_call" | custom-call | flops 24159191040 | bytes 34471936 | tf_op jit(solution)/shard_map/pallas_call | solution.py:430
  512.9 12.5 %shard_map.291 = (bf16[512,2048]{1,0:T(8,128)(2,1)}, bf16[512,2048]{1,0:T(8,128)(2,1)}, bf16[512,2048]{1,0:T(8,128)(2,1)}, bf16[512,2048]{1,0:T(8,128)(2,1)}) custom-call(s32[2]{0:T(128)} %pad_add_fusion.2.at_ref, bf16[576,1024]{1,0:T(8,128)(2,1)} %get-tuple-element.86.n_ref, bf16[576,1024]{1,0:T(8,128)(2,1)} %get-tuple-element.87.e_ref, ...), custom_call_target="tpu_custom_call" | custom-call | flops 4831838208 | bytes 17825792 | tf_op jit(solution)/shard_map/pallas_call | solution.py:550
  535.9 8.7 collective-permute-done.19
  554.8 7.6 shard_map.295
  576.1 7.3 all-to-all-done.9.refs_1_.refs_0_
  591.7 14.9 %shard_map.292 = (bf16[512,2048]{1,0:T(8,128)(2,1)}, bf16[512,2048]{1,0:T(8,128)(2,1)}, bf16[512,2048]{1,0:T(8,128)(2,1)}, bf16[512,2048]{1,0:T(8,128)(2,1)}) custom-call(s32[2]{0:T(128)} %pad_add_fusion.2.at_ref, bf16[576,1024]{1,0:T(8,128)(2,1)} %get-tuple-element.86.n_ref, bf16[576,1024]{1,0:T(8,128)(2,1)} %get-tuple-element.87.e_ref, ...), custom_call_target="tpu_custom_call" | custom-call | flops 4831838208 | bytes 17825792 | tf_op jit(solution)/shard_map/pallas_call | solution.py:550
  610.9 60.9 %shard_map.293 = (bf16[3072,128]{1,0:T(8,128)(2,1)S(1)}, bf16[3072,256]{1,0:T(8,128)(2,1)}) custom-call(s32[2]{0:T(128)S(1)} %copy-done.71, bf16[2,3072,128]{2,1,0:T(8,128)(2,1)} %copy-done.75, bf16[8,384,128]{2,1,0:T(8,128)(2,1)S(1)} %all-to-all-done.9.refs_1_.refs_0_, bf16[3072,128]{1,0:T(8,128)(2,1)} %get-tuple-element.76.refs_2_, ...), custom_call_target="tpu_custom_call" | custom-call | flops 48318382080 | bytes 9437184 | tf_op jit(solution)/shard_map/pallas_call | solution.py:224
  683.5 34.3 %shard_map.298 = (bf16[1536,128]{1,0:T(8,128)(2,1)S(1)}, bf16[3072,256]{1,0:T(8,128)(2,1)}) custom-call(s32[2]{0:T(128)S(1)} %copy-done.71, bf16[2,1536,128]{2,1,0:T(8,128)(2,1)} %copy-done.74, bf16[8,192,128]{2,1,0:T(8,128)(2,1)S(1)} %copy-done.37, bf16[1536,128]{1,0:T(8,128)(2,1)S(1)} %copy-done.55, bf16[8,192,384]{2,1,0:T(8,128)(2,1)} %copy-done.17, ...), custom_call_target="tpu_custom_call" | custom-call | flops 24159191040 | bytes 4718592 | tf_op jit(solution)/shard_map/pallas_call | solution.py:224
  719.9 43.0 %collective-permute-done.43 = bf16[1536,256]{1,0:T(8,128)(2,1)S(1)} collective-permute-done((bf16[1536,256]{1,0:T(8,128)(2,1)S(1)}, bf16[1536,256]{1,0:T(8,128)(2,1)S(1)}, u32[]{:S(2)}, u32[]{:S(2)}) %collective-permute-start.43) | collective-permute-done | bytes 786464 | tf_op jit(solution)/shard_map/ppermute | solution.py:826
  770.1 11.1 shard_map.294
  787.9 6.8 add_convert_fusion
  806.7 26.9 %shard_map.297 = (bf16[3072,128]{1,0:T(8,128)(2,1)}, bf16[1536,256]{1,0:T(8,128)(2,1)}) custom-call(s32[2]{0:T(128)S(1)} %copy-done.68, bf16[2,3072,128]{2,1,0:T(8,128)(2,1)} %copy-done.73, bf16[8,384,128]{2,1,0:T(8,128)(2,1)} %copy-done.83, bf16[3072,128]{1,0:T(8,128)(2,1)} %copy-done.45, bf16[8,384,256]{2,1,0:T(8,128)(2,1)} %get-tuple-element.73.refs_1_.refs_3_, ...), custom_call_target="tpu_custom_call" | custom-call | flops 24159191040 | bytes 9437184 | tf_op jit(solution)/shard_map/pallas_call | solution.py:224
  835.1 9.8 shard_map.299
  847.1 11.6 %shard_map.300.refs_4_ = bf16[1024,4096]{1,0:T(8,128)(2,1)} custom-call(bf16[384,1024]{1,0:T(8,128)(2,1)} %copy-done.51, bf16[192,1024]{1,0:T(8,128)(2,1)} %copy-done.57, bf16[384,1024]{1,0:T(8,128)(2,1)} %copy-done.53, bf16[192,1024]{1,0:T(8,128)(2,1)} %copy-done.59, bf16[8,384,384]{2,1,0:T(8,128)(2,1)} %copy-done.2, bf16[8,192,384]{2,1,0:T(8,128)(2,1)} %copy-done.7, ...), custom_call_target="tpu_custom_call" | custom-call | flops 2415919104 | bytes 16777216 | tf_op jit(solution)/shard_map/pallas_call | solution.py:656
  870.6 8.8 collective-permute-done.25
  880.6 10.7 collective-permute-done.24
  894.6 11.7 %shard_map.290 = bf16[18,32,256]{2,1,0:T(8,128)(2,1)S(1)} custom-call(bf16[18,160,128]{2,1,0:T(8,128)(2,1)S(1)} %concatenate.44.x_ref, bf16[18,561,256]{2,1,0:T(8,128)(2,1)S(1)} %bitcast.225), custom_call_target="tpu_custom_call" | custom-call | flops 600000000 | bytes 7000000 | tf_op jit(solution)/shard_map/pallas_call | solution.py:798
  907.0 11.7 %all-to-all-start.15 = ((bf16[8,192,128]{2,1,0:T(8,128)(2,1)}), bf16[8,192,128]{2,1,0:T(8,128)(2,1)S(1)}, u32[]{:S(2)}, u32[]{:S(2)}) async-start(bf16[8,192,128]{2,1,0:T(8,128)(2,1)} %get-tuple-element.115), calls=%async_computation.16 | async-start | bytes 786432 | tf_op jit(solution)/shard_map/all_to_all | solution.py:813
  921.1 10.2 all-to-all-done.15.refs_1_
  931.3 20.4 %shard_map.301 = (bf16[1536,128]{1,0:T(8,128)(2,1)}, bf16[1536,256]{1,0:T(8,128)(2,1)}) custom-call(s32[2]{0:T(128)S(1)} %copy-done.66, bf16[2,1536,128]{2,1,0:T(8,128)(2,1)} %copy-done.72, bf16[8,192,128]{2,1,0:T(8,128)(2,1)S(1)} %all-to-all-done.15.refs_1_, bf16[1536,128]{1,0:T(8,128)(2,1)} %get-tuple-element.77.refs_2_, ...), custom_call_target="tpu_custom_call" | custom-call | flops 12079595520 | bytes 4718592 | tf_op jit(solution)/shard_map/pallas_call | solution.py:224
  951.8 8.2 shard_map.302
  962.9 6.5 all-to-all-start.17
  972.8 15.8 %collective-permute-start.60 = (bf16[320,128]{1,0:T(8,128)(2,1)S(1)}, bf16[320,128]{1,0:T(8,128)(2,1)S(1)}, u32[]{:S(2)}, u32[]{:S(2)}) collective-permute-start(bf16[320,128]{1,0:T(8,128)(2,1)S(1)} %copy-done.92), channel_id=1, source_target_pairs={{1,0},{9,1},{17,2},{25,3},{5,4},{13,5},{21,6},{29,7},{0,8},{8,9},{... | collective-permute-start | bytes 245768 | tf_op jit(solution)/shard_map/ppermute | solution.py:1198
  993.0 7.3 collective-permute-done.60
  1003.9 6.5 all-to-all-start.13
  1014.7 8.3 all-to-all-done.13
  1066.0 21.6 %collective-permute-done.41 = bf16[96,1024]{1,0:T(8,128)(2,1)S(1)} collective-permute-done((bf16[96,1024]{1,0:T(8,128)(2,1)S(1)}, bf16[96,1024]{1,0:T(8,128)(2,1)S(1)}, u32[]{:S(2)}, u32[]{:S(2)}) %collective-permute-start.41) | collective-permute-done | bytes 196640 | tf_op jit(solution)/shard_map/ppermute | solution.py:858
  1088.3 11.8 %collective-permute-start.45 = (bf16[96,1024]{1,0:T(8,128)(2,1)S(1)}, bf16[96,1024]{1,0:T(8,128)(2,1)S(1)}, u32[]{:S(2)}, u32[]{:S(2)}) collective-permute-start(bf16[96,1024]{1,0:T(8,128)(2,1)S(1)} %get-tuple-element.229), channel_id=1, source_target_pairs={{0,1},{1,3},{2,0},{3,2},{4,5},{5,7},{6,4},{7,6},{8,9},{9,11},{10,8... | collective-permute-start | bytes 589832 | tf_op jit(solution)/shard_map/ppermute | solution.py:893
  1101.0 12.9 %collective-permute-done.45 = bf16[96,1024]{1,0:T(8,128)(2,1)S(1)} collective-permute-done((bf16[96,1024]{1,0:T(8,128)(2,1)S(1)}, bf16[96,1024]{1,0:T(8,128)(2,1)S(1)}, u32[]{:S(2)}, u32[]{:S(2)}) %collective-permute-start.45) | collective-permute-done | bytes 196640 | tf_op jit(solution)/shard_map/ppermute | solution.py:893
  1131.8 10.7 collective-permute-done.50
  (520 shorter events, 303.5 us)
Async XLA Ops:
  7.2 82.8 %all-gather.5.cloned.1.call-start = ((), (), s32[]{:S(2)}) async-start(), calls=%async_computation.27 | async-start | bytes 6488064 | tf_op jit(solution)/shard_map/all_gather | solution.py:830
  12.7 172.2 %all-gather.7.cloned.1.call-start = ((), (), s32[]{:S(2)}) async-start(), calls=%async_computation.28 | async-start | bytes 11894784 | tf_op jit(solution)/shard_map/all_gather | solution.py:830
  20.5 30.1 %collective-permute-start.3 = (bf16[384,768]{1,0:T(8,128)(2,1)S(1)}, bf16[384,768]{1,0:T(8,128)(2,1)S(1)}, u32[]{:S(2)}, u32[]{:S(2)}) collective-permute-start(bf16[384,768]{1,0:T(8,128)(2,1)S(1)} %pad_maximum_fusion.6.refs_0_.refs_8_), channel_id=1, source_target_pairs={{0,16},{4,20},{8,24},{12,28},{16,0},{20,4},{24,8},{28,12},{1,17},{... | collective-permute-start | bytes 1769480 | tf_op jit(solution)/shard_map/ppermute | solution.py:877
  22.0 31.6 %collective-permute-start.5 = (bf16[384,768]{1,0:T(8,128)(2,1)S(1)}, bf16[384,768]{1,0:T(8,128)(2,1)S(1)}, u32[]{:S(2)}, u32[]{:S(2)}) collective-permute-start(bf16[384,768]{1,0:T(8,128)(2,1)S(1)} %pad_maximum_fusion.6.refs_0_.refs_8_), channel_id=1, source_target_pairs={{0,24},{4,28},{8,16},{12,20},{16,8},{20,12},{24,0},{28,4},{1,25},{... | collective-permute-start | bytes 1769480 | tf_op jit(solution)/shard_map/ppermute | solution.py:877
  22.0 39.0 %collective-permute-start = (bf16[384,768]{1,0:T(8,128)(2,1)S(1)}, bf16[384,768]{1,0:T(8,128)(2,1)S(1)}, u32[]{:S(2)}, u32[]{:S(2)}) collective-permute-start(bf16[384,768]{1,0:T(8,128)(2,1)S(1)} %pad_maximum_fusion.6.refs_0_.refs_8_), channel_id=1, source_target_pairs={{0,4},{4,0},{8,12},{12,8},{16,20},{20,16},{24,28},{28,24},{1,5},{5... | collective-permute-start | bytes 1769480 | tf_op jit(solution)/shard_map/ppermute | solution.py:879
  164.5 32.5 %all-to-all-start.1 = ((bf16[8,384,128]{2,1,0:T(8,128)(2,1)}), bf16[8,384,128]{2,1,0:T(8,128)(2,1)S(1)}, u32[]{:S(2)}, u32[]{:S(2)}) async-start(bf16[8,384,128]{2,1,0:T(8,128)(2,1)} %bitcast.229), calls=%async_computation.1 | async-start | bytes 1572864 | tf_op jit(solution)/shard_map/all_to_all | solution.py:813
  205.7 92.5 %collective-permute-start.12 = (bf16[1024,1024]{1,0:T(8,128)(2,1)}, bf16[1024,1024]{1,0:T(8,128)(2,1)}, u32[]{:S(2)}, u32[]{:S(2)}) collective-permute-start(bf16[1024,1024]{1,0:T(8,128)(2,1)} %shard_map.288.refs_0_), channel_id=1, source_target_pairs={{0,1},{1,0},{2,3},{3,2},{4,5},{5,4},{6,7},{7,6},{8,9},{9,8},{10,11... | collective-permute-start | bytes 6291464 | tf_op jit(solution)/shard_map/ppermute | solution.py:990
  207.2 139.6 %collective-permute-start.14 = (bf16[1024,1024]{1,0:T(8,128)(2,1)}, bf16[1024,1024]{1,0:T(8,128)(2,1)}, u32[]{:S(2)}, u32[]{:S(2)}) collective-permute-start(bf16[1024,1024]{1,0:T(8,128)(2,1)} %shard_map.288.refs_0_), channel_id=1, source_target_pairs={{0,2},{1,3},{2,0},{3,1},{4,6},{5,7},{6,4},{7,5},{8,10},{9,11},{10,... | collective-permute-start | bytes 6291464 | tf_op jit(solution)/shard_map/ppermute | solution.py:990
  209.5 137.3 %collective-permute-start.16 = (bf16[1024,1024]{1,0:T(8,128)(2,1)}, bf16[1024,1024]{1,0:T(8,128)(2,1)}, u32[]{:S(2)}, u32[]{:S(2)}) collective-permute-start(bf16[1024,1024]{1,0:T(8,128)(2,1)} %shard_map.288.refs_0_), channel_id=1, source_target_pairs={{0,3},{1,2},{2,1},{3,0},{4,7},{5,6},{6,5},{7,4},{8,11},{9,10},{10,... | collective-permute-start | bytes 6291464 | tf_op jit(solution)/shard_map/ppermute | solution.py:990
  224.4 167.2 %all-to-all-start.2 = ((bf16[8,384,384]{2,1,0:T(8,128)(2,1)}), bf16[8,384,384]{2,1,0:T(8,128)(2,1)}, u32[]{:S(2)}, u32[]{:S(2)}) async-start(bf16[8,384,384]{2,1,0:T(8,128)(2,1)} %copy-done.30), calls=%async_computation.2 | async-start | bytes 4718592 | tf_op jit(solution)/shard_map/all_to_all | solution.py:813
  261.8 207.6 %collective-permute-start.11 = (bf16[1024,1024]{1,0:T(8,128)(2,1)}, bf16[1024,1024]{1,0:T(8,128)(2,1)}, u32[]{:S(2)}, u32[]{:S(2)}) collective-permute-start(bf16[1024,1024]{1,0:T(8,128)(2,1)} %shard_map.288.refs_0_), channel_id=1, source_target_pairs={{0,4},{4,0},{8,12},{12,8},{16,20},{20,16},{24,28},{28,24},{1,5},{5... | collective-permute-start | bytes 6291464 | tf_op jit(solution)/shard_map/ppermute | solution.py:991
  298.2 171.2 %collective-permute-start.13 = (bf16[1024,1024]{1,0:T(8,128)(2,1)}, bf16[1024,1024]{1,0:T(8,128)(2,1)}, u32[]{:S(2)}, u32[]{:S(2)}) collective-permute-start(bf16[1024,1024]{1,0:T(8,128)(2,1)} %collective-permute-done.12.refs_2_), channel_id=1, source_target_pairs={{0,4},{4,0},{8,12},{12,8},{16,20},{20,16},{24,28},{28,24},{1,5},{5... | collective-permute-start | bytes 6291464 | tf_op jit(solution)/shard_map/ppermute | solution.py:991
  346.8 122.5 %collective-permute-start.15 = (bf16[1024,1024]{1,0:T(8,128)(2,1)}, bf16[1024,1024]{1,0:T(8,128)(2,1)}, u32[]{:S(2)}, u32[]{:S(2)}) collective-permute-start(bf16[1024,1024]{1,0:T(8,128)(2,1)} %collective-permute-done.14.refs_4_), channel_id=1, source_target_pairs={{0,4},{4,0},{8,12},{12,8},{16,20},{20,16},{24,28},{28,24},{1,5},{5... | collective-permute-start | bytes 6291464 | tf_op jit(solution)/shard_map/ppermute | solution.py:991
  346.8 122.5 %collective-permute-start.17 = (bf16[1024,1024]{1,0:T(8,128)(2,1)}, bf16[1024,1024]{1,0:T(8,128)(2,1)}, u32[]{:S(2)}, u32[]{:S(2)}) collective-permute-start(bf16[1024,1024]{1,0:T(8,128)(2,1)} %collective-permute-done.16.refs_6_), channel_id=1, source_target_pairs={{0,4},{4,0},{8,12},{12,8},{16,20},{20,16},{24,28},{28,24},{1,5},{5... | collective-permute-start | bytes 6291464 | tf_op jit(solution)/shard_map/ppermute | solution.py:991
  347.4 81.9 %collective-permute-start.7 = (bf16[8,192,256]{2,1,0:T(8,128)(2,1)S(1)}, bf16[8,192,256]{2,1,0:T(8,128)(2,1)S(1)}, u32[]{:S(2)}, u32[]{:S(2)}) collective-permute-start(bf16[8,192,256]{2,1,0:T(8,128)(2,1)S(1)} %slice.178), channel_id=1, source_target_pairs={{0,1},{1,0},{2,3},{3,2},{4,5},{5,4},{6,7},{7,6},{8,9},{9,8},{10,11... | collective-permute-start | bytes 2359304 | tf_op jit(solution)/shard_map/ppermute | solution.py:826
  391.6 54.4 %all-to-all-start.7 = ((bf16[32,72,128]{2,1,0:T(8,128)(2,1)}), bf16[32,72,128]{2,1,0:T(8,128)(2,1)}, u32[]{:S(2)}, u32[]{:S(2)}) async-start(bf16[32,72,128]{2,1,0:T(8,128)(2,1)} %bitcast.31), calls=%async_computation.7 | async-start | bytes 1179648 | tf_op jit(solution)/shard_map/all_to_all | solution.py:821
  525.4 64.7 %collective-permute-start.26 = (bf16[512,2048]{1,0:T(8,128)(2,1)}, bf16[512,2048]{1,0:T(8,128)(2,1)}, u32[]{:S(2)}, u32[]{:S(2)}) collective-permute-start(bf16[512,2048]{1,0:T(8,128)(2,1)} %get-tuple-element.90), channel_id=1, source_target_pairs={{0,4},{4,0},{8,12},{12,8},{16,20},{20,16},{24,28},{28,24},{1,5},{5... | collective-permute-start | bytes 6291464 | tf_op jit(solution)/shard_map/ppermute | solution.py:1078
  525.4 66.1 %collective-permute-start.27 = (bf16[512,2048]{1,0:T(8,128)(2,1)}, bf16[512,2048]{1,0:T(8,128)(2,1)}, u32[]{:S(2)}, u32[]{:S(2)}) collective-permute-start(bf16[512,2048]{1,0:T(8,128)(2,1)} %get-tuple-element.91), channel_id=1, source_target_pairs={{0,4},{4,0},{8,12},{12,8},{16,20},{20,16},{24,28},{28,24},{1,5},{5... | collective-permute-start | bytes 6291464 | tf_op jit(solution)/shard_map/ppermute | solution.py:1078
  526.0 65.8 %collective-permute-start.28 = (bf16[512,2048]{1,0:T(8,128)(2,1)}, bf16[512,2048]{1,0:T(8,128)(2,1)}, u32[]{:S(2)}, u32[]{:S(2)}) collective-permute-start(bf16[512,2048]{1,0:T(8,128)(2,1)} %get-tuple-element.92), channel_id=1, source_target_pairs={{0,4},{4,0},{8,12},{12,8},{16,20},{20,16},{24,28},{28,24},{1,5},{5... | collective-permute-start | bytes 6291464 | tf_op jit(solution)/shard_map/ppermute | solution.py:1078
  526.0 65.8 %collective-permute-start.29 = (bf16[512,2048]{1,0:T(8,128)(2,1)}, bf16[512,2048]{1,0:T(8,128)(2,1)}, u32[]{:S(2)}, u32[]{:S(2)}) collective-permute-start(bf16[512,2048]{1,0:T(8,128)(2,1)} %get-tuple-element.93), channel_id=1, source_target_pairs={{0,4},{4,0},{8,12},{12,8},{16,20},{20,16},{24,28},{28,24},{1,5},{5... | collective-permute-start | bytes 6291464 | tf_op jit(solution)/shard_map/ppermute | solution.py:1078
  551.3 243.4 %reduce-scatter.7.cloned.1.call-start = ((), (), s32[]{:S(2)}) async-start(), calls=%async_computation.24 | async-start | bytes 3538944 | tf_op jit(solution)/shard_map/reduce_scatter | solution.py:849
  583.3 92.0 %all-to-all-start.8 = ((bf16[32,72,128]{2,1,0:T(8,128)(2,1)}), bf16[32,72,128]{2,1,0:T(8,128)(2,1)S(1)}, u32[]{:S(2)}, u32[]{:S(2)}) async-start(bf16[32,72,128]{2,1,0:T(8,128)(2,1)} %bitcast.49), calls=%async_computation.8 | async-start | bytes 1179648 | tf_op jit(solution)/shard_map/all_to_all | solution.py:821
  588.2 87.1 %collective-permute-start.34 = (bf16[576,1024]{1,0:T(8,128)(2,1)S(1)}, bf16[576,1024]{1,0:T(8,128)(2,1)}, u32[]{:S(2)}, u32[]{:S(2)}) collective-permute-start(bf16[576,1024]{1,0:T(8,128)(2,1)S(1)} %shard_map.296.refs_8_.refs_0_), channel_id=1, source_target_pairs={{0,8},{4,12},{8,0},{12,4},{16,24},{20,28},{24,16},{28,20},{1,9},{5... | collective-permute-start | bytes 3538952 | tf_op jit(solution)/shard_map/ppermute | solution.py:877
  590.1 90.3 %collective-permute-start.36 = (bf16[576,1024]{1,0:T(8,128)(2,1)S(1)}, bf16[576,1024]{1,0:T(8,128)(2,1)}, u32[]{:S(2)}, u32[]{:S(2)}) collective-permute-start(bf16[576,1024]{1,0:T(8,128)(2,1)S(1)} %shard_map.296.refs_8_.refs_0_), channel_id=1, source_target_pairs={{0,16},{4,20},{8,24},{12,28},{16,0},{20,4},{24,8},{28,12},{1,17},{... | collective-permute-start | bytes 3538952 | tf_op jit(solution)/shard_map/ppermute | solution.py:877
  591.6 88.8 %collective-permute-start.38 = (bf16[576,1024]{1,0:T(8,128)(2,1)S(1)}, bf16[576,1024]{1,0:T(8,128)(2,1)}, u32[]{:S(2)}, u32[]{:S(2)}) collective-permute-start(bf16[576,1024]{1,0:T(8,128)(2,1)S(1)} %shard_map.296.refs_8_.refs_0_), channel_id=1, source_target_pairs={{0,24},{4,28},{8,16},{12,20},{16,8},{20,12},{24,0},{28,4},{1,25},{... | collective-permute-start | bytes 3538952 | tf_op jit(solution)/shard_map/ppermute | solution.py:877
  606.6 157.8 %collective-permute-start.30 = (bf16[512,2048]{1,0:T(8,128)(2,1)}, bf16[512,2048]{1,0:T(8,128)(2,1)}, u32[]{:S(2)}, u32[]{:S(2)}) collective-permute-start(bf16[512,2048]{1,0:T(8,128)(2,1)} %get-tuple-element.103), channel_id=1, source_target_pairs={{0,1},{1,0},{2,3},{3,2},{4,5},{5,4},{6,7},{7,6},{8,9},{9,8},{10,11... | collective-permute-start | bytes 6291464 | tf_op jit(solution)/shard_map/ppermute | solution.py:1083
  608.5 156.4 %collective-permute-start.31 = (bf16[512,2048]{1,0:T(8,128)(2,1)}, bf16[512,2048]{1,0:T(8,128)(2,1)}, u32[]{:S(2)}, u32[]{:S(2)}) collective-permute-start(bf16[512,2048]{1,0:T(8,128)(2,1)} %get-tuple-element.104), channel_id=1, source_target_pairs={{0,2},{1,3},{2,0},{3,1},{4,6},{5,7},{6,4},{7,5},{8,10},{9,11},{10,... | collective-permute-start | bytes 6291464 | tf_op jit(solution)/shard_map/ppermute | solution.py:1083
  675.2 112.7 %collective-permute-start.32 = (bf16[512,2048]{1,0:T(8,128)(2,1)}, bf16[512,2048]{1,0:T(8,128)(2,1)}, u32[]{:S(2)}, u32[]{:S(2)}) collective-permute-start(bf16[512,2048]{1,0:T(8,128)(2,1)} %get-tuple-element.105), channel_id=1, source_target_pairs={{0,3},{1,2},{2,1},{3,0},{4,7},{5,6},{6,5},{7,4},{8,11},{9,10},{10,... | collective-permute-start | bytes 6291464 | tf_op jit(solution)/shard_map/ppermute | solution.py:1083
  676.1 90.1 %all-to-all-start.10 = ((bf16[8,384,384]{2,1,0:T(8,128)(2,1)}), bf16[8,384,384]{2,1,0:T(8,128)(2,1)S(1)}, u32[]{:S(2)}, u32[]{:S(2)}) async-start(bf16[8,384,384]{2,1,0:T(8,128)(2,1)} %bitcast.243), calls=%async_computation.10 | async-start | bytes 4718592 | tf_op jit(solution)/shard_map/all_to_all | solution.py:813
  719.1 43.8 %collective-permute-start.43 = (bf16[1536,256]{1,0:T(8,128)(2,1)S(1)}, bf16[1536,256]{1,0:T(8,128)(2,1)S(1)}, u32[]{:S(2)}, u32[]{:S(2)}) collective-permute-start(bf16[1536,256]{1,0:T(8,128)(2,1)S(1)} %slice.161), channel_id=1, source_target_pairs={{0,1},{1,0},{2,3},{3,2},{4,5},{5,4},{6,7},{7,6},{8,9},{9,8},{10,11... | collective-permute-start | bytes 2359304 | tf_op jit(solution)/shard_map/ppermute | solution.py:826
  719.7 85.3 %collective-permute-start.33 = (bf16[576,1024]{1,0:T(8,128)(2,1)S(1)}, bf16[576,1024]{1,0:T(8,128)(2,1)}, u32[]{:S(2)}, u32[]{:S(2)}) collective-permute-start(bf16[576,1024]{1,0:T(8,128)(2,1)S(1)} %copy-done.15), channel_id=1, source_target_pairs={{0,4},{4,0},{8,12},{12,8},{16,20},{20,16},{24,28},{28,24},{1,5},{5... | collective-permute-start | bytes 3538952 | tf_op jit(solution)/shard_map/ppermute | solution.py:879
  762.9 42.1 %collective-permute-start.35 = (bf16[576,1024]{1,0:T(8,128)(2,1)}, bf16[576,1024]{1,0:T(8,128)(2,1)}, u32[]{:S(2)}, u32[]{:S(2)}) collective-permute-start(bf16[576,1024]{1,0:T(8,128)(2,1)} %collective-permute-done.34.refs_9_.refs_2_), channel_id=1, source_target_pairs={{0,4},{4,0},{8,12},{12,8},{16,20},{20,16},{24,28},{28,24},{1,5},{5... | collective-permute-start | bytes 3538952 | tf_op jit(solution)/shard_map/ppermute | solution.py:879
  764.4 40.6 %collective-permute-start.37 = (bf16[576,1024]{1,0:T(8,128)(2,1)}, bf16[576,1024]{1,0:T(8,128)(2,1)}, u32[]{:S(2)}, u32[]{:S(2)}) collective-permute-start(bf16[576,1024]{1,0:T(8,128)(2,1)} %collective-permute-done.36.refs_10_.refs_4_), channel_id=1, source_target_pairs={{0,4},{4,0},{8,12},{12,8},{16,20},{20,16},{24,28},{28,24},{1,5},{5... | collective-permute-start | bytes 3538952 | tf_op jit(solution)/shard_map/ppermute | solution.py:879
  764.9 40.1 %collective-permute-start.39 = (bf16[576,1024]{1,0:T(8,128)(2,1)}, bf16[576,1024]{1,0:T(8,128)(2,1)}, u32[]{:S(2)}, u32[]{:S(2)}) collective-permute-start(bf16[576,1024]{1,0:T(8,128)(2,1)} %collective-permute-done.38.refs_11_.refs_6_), channel_id=1, source_target_pairs={{0,4},{4,0},{8,12},{12,8},{16,20},{20,16},{24,28},{28,24},{1,5},{5... | collective-permute-start | bytes 3538952 | tf_op jit(solution)/shard_map/ppermute | solution.py:879
  787.9 215.1 %reduce-scatter.13.cloned.1.call-start = ((), (), s32[]{:S(2)}) async-start(), calls=%async_computation.29 | async-start | bytes 491520
  801.4 32.2 %all-to-all-start.14 = ((bf16[8,192,384]{2,1,0:T(8,128)(2,1)}), bf16[8,192,384]{2,1,0:T(8,128)(2,1)S(1)}, u32[]{:S(2)}, u32[]{:S(2)}) async-start(bf16[8,192,384]{2,1,0:T(8,128)(2,1)} %bitcast.76), calls=%async_computation.15 | async-start | bytes 2359296 | tf_op jit(solution)/shard_map/all_to_all | solution.py:813
  804.9 258.1 %reduce-scatter.9.cloned.1.call-start = ((), (), s32[]{:S(2)}) async-start(), calls=%async_computation.25 | async-start | bytes 9437184 | tf_op jit(solution)/shard_map/reduce_scatter | solution.py:849
  864.3 54.4 %collective-permute-start.63 = (bf16[128,2048]{1,0:T(8,128)(2,1)}, bf16[128,2048]{1,0:T(8,128)(2,1)}, u32[]{:S(2)}, u32[]{:S(2)}) collective-permute-start(bf16[128,2048]{1,0:T(8,128)(2,1)} %get-tuple-element.201), channel_id=1, source_target_pairs={{0,8},{4,12},{8,0},{12,4},{16,24},{20,28},{24,16},{28,20},{1,9},{5... | collective-permute-start | bytes 1572872 | tf_op jit(solution)/shard_map/ppermute | solution.py:1144
  866.2 52.5 %collective-permute-start.64 = (bf16[128,2048]{1,0:T(8,128)(2,1)}, bf16[128,2048]{1,0:T(8,128)(2,1)}, u32[]{:S(2)}, u32[]{:S(2)}) collective-permute-start(bf16[128,2048]{1,0:T(8,128)(2,1)} %get-tuple-element.203), channel_id=1, source_target_pairs={{0,16},{4,20},{8,24},{12,28},{16,0},{20,4},{24,8},{28,12},{1,17},{... | collective-permute-start | bytes 1572872 | tf_op jit(solution)/shard_map/ppermute | solution.py:1144
  867.7 51.0 %collective-permute-start.65 = (bf16[128,2048]{1,0:T(8,128)(2,1)S(1)}, bf16[128,2048]{1,0:T(8,128)(2,1)}, u32[]{:S(2)}, u32[]{:S(2)}) collective-permute-start(bf16[128,2048]{1,0:T(8,128)(2,1)S(1)} %get-tuple-element.202), channel_id=1, source_target_pairs={{0,24},{4,28},{8,16},{12,20},{16,8},{20,12},{24,0},{28,4},{1,25},{... | collective-permute-start | bytes 1572872 | tf_op jit(solution)/shard_map/ppermute | solution.py:1144
  962.9 41.0 %all-to-all-start.17 = ((bf16[8,192,256]{2,1,0:T(8,128)(2,1)}), bf16[8,192,256]{2,1,0:T(8,128)(2,1)S(1)}, u32[]{:S(2)}, u32[]{:S(2)}) async-start(bf16[8,192,256]{2,1,0:T(8,128)(2,1)} %bitcast.84.ka_ref), calls=%async_computation.18 | async-start | bytes 1572864 | tf_op jit(solution)/shard_map/all_to_all | solution.py:813
  1014.5 106.4 %collective-permute-start.46 = (bf16[192,768]{1,0:T(8,128)(2,1)S(1)}, bf16[192,768]{1,0:T(8,128)(2,1)}, u32[]{:S(2)}, u32[]{:S(2)}) collective-permute-start(bf16[192,768]{1,0:T(8,128)(2,1)S(1)} %convolution_convert_fusion.1), channel_id=1, source_target_pairs={{0,1},{1,0},{2,3},{3,2},{4,5},{5,4},{6,7},{7,6},{8,9},{9,8},{10,11... | collective-permute-start | bytes 884744 | tf_op jit(solution)/shard_map/ppermute | solution.py:1175
  1014.7 113.2 %collective-permute-start.47 = (bf16[192,768]{1,0:T(8,128)(2,1)S(1)}, bf16[192,768]{1,0:T(8,128)(2,1)}, u32[]{:S(2)}, u32[]{:S(2)}) collective-permute-start(bf16[192,768]{1,0:T(8,128)(2,1)S(1)} %convolution_convert_fusion.1), channel_id=1, source_target_pairs={{0,2},{1,3},{2,0},{3,1},{4,6},{5,7},{6,4},{7,5},{8,10},{9,11},{10,... | collective-permute-start | bytes 884744 | tf_op jit(solution)/shard_map/ppermute | solution.py:1175
  1046.8 70.0 %all-to-all-start.18 = ((bf16[8,192,256]{2,1,0:T(8,128)(2,1)}), bf16[8,192,256]{2,1,0:T(8,128)(2,1)}, u32[]{:S(2)}, u32[]{:S(2)}) async-start(bf16[8,192,256]{2,1,0:T(8,128)(2,1)} %bitcast.90.kb_ref), calls=%async_computation.19 | async-start | bytes 1572864 | tf_op jit(solution)/shard_map/all_to_all | solution.py:813
  1051.0 95.9 %reduce-scatter.11.cloned.1.call-start = ((), (), s32[]{:S(2)}) async-start(), calls=%async_computation.26 | async-start | bytes 1310720 | tf_op jit(solution)/shard_map/reduce_scatter | solution.py:869
  1056.0 31.5 %collective-permute-start.41 = (bf16[96,1024]{1,0:T(8,128)(2,1)S(1)}, bf16[96,1024]{1,0:T(8,128)(2,1)S(1)}, u32[]{:S(2)}, u32[]{:S(2)}) collective-permute-start(bf16[96,1024]{1,0:T(8,128)(2,1)S(1)} %get-tuple-element.210), channel_id=1, source_target_pairs={{0,2},{1,3},{2,0},{3,1},{4,6},{5,7},{6,4},{7,5},{8,10},{9,11},{10,... | collective-permute-start | bytes 589832 | tf_op jit(solution)/shard_map/ppermute | solution.py:858
  1057.5 30.8 %collective-permute-start.42 = (bf16[96,1024]{1,0:T(8,128)(2,1)S(1)}, bf16[96,1024]{1,0:T(8,128)(2,1)S(1)}, u32[]{:S(2)}, u32[]{:S(2)}) collective-permute-start(bf16[96,1024]{1,0:T(8,128)(2,1)S(1)} %get-tuple-element.209), channel_id=1, source_target_pairs={{0,3},{1,2},{2,1},{3,0},{4,7},{5,6},{6,5},{7,4},{8,11},{9,10},{10,... | collective-permute-start | bytes 589832 | tf_op jit(solution)/shard_map/ppermute | solution.py:858
  1064.4 63.4 %collective-permute-start.48 = (bf16[192,768]{1,0:T(8,128)(2,1)S(1)}, bf16[192,768]{1,0:T(8,128)(2,1)}, u32[]{:S(2)}, u32[]{:S(2)}) collective-permute-start(bf16[192,768]{1,0:T(8,128)(2,1)S(1)} %convolution_convert_fusion.1), channel_id=1, source_target_pairs={{0,3},{1,2},{2,1},{3,0},{4,7},{5,6},{6,5},{7,4},{8,11},{9,10},{10,... | collective-permute-start | bytes 884744 | tf_op jit(solution)/shard_map/ppermute | solution.py:1175
  (148 other events, 2050.2 us)
Sparse Core Ops, SparseCore 0:
  12.9 77.1 all-gather.4
  93.4 91.4 all-gather.6
  562.6 64.3 reduce-scatter.6
  796.8 22.8 reduce-scatter.12
  858.9 79.9 reduce-scatter.8
  1063.2 36.1 reduce-scatter.10

commit v5 on v3

--- a/solution.py
+++ b/solution.py
@@ -306,7 +306,7 @@
             once((S, rows, W)),
             once((rows, D)),
             once((2, D)),
-            w_out[1],
+            once(*w_out[1]),
             w_triple[1],
         ],
         out_specs=(
@@ -376,6 +376,7 @@
         back[...] = jnp.zeros_like(back)
 
     up = flat(up_ref)
+    down = flat(down_ref)
     u = dot(n_ref[...], up, NT)
     slope = math.sqrt(2.0 / math.pi)
     square = u * u
@@ -383,10 +384,10 @@
     half = 0.5 * (1.0 + bend)
     g = (u * half).astype(bf16)
     rise = half + 0.5 * slope * u * (1.0 - bend * bend) * (1.0 + 0.134145 * square)
-    du = (dot(e3_ref[...], down_ref[...], NT) * rise).astype(bf16)
+    du = (dot(e3_ref[...], down, NT) * rise).astype(bf16)
     g_ref[...] = g
     du_ref[...] = du
-    acc[...] += dot(g, down_ref[...], NN)
+    acc[...] += dot(g, down, NN)
     back[...] += dot(du, up, NN)
 
     @pl.when(step == steps - 1)
@@ -406,11 +407,10 @@
             db_ref[i] = da[R:, i * W : (i + 1) * W]
 
 
-def feed_forward(a, x1, cot, d_pix, norm, w_out, w_dec, w_up, w_down, steps):
+def feed_forward(a, x1, cot, d_pix, norm, w_out, w_dec, w_up, w_down, hidden, steps):
     S, R, W = a[0].shape
     RB = a[1].shape[1]
     D, total, pixels = S * W, R + RB, d_pix.shape[1]
-    hidden = w_down.shape[0]
     part = hidden // steps
     row = jax.ShapeDtypeStruct((total, D), bf16)
     wide = jax.ShapeDtypeStruct((total, hidden), bf16)
@@ -442,10 +442,10 @@
             once((RB, D)),
             once((total, pixels)),
             once((2, D)),
-            w_out[1],
-            w_dec[1],
+            once(*w_out[1]),
+            once(*w_dec[1]),
             w_up[1],
-            pl.BlockSpec((part, D), lambda i: (i, 0)),
+            w_down[1],
         ],
         out_specs=(
             full,
@@ -468,7 +468,22 @@
             bytes_accessed=4 * D * hidden + 30 * total * D,
             transcendentals=total * hidden,
         ),
-    )(*a, *x1, *cot, d_pix, norm, w_out[0], w_dec[0], w_up[0], w_down)
+    )(*a, *x1, *cot, d_pix, norm, w_out[0], w_dec[0], w_up[0], w_down[0])
+
+
+def hold_kernel(*refs):
+    pass
+
+
+def hold(value, deps):
+    return pl.pallas_call(
+        hold_kernel,
+        out_shape=jax.ShapeDtypeStruct(value.shape, value.dtype),
+        in_specs=[AN] * (1 + len(deps)),
+        out_specs=AN,
+        input_output_aliases={0: 0},
+        cost_estimate=pl.CostEstimate(flops=0, bytes_accessed=0, transcendentals=0),
+    )(value, *deps)
 
 
 def back_kernel(
@@ -518,7 +533,7 @@
             once((rows, D)),
             once((rows, D), (at, 0)),
             once((2, D)),
-            w_out[1],
+            once(*w_out[1]),
             w_triple[1],
         ]
         + [AN] * len(deps),
@@ -584,88 +599,74 @@
     )(*lefts, *rights)
 
 
-def start_kernel(at_ref, xa_ref, xb_ref, norm_ref, *refs, pieces, weights, parts, rows):
-    w_in, refs = refs[:weights], refs[weights:]
-    p_in, kv_in, (q_ref, k_ref, n_ref, wq_ref) = refs[:pieces], refs[pieces:-4], refs[-4:]
-    seq, rank = at_ref[0], at_ref[1]
+def start_kernel(at_ref, xa_ref, xb_ref, norm_ref, wk_ref, wq_in, *refs, pieces, width):
+    p_in, (q_ref, k_ref, n_ref, wq_ref, wkv_ref) = refs[:pieces], refs[pieces:]
+    seq = at_ref[0]
     R = xa_ref.shape[0]
-    for i in range(weights):
-        for j in range(w_in[i].shape[0]):
-            at = 0 if weights == 1 else ((rank ^ j) * pieces + (seq ^ i)) * rows
-            wq_ref[pl.ds(pl.multiple_of(at, 16), w_in[i].shape[1]), :] = w_in[i][j]
+    W = q_ref.shape[2]
+    wq_ref[...] = flat(wq_in)
+    wkv_ref[...] = flat(wk_ref)[:, :width]
     for block, x_ref in ((slice(0, R), xa_ref), (slice(R, n_ref.shape[0]), xb_ref)):
         n_ref[block, :] = layer_norm(x_ref[...].astype(f32), norm_ref[0:1, :], norm_ref[1:2, :])
-    W = q_ref.shape[2]
     for i in range(pieces):
         q_ref[i] = dot(n_ref[...], wq_ref[i * W : (i + 1) * W, :], NT).astype(bf16)
-    w_kv = sum(v[...] for v in kv_in)
+    own = wkv_ref[pl.ds(pl.multiple_of(seq * 2 * W, 16), 2 * W), :]
     for i in range(pieces):
-        k_ref[seq ^ i] = dot(p_in[i][...], w_kv, NT).astype(bf16)
-
-
-def start(at, x0, norm, w_pieces, patch_pieces, kv_parts, W):
+        k_ref[seq ^ i] = dot(p_in[i][...], own, NT).astype(bf16)
+
+
+def start(at, x0, norm, w_kv, w_query, patch_pieces, W):
     S, D = len(patch_pieces), x0[0].shape[1]
     total = x0[0].shape[0] + x0[1].shape[0]
-    slots = patch_pieces[0].shape[0]
-    body = functools.partial(
-        start_kernel,
-        pieces=S,
-        weights=len(w_pieces),
-        parts=len(kv_parts),
-        rows=w_pieces[0].shape[1],
-    )
+    slots, width = patch_pieces[0].shape
+    whole = [x0[0].shape, x0[1].shape, norm.shape]
+    outs = [(S, total, W), (S, slots, 2 * W), (total, D), (D, D), (2 * D, width)]
     return pl.pallas_call(
-        body,
-        out_shape=(
-            jax.ShapeDtypeStruct((S, total, W), bf16),
-            jax.ShapeDtypeStruct((S, slots, 2 * W), bf16),
-            jax.ShapeDtypeStruct((total, D), bf16),
-            jax.ShapeDtypeStruct((D, D), bf16),
-        ),
-        in_specs=[SM] + [VM] * (3 + len(w_pieces) + S + len(kv_parts)),
-        out_specs=(VM,) * 4,
-        compiler_params=pltpu.CompilerParams(vmem_limit_bytes=44 * 2**20),
+        functools.partial(start_kernel, pieces=S, width=width),
+        grid=(1,),
+        out_shape=tuple(jax.ShapeDtypeStruct(v, bf16) for v in outs),
+        in_specs=[SM]
+        + [once(v) for v in whole]
+        + [once(*w_kv[1]), once(*w_query[1])]
+        + [once((slots, width))] * S,
+        out_specs=tuple(held(v) for v in outs),
+        compiler_params=pltpu.CompilerParams(vmem_limit_bytes=56 * 2**20),
         cost_estimate=pl.CostEstimate(
-            flops=2 * total * D * D + 4 * S * slots * 768 * W,
+            flops=2 * total * D * D + 4 * S * slots * width * W,
             bytes_accessed=6 * D * D + 12 * total * D,
             transcendentals=0,
         ),
-    )(at, *x0, norm, *w_pieces, *patch_pieces, *kv_parts)
-
-
-def finish_kernel(at_ref, qa_ref, qb_ref, ka_ref, kb_ref, *refs, pieces):
-    n_in, p_in, out_ref = refs[:pieces], refs[pieces:-1], refs[-1]
+    )(at, *x0, norm, w_kv[0], w_query[0], *patch_pieces)
+
+
+def finish_kernel(at_ref, ka_ref, kb_ref, *refs, pieces):
+    p_in, out_ref = refs[:pieces], refs[-1]
     seq = at_ref[0]
-    R, slots, W = qa_ref.shape[1], ka_ref.shape[1], qa_ref.shape[2]
-    by_q, by_kv = 0.0, 0.0
+    slots, W = ka_ref.shape[1], ka_ref.shape[2] // 2
+    by_kv = 0.0
     for i in range(pieces):
         j = seq ^ i
-        by_q += dot(qa_ref[j], n_in[i][:R, :], TN) + dot(qb_ref[j], n_in[i][R:, :], TN)
         by_kv += dot(ka_ref[j], p_in[i][:slots, :], TN) + dot(kb_ref[j], p_in[i][slots:, :], TN)
-    grad = by_q.T.astype(bf16)
-    rows = grad.shape[0] // pieces
     wide = by_kv.shape[1] // pieces
     grad_k, grad_v = by_kv[:W].T.astype(bf16), by_kv[W:].T.astype(bf16)
     for i in range(pieces):
-        out_ref[i, :rows, :] = grad[i * rows : (i + 1) * rows, :]
-        out_ref[i, rows : rows + wide, :] = grad_k[i * wide : (i + 1) * wide, :]
-        out_ref[i, rows + wide :, :] = grad_v[i * wide : (i + 1) * wide, :]
-
-
-def finish(at, dq, dkv, n_pieces, patch_pieces):
-    S, _, W = dq[0].shape
-    D, width = n_pieces[0].shape[1], patch_pieces[0].shape[1]
-    rows = D // S + 2 * width // S
+        out_ref[i, :wide, :] = grad_k[i * wide : (i + 1) * wide, :]
+        out_ref[i, wide:, :] = grad_v[i * wide : (i + 1) * wide, :]
+
+
+def finish(at, dkv, patch_pieces):
+    S, W = dkv[0].shape[0], dkv[0].shape[2] // 2
+    rows = 2 * patch_pieces[0].shape[1] // S
     return pl.pallas_call(
         functools.partial(finish_kernel, pieces=S),
         out_shape=jax.ShapeDtypeStruct((S, rows, W), bf16),
-        in_specs=[SM] + [VM] * (4 + 2 * S),
+        in_specs=[SM] + [VM] * (2 + S),
         out_specs=VM,
-        compiler_params=pltpu.CompilerParams(vmem_limit_bytes=48 * 2**20),
+        compiler_params=pltpu.CompilerParams(vmem_limit_bytes=32 * 2**20),
         cost_estimate=pl.CostEstimate(
-            flops=3 * 10**9, bytes_accessed=18 * 10**6, transcendentals=0
-        ),
-    )(at, *dq, *dkv, *n_pieces, *patch_pieces)
+            flops=13 * 10**8, bytes_accessed=8 * 10**6, transcendentals=0
+        ),
+    )(at, *dkv, *patch_pieces)
 
 
 CP = 32
@@ -750,17 +751,19 @@
     return lax.all_gather(piece, ("mp", "seq"), axis=0, tiled=False)
 
 
-def bundle_part(bundle, at, rows, per_step=None):
+def bundle_part(bundle, at, rows):
     pieces, _, D = bundle.shape
     if rows % 16 == 0 and at % rows == 0:
-        place = at // rows
-        if per_step is None:
-            return bundle, once((pieces, rows, D), (0, place, 0))
-        return bundle, pl.BlockSpec((per_step, rows, D), lambda i: (i, place, 0))
+        return bundle, ((pieces, rows, D), (0, at // rows, 0))
     value = bundle[:, at : at + rows].reshape(1, -1, D)
-    if per_step is None:
-        return value, once(value.shape)
-    return value, pl.BlockSpec((1, per_step * rows, D), lambda i: (0, i, 0))
+    return value, (value.shape, None)
+
+
+def by_step(part, steps):
+    (pieces, rows, D), at = part[1]
+    if pieces > 1:
+        return part[0], pl.BlockSpec((pieces // steps, rows, D), lambda i: (i, at[1], 0))
+    return part[0], pl.BlockSpec((1, rows // steps, D), lambda i: (0, i, 0))
 
 
 def reduce_rows(value):
@@ -871,49 +874,38 @@
     local_qkv = self_qkv.reshape(D, 3, 2, W).transpose(2, 1, 3, 0).reshape(-1, D)
     local_kv = cross_kv.reshape(width, 2, 2, W).transpose(2, 1, 3, 0).reshape(-1, width)
     per = D // (S * M)
+    dec_rows = 4 * CP // S
+    kv_rows = 2 * per
+    local_kv = jnp.pad(local_kv, ((0, 0), (0, D - width)))
+    lead = gather_rows(jnp.concatenate([mine(local_kv, 0), mine(cross_query, 1).T], axis=0))
+    w_kv, w_query = bundle_part(lead, 0, kv_rows), bundle_part(lead, kv_rows, per)
+    first = gather_rows(
+        jnp.concatenate(
+            [
+                mine(local_qkv, 0),
+                mine(cross_out, 0),
+                mine(self_out, 0),
+                mine(local_dec.reshape(-1, D), 0),
+            ],
+            axis=0,
+        )
+    )
     up_rows = mlp_up.shape[1] // S
-    dec_rows = 4 * CP // S
-    first = gather_rows(jnp.concatenate([mine(local_qkv, 0), mine(cross_out, 0)], axis=0))
-    w_triple = bundle_part(first, 0, 3 * per, M)
+    second = gather_rows(jnp.concatenate([mine(mlp_up, 1).T, mine(mlp_down, 0)], axis=0))
+    steps = 8
+    w_up = by_step(bundle_part(second, 0, up_rows), steps)
+    w_down = by_step(bundle_part(second, up_rows, up_rows), steps)
+    w_triple = by_step(bundle_part(first, 0, 3 * per), S)
     w_cross_out = bundle_part(first, 3 * per, per)
-    second = gather_rows(
-        jnp.concatenate(
-            [mine(mlp_up, 1).T, mine(self_out, 0), mine(local_dec.reshape(-1, D), 0)], axis=0
-        )
-    )
-    steps = 8
-    w_up = bundle_part(second, 0, up_rows, S * M // steps)
-    w_self_out = bundle_part(second, up_rows, per)
-    w_dec = bundle_part(second, up_rows + per, dec_rows)
-    w_down = gather_rows(mine(mlp_down, 0)).reshape(-1, D)
-    w_kv = gather_rows(mine(local_kv, 0)).reshape(-1, width)
+    w_self_out = bundle_part(first, 4 * per, per)
+    w_dec = bundle_part(first, 5 * per, dec_rows)
 
     x0 = pick(tokens)
     norms = [jnp.stack([norm_gains[i], norm_shifts[i]]) for i in range(3)]
     at = jnp.stack([s, m])
     both = [lax.dynamic_index_in_dim(patches, o, 0, keepdims=False) for o in (at_a, at_b)]
     patch_pieces = gather_pieces(jnp.concatenate(both, axis=0))
-    piece = mine(cross_query, 1).T
-    ranks = [piece]
-    for step in range(1, M):
-        ranks.append(lax.ppermute(piece, "mp", [(i, i ^ step) for i in range(M)]))
-    w_pieces = gather_pieces(jnp.stack(ranks))
-    if per % 16 != 0:
-        w_pieces = jnp.stack(w_pieces)
-        w_pieces = [
-            lax.dynamic_index_in_dim(w_pieces, s ^ i, 0, keepdims=False) for i in range(S)
-        ]
-        w_pieces = jnp.stack(w_pieces, axis=1)
-        w_pieces = [
-            lax.dynamic_index_in_dim(w_pieces, m ^ i, 0, keepdims=False) for i in range(M)
-        ]
-        w_pieces = [jnp.stack(w_pieces).reshape(1, D, D)]
-    own_kv = lax.dynamic_slice_in_dim(local_kv, (s % 2) * 2 * W, 2 * W, 0)
-    kv_parts = [jnp.where(m == s // 2, own_kv, jnp.zeros_like(own_kv))]
-    for step in range(1, M):
-        moves = [(i * M + i // 2, i * M + ((i // 2) ^ step)) for i in range(S)]
-        kv_parts.append(lax.ppermute(own_kv, ("seq", "mp"), moves))
-    q1, keys_one, n1, w_query = start(at, x0, norms[0], w_pieces, patch_pieces, kv_parts, W)
+    q1, keys_one, n1, w_query, w_kv = start(at, x0, norms[0], w_kv, w_query, patch_pieces, W)
     heads_one = swap_seq(q1)
 
     TC = PLANE // 4
@@ -990,15 +982,29 @@
         row_total,
         hpd,
         True,
+        [o_a2],
     )
     a2 = [swap_seq(o_a2.reshape(S, R, W)), swap_seq(o_b2.reshape(S, RB, W))]
 
+    hidden = mlp_up.shape[1] * M
     n3, a2, g, du, x3b, pix, e3, d2, e2, da2_a, da2_b, sums_three = feed_forward(
-        a2, x1, pick(tokens_cot), d_pix, norms[2], w_self_out, w_dec, w_up, w_down, steps
+        a2,
+        x1,
+        pick(tokens_cot),
+        d_pix,
+        norms[2],
+        w_self_out,
+        w_dec,
+        w_up,
+        w_down,
+        hidden,
+        steps,
     )
 
     da2 = [swap_seq(da2_a), swap_seq(da2_b)]
     grads_one = weight_grads([[(n3, du)], [(e3, g)], [(e2, a2)], [(x3b, d_pix)]], M)
+    grads_one = hold(grads_one, da2)
+    x3b, pix = hold(x3b, [grads_one]), hold(pix, [grads_one])
     dq_a2, dkv_a2 = attend_back(
         wide,
         [res_a2, da2[0], o_a2, heads_two[0]],
@@ -1011,7 +1017,6 @@
         [grads_one],
     )
     grads_one = reduce_rows(grads_one)
-    n_pieces = gather_pieces(n1)
     tokens_out = own_blocks(x3b[:R], x3b[R:])
     pix = pix.reshape(KA + KB, S, M, cu).transpose(1, 2, 0, 3)
     got = swap_all(pix.reshape(S * M, KA + KB, cu)).reshape(S, pairs, 2, KA + KB, cu)
@@ -1024,7 +1029,7 @@
         row_total,
         hpd,
         True,
-        [dq_a2, tokens_out, got] + n_pieces[::2],
+        [dq_a2, got],
     )
     kept, given = dkv_b2[: row_total // 2], dkv_b2[row_total // 2 :]
     dkv_b2 = (kept.astype(f32) + swap_pair(given).astype(f32)).astype(bf16)
@@ -1052,9 +1057,17 @@
         return dq.reshape(S, rows[i], W), dkv.reshape(S, slots, 2 * W)
 
     low_a = below(0, [])
-    cross_a = cross_back(0, swap_seq(low_a[2]), [grads_one] + n_pieces[1::2])
+    cross_a = cross_back(0, swap_seq(low_a[2]), [grads_one, tokens_out])
+    grads_one = sum_ranks(grads_one)
     low_b = below(1, [cross_a[0]])
     d1, e1, da1, sums_two = zip(low_a, low_b)
+
+    grads_two = weight_grads(
+        [[(n2[i], dt2[i]) for i in range(2)], [(e1[i], a1[i]) for i in range(2)]], M
+    )
+    cross_b = cross_back(1, swap_seq(da1[1]), [grads_two, grads_one])
+    dq1, dkv1 = zip(cross_a, cross_b)
+    grads_two = reduce_rows(grads_two)
 
     px_a = got[:, :, :, :KA].transpose(1, 2, 0, 3, 4).reshape(pairs, 2, S * KA, cu)
     px_b = got[:, :, :, KA:].transpose(1, 0, 2, 3, 4).reshape(pairs, S * KA, cu)
@@ -1064,17 +1077,11 @@
     corner = lax.ppermute(tile[:, 0, :1], "seq", [(i + 5, i) for i in ways[5]])
     fill = jnp.zeros((planes, toks - rim - TC - 1, cu), bf16)
     ext = jnp.concatenate([tile.reshape(planes, own, cu), rights, belows, corner, fill], axis=1)
+    ext = hold(ext, [dq1[1]])
     sampled = per_plane(
         pixel_sample_kernel, ext, weights_in, CP, weights_in.shape[2], bf16, toks, TR, TC
     )
     sampled = sampled[:, :channels].reshape(objects, 3, channels, 1, -1)
-
-    grads_two = weight_grads(
-        [[(n2[i], dt2[i]) for i in range(2)], [(e1[i], a1[i]) for i in range(2)]], M
-    )
-    cross_b = cross_back(1, swap_seq(da1[1]), [grads_two, sampled])
-    dq1, dkv1 = zip(cross_a, cross_b)
-    grads_two = reduce_rows(grads_two)
 
     parts = [mm(to_rows(v), w_kv).astype(bf16) for v in dkv1]
     every = [[p] for p in parts]
@@ -1089,13 +1096,14 @@
         patch_grad += [from_a[2 * p].astype(f32), shared, from_a[2 * p + 1].astype(f32)]
     patch_grad = jnp.stack(patch_grad)
 
-    grads = [mm(to_rows(v), w_query) for v in dq1]
+    dq1 = [to_rows(v) for v in dq1]
+    grads = [mm(v, w_query) for v in dq1]
     back_one = [norm_back(x0[i].astype(f32), norm_gains[0], grads[i]) for i in range(2)]
     d0 = [(d1[i] + back_one[i][0]).astype(bf16) for i in range(2)]
     grad_tokens = own_blocks(d0[0], d0[1]).astype(f32)
 
     order = 2 * m + s % 2
-    by_head = finish(at, dq1, dkv1, n_pieces, patch_pieces)
+    by_head = finish(at, dkv1, patch_pieces)
     sums = [0.0, 0.0]
     for step in range(S):
         moves = []
@@ -1109,11 +1117,14 @@
     owned = jnp.concatenate(
         [jnp.where(swap, sums[1], sums[0]), jnp.where(swap, sums[0], sums[1])], axis=1
     )
-    grad_cross_query = owned[: D // S]
-    grad_cross_kv = owned[D // S :].reshape(2, width // S, 2 * W).transpose(1, 0, 2)
-
-    grads_one, grads_two = sum_ranks(grads_one), sum_ranks(grads_two)
-    ff = g.shape[1] // M
+    grad_cross_kv = owned.reshape(2, width // S, 2 * W).transpose(1, 0, 2)
+    grad_q = dot(n1[:R], dq1[0], TN) + dot(n1[R:], dq1[1], TN)
+    grad_q = swap_seq(grad_q.astype(bf16).reshape(S, D // S, D))
+    grad_q = jnp.sum(grad_q.astype(f32), axis=0).astype(bf16).reshape(D // S, M, -1)
+    grad_cross_query = sum(v.astype(f32) for v in from_ranks(grad_q.transpose(1, 0, 2)))
+
+    grads_two = sum_ranks(grads_two)
+    ff = hidden // M
     grad_mlp_up, grad_mlp_down = grads_one[:, :ff], grads_one[:, ff : 2 * ff].T
     grad_self_out = grads_one[:, 2 * ff : 2 * ff + D // M].T
     grad_decoder = grads_one[:, 2 * ff + D // M :]

time: 1060 us -> 1040 us (0.981)
  starting transfers between devices: 208 us -> 163 us
  blocking collectives: 0 us -> 38.5 us
  waiting for transfers between devices: 283 us -> 256 us
  Pallas kernels: 374 us -> 396 us
    all_to_all x18 -> x17, waiting for transfers between devices: 120 us -> 56.3 us  [swap_seq(): return lax.all_to_all(value, 'seq', split_axis=0, concat_axis=0, tiled=True)]
    reduce_scatter x2, waiting for transfers between devices: 0.02 us -> 47.2 us  [reduce_rows(): return lax.psum_scatter(value, 'seq', scatter_dimension=0, tiled=True)]
    ppermute x2, waiting for transfers between devices: 39 us -> 0.01 us  [swap_pair(): return lax.ppermute(value, 'mp', [(i, i ^ 1) for i in range(count)])]
    all_to_all x0 -> x2, blocking collectives: none -> 38.5 us  [swap_seq(): return lax.all_to_all(value, 'seq', split_axis=0, concat_axis=0, tiled=True)]
    ppermute x6 -> x0, waiting for transfers between devices: 33.6 us -> none  [the longest x3 27.3 us: per_device(): kv_parts.append(lax.ppermute(own_kv, ('seq', 'mp'), moves))]
    ppermute x9 -> x3, waiting for transfers between devices: 0.18 us -> 30.6 us  [gather_pieces(): pieces.append(value if step == 0 else lax.ppermute(value, 'seq', moves))]
    all_gather x4 -> x3, waiting for transfers between devices: 0.04 us -> 28.7 us  [gather_rows(): return lax.all_gather(piece, ('mp', 'seq'), axis=0, tiled=False)]
    ppermute x9 -> x12, waiting for transfers between devices: 21.7 us -> 40.5 us  [from_ranks(): block = lax.ppermute(block, 'mp', [(i, i ^ step) for i in range(ranks)])]
  transfers between devices with their start and end apart: 90 -> 71, of which waited for: 30 -> 24; matrix products, arithmetic and copies ran while one was open for 9% -> 11% of each run, Pallas kernels for 30% -> 35%
where the time goes in v5:
time: 1040 us; the launch traced here: 1030 us
  Pallas kernels  396 us (38%)
  waiting for transfers between devices  256 us (25%)
  starting transfers between devices  163 us (16%)
  local copies, waits for them, and re-layouts  110 us (11%)
  blocking collectives  38.5 us (4%)
  other arithmetic  35.8 us (3%)
  matrix products  16.5 us (2%)
  between operations  16.2 us (2%)
    pallas_call x4, Pallas kernels, attend_back(): pl.pallas_call(body, out_shape=(jax.ShapeDtypeStruct((queries, hpd * HD),...  152 us
    pallas_call x4, Pallas kernels, attend(): pl.pallas_call(body, out_shape=(jax.ShapeDtypeStruct((queries, hpd * HD),...  89.3 us
    all_to_all x17, starting transfers between devices, swap_seq(): return lax.all_to_all(value, 'seq', split_axis=0, concat_axis=0, tiled=True)  74.7 us
    unnamed x224, local copies, waits for them, and re-layouts  56.7 us
    all_to_all x17, waiting for transfers between devices, swap_seq(): return lax.all_to_all(value, 'seq', split_axis=0, concat_axis=0, tiled=True)  56.3 us
    reduce_scatter x2, waiting for transfers between devices, reduce_rows(): return lax.psum_scatter(value, 'seq', scatter_dimension=0, tiled=True)  47.2 us
    ppermute x12, waiting for transfers between devices, from_ranks(): block = lax.ppermute(block, 'mp', [(i, i ^ step) for i in range(ranks)])  40.5 us
    all_to_all x2, blocking collectives, swap_seq(): return lax.all_to_all(value, 'seq', split_axis=0, concat_axis=0, tiled=True)  38.5 us
  transfers between devices with their start and end apart: 71, of which 24 were waited for; matrix products, arithmetic and copies ran while one was open for 11% of the time, Pallas kernels for 35%

profile of v5, /device:TPU:0, one launch (start us, length us, event | category | flops | bytes accessed | tf_op | source)
XLA Modules:
  0.0 1031.8 jit_solution(14755017360344653283)
XLA Ops:
  18.7 4.9 copy.117
  34.9 14.2 %collective-permute-done.1.refs_2_ = bf16[384,768]{1,0:T(8,128)(2,1)S(1)} collective-permute-done((bf16[384,768]{1,0:T(8,128)(2,1)S(1)}, bf16[384,768]{1,0:T(8,128)(2,1)S(1)}, u32[]{:S(2)}, u32[]{:S(2)}) %collective-permute-start.1) | collective-permute-done | bytes 589856 | tf_op jit(solution)/shard_map/ppermute | solution.py:798
  49.1 4.4 collective-permute-done.3.refs_4_
  53.5 12.0 %collective-permute-done.5.refs_6_ = bf16[384,768]{1,0:T(8,128)(2,1)S(1)} collective-permute-done((bf16[384,768]{1,0:T(8,128)(2,1)S(1)}, bf16[384,768]{1,0:T(8,128)(2,1)S(1)}, u32[]{:S(2)}, u32[]{:S(2)}) %collective-permute-start.5) | collective-permute-done | bytes 589856 | tf_op jit(solution)/shard_map/ppermute | solution.py:798
  74.4 17.7 %all-gather.7.cloned.1.call-done = bf16[3072,1024]{1,0:T(8,128)(2,1)} async-done(((bf16[96,1024]{1,0:T(8,128)(2,1)}), bf16[3072,1024]{1,0:T(8,128)(2,1)}) %all-gather.7.cloned.1.call-update) | async-done | bytes 6291472 | tf_op jit(solution)/shard_map/all_gather | solution.py:751
  92.1 11.8 %shard_map.280 = (bf16[8,576,128]{2,1,0:T(8,128)(2,1)}, bf16[8,384,256]{2,1,0:T(8,128)(2,1)}, bf16[576,1024]{1,0:T(8,128)(2,1)}, bf16[1024,1024]{1,0:T(8,128)(2,1)}, bf16[2048,768]{1,0:T(8,128)(2,1)}) custom-call(s32[2]{0:T(128)} %pad_add_fusion.2.at_ref, bf16[384,1024]{1,0:T(8,128)(2,1)} %get-tuple-element.184.xa_ref.x_ref, ...), custom_call_target="tpu_custom_call" | custom-call | flops 2415919104 | bytes 13369344 | tf_op jit(solution)/shard_map/pallas_call | solution.py:624
  109.7 14.9 %all-to-all-done.refs_0_ = bf16[8,576,128]{2,1,0:T(8,128)(2,1)S(1)} async-done(((bf16[8,576,128]{2,1,0:T(8,128)(2,1)}), bf16[8,576,128]{2,1,0:T(8,128)(2,1)S(1)}, u32[]{:S(2)}, u32[]{:S(2)}) %all-to-all-start) | async-done | bytes 1179680 | tf_op jit(solution)/shard_map/all_to_all | solution.py:734
  124.5 15.1 %shard_map.284 = (bf16[1536,128]{1,0:T(8,128)(2,1)}, bf16[2,1536,128]{2,1,0:T(8,128)(2,1)S(1)}) custom-call(s32[2]{0:T(128)S(1)} %get-tuple-element.231.n_ref, bf16[8,576,128]{2,1,0:T(8,128)(2,1)S(1)} %all-to-all-done.refs_0_, bf16[8,384,256]{2,1,0:T(8,128)(2,1)S(1)} %copy-done.63), custom_call_target="tpu_custom_call" | custom-call | flops 4831838208 | bytes 3145728 | tf_op jit(solution)/shard_map/pallas_call | solution.py:194
  144.5 27.2 %shard_map.281 = (bf16[3072,128]{1,0:T(8,128)(2,1)}, bf16[2,3072,128]{2,1,0:T(8,128)(2,1)S(1)}) custom-call(s32[2]{0:T(128)S(1)} %get-tuple-element.232.n_ref, bf16[8,576,128]{2,1,0:T(8,128)(2,1)S(1)} %all-to-all-done.refs_0_, bf16[8,384,256]{2,1,0:T(8,128)(2,1)S(1)} %copy-done.63), custom_call_target="tpu_custom_call" | custom-call | flops 9663676416 | bytes 6291456 | tf_op jit(solution)/shard_map/pallas_call | solution.py:194
  172.9 4.3 all-to-all-start.1
  177.2 11.0 %all-gather.9.cloned.1.call-done = bf16[5632,1024]{1,0:T(8,128)(2,1)} async-done(((bf16[176,1024]{1,0:T(8,128)(2,1)}), bf16[5632,1024]{1,0:T(8,128)(2,1)}) %all-gather.9.cloned.1.call-update) | async-done | bytes 11534352 | tf_op jit(solution)/shard_map/all_gather | solution.py:751
  188.2 8.6 shard_map.285
  203.8 10.0 shard_map.282
  227.7 15.2 %shard_map.287 = f32[18,160,128]{2,1,0:T(8,128)S(1)} custom-call(bf16[18,32,256]{2,1,0:T(8,128)(2,1)S(1)} %pad.22.cot_ref, bf16[18,561,256]{2,1,0:T(8,128)(2,1)S(1)} %bitcast.231), custom_call_target="tpu_custom_call" | custom-call | flops 600000000 | bytes 7000000 | tf_op jit(solution)/shard_map/pallas_call | solution.py:719
  254.8 10.3 all-to-all-done.2.refs_0_.refs_3_
  265.1 8.6 all-to-all-start.7
  273.8 29.7 %shard_map.283 = (bf16[3072,128]{1,0:T(8,128)(2,1)S(1)}, bf16[2,3072,128]{2,1,0:T(8,128)(2,1)S(1)}) custom-call(s32[2]{0:T(128)S(1)} %copy-done.64, bf16[8,384,384]{2,1,0:T(8,128)(2,1)S(1)} %all-to-all-done.2.refs_0_.refs_3_), custom_call_target="tpu_custom_call" | custom-call | flops 19327352832 | bytes 6291456 | tf_op jit(solution)/shard_map/pallas_call | solution.py:194
  305.6 17.3 %shard_map.286 = (bf16[1536,128]{1,0:T(8,128)(2,1)S(1)}, bf16[2,1536,128]{2,1,0:T(8,128)(2,1)S(1)}) custom-call(s32[2]{0:T(128)S(1)} %copy-done.64, bf16[8,192,384]{2,1,0:T(8,128)(2,1)S(1)} %all-to-all-done.5.refs_0_.refs_3_, bf16[8,192,256]{2,1,0:T(8,128)(2,1)} %collective-permute-done.7.refs_1_.refs_4_, bf16[3072,128]{1,0:T(8,128)(2,1)S(1)} %get-tuple-element.68.refs_2_), custom_call_target="tpu_custom_call" | custom-call | flops 9663676416 | bytes 3145728 | tf_op jit(solution)/shard_map/pallas_call | solution.py:194
  323.8 7.7 all-to-all-done.7
  331.5 26.0 %all_to_all.105.ab_ref = bf16[8,192,128]{2,1,0:T(8,128)(2,1)} all-to-all(bf16[8,192,128]{2,1,0:T(8,128)(2,1)S(1)} %bitcast.237), channel_id=1, replica_groups=mesh['seq'=8,'mp'=4] {'seq'}, dimensions={0} | all-to-all | bytes 786432 | tf_op jit(solution)/shard_map/all_to_all | solution.py:734
  368.0 5.8 all-to-all-done.3.aa_ref
  374.6 36.8 %shard_map.288 = (bf16[576,1024]{1,0:T(8,128)(2,1)}, bf16[576,1024]{1,0:T(8,128)(2,1)}, bf16[576,4096]{1,0:T(8,128)(2,1)}, bf16[576,4096]{1,0:T(8,128)(2,1)}, bf...) custom-call(bf16[8,384,128]{2,1,0:T(8,128)(2,1)} %copy-done.85, ...), custom_call_target="tpu_custom_call" | custom-call | flops 24159191040 | bytes 34471936 | tf_op jit(solution)/shard_map/pallas_call | solution.py:419
  411.5 12.4 %all_to_all.106.refs_2_.refs_1_ = bf16[8,192,128]{2,1,0:T(8,128)(2,1)} all-to-all(bf16[8,192,128]{2,1,0:T(8,128)(2,1)} %get-tuple-element.82), channel_id=1, replica_groups=mesh['seq'=8,'mp'=4] {'seq'}, dimensions={0} | all-to-all | bytes 786432 | tf_op jit(solution)/shard_map/all_to_all | solution.py:734
  427.8 24.1 %shard_map.289.refs_0_ = bf16[1024,9728]{1,0:T(8,128)(2,1)} custom-call(bf16[576,1024]{1,0:T(8,128)(2,1)} %get-tuple-element.75.refs_0_, bf16[576,1024]{1,0:T(8,128)(2,1)} %get-tuple-element.76.refs_1_, bf16[576,1024]{1,0:T(8,128)(2,1)} %get-tuple-element.77.refs_2_, bf16[576,1024]{1,0:T(8,128)(2,1)} %get-tuple-element.74.refs_3_.refs_0_, ...), custom_call_target="tpu_custom_call" | custom-call | flops 11475615744 | bytes 39845888 | tf_op jit(solution)/shard_map/pallas_call | solution.py:582
  466.3 4.6 all-to-all-start.10
  470.9 61.9 %shard_map.293 = (bf16[3072,128]{1,0:T(8,128)(2,1)S(1)}, bf16[3072,256]{1,0:T(8,128)(2,1)}) custom-call(s32[2]{0:T(128)S(1)} %copy-done.64, bf16[2,3072,128]{2,1,0:T(8,128)(2,1)} %copy-done.68, bf16[8,384,128]{2,1,0:T(8,128)(2,1)S(1)} %copy-done.17, bf16[3072,128]{1,0:T(8,128)(2,1)} %copy-done.41, bf16[8,384,384]{2,1,0:T(8,128)(2,1)} %copy-done.30, ...), custom_call_target="tpu_custom_call" | custom-call | flops 48318382080 | bytes 9437184 | tf_op jit(solution)/shard_map/pallas_call | solution.py:224
  539.0 47.2 %reduce-scatter.7.cloned.1.call-done.refs_4_ = bf16[128,9728]{1,0:T(8,128)(2,1)} async-done(((bf16[1024,9728]{1,0:T(8,128)(2,1)}), bf16[128,9728]{1,0:T(8,128)(2,1)}) %reduce-scatter.7.cloned.1.call-update) | async-done | bytes 2490384 | tf_op jit(solution)/shard_map/reduce_scatter | solution.py:770
  586.2 4.3 copy.153
  595.8 34.8 %shard_map.294 = (bf16[1536,128]{1,0:T(8,128)(2,1)S(1)}, bf16[3072,256]{1,0:T(8,128)(2,1)}) custom-call(s32[2]{0:T(128)S(1)} %copy-done.64, bf16[2,1536,128]{2,1,0:T(8,128)(2,1)} %copy-done.67, bf16[8,192,128]{2,1,0:T(8,128)(2,1)S(1)} %copy-done.34, bf16[1536,128]{1,0:T(8,128)(2,1)S(1)} %copy-done.52, bf16[8,192,384]{2,1,0:T(8,128)(2,1)} %copy-done.15, ...), custom_call_target="tpu_custom_call" | custom-call | flops 24159191040 | bytes 4718592 | tf_op jit(solution)/shard_map/pallas_call | solution.py:224
  642.9 11.9 %shard_map.295 = (f32[384,1024]{1,0:T(8,128)S(1)}, bf16[384,1024]{1,0:T(8,128)(2,1)S(1)}, bf16[8,384,128]{2,1,0:T(8,128)(2,1)}, f32[2,1024]{1,0:T(2,128)S(1)}) custom-call(bf16[8,384,384]{2,1,0:T(8,128)(2,1)S(1)} %all-to-all-done.12.t_ref.refs_4_, f32[384,1024]{1,0:T(8,128)S(1)} %copy-done.38, f32[576,1024]{1,0:T(8,128)S(1)} %copy-done.10, ...), custom_call_target="tpu_custom_call" | custom-call | flops 3221225472 | bytes 17825792 | tf_op jit(solution)/shard_map/pallas_call | solution.py:522
  663.8 10.0 all-to-all-done.13.refs_1_
  678.2 35.1 %shard_map.296 = (bf16[3072,128]{1,0:T(8,128)(2,1)}, bf16[1536,256]{1,0:T(8,128)(2,1)}) custom-call(s32[2]{0:T(128)S(1)} %copy-done.62, bf16[2,3072,128]{2,1,0:T(8,128)(2,1)} %copy-done.66, bf16[8,384,128]{2,1,0:T(8,128)(2,1)} %copy-done.86, bf16[3072,128]{1,0:T(8,128)(2,1)} %get-tuple-element.66.refs_2_, ...), custom_call_target="tpu_custom_call" | custom-call | flops 24159191040 | bytes 9437184 | tf_op jit(solution)/shard_map/pallas_call | solution.py:224
  714.9 9.7 shard_map.297
  726.8 11.6 %shard_map.298.refs_4_ = bf16[1024,4096]{1,0:T(8,128)(2,1)} custom-call(bf16[384,1024]{1,0:T(8,128)(2,1)} %copy-done.46, bf16[192,1024]{1,0:T(8,128)(2,1)} %copy-done.53, bf16[384,1024]{1,0:T(8,128)(2,1)} %copy-done.48, bf16[192,1024]{1,0:T(8,128)(2,1)} %copy-done.55, bf16[8,384,384]{2,1,0:T(8,128)(2,1)} %copy-done.2, bf16[8,192,384]{2,1,0:T(8,128)(2,1)} %copy-done.7, ...), custom_call_target="tpu_custom_call" | custom-call | flops 2415919104 | bytes 16777216 | tf_op jit(solution)/shard_map/pallas_call | solution.py:582
  746.6 11.7 %all-to-all-done.15 = bf16[8,384,128]{2,1,0:T(8,128)(2,1)S(1)} async-done(((bf16[8,384,128]{2,1,0:T(8,128)(2,1)}), bf16[8,384,128]{2,1,0:T(8,128)(2,1)S(1)}, u32[]{:S(2)}, u32[]{:S(2)}) %all-to-all-start.15) | async-done | bytes 786464 | tf_op jit(solution)/shard_map/all_to_all | solution.py:734
  767.0 8.3 collective-permute-done.18
  782.1 9.7 all-to-all-start.14
  805.0 35.8 %collective-permute-done.21 = bf16[96,1024]{1,0:T(8,128)(2,1)S(1)} collective-permute-done((bf16[96,1024]{1,0:T(8,128)(2,1)S(1)}, bf16[96,1024]{1,0:T(8,128)(2,1)S(1)}, u32[]{:S(2)}, u32[]{:S(2)}) %collective-permute-start.21) | collective-permute-done | bytes 196640 | tf_op jit(solution)/shard_map/ppermute | solution.py:779
  847.4 20.4 %shard_map.299 = (bf16[1536,128]{1,0:T(8,128)(2,1)}, bf16[1536,256]{1,0:T(8,128)(2,1)}) custom-call(s32[2]{0:T(128)S(1)} %copy-done.60, bf16[2,1536,128]{2,1,0:T(8,128)(2,1)} %copy-done.65, bf16[8,192,128]{2,1,0:T(8,128)(2,1)S(1)} %all-to-all-done.14.refs_1_, bf16[1536,128]{1,0:T(8,128)(2,1)} %get-tuple-element.69.refs_2_, ...), custom_call_target="tpu_custom_call" | custom-call | flops 12079595520 | bytes 4718592 | tf_op jit(solution)/shard_map/pallas_call | solution.py:224
  872.0 5.5 collective-permute-start.38
  882.2 7.4 all-to-all-start.16
  900.7 11.7 %shard_map.301 = bf16[18,32,256]{2,1,0:T(8,128)(2,1)S(1)} custom-call(bf16[18,160,128]{2,1,0:T(8,128)(2,1)S(1)} %copy-done.12, bf16[18,561,256]{2,1,0:T(8,128)(2,1)S(1)} %bitcast.232), custom_call_target="tpu_custom_call" | custom-call | flops 600000000 | bytes 7000000 | tf_op jit(solution)/shard_map/pallas_call | solution.py:719
  933.7 4.8 add_convert_fusion
  947.5 4.3 all-to-all-start.20
  966.5 18.5 %collective-permute-done.28 = bf16[192,768]{1,0:T(8,128)(2,1)S(1)} collective-permute-done((bf16[192,768]{1,0:T(8,128)(2,1)S(1)}, bf16[192,768]{1,0:T(8,128)(2,1)S(1)}, u32[]{:S(2)}, u32[]{:S(2)}) %collective-permute-start.28) | collective-permute-done | bytes 294944 | tf_op jit(solution)/shard_map/ppermute | solution.py:1091
  985.0 12.5 %collective-permute-done.29 = bf16[192,768]{1,0:T(8,128)(2,1)S(1)} collective-permute-done((bf16[192,768]{1,0:T(8,128)(2,1)S(1)}, bf16[192,768]{1,0:T(8,128)(2,1)S(1)}, u32[]{:S(2)}, u32[]{:S(2)}) %collective-permute-start.29) | collective-permute-done | bytes 294944 | tf_op jit(solution)/shard_map/ppermute | solution.py:1091
  1004.9 8.1 collective-permute-start.34
  1016.3 4.6 collective-permute-done.35
  (487 shorter events, 271.1 us)
Async XLA Ops:
  7.2 84.9 %all-gather.7.cloned.1.call-start = ((), (), s32[]{:S(2)}) async-start(), calls=%async_computation.28 | async-start | bytes 6488064 | tf_op jit(solution)/shard_map/all_gather | solution.py:751
  15.2 173.0 %all-gather.9.cloned.1.call-start = ((), (), s32[]{:S(2)}) async-start(), calls=%async_computation.29 | async-start | bytes 11894784 | tf_op jit(solution)/shard_map/all_gather | solution.py:751
  26.4 347.4 %all-gather.11.cloned.1.call-start = ((), (), s32[]{:S(2)}) async-start(), calls=%async_computation.30 | async-start | bytes 17301504 | tf_op jit(solution)/shard_map/all_gather | solution.py:751
  29.7 19.4 %collective-permute-start.1 = (bf16[384,768]{1,0:T(8,128)(2,1)S(1)}, bf16[384,768]{1,0:T(8,128)(2,1)S(1)}, u32[]{:S(2)}, u32[]{:S(2)}) collective-permute-start(bf16[384,768]{1,0:T(8,128)(2,1)S(1)} %pad_maximum_fusion.6.refs_0_), channel_id=1, source_target_pairs={{0,8},{4,12},{8,0},{12,4},{16,24},{20,28},{24,16},{28,20},{1,9},{5... | collective-permute-start | bytes 1769480 | tf_op jit(solution)/shard_map/ppermute | solution.py:798
  32.7 20.7 %collective-permute-start.3 = (bf16[384,768]{1,0:T(8,128)(2,1)S(1)}, bf16[384,768]{1,0:T(8,128)(2,1)S(1)}, u32[]{:S(2)}, u32[]{:S(2)}) collective-permute-start(bf16[384,768]{1,0:T(8,128)(2,1)S(1)} %pad_maximum_fusion.6.refs_0_), channel_id=1, source_target_pairs={{0,16},{4,20},{8,24},{12,28},{16,0},{20,4},{24,8},{28,12},{1,17},{... | collective-permute-start | bytes 1769480 | tf_op jit(solution)/shard_map/ppermute | solution.py:798
  34.3 31.3 %collective-permute-start.5 = (bf16[384,768]{1,0:T(8,128)(2,1)S(1)}, bf16[384,768]{1,0:T(8,128)(2,1)S(1)}, u32[]{:S(2)}, u32[]{:S(2)}) collective-permute-start(bf16[384,768]{1,0:T(8,128)(2,1)S(1)} %pad_maximum_fusion.6.refs_0_), channel_id=1, source_target_pairs={{0,24},{4,28},{8,16},{12,20},{16,8},{20,12},{24,0},{28,4},{1,25},{... | collective-permute-start | bytes 1769480 | tf_op jit(solution)/shard_map/ppermute | solution.py:798
  34.3 39.2 %collective-permute-start = (bf16[384,768]{1,0:T(8,128)(2,1)S(1)}, bf16[384,768]{1,0:T(8,128)(2,1)S(1)}, u32[]{:S(2)}, u32[]{:S(2)}) collective-permute-start(bf16[384,768]{1,0:T(8,128)(2,1)S(1)} %pad_maximum_fusion.6.refs_0_), channel_id=1, source_target_pairs={{0,4},{4,0},{8,12},{12,8},{16,20},{20,16},{24,28},{28,24},{1,5},{5... | collective-permute-start | bytes 1769480 | tf_op jit(solution)/shard_map/ppermute | solution.py:800
  49.1 24.4 %collective-permute-start.2 = (bf16[384,768]{1,0:T(8,128)(2,1)S(1)}, bf16[384,768]{1,0:T(8,128)(2,1)S(1)}, u32[]{:S(2)}, u32[]{:S(2)}) collective-permute-start(bf16[384,768]{1,0:T(8,128)(2,1)S(1)} %collective-permute-done.1.refs_2_), channel_id=1, source_target_pairs={{0,4},{4,0},{8,12},{12,8},{16,20},{20,16},{24,28},{28,24},{1,5},{5... | collective-permute-start | bytes 1769480 | tf_op jit(solution)/shard_map/ppermute | solution.py:800
  53.5 20.0 %collective-permute-start.4 = (bf16[384,768]{1,0:T(8,128)(2,1)S(1)}, bf16[384,768]{1,0:T(8,128)(2,1)S(1)}, u32[]{:S(2)}, u32[]{:S(2)}) collective-permute-start(bf16[384,768]{1,0:T(8,128)(2,1)S(1)} %collective-permute-done.3.refs_4_), channel_id=1, source_target_pairs={{0,4},{4,0},{8,12},{12,8},{16,20},{20,16},{24,28},{28,24},{1,5},{5... | collective-permute-start | bytes 1769480 | tf_op jit(solution)/shard_map/ppermute | solution.py:800
  104.0 20.6 %all-to-all-start = ((bf16[8,576,128]{2,1,0:T(8,128)(2,1)}), bf16[8,576,128]{2,1,0:T(8,128)(2,1)S(1)}, u32[]{:S(2)}, u32[]{:S(2)}) async-start(bf16[8,576,128]{2,1,0:T(8,128)(2,1)} %get-tuple-element.64), calls=%async_computation | async-start | bytes 2359296 | tf_op jit(solution)/shard_map/all_to_all | solution.py:734
  140.5 32.4 %all-to-all-start.4 = ((bf16[8,192,128]{2,1,0:T(8,128)(2,1)}), bf16[8,192,128]{2,1,0:T(8,128)(2,1)S(1)}, u32[]{:S(2)}, u32[]{:S(2)}) async-start(bf16[8,192,128]{2,1,0:T(8,128)(2,1)} %bitcast.17), calls=%async_computation.4 | async-start | bytes 786432 | tf_op jit(solution)/shard_map/all_to_all | solution.py:734
  172.9 27.2 %all-to-all-start.1 = ((bf16[8,384,128]{2,1,0:T(8,128)(2,1)}), bf16[8,384,128]{2,1,0:T(8,128)(2,1)S(1)}, u32[]{:S(2)}, u32[]{:S(2)}) async-start(bf16[8,384,128]{2,1,0:T(8,128)(2,1)} %bitcast.10), calls=%async_computation.1 | async-start | bytes 1572864 | tf_op jit(solution)/shard_map/all_to_all | solution.py:734
  200.1 20.4 %all-to-all-start.5 = ((bf16[8,192,384]{2,1,0:T(8,128)(2,1)}), bf16[8,192,384]{2,1,0:T(8,128)(2,1)S(1)}, u32[]{:S(2)}, u32[]{:S(2)}) async-start(bf16[8,192,384]{2,1,0:T(8,128)(2,1)} %copy-done.39), calls=%async_computation.5 | async-start | bytes 2359296 | tf_op jit(solution)/shard_map/all_to_all | solution.py:734
  220.6 44.6 %all-to-all-start.2 = ((bf16[8,384,384]{2,1,0:T(8,128)(2,1)}), bf16[8,384,384]{2,1,0:T(8,128)(2,1)S(1)}, u32[]{:S(2)}, u32[]{:S(2)}) async-start(bf16[8,384,384]{2,1,0:T(8,128)(2,1)} %copy-done.31), calls=%async_computation.2 | async-start | bytes 4718592 | tf_op jit(solution)/shard_map/all_to_all | solution.py:734
  254.5 50.2 %collective-permute-start.7 = (bf16[8,192,256]{2,1,0:T(8,128)(2,1)}, bf16[8,192,256]{2,1,0:T(8,128)(2,1)}, u32[]{:S(2)}, u32[]{:S(2)}) collective-permute-start(bf16[8,192,256]{2,1,0:T(8,128)(2,1)} %slice.178), channel_id=1, source_target_pairs={{0,1},{1,0},{2,3},{3,2},{4,5},{5,4},{6,7},{7,6},{8,9},{9,8},{10,11... | collective-permute-start | bytes 2359304 | tf_op jit(solution)/shard_map/ppermute | solution.py:747
  265.1 66.3 %all-to-all-start.7 = ((bf16[32,72,128]{2,1,0:T(8,128)(2,1)}), bf16[32,72,128]{2,1,0:T(8,128)(2,1)}, u32[]{:S(2)}, u32[]{:S(2)}) async-start(bf16[32,72,128]{2,1,0:T(8,128)(2,1)} %bitcast.269), calls=%async_computation.7 | async-start | bytes 1179648 | tf_op jit(solution)/shard_map/all_to_all | solution.py:742
  423.9 27.9 %all-to-all-start.8 = ((bf16[8,384,128]{2,1,0:T(8,128)(2,1)}), bf16[8,384,128]{2,1,0:T(8,128)(2,1)S(1)}, u32[]{:S(2)}, u32[]{:S(2)}) async-start(bf16[8,384,128]{2,1,0:T(8,128)(2,1)} %get-tuple-element.81), calls=%async_computation.8 | async-start | bytes 1572864 | tf_op jit(solution)/shard_map/all_to_all | solution.py:734
  427.5 158.7 %reduce-scatter.7.cloned.1.call-start = ((), (), s32[]{:S(2)}) async-start(), calls=%async_computation.25 | async-start | bytes 22413312 | tf_op jit(solution)/shard_map/reduce_scatter | solution.py:770
  455.1 81.3 %collective-permute-start.11 = (bf16[96,1024]{1,0:T(8,128)(2,1)S(1)}, bf16[96,1024]{1,0:T(8,128)(2,1)S(1)}, u32[]{:S(2)}, u32[]{:S(2)}) collective-permute-start(bf16[96,1024]{1,0:T(8,128)(2,1)S(1)} %get-tuple-element.194), channel_id=1, source_target_pairs={{0,1},{1,0},{2,3},{3,2},{4,5},{5,4},{6,7},{7,6},{8,9},{9,8},{10,11... | collective-permute-start | bytes 589832 | tf_op jit(solution)/shard_map/ppermute | solution.py:779
  455.2 81.2 %collective-permute-start.12 = (bf16[96,1024]{1,0:T(8,128)(2,1)S(1)}, bf16[96,1024]{1,0:T(8,128)(2,1)S(1)}, u32[]{:S(2)}, u32[]{:S(2)}) collective-permute-start(bf16[96,1024]{1,0:T(8,128)(2,1)S(1)} %get-tuple-element.193), channel_id=1, source_target_pairs={{0,2},{1,3},{2,0},{3,1},{4,6},{5,7},{6,4},{7,5},{8,10},{9,11},{10,... | collective-permute-start | bytes 589832 | tf_op jit(solution)/shard_map/ppermute | solution.py:779
  459.2 77.2 %collective-permute-start.13 = (bf16[96,1024]{1,0:T(8,128)(2,1)S(1)}, bf16[96,1024]{1,0:T(8,128)(2,1)}, u32[]{:S(2)}, u32[]{:S(2)}) collective-permute-start(bf16[96,1024]{1,0:T(8,128)(2,1)S(1)} %get-tuple-element.192), channel_id=1, source_target_pairs={{0,3},{1,2},{2,1},{3,0},{4,7},{5,6},{6,5},{7,4},{8,11},{9,10},{10,... | collective-permute-start | bytes 589832 | tf_op jit(solution)/shard_map/ppermute | solution.py:779
  460.3 174.1 %collective-permute-start.14 = (bf16[96,1024]{1,0:T(8,128)(2,1)}, bf16[96,1024]{1,0:T(8,128)(2,1)S(1)}, u32[]{:S(2)}, u32[]{:S(2)}) collective-permute-start(bf16[96,1024]{1,0:T(8,128)(2,1)} %get-tuple-element.213), channel_id=1, source_target_pairs={{0,0},{1,2},{2,1},{3,3},{4,4},{5,6},{6,5},{7,7},{8,8},{9,10},{10,9... | collective-permute-start | bytes 589832 | tf_op jit(solution)/shard_map/ppermute | solution.py:814
  461.9 172.5 %collective-permute-start.15 = (bf16[96,1024]{1,0:T(8,128)(2,1)}, bf16[96,1024]{1,0:T(8,128)(2,1)}, u32[]{:S(2)}, u32[]{:S(2)}) collective-permute-start(bf16[96,1024]{1,0:T(8,128)(2,1)} %get-tuple-element.212), channel_id=1, source_target_pairs={{0,1},{1,3},{2,0},{3,2},{4,5},{5,7},{6,4},{7,6},{8,9},{9,11},{10,8... | collective-permute-start | bytes 589832 | tf_op jit(solution)/shard_map/ppermute | solution.py:814
  466.3 124.3 %all-to-all-start.10 = ((bf16[32,72,128]{2,1,0:T(8,128)(2,1)}), bf16[32,72,128]{2,1,0:T(8,128)(2,1)S(1)}, u32[]{:S(2)}, u32[]{:S(2)}) async-start(bf16[32,72,128]{2,1,0:T(8,128)(2,1)} %bitcast.50), calls=%async_computation.10 | async-start | bytes 1179648 | tf_op jit(solution)/shard_map/all_to_all | solution.py:742
  470.8 373.1 %reduce-scatter.13.cloned.1.call-start = ((), (), s32[]{:S(2)}) async-start(), calls=%async_computation.31 | async-start | bytes 3112960
  590.6 48.4 %all-to-all-start.12 = ((bf16[8,384,384]{2,1,0:T(8,128)(2,1)}), bf16[8,384,384]{2,1,0:T(8,128)(2,1)S(1)}, u32[]{:S(2)}, u32[]{:S(2)}) async-start(bf16[8,384,384]{2,1,0:T(8,128)(2,1)} %bitcast.251), calls=%async_computation.12 | async-start | bytes 4718592 | tf_op jit(solution)/shard_map/all_to_all | solution.py:734
  632.9 28.2 %collective-permute-start.19 = (bf16[1536,256]{1,0:T(8,128)(2,1)}, bf16[1536,256]{1,0:T(8,128)(2,1)}, u32[]{:S(2)}, u32[]{:S(2)}) collective-permute-start(bf16[1536,256]{1,0:T(8,128)(2,1)} %slice.160), channel_id=1, source_target_pairs={{0,1},{1,0},{2,3},{3,2},{4,5},{5,4},{6,7},{7,6},{8,9},{9,8},{10,11... | collective-permute-start | bytes 2359304 | tf_op jit(solution)/shard_map/ppermute | solution.py:747
  673.7 39.6 %all-to-all-start.11 = ((bf16[8,192,384]{2,1,0:T(8,128)(2,1)}), bf16[8,192,384]{2,1,0:T(8,128)(2,1)S(1)}, u32[]{:S(2)}, u32[]{:S(2)}) async-start(bf16[8,192,384]{2,1,0:T(8,128)(2,1)} %bitcast.62), calls=%async_computation.11 | async-start | bytes 2359296 | tf_op jit(solution)/shard_map/all_to_all | solution.py:734
  677.3 274.6 %reduce-scatter.9.cloned.1.call-start = ((), (), s32[]{:S(2)}) async-start(), calls=%async_computation.26 | async-start | bytes 9437184 | tf_op jit(solution)/shard_map/reduce_scatter | solution.py:770
  758.3 23.8 %all-to-all-start.17 = ((bf16[8,192,256]{2,1,0:T(8,128)(2,1)}), bf16[8,192,256]{2,1,0:T(8,128)(2,1)S(1)}, u32[]{:S(2)}, u32[]{:S(2)}) async-start(bf16[8,192,256]{2,1,0:T(8,128)(2,1)} %bitcast.84.ka_ref), calls=%async_computation.18 | async-start | bytes 1572864 | tf_op jit(solution)/shard_map/all_to_all | solution.py:734
  782.1 65.3 %all-to-all-start.14 = ((bf16[8,192,128]{2,1,0:T(8,128)(2,1)}), bf16[8,192,128]{2,1,0:T(8,128)(2,1)S(1)}, u32[]{:S(2)}, u32[]{:S(2)}) async-start(bf16[8,192,128]{2,1,0:T(8,128)(2,1)} %get-tuple-element.95), calls=%async_computation.15 | async-start | bytes 786432 | tf_op jit(solution)/shard_map/all_to_all | solution.py:734
  797.8 43.9 %collective-permute-start.25 = (bf16[192,768]{1,0:T(8,128)(2,1)S(1)}, bf16[192,768]{1,0:T(8,128)(2,1)S(1)}, u32[]{:S(2)}, u32[]{:S(2)}) collective-permute-start(bf16[192,768]{1,0:T(8,128)(2,1)S(1)} %convolution_convert_fusion.1), channel_id=1, source_target_pairs={{0,1},{1,0},{2,3},{3,2},{4,5},{5,4},{6,7},{7,6},{8,9},{9,8},{10,11... | collective-permute-start | bytes 884744 | tf_op jit(solution)/shard_map/ppermute | solution.py:1091
  798.7 43.0 %collective-permute-start.26 = (bf16[192,768]{1,0:T(8,128)(2,1)S(1)}, bf16[192,768]{1,0:T(8,128)(2,1)S(1)}, u32[]{:S(2)}, u32[]{:S(2)}) collective-permute-start(bf16[192,768]{1,0:T(8,128)(2,1)S(1)} %convolution_convert_fusion.1), channel_id=1, source_target_pairs={{0,2},{1,3},{2,0},{3,1},{4,6},{5,7},{6,4},{7,5},{8,10},{9,11},{10,... | collective-permute-start | bytes 884744 | tf_op jit(solution)/shard_map/ppermute | solution.py:1091
  801.2 40.6 %collective-permute-start.27 = (bf16[192,768]{1,0:T(8,128)(2,1)S(1)}, bf16[192,768]{1,0:T(8,128)(2,1)S(1)}, u32[]{:S(2)}, u32[]{:S(2)}) collective-permute-start(bf16[192,768]{1,0:T(8,128)(2,1)S(1)} %convolution_convert_fusion.1), channel_id=1, source_target_pairs={{0,3},{1,2},{2,1},{3,0},{4,7},{5,6},{6,5},{7,4},{8,11},{9,10},{10,... | collective-permute-start | bytes 884744 | tf_op jit(solution)/shard_map/ppermute | solution.py:1091
  802.3 38.6 %collective-permute-start.21 = (bf16[96,1024]{1,0:T(8,128)(2,1)S(1)}, bf16[96,1024]{1,0:T(8,128)(2,1)S(1)}, u32[]{:S(2)}, u32[]{:S(2)}) collective-permute-start(bf16[96,1024]{1,0:T(8,128)(2,1)S(1)} %get-tuple-element.189), channel_id=1, source_target_pairs={{0,2},{1,3},{2,0},{3,1},{4,6},{5,7},{6,4},{7,5},{8,10},{9,11},{10,... | collective-permute-start | bytes 589832 | tf_op jit(solution)/shard_map/ppermute | solution.py:779
  803.8 37.0 %collective-permute-start.22 = (bf16[96,1024]{1,0:T(8,128)(2,1)S(1)}, bf16[96,1024]{1,0:T(8,128)(2,1)S(1)}, u32[]{:S(2)}, u32[]{:S(2)}) collective-permute-start(bf16[96,1024]{1,0:T(8,128)(2,1)S(1)} %get-tuple-element.188), channel_id=1, source_target_pairs={{0,3},{1,2},{2,1},{3,0},{4,7},{5,6},{6,5},{7,4},{8,11},{9,10},{10,... | collective-permute-start | bytes 589832 | tf_op jit(solution)/shard_map/ppermute | solution.py:779
  872.0 19.9 %collective-permute-start.38 = (bf16[192,128]{1,0:T(8,128)(2,1)S(1)}, bf16[192,128]{1,0:T(8,128)(2,1)S(1)}, u32[]{:S(2)}, u32[]{:S(2)}) collective-permute-start(bf16[192,128]{1,0:T(8,128)(2,1)S(1)} %get-tuple-element.206), channel_id=1, source_target_pairs={{5,0},{13,1},{21,2},{29,3},{1,4},{9,5},{17,6},{25,7},{4,8},{12,9},... | collective-permute-start | bytes 147464 | tf_op jit(solution)/shard_map/ppermute | solution.py:1115
  879.7 35.7 %collective-permute-start.40 = (bf16[192,128]{1,0:T(8,128)(2,1)S(1)}, bf16[192,128]{1,0:T(8,128)(2,1)S(1)}, u32[]{:S(2)}, u32[]{:S(2)}) collective-permute-start(bf16[192,128]{1,0:T(8,128)(2,1)S(1)} %get-tuple-element.204), channel_id=1, source_target_pairs={{7,0},{15,1},{23,2},{31,3},{3,4},{11,5},{19,6},{27,7},{6,8},{14,9}... | collective-permute-start | bytes 147464 | tf_op jit(solution)/shard_map/ppermute | solution.py:1115
  881.6 33.9 %collective-permute-start.41 = (bf16[192,128]{1,0:T(8,128)(2,1)S(1)}, bf16[192,128]{1,0:T(8,128)(2,1)S(1)}, u32[]{:S(2)}, u32[]{:S(2)}) collective-permute-start(bf16[192,128]{1,0:T(8,128)(2,1)S(1)} %get-tuple-element.200), channel_id=1, source_target_pairs={{0,0},{8,1},{16,2},{24,3},{4,4},{12,5},{20,6},{28,7},{1,8},{9,9},{... | collective-permute-start | bytes 147464 | tf_op jit(solution)/shard_map/ppermute | solution.py:1115
  882.2 34.2 %all-to-all-start.16 = ((bf16[8,192,128]{2,1,0:T(8,128)(2,1)}), bf16[8,192,128]{2,1,0:T(8,128)(2,1)S(1)}, u32[]{:S(2)}, u32[]{:S(2)}) async-start(bf16[8,192,128]{2,1,0:T(8,128)(2,1)} %bitcast.65.refs_1_), calls=%async_computation.17 | async-start | bytes 786432 | tf_op jit(solution)/shard_map/all_to_all | solution.py:734
  889.8 25.7 %collective-permute-start.42 = (bf16[192,128]{1,0:T(8,128)(2,1)S(1)}, bf16[192,128]{1,0:T(8,128)(2,1)S(1)}, u32[]{:S(2)}, u32[]{:S(2)}) collective-permute-start(bf16[192,128]{1,0:T(8,128)(2,1)S(1)} %get-tuple-element.203), channel_id=1, source_target_pairs={{1,0},{9,1},{17,2},{25,3},{5,4},{13,5},{21,6},{29,7},{0,8},{8,9},{... | collective-permute-start | bytes 147464 | tf_op jit(solution)/shard_map/ppermute | solution.py:1115
  891.9 23.6 %collective-permute-start.43 = (bf16[192,128]{1,0:T(8,128)(2,1)S(1)}, bf16[192,128]{1,0:T(8,128)(2,1)S(1)}, u32[]{:S(2)}, u32[]{:S(2)}) collective-permute-start(bf16[192,128]{1,0:T(8,128)(2,1)S(1)} %get-tuple-element.202), channel_id=1, source_target_pairs={{2,0},{10,1},{18,2},{26,3},{6,4},{14,5},{22,6},{30,7},{3,8},{11,9}... | collective-permute-start | bytes 147464 | tf_op jit(solution)/shard_map/ppermute | solution.py:1115
  895.6 19.9 %collective-permute-start.44 = (bf16[192,128]{1,0:T(8,128)(2,1)S(1)}, bf16[192,128]{1,0:T(8,128)(2,1)S(1)}, u32[]{:S(2)}, u32[]{:S(2)}) collective-permute-start(bf16[192,128]{1,0:T(8,128)(2,1)S(1)} %get-tuple-element.201), channel_id=1, source_target_pairs={{3,0},{11,1},{19,2},{27,3},{7,4},{15,5},{23,6},{31,7},{2,8},{10,9}... | collective-permute-start | bytes 147464 | tf_op jit(solution)/shard_map/ppermute | solution.py:1115
  947.5 55.3 %all-to-all-start.20 = ((bf16[8,128,1024]{2,1,0:T(8,128)(2,1)}), bf16[8,128,1024]{2,1,0:T(8,128)(2,1)}, u32[]{:S(2)}, u32[]{:S(2)}) async-start(bf16[8,128,1024]{2,1,0:T(8,128)(2,1)} %bitcast.108), calls=%async_computation.21 | async-start | bytes 4194304 | tf_op jit(solution)/shard_map/all_to_all | solution.py:734
  951.8 69.9 %reduce-scatter.11.cloned.1.call-start = ((), (), s32[]{:S(2)}) async-start(), calls=%async_computation.27 | async-start | bytes 1310720 | tf_op jit(solution)/shard_map/reduce_scatter | solution.py:790
  960.2 24.8 %collective-permute-start.28 = (bf16[192,768]{1,0:T(8,128)(2,1)S(1)}, bf16[192,768]{1,0:T(8,128)(2,1)S(1)}, u32[]{:S(2)}, u32[]{:S(2)}) collective-permute-start(bf16[192,768]{1,0:T(8,128)(2,1)S(1)} %convolution_convert_fusion), channel_id=1, source_target_pairs={{0,1},{1,0},{2,3},{3,2},{4,5},{5,4},{6,7},{7,6},{8,9},{9,8},{10,11... | collective-permute-start | bytes 884744 | tf_op jit(solution)/shard_map/ppermute | solution.py:1091
  960.6 36.9 %collective-permute-start.29 = (bf16[192,768]{1,0:T(8,128)(2,1)S(1)}, bf16[192,768]{1,0:T(8,128)(2,1)S(1)}, u32[]{:S(2)}, u32[]{:S(2)}) collective-permute-start(bf16[192,768]{1,0:T(8,128)(2,1)S(1)} %convolution_convert_fusion), channel_id=1, source_target_pairs={{0,2},{1,3},{2,0},{3,1},{4,6},{5,7},{6,4},{7,5},{8,10},{9,11},{10,... | collective-permute-start | bytes 884744 | tf_op jit(solution)/shard_map/ppermute | solution.py:1091
  963.0 35.7 %collective-permute-start.30 = (bf16[192,768]{1,0:T(8,128)(2,1)S(1)}, bf16[192,768]{1,0:T(8,128)(2,1)S(1)}, u32[]{:S(2)}, u32[]{:S(2)}) collective-permute-start(bf16[192,768]{1,0:T(8,128)(2,1)S(1)} %convolution_convert_fusion), channel_id=1, source_target_pairs={{0,3},{1,2},{2,1},{3,0},{4,7},{5,6},{6,5},{7,4},{8,11},{9,10},{10,... | collective-permute-start | bytes 884744 | tf_op jit(solution)/shard_map/ppermute | solution.py:1091
  (126 other events, 1285.7 us)
Sparse Core Ops, SparseCore 0:
  15.3 76.7 all-gather.6
  95.5 92.5 all-gather.8
  191.6 143.9 all-gather.10
  452.9 133.2 reduce-scatter.6
  590.7 51.2 reduce-scatter.12
  738.6 82.9 reduce-scatter.8
  955.1 42.7 reduce-scatter.10

commit v6 on v5

--- a/solution.py
+++ b/solution.py
@@ -169,6 +169,7 @@
 
 VM = pl.BlockSpec(memory_space=pltpu.VMEM)
 SM = pl.BlockSpec(memory_space=pltpu.SMEM)
+BRIEF = pl.CostEstimate(flops=10**6, bytes_accessed=10**5, transcendentals=0)
 AN = pl.BlockSpec(memory_space=pl.ANY)
 
 
@@ -201,9 +202,7 @@
         out_specs=(VM, VM),
         scratch_shapes=[pltpu.VMEM((hpd, total, LANES), bf16)] * 2,
         compiler_params=pltpu.CompilerParams(vmem_limit_bytes=44 * 2**20),
-        cost_estimate=pl.CostEstimate(
-            flops=1024 * work, bytes_accessed=16 * queries * hpd * HD, transcendentals=work
-        ),
+        cost_estimate=BRIEF,
     )(limits, *ins, *deps)
 
 
@@ -233,9 +232,7 @@
         + [pltpu.VMEM((hpd, queries, LANES), bf16)]
         + [pltpu.VMEM((hpd, total, LANES), f32)] * 2,
         compiler_params=pltpu.CompilerParams(vmem_limit_bytes=52 * 2**20),
-        cost_estimate=pl.CostEstimate(
-            flops=2560 * work, bytes_accessed=24 * queries * hpd * HD, transcendentals=work
-        ),
+        cost_estimate=BRIEF,
     )(limits, *ins, *deps)
 
 
@@ -316,9 +313,7 @@
             pl.BlockSpec((1, rows, 3 * W), lambda i: (i, 0, 0)),
         ),
         compiler_params=pltpu.CompilerParams(vmem_limit_bytes=40 * 2**20),
-        cost_estimate=pl.CostEstimate(
-            flops=8 * rows * D * D, bytes_accessed=8 * D * D + 14 * rows * D, transcendentals=0
-        ),
+        cost_estimate=BRIEF,
     )(a, x, norm, w_out[0], w_triple[0])
 
 
@@ -345,7 +340,6 @@
     d2_ref,
     e2_ref,
     da_ref,
-    db_ref,
     sum_ref,
     x2,
     d3,
@@ -403,8 +397,7 @@
         sum_ref[...] = jnp.concatenate([gain, shift], axis=0)
         da = dot(e2, flat(ws_ref), NT).astype(bf16)
         for i in range(S):
-            da_ref[i] = da[:R, i * W : (i + 1) * W]
-            db_ref[i] = da[R:, i * W : (i + 1) * W]
+            da_ref[i] = da[:, i * W : (i + 1) * W]
 
 
 def feed_forward(a, x1, cot, d_pix, norm, w_out, w_dec, w_up, w_down, hidden, steps):
@@ -429,8 +422,7 @@
             row,
             jax.ShapeDtypeStruct((total, D), f32),
             row,
-            jax.ShapeDtypeStruct((S, R, W), bf16),
-            jax.ShapeDtypeStruct((S, RB, W), bf16),
+            jax.ShapeDtypeStruct((S, total, W), bf16),
             jax.ShapeDtypeStruct((2, D), f32),
         ),
         in_specs=[
@@ -457,17 +449,12 @@
             full,
             full,
             full,
-            held((S, R, W)),
-            held((S, RB, W)),
+            held((S, total, W)),
             held((2, D)),
         ),
         scratch_shapes=[pltpu.VMEM((total, D), f32)] * 4,
         compiler_params=pltpu.CompilerParams(vmem_limit_bytes=60 * 2**20),
-        cost_estimate=pl.CostEstimate(
-            flops=8 * total * D * hidden + 8 * total * D * D,
-            bytes_accessed=4 * D * hidden + 30 * total * D,
-            transcendentals=total * hidden,
-        ),
+        cost_estimate=BRIEF,
     )(*a, *x1, *cot, d_pix, norm, w_out[0], w_dec[0], w_up[0], w_down[0])
 
 
@@ -482,7 +469,7 @@
         in_specs=[AN] * (1 + len(deps)),
         out_specs=AN,
         input_output_aliases={0: 0},
-        cost_estimate=pl.CostEstimate(flops=0, bytes_accessed=0, transcendentals=0),
+        cost_estimate=BRIEF,
     )(value, *deps)
 
 
@@ -545,16 +532,14 @@
         ),
         scratch_shapes=[pltpu.VMEM((rows, D), f32)],
         compiler_params=pltpu.CompilerParams(vmem_limit_bytes=40 * 2**20),
-        cost_estimate=pl.CostEstimate(
-            flops=8 * rows * D * D, bytes_accessed=8 * D * D + 24 * rows * D, transcendentals=0
-        ),
+        cost_estimate=BRIEF,
     )(t, x1, d2, norm, w_out[0], w_triple[0], *deps)
 
 
 def grads_kernel(*refs, shape, widths):
     count = sum(shape)
     lefts, rights = refs[:count], refs[count : 2 * count]
-    out_ref, turned = refs[2 * count], refs[2 * count + 1 :]
+    out_ref, turned = refs[-1 - count], refs[-count:]
 
     @pl.when(pl.program_id(0) == 0)
     def _():
@@ -571,7 +556,7 @@
         at, n = at + width, n + pieces
 
 
-def weight_grads(terms, ranks):
+def weight_grads(terms, ranks, deps=()):
     pieces = [p for term in terms for p in term]
     shape = [len(term) for term in terms]
     widths = [term[0][1].size // term[0][0].shape[0] // ranks for term in terms]
@@ -589,18 +574,17 @@
             if v.ndim == 3
             else pl.BlockSpec((v.shape[0], v.shape[1] // ranks), lambda i: (0, i))
             for v in rights
-        ],
+        ]
+        + [AN] * len(deps),
         out_specs=pl.BlockSpec((D, per), lambda i: (0, i)),
         scratch_shapes=[pltpu.VMEM(v.shape[::-1], bf16) for v in lefts],
         compiler_params=pltpu.CompilerParams(vmem_limit_bytes=56 * 2**20),
-        cost_estimate=pl.CostEstimate(
-            flops=2 * work, bytes_accessed=4 * D * per * ranks, transcendentals=0
-        ),
-    )(*lefts, *rights)
+        cost_estimate=BRIEF,
+    )(*lefts, *rights, *deps)
 
 
 def start_kernel(at_ref, xa_ref, xb_ref, norm_ref, wk_ref, wq_in, *refs, pieces, width):
-    p_in, (q_ref, k_ref, n_ref, wq_ref, wkv_ref) = refs[:pieces], refs[pieces:]
+    p_in, (q_ref, k_ref, n_ref, wq_ref, wkv_ref) = refs[:pieces], refs[-5:]
     seq = at_ref[0]
     R = xa_ref.shape[0]
     W = q_ref.shape[2]
@@ -615,7 +599,7 @@
         k_ref[seq ^ i] = dot(p_in[i][...], own, NT).astype(bf16)
 
 
-def start(at, x0, norm, w_kv, w_query, patch_pieces, W):
+def start(at, x0, norm, w_kv, w_query, patch_pieces, W, deps):
     S, D = len(patch_pieces), x0[0].shape[1]
     total = x0[0].shape[0] + x0[1].shape[0]
     slots, width = patch_pieces[0].shape
@@ -628,15 +612,12 @@
         in_specs=[SM]
         + [once(v) for v in whole]
         + [once(*w_kv[1]), once(*w_query[1])]
-        + [once((slots, width))] * S,
+        + [once((slots, width))] * S
+        + [AN] * len(deps),
         out_specs=tuple(held(v) for v in outs),
         compiler_params=pltpu.CompilerParams(vmem_limit_bytes=56 * 2**20),
-        cost_estimate=pl.CostEstimate(
-            flops=2 * total * D * D + 4 * S * slots * width * W,
-            bytes_accessed=6 * D * D + 12 * total * D,
-            transcendentals=0,
-        ),
-    )(at, *x0, norm, w_kv[0], w_query[0], *patch_pieces)
+        cost_estimate=BRIEF,
+    )(at, *x0, norm, w_kv[0], w_query[0], *patch_pieces, *deps)
 
 
 def finish_kernel(at_ref, ka_ref, kb_ref, *refs, pieces):
@@ -663,10 +644,193 @@
         in_specs=[SM] + [VM] * (2 + S),
         out_specs=VM,
         compiler_params=pltpu.CompilerParams(vmem_limit_bytes=32 * 2**20),
-        cost_estimate=pl.CostEstimate(
-            flops=13 * 10**8, bytes_accessed=8 * 10**6, transcendentals=0
-        ),
+        cost_estimate=BRIEF,
     )(at, *dkv, *patch_pieces)
+
+
+def end_kernel(
+    at_ref,
+    qa_ref,
+    b_ref,
+    ka_ref,
+    wq_ref,
+    wkv_ref,
+    xa_ref,
+    xb_ref,
+    n_ref,
+    da_ref,
+    db_ref,
+    small_ref,
+    gain_ref,
+    head_ref,
+    *refs,
+    ranks,
+):
+    outs_a, outs_b = refs[:ranks], refs[ranks : ranks + ranks // 2]
+    part_ref, pay_ref, n_t, dq = refs[ranks + ranks // 2 :]
+    S, R, W = qa_ref.shape
+    own = R // ranks
+    dq[:R, :] = joined(qa_ref)
+    dq[R:, :] = jnp.concatenate([b_ref[i, :, :W] for i in range(S)], axis=1)
+    n_t[...] = n_ref[...].T
+    back = dot(dq[...], wq_ref[...], NN)
+    gain = gain_ref[...]
+    got_a = norm_back(xa_ref[...].astype(f32), gain, back[:R])
+    got_b = norm_back(xb_ref[...].astype(f32), gain, back[R:])
+    da_ref[...] += got_a[0]
+    db_ref[...] += got_b[0]
+    for i in range(ranks):
+        rows = pl.ds(pl.multiple_of((at_ref[1] ^ i) * own, 8), own)
+        outs_a[i][...] = da_ref[rows, :].astype(bf16)
+    for i in range(ranks // 2):
+        rows = pl.ds(pl.multiple_of((at_ref[1] // 2 ^ i) * own, 8), own)
+        outs_b[i][...] = db_ref[rows, :].astype(bf16)
+    for i, keys in enumerate((joined(ka_ref), None)):
+        if keys is None:
+            keys = jnp.concatenate([b_ref[j, :, W:] for j in range(S)], axis=1)
+        part_ref[i] = dot(keys, wkv_ref[...], NN).astype(bf16)
+    rows = n_t.shape[0] // S
+    for i in range(0, S, 2):
+        pair = dot(n_t[...], dq[:, i * W : (i + 2) * W], NN).astype(bf16)
+        for j in range(S):
+            block = pair[j * rows : (j + 1) * rows, :]
+            pay_ref[j, i * rows : (i + 1) * rows, :] = block[:, :W]
+            pay_ref[j, (i + 1) * rows : (i + 2) * rows, :] = block[:, W:]
+    at = S * rows
+    heads = head_ref.shape[1]
+    lift = jnp.concatenate([got_a[1] + got_b[1], got_a[2] + got_b[2]], axis=0)
+    sums = jnp.concatenate([lift, small_ref[...], jnp.zeros((2, n_t.shape[0]), f32)], axis=0)
+    hi = sums.astype(bf16).astype(f32)
+    both = jnp.concatenate([hi, sums - hi], axis=0).astype(bf16)
+    for j in range(S):
+        pay_ref[j, at : at + heads, :] = head_ref[j]
+        pay_ref[j, at + heads :, :] = both[:, j * W : (j + 1) * W]
+
+
+def end(at, dq_a, both_b, dkv_a, w_query, w_kv, x0, n1, d1, small, gain, by_head, ranks):
+    S, R, W = dq_a.shape
+    RB = both_b.shape[1]
+    D, total = S * W, R + RB
+    own = R // ranks
+    slots, width = dkv_a.shape[1], w_kv.shape[1]
+    rows = D + by_head.shape[1] + 16
+    outs = [(own, D)] * (ranks + ranks // 2) + [(2, slots, width), (S, rows, W)]
+    whole = [dq_a, both_b, dkv_a, w_query, w_kv, *x0, n1, *d1, small, gain, by_head]
+    return pl.pallas_call(
+        functools.partial(end_kernel, ranks=ranks),
+        out_shape=tuple(jax.ShapeDtypeStruct(v, bf16) for v in outs),
+        in_specs=[SM] + [VM] * len(whole),
+        out_specs=(VM,) * len(outs),
+        scratch_shapes=[pltpu.VMEM((D, total), bf16), pltpu.VMEM((total, D), bf16)],
+        compiler_params=pltpu.CompilerParams(vmem_limit_bytes=56 * 2**20),
+        cost_estimate=BRIEF,
+    )(at, *whole)
+
+
+def mix_kernel(at_ref, x_ref, *outs, heads):
+    S, rows, W = x_ref.shape
+    blocks = rows - heads - 16
+    pair = blocks // len(outs)
+    small = sum(x_ref[j, blocks + heads :, :].astype(f32) for j in range(S))
+    total = small[:8] + small[8:]
+    hi = total.astype(bf16).astype(f32)
+    for i in range(len(outs)):
+        rank = at_ref[1] ^ i
+        src = pl.ds(pl.multiple_of(rank * pair, 16), pair)
+        outs[i][:pair, :] = sum(x_ref[j, src, :].astype(f32) for j in range(S)).astype(bf16)
+        for k in range(2):
+            outs[i][pair + k * heads : pair + (k + 1) * heads, :] = x_ref[
+                2 * rank + k, blocks : blocks + heads, :
+            ]
+        outs[i][pair + 2 * heads :, :] = jnp.concatenate([hi, total - hi], axis=0).astype(bf16)
+
+
+def mix(at, got, ranks, heads):
+    S, rows, W = got.shape
+    shape = ((rows - heads - 16) // ranks + 2 * heads + 16, W)
+    return pl.pallas_call(
+        functools.partial(mix_kernel, heads=heads),
+        out_shape=(jax.ShapeDtypeStruct(shape, bf16),) * ranks,
+        in_specs=[SM, VM],
+        out_specs=(VM,) * ranks,
+        compiler_params=pltpu.CompilerParams(vmem_limit_bytes=24 * 2**20),
+        cost_estimate=BRIEF,
+    )(at, got)
+
+
+def last_kernel(*refs, heads):
+    ins, (q_ref, k_ref, v_ref, small_ref) = refs[:-4], refs[-4:]
+    total = sum(v[...].astype(f32) for v in ins)
+    pair = total.shape[0] - 2 * heads - 16
+    q_ref[...] = jnp.concatenate([total[: pair // 2], total[pair // 2 : pair]], axis=1)
+    one, two = total[pair : pair + heads], total[pair + heads : pair + 2 * heads]
+    k_ref[...] = jnp.concatenate([one[: heads // 2], two[: heads // 2]], axis=1)
+    v_ref[...] = jnp.concatenate([one[heads // 2 :], two[heads // 2 :]], axis=1)
+    small_ref[...] = total[pair + 2 * heads : pair + 2 * heads + 8] + total[pair + 2 * heads + 8 :]
+
+
+def last(parts, heads):
+    rows, W = parts[0].shape
+    pair = rows - 2 * heads - 16
+    outs = [(pair // 2, 2 * W), (heads // 2, 2 * W), (heads // 2, 2 * W), (8, W)]
+    return pl.pallas_call(
+        functools.partial(last_kernel, heads=heads),
+        out_shape=tuple(jax.ShapeDtypeStruct(v, f32) for v in outs),
+        in_specs=[VM] * len(parts),
+        out_specs=(VM,) * 4,
+        compiler_params=pltpu.CompilerParams(vmem_limit_bytes=24 * 2**20),
+        cost_estimate=BRIEF,
+    )(*parts)
+
+
+def place_kernel(at_ref, *refs, ranks):
+    whole, halves, out_ref = refs[:ranks], refs[ranks:-1], refs[-1]
+    for i in range(ranks):
+        src = at_ref[1] ^ i
+        out_ref[3 * (src // 2) + 2 * (src % 2)] = whole[i][...].astype(out_ref.dtype)
+    for i in range(ranks // 2):
+        src = at_ref[1] % (ranks // 2) ^ i
+        out_ref[3 * src + 1] = halves[i][...].astype(out_ref.dtype)
+
+
+def place_rows(at, whole, halves, kind, deps=()):
+    ranks = len(whole)
+    shape = (3 * ranks // 2,) + whole[0].shape
+
+    def kernel(at_ref, *refs):
+        place_kernel(at_ref, *refs[: ranks + ranks // 2], refs[-1], ranks=ranks)
+
+    return pl.pallas_call(
+        kernel,
+        out_shape=jax.ShapeDtypeStruct(shape, kind),
+        in_specs=[SM] + [VM] * (ranks + ranks // 2) + [AN] * len(deps),
+        out_specs=VM,
+        compiler_params=pltpu.CompilerParams(vmem_limit_bytes=24 * 2**20),
+        cost_estimate=BRIEF,
+    )(at, *whole, *halves, *deps)
+
+
+def patches_kernel(at_ref, *refs):
+    ins, out_ref = refs[:-1], refs[-1]
+    pairs = len(ins) // 2
+    for i in range(pairs):
+        out_ref[3 * i + 1] = jnp.zeros(out_ref.shape[1:], f32)
+    for i in range(len(ins)):
+        src = at_ref[1] ^ i
+        out_ref[3 * (src // 2) + 2 * (src % 2)] = ins[i][0].astype(f32)
+        out_ref[3 * (src // 2) + 1] += ins[i][1].astype(f32)
+
+
+def place_patches(at, parts):
+    shape = (3 * len(parts) // 2,) + parts[0].shape[1:]
+    return pl.pallas_call(
+        patches_kernel,
+        out_shape=jax.ShapeDtypeStruct(shape, f32),
+        in_specs=[SM] + [VM] * len(parts),
+        out_specs=VM,
+        compiler_params=pltpu.CompilerParams(vmem_limit_bytes=24 * 2**20),
+        cost_estimate=BRIEF,
+    )(at, *parts)
 
 
 CP = 32
@@ -724,9 +888,7 @@
         out_specs=whole((out_rows, out_lanes)),
         scratch_shapes=[pltpu.VMEM((4, toks, ext), bf16)],
         compiler_params=pltpu.CompilerParams(vmem_limit_bytes=24 * 2**20),
-        cost_estimate=pl.CostEstimate(
-            flops=6 * 10**8, bytes_accessed=7 * 10**6, transcendentals=0
-        ),
+        cost_estimate=BRIEF,
     )(first, weights)
 
 
@@ -770,20 +932,18 @@
     return lax.psum_scatter(value, "seq", scatter_dimension=0, tiled=True)
 
 
-def from_ranks(blocks):
-    ranks, rank = lax.axis_size("mp"), lax.axis_index("mp")
-    got = []
-    for step in range(ranks):
-        block = lax.dynamic_index_in_dim(blocks, rank ^ step, 0, keepdims=False)
-        if step > 0:
-            block = lax.ppermute(block, "mp", [(i, i ^ step) for i in range(ranks)])
-        got.append(block)
-    return got
-
-
-def in_order(got, at):
-    got = jnp.stack(got)
-    return [lax.dynamic_index_in_dim(got, at ^ i, 0, keepdims=False) for i in range(got.shape[0])]
+def to_ranks(blocks):
+    moves = [[(i, i ^ step) for i in range(len(blocks))] for step in range(len(blocks))]
+    return [v if i == 0 else lax.ppermute(v, "mp", moves[i]) for i, v in enumerate(blocks)]
+
+
+def to_halves(blocks):
+    pairs = len(blocks)
+    arrived = []
+    for step in range(pairs):
+        moves = [(2 * p + h, pairs * h + (p ^ step)) for p in range(pairs) for h in range(2)]
+        arrived.append(lax.ppermute(blocks[step], "mp", moves))
+    return arrived
 
 
 def sum_ranks(value):
@@ -798,29 +958,6 @@
         pieces.append(value if step == 0 else lax.ppermute(value, "seq", moves))
     cores = [(i, i ^ 1) for i in range(shares)]
     return [p for piece in pieces for p in (piece, lax.ppermute(piece, "seq", cores))]
-
-
-def own_blocks(whole, blocks):
-    ranks, rank = lax.axis_size("mp"), lax.axis_index("mp")
-    pairs = ranks // 2
-    pair = rank // 2
-    own = whole.shape[0] // ranks
-    whole = in_order(from_ranks(whole.reshape(ranks, own, -1)), rank)
-    blocks = blocks.reshape(pairs, own, -1)
-    arrived = []
-    for step in range(pairs):
-        moves = [(2 * p + h, pairs * h + (p ^ step)) for p in range(pairs) for h in range(2)]
-        block = lax.dynamic_index_in_dim(blocks, pair ^ step, 0, keepdims=False)
-        arrived.append(lax.ppermute(block, "mp", moves))
-    arrived = in_order(arrived, rank % pairs)
-    rows = []
-    for p in range(pairs):
-        rows += [whole[2 * p], arrived[p], whole[2 * p + 1]]
-    return jnp.stack(rows)
-
-
-def to_rows(value):
-    return swap_seq(value).transpose(1, 0, 2).reshape(value.shape[1], -1)
 
 
 def per_device(
@@ -872,42 +1009,46 @@
     channels = decoder.shape[1]
     local_dec = jnp.pad(decoder.transpose(2, 1, 0), ((0, 0), (0, CP - channels), (0, 0)))
     local_qkv = self_qkv.reshape(D, 3, 2, W).transpose(2, 1, 3, 0).reshape(-1, D)
-    local_kv = cross_kv.reshape(width, 2, 2, W).transpose(2, 1, 3, 0).reshape(-1, width)
     per = D // (S * M)
     dec_rows = 4 * CP // S
     kv_rows = 2 * per
-    local_kv = jnp.pad(local_kv, ((0, 0), (0, D - width)))
-    lead = gather_rows(jnp.concatenate([mine(local_kv, 0), mine(cross_query, 1).T], axis=0))
+    at = s * kv_rows
+    kv_piece = lax.dynamic_slice(
+        cross_kv, (0, (at // W) % 2, at // (2 * W) * W + at % W), (width, 1, kv_rows)
+    )
+    kv_piece = jnp.pad(kv_piece[:, 0].T, ((0, 0), (0, D - width)))
+    lead = gather_rows(jnp.concatenate([kv_piece, mine(cross_query, 1).T], axis=0))
     w_kv, w_query = bundle_part(lead, 0, kv_rows), bundle_part(lead, kv_rows, per)
     first = gather_rows(
         jnp.concatenate(
+            [mine(local_qkv, 0), mine(cross_out, 0)], axis=0
+        )
+    )
+    up_rows = mlp_up.shape[1] // S
+    second = gather_rows(
+        jnp.concatenate(
             [
-                mine(local_qkv, 0),
-                mine(cross_out, 0),
+                mine(mlp_up, 1).T,
+                mine(mlp_down, 0),
                 mine(self_out, 0),
                 mine(local_dec.reshape(-1, D), 0),
             ],
             axis=0,
         )
     )
-    up_rows = mlp_up.shape[1] // S
-    second = gather_rows(jnp.concatenate([mine(mlp_up, 1).T, mine(mlp_down, 0)], axis=0))
     steps = 8
     w_up = by_step(bundle_part(second, 0, up_rows), steps)
     w_down = by_step(bundle_part(second, up_rows, up_rows), steps)
     w_triple = by_step(bundle_part(first, 0, 3 * per), S)
     w_cross_out = bundle_part(first, 3 * per, per)
-    w_self_out = bundle_part(first, 4 * per, per)
-    w_dec = bundle_part(first, 5 * per, dec_rows)
+    w_self_out = bundle_part(second, 2 * up_rows, per)
+    w_dec = bundle_part(second, 2 * up_rows + per, dec_rows)
 
     x0 = pick(tokens)
     norms = [jnp.stack([norm_gains[i], norm_shifts[i]]) for i in range(3)]
     at = jnp.stack([s, m])
     both = [lax.dynamic_index_in_dim(patches, o, 0, keepdims=False) for o in (at_a, at_b)]
     patch_pieces = gather_pieces(jnp.concatenate(both, axis=0))
-    q1, keys_one, n1, w_query, w_kv = start(at, x0, norms[0], w_kv, w_query, patch_pieces, W)
-    heads_one = swap_seq(q1)
-
     TC = PLANE // 4
     TR = PLANE * 4 // S
     own, rim = TR * TC, TR * TC + TR
@@ -935,8 +1076,13 @@
     gp_a = jnp.stack([grad_pix[:, 0], grad_pix[:, 2]], axis=1).transpose(2, 0, 1, 3, 4)
     gp_b = grad_pix[:, 1].reshape(pairs, S, 2, KB, cu).transpose(1, 0, 2, 3, 4)
     sent = jnp.concatenate([gp_a, gp_b], axis=3).reshape(S * M, KA + KB, cu)
-    back = swap_all(sent).reshape(S, M, KA + KB, cu).transpose(2, 0, 1, 3)
-    d_pix = back.reshape(RS, M * cu)
+
+    q1, keys_one, n1, w_query, w_kv = start(
+        at, x0, norms[0], w_kv, w_query, patch_pieces, W, [sent]
+    )
+    heads_one = swap_seq(q1)
+    back = swap_all(hold(sent, [heads_one]))
+    d_pix = back.reshape(S, M, KA + KB, cu).transpose(2, 0, 1, 3).reshape(RS, M * cu)
 
     limits = [
         jnp.stack([lax.dynamic_index_in_dim(counts, o, 0, keepdims=False), jnp.int32(0)])
@@ -954,6 +1100,7 @@
             slot_total,
             hpd,
             False,
+            [(back,), ()][i],
         )
         o1.append(out)
         res1.append(res)
@@ -984,10 +1131,11 @@
         True,
         [o_a2],
     )
-    a2 = [swap_seq(o_a2.reshape(S, R, W)), swap_seq(o_b2.reshape(S, RB, W))]
+    a2_a = swap_seq(o_a2.reshape(S, R, W))
+    a2 = [a2_a, swap_seq(hold(o_b2.reshape(S, RB, W), [a2_a]))]
 
     hidden = mlp_up.shape[1] * M
-    n3, a2, g, du, x3b, pix, e3, d2, e2, da2_a, da2_b, sums_three = feed_forward(
+    n3, a2, g, du, x3b, pix, e3, d2, e2, da2, sums_three = feed_forward(
         a2,
         x1,
         pick(tokens_cot),
@@ -1001,13 +1149,13 @@
         steps,
     )
 
-    da2 = [swap_seq(da2_a), swap_seq(da2_b)]
+    da2 = swap_seq(da2)
     grads_one = weight_grads([[(n3, du)], [(e3, g)], [(e2, a2)], [(x3b, d_pix)]], M)
-    grads_one = hold(grads_one, da2)
-    x3b, pix = hold(x3b, [grads_one]), hold(pix, [grads_one])
+    grads_one = hold(grads_one, [da2])
+    pix = hold(pix, [grads_one])
     dq_a2, dkv_a2 = attend_back(
         wide,
-        [res_a2, da2[0], o_a2, heads_two[0]],
+        [res_a2, da2, o_a2, heads_two[0]],
         S,
         (R, 0),
         [(3,) + kv_a2],
@@ -1017,26 +1165,40 @@
         [grads_one],
     )
     grads_one = reduce_rows(grads_one)
-    tokens_out = own_blocks(x3b[:R], x3b[R:])
     pix = pix.reshape(KA + KB, S, M, cu).transpose(1, 2, 0, 3)
     got = swap_all(pix.reshape(S * M, KA + KB, cu)).reshape(S, pairs, 2, KA + KB, cu)
-    dq_b2, dkv_b2 = attend_back(
+    half_total = row_total // 2
+    kv_p2 = (RB, (0, 0), (0, W), 0)
+    dq_p2, dkv_p2 = attend_back(
         wide,
-        [res_b2, da2[1], o_b2, heads_two[1], pair_kv],
+        [res_b2, da2, o_b2, pair_kv],
         S,
-        (RB, 0),
-        [(3,) + kv_b2, (4,) + kv_p2],
-        row_total,
+        (RB, R),
+        [(3,) + kv_p2],
+        half_total,
         hpd,
         True,
         [dq_a2, got],
     )
-    kept, given = dkv_b2[: row_total // 2], dkv_b2[row_total // 2 :]
-    dkv_b2 = (kept.astype(f32) + swap_pair(given).astype(f32)).astype(bf16)
+    given = swap_pair(dkv_p2)
+    dq_b2, dkv_b2 = attend_back(
+        wide,
+        [res_b2, da2, o_b2, heads_two[1]],
+        S,
+        (RB, R),
+        [(3,) + kv_b2],
+        half_total,
+        hpd,
+        True,
+        [dq_p2],
+    )
+    dq_b2 = (dq_b2.astype(f32) + dq_p2.astype(f32)).astype(bf16)
+    dkv_b2 = (dkv_b2.astype(f32) + given.astype(f32)).astype(bf16)
     dt2 = [
         swap_seq(jnp.concatenate([dq_a2, dkv_a2], axis=1).reshape(S, R, 3 * W)),
-        swap_seq(jnp.concatenate([dq_b2, dkv_b2], axis=1).reshape(S, RB, 3 * W)),
+        jnp.concatenate([dq_b2, dkv_b2], axis=1).reshape(S, RB, 3 * W),
     ]
+
     def below(i, deps):
         return middle_back(
             dt2[i], x1[i], d2, (0, R // RB)[i], norms[1], w_cross_out, w_triple, deps
@@ -1056,18 +1218,56 @@
         )
         return dq.reshape(S, rows[i], W), dkv.reshape(S, slots, 2 * W)
 
-    low_a = below(0, [])
-    cross_a = cross_back(0, swap_seq(low_a[2]), [grads_one, tokens_out])
-    grads_one = sum_ranks(grads_one)
-    low_b = below(1, [cross_a[0]])
+    low_a = below(0, [dq_b2])
+    x3b = hold(x3b, [low_a[0]])
+    blocks_a, blocks_b = x3b[:R].reshape(M, R // M, D), x3b[R:].reshape(pairs, R // M, D)
+    blocks_a = [lax.dynamic_index_in_dim(blocks_a, m ^ i, 0, keepdims=False) for i in range(M)]
+    blocks_b = [
+        lax.dynamic_index_in_dim(blocks_b, pair ^ i, 0, keepdims=False) for i in range(pairs)
+    ]
+    blocks_a, blocks_b = to_ranks(blocks_a), to_halves(blocks_b)
+    da1_a = swap_seq(low_a[2])
+    dt2[1] = swap_seq(hold(dt2[1], [da1_a]))
+    dq1_a, dkv1_a = cross_back(0, da1_a, [])
+    grads_one = sum_ranks(hold(grads_one, [low_a[0]]))
+    low_b = below(1, [dkv1_a])
+    da1_b = swap_seq(low_b[2])
+    dq1_a = swap_seq(hold(dq1_a, [da1_b]))
+    dkv1_a_rows = swap_seq(hold(dkv1_a, [da1_b]))
     d1, e1, da1, sums_two = zip(low_a, low_b)
 
     grads_two = weight_grads(
-        [[(n2[i], dt2[i]) for i in range(2)], [(e1[i], a1[i]) for i in range(2)]], M
-    )
-    cross_b = cross_back(1, swap_seq(da1[1]), [grads_two, grads_one])
-    dq1, dkv1 = zip(cross_a, cross_b)
+        [[(n2[i], dt2[i]) for i in range(2)], [(e1[i], a1[i]) for i in range(2)]], M, [grads_one] + blocks_a + blocks_b
+    )
+    dq1_b, dkv1_b = cross_back(1, da1_b, [grads_two])
+    dkv1 = (dkv1_a, dkv1_b)
     grads_two = reduce_rows(grads_two)
+    both_b = swap_seq(jnp.concatenate([dq1_b, dkv1_b], axis=2))
+    two = sums_two[0] + sums_two[1]
+    small = jnp.concatenate([two, sums_three], axis=0)
+    by_head = finish(at, dkv1, patch_pieces)
+    done = end(
+        at,
+        dq1_a,
+        both_b,
+        dkv1_a_rows,
+        w_query,
+        w_kv,
+        x0,
+        n1,
+        d1,
+        small,
+        norm_gains[:1],
+        by_head,
+        M,
+    )
+    got_last = swap_seq(done[-1])
+    grad_tokens = place_rows(at, to_ranks(done[:M]), to_halves(done[M : M + pairs]), f32)
+    patch_grad = place_patches(at, to_ranks([done[-2]] * M))
+    heads = by_head.shape[1]
+    final = last(to_ranks(mix(at, got_last, M, heads)), heads)
+    grad_cross_query, grad_keys, grad_values, small = final
+    grad_cross_kv = jnp.stack([grad_keys, grad_values], axis=1)
 
     px_a = got[:, :, :, :KA].transpose(1, 2, 0, 3, 4).reshape(pairs, 2, S * KA, cu)
     px_b = got[:, :, :, KA:].transpose(1, 0, 2, 3, 4).reshape(pairs, S * KA, cu)
@@ -1077,51 +1277,12 @@
     corner = lax.ppermute(tile[:, 0, :1], "seq", [(i + 5, i) for i in ways[5]])
     fill = jnp.zeros((planes, toks - rim - TC - 1, cu), bf16)
     ext = jnp.concatenate([tile.reshape(planes, own, cu), rights, belows, corner, fill], axis=1)
-    ext = hold(ext, [dq1[1]])
+    ext = hold(ext, [done[-1]])
+    tokens_out = place_rows(at, blocks_a, blocks_b, bf16, [done[-1]])
     sampled = per_plane(
         pixel_sample_kernel, ext, weights_in, CP, weights_in.shape[2], bf16, toks, TR, TC
     )
     sampled = sampled[:, :channels].reshape(objects, 3, channels, 1, -1)
-
-    parts = [mm(to_rows(v), w_kv).astype(bf16) for v in dkv1]
-    every = [[p] for p in parts]
-    for step in range(1, M):
-        moves = [(i, i ^ step) for i in range(M)]
-        for i in range(2):
-            every[i].append(lax.ppermute(parts[i], "mp", moves))
-    from_a, from_b = [in_order(v, m) for v in every]
-    patch_grad = []
-    for p in range(pairs):
-        shared = from_b[2 * p].astype(f32) + from_b[2 * p + 1].astype(f32)
-        patch_grad += [from_a[2 * p].astype(f32), shared, from_a[2 * p + 1].astype(f32)]
-    patch_grad = jnp.stack(patch_grad)
-
-    dq1 = [to_rows(v) for v in dq1]
-    grads = [mm(v, w_query) for v in dq1]
-    back_one = [norm_back(x0[i].astype(f32), norm_gains[0], grads[i]) for i in range(2)]
-    d0 = [(d1[i] + back_one[i][0]).astype(bf16) for i in range(2)]
-    grad_tokens = own_blocks(d0[0], d0[1]).astype(f32)
-
-    order = 2 * m + s % 2
-    by_head = finish(at, dkv1, patch_pieces)
-    sums = [0.0, 0.0]
-    for step in range(S):
-        moves = []
-        for i in range(S):
-            for j in range(M):
-                t = i ^ step
-                moves.append(((2 * j + t % 2) * M + t // 2, i * M + j))
-        piece = lax.dynamic_index_in_dim(by_head, order ^ step, 0, keepdims=False)
-        sums[step % 2] += lax.ppermute(piece, ("seq", "mp"), moves).astype(f32)
-    swap = s % 2 == 1
-    owned = jnp.concatenate(
-        [jnp.where(swap, sums[1], sums[0]), jnp.where(swap, sums[0], sums[1])], axis=1
-    )
-    grad_cross_kv = owned.reshape(2, width // S, 2 * W).transpose(1, 0, 2)
-    grad_q = dot(n1[:R], dq1[0], TN) + dot(n1[R:], dq1[1], TN)
-    grad_q = swap_seq(grad_q.astype(bf16).reshape(S, D // S, D))
-    grad_q = jnp.sum(grad_q.astype(f32), axis=0).astype(bf16).reshape(D // S, M, -1)
-    grad_cross_query = sum(v.astype(f32) for v in from_ranks(grad_q.transpose(1, 0, 2)))
 
     grads_two = sum_ranks(grads_two)
     ff = hidden // M
@@ -1132,21 +1293,13 @@
     grad_self_qkv = grads_two[:, : 3 * D // M].reshape(D // S, 2, 3, W).transpose(0, 2, 1, 3)
     grad_cross_out = grads_two[:, 3 * D // M :].T
 
-    one = [back_one[0][i] + back_one[1][i] for i in (1, 2)]
-    two = sums_two[0] + sums_two[1]
-    small = jnp.concatenate(
-        [one[0], two[:1], sums_three[:1], one[1], two[1:], sums_three[1:]], axis=0
-    )
-    small = jnp.sum(swap_seq(small.reshape(6, S, D // S).transpose(1, 0, 2)), axis=0)
-    small = sum(from_ranks(jnp.broadcast_to(small, (M,) + small.shape)))
-
     return (
         tokens_out,
         sampled,
         grad_tokens,
         patch_grad,
-        small[:3],
-        small[3:5],
+        jnp.stack([small[0], small[2], small[4]]),
+        jnp.stack([small[1], small[3]]),
         small[5],
         grad_cross_query,
         grad_cross_kv,

time: 1040 us -> 950 us (0.913)
  starting transfers between devices: 163 us -> 123 us
  waiting for transfers between devices: 256 us -> 235 us
  other arithmetic: 35.8 us -> 17.2 us
  matrix products: 16.5 us -> 0 us
  Pallas kernels: 396 us -> 407 us
    ppermute x2, waiting for transfers between devices: 0.01 us -> 38.6 us  [swap_pair(): return lax.ppermute(value, 'mp', [(i, i ^ 1) for i in range(count)])]
    ppermute x3, waiting for transfers between devices: 30.6 us -> 0.01 us  [gather_pieces(): pieces.append(value if step == 0 else lax.ppermute(value, 'seq', moves))]
    ppermute x30 -> x16, starting transfers between devices: 55.7 us -> 30.1 us  [the longest x12 21.1 us: to_ranks(): lax.ppermute(v, 'mp', moves[i])]
    reduce_scatter x2, waiting for transfers between devices: 47.2 us -> 21.6 us  [reduce_rows(): return lax.psum_scatter(value, 'seq', scatter_dimension=0, tiled=True)]
    pallas_call x0 -> x6, Pallas kernels: none -> 24.5 us  [the longest x1 12.2 us: end(): pl.pallas_call(functools.partial(end_kernel, ranks=ranks), out_shape=tupl...]
    dot_general x6 -> x0, matrix products: 16.5 us -> none  [the longest x2 8.57 us: dot(): return lax.dot_general(a, b, dims, preferred_element_type=f32)]
    all_to_all x17 -> x14, starting transfers between devices: 74.7 us -> 59 us  [swap_seq(): return lax.all_to_all(value, 'seq', split_axis=0, concat_axis=0, tiled=True)]
    all_to_all x17 -> x14, waiting for transfers between devices: 56.3 us -> 69.1 us  [swap_seq(): return lax.all_to_all(value, 'seq', split_axis=0, concat_axis=0, tiled=True)]
  transfers between devices with their start and end apart: 71 -> 54, of which waited for: 24 -> 21; matrix products, arithmetic and copies ran while one was open for 11% -> 7% of each run, Pallas kernels for 35% -> 38%
where the time goes in v6:
time: 950 us; the launch traced here: 934 us
  Pallas kernels  407 us (43%)
  waiting for transfers between devices  235 us (25%)
  starting transfers between devices  123 us (13%)
  local copies, waits for them, and re-layouts  102 us (11%)
  blocking collectives  34.3 us (4%)
  other arithmetic  17.2 us (2%)
  between operations  15.9 us (2%)
    pallas_call x5, Pallas kernels, attend_back(): pl.pallas_call(body, out_shape=(jax.ShapeDtypeStruct((queries, hpd * HD),...  147 us
    pallas_call x4, Pallas kernels, attend(): pl.pallas_call(body, out_shape=(jax.ShapeDtypeStruct((queries, hpd * HD),...  84 us
    all_to_all x14, waiting for transfers between devices, swap_seq(): return lax.all_to_all(value, 'seq', split_axis=0, concat_axis=0, tiled=True)  69.1 us
    ppermute x12, waiting for transfers between devices, to_ranks(): lax.ppermute(v, 'mp', moves[i])  60.6 us
    all_to_all x14, starting transfers between devices, swap_seq(): return lax.all_to_all(value, 'seq', split_axis=0, concat_axis=0, tiled=True)  59 us
    unnamed x191, local copies, waits for them, and re-layouts  57.7 us
    ppermute x2, waiting for transfers between devices, swap_pair(): return lax.ppermute(value, 'mp', [(i, i ^ 1) for i in range(count)])  38.6 us
    pallas_call x1, Pallas kernels, feed_forward(): pl.pallas_call(functools.partial(mlp_kernel, steps=steps), grid=(steps,),...  36.9 us
  transfers between devices with their start and end apart: 54, of which 21 were waited for; matrix products, arithmetic and copies ran while one was open for 7% of the time, Pallas kernels for 38%

profile of v6, /device:TPU:0, one launch (start us, length us, event | category | flops | bytes accessed | tf_op | source)
XLA Modules:
  0.0 934.1 jit_solution(18136292354612963178)
XLA Ops:
  15.3 4.9 copy.118
  34.3 15.2 %shard_map.280 = f32[18,160,128]{2,1,0:T(8,128)S(1)} custom-call(bf16[18,32,256]{2,1,0:T(8,128)(2,1)S(1)} %pad.21.cot_ref, bf16[18,561,256]{2,1,0:T(8,128)(2,1)S(1)} %bitcast.130), custom_call_target="tpu_custom_call" | custom-call | flops 1000000 | bytes 100000 | tf_op jit(solution)/shard_map/pallas_call | solution.py:883
  66.1 5.7 collective-permute-start.2
  75.9 12.7 %all-gather.7.cloned.1.call-done = bf16[3072,1024]{1,0:T(8,128)(2,1)} async-done(((bf16[96,1024]{1,0:T(8,128)(2,1)}), bf16[3072,1024]{1,0:T(8,128)(2,1)}) %all-gather.7.cloned.1.call-update) | async-done | bytes 6291472 | tf_op jit(solution)/shard_map/all_gather | solution.py:913
  88.6 11.8 %shard_map.281 = (bf16[8,576,128]{2,1,0:T(8,128)(2,1)}, bf16[8,384,256]{2,1,0:T(8,128)(2,1)}, bf16[576,1024]{1,0:T(8,128)(2,1)}, bf16[1024,1024]{1,0:T(8,128)(2,1)}, bf16[2048,768]{1,0:T(8,128)(2,1)}) custom-call(s32[2]{0:T(128)} %pad_add_fusion.2.at_ref, bf16[384,1024]{1,0:T(8,128)(2,1)} %dynamic-slice_bitcast_fusion.1.xa_ref.x_ref, ...), custom_call_target="tpu_custom_call" | custom-call | flops 1000000 | bytes 100000 | tf_op jit(solution)/shard_map/pallas_call | solution.py:608
  100.5 22.1 %all_to_all.90.refs_1_.refs_0_ = bf16[8,576,128]{2,1,0:T(8,128)(2,1)} all-to-all(bf16[8,576,128]{2,1,0:T(8,128)(2,1)} %get-tuple-element.81), channel_id=1, replica_groups=mesh['seq'=8,'mp'=4] {'seq'}, dimensions={0} | all-to-all | bytes 2359296 | tf_op jit(solution)/shard_map/all_to_all | solution.py:896
  127.4 15.0 %shard_map.286 = (bf16[1536,128]{1,0:T(8,128)(2,1)}, bf16[2,1536,128]{2,1,0:T(8,128)(2,1)S(1)}) custom-call(s32[2]{0:T(128)S(1)} %pad_add_fusion.n_ref, bf16[8,576,128]{2,1,0:T(8,128)(2,1)S(1)} %copy-done.7, bf16[8,384,256]{2,1,0:T(8,128)(2,1)S(1)} %copy-done.3), custom_call_target="tpu_custom_call" | custom-call | flops 1000000 | bytes 100000 | tf_op jit(solution)/shard_map/pallas_call | solution.py:195
  146.2 3.9 all-to-all-start.5
  150.8 20.0 %shard_map.283 = (bf16[3072,128]{1,0:T(8,128)(2,1)S(1)}, bf16[2,3072,128]{2,1,0:T(8,128)(2,1)S(1)}) custom-call(s32[2]{0:T(128)S(1)} %pad_add_fusion.1.n_ref, bf16[8,576,128]{2,1,0:T(8,128)(2,1)S(1)} %copy-done.7, bf16[8,384,256]{2,1,0:T(8,128)(2,1)S(1)} %copy-done.3, bf16[32,72,128]{2,1,0:T(8,128)(2,1)} %all-to-all-done.1.refs_2_), custom_call_target="tpu_custom_call" | custom-call | flops 1000000 | bytes 100000 | tf_op jit(solution)/shard_map/pallas_call | solution.py:195
  172.9 4.3 all-to-all-start.2
  185.1 5.1 shard_map.287
  198.4 9.9 %shard_map.284 = (f32[384,1024]{1,0:T(8,128)S(1)}, bf16[384,1024]{1,0:T(8,128)(2,1)S(1)}, bf16[384,1024]{1,0:T(8,128)(2,1)S(1)}, bf16[8,384,384]{2,1,0:T(8,128)(2,1)S(1)}) custom-call(bf16[8,384,128]{2,1,0:T(8,128)(2,1)S(1)} %all-to-all-done.2.a_ref, bf16[384,1024]{1,0:T(8,128)(2,1)S(1)} %copy-done.10, f32[2,1024]{1,0:T(2,128)S(1)} %pad_maximum_fusion.11.norm_ref, ...), custom_call_target="tpu_custom_call" | custom-call | flops 1000000 | bytes 100000 | tf_op jit(solution)/shard_map/pallas_call | solution.py:293
  214.0 4.4 all-to-all-start.3
  220.9 38.4 %all-to-all-done.3.refs_0_.refs_3_ = bf16[8,384,384]{2,1,0:T(8,128)(2,1)} async-done(((bf16[8,384,384]{2,1,0:T(8,128)(2,1)}), bf16[8,384,384]{2,1,0:T(8,128)(2,1)}, u32[]{:S(2)}, u32[]{:S(2)}) %all-to-all-start.3) | async-done | bytes 2359328 | tf_op jit(solution)/shard_map/all_to_all | solution.py:896
  259.3 31.7 %shard_map.285 = (bf16[3072,128]{1,0:T(8,128)(2,1)}, bf16[2,3072,128]{2,1,0:T(8,128)(2,1)S(1)}) custom-call(s32[2]{0:T(128)S(1)} %copy-done.71, bf16[8,384,384]{2,1,0:T(8,128)(2,1)} %all-to-all-done.3.refs_0_.refs_3_), custom_call_target="tpu_custom_call" | custom-call | flops 1000000 | bytes 100000 | tf_op jit(solution)/shard_map/pallas_call | solution.py:195
  291.0 4.4 all-to-all-start.4
  295.5 17.2 %shard_map.288 = (bf16[1536,128]{1,0:T(8,128)(2,1)S(1)}, bf16[2,1536,128]{2,1,0:T(8,128)(2,1)S(1)}) custom-call(s32[2]{0:T(128)S(1)} %copy-done.71, bf16[8,192,384]{2,1,0:T(8,128)(2,1)S(1)} %all-to-all-done.6.refs_0_.refs_3_, bf16[8,192,256]{2,1,0:T(8,128)(2,1)} %collective-permute-done.10.refs_1_.refs_3_, bf16[3072,128]{1,0:T(8,128)(2,1)} %get-tuple-element.85.refs_2_), custom_call_target="tpu_custom_call" | custom-call | flops 1000000 | bytes 100000 | tf_op jit(solution)/shard_map/pallas_call | solution.py:195
  314.4 4.2 all-to-all-start.7
  330.6 36.9 %shard_map.290 = (bf16[576,1024]{1,0:T(8,128)(2,1)}, bf16[576,1024]{1,0:T(8,128)(2,1)}, bf16[576,4096]{1,0:T(8,128)(2,1)}, bf16[576,4096]{1,0:T(8,128)(2,1)}, bf...) custom-call(bf16[8,384,128]{2,1,0:T(8,128)(2,1)} %all-to-all-done.4., ...), custom_call_target="tpu_custom_call" | custom-call | flops 1000000 | bytes 100000 | tf_op jit(solution)/shard_map/pallas_call | solution.py:412
  367.5 6.0 all-to-all-start.8
  374.0 24.1 %shard_map.291.refs_0_ = bf16[1024,9728]{1,0:T(8,128)(2,1)} custom-call(bf16[576,1024]{1,0:T(8,128)(2,1)} %get-tuple-element.94.refs_0_, bf16[576,1024]{1,0:T(8,128)(2,1)} %get-tuple-element.95.refs_1_, bf16[576,1024]{1,0:T(8,128)(2,1)} %get-tuple-element.96.refs_2_, bf16[576,1024]{1,0:T(8,128)(2,1)} %get-tuple-element.91.refs_3_.refs_0_, ...), custom_call_target="tpu_custom_call" | custom-call | flops 1000000 | bytes 100000 | tf_op jit(solution)/shard_map/pallas_call | solution.py:567
  401.2 4.6 all-to-all-start.10
  405.9 62.5 %shard_map.293 = (bf16[3072,128]{1,0:T(8,128)(2,1)S(1)}, bf16[3072,256]{1,0:T(8,128)(2,1)}) custom-call(s32[2]{0:T(128)S(1)} %copy-done.71, bf16[2,3072,128]{2,1,0:T(8,128)(2,1)} %copy-done.40, bf16[8,576,128]{2,1,0:T(8,128)(2,1)} %copy-done.72, bf16[3072,128]{1,0:T(8,128)(2,1)} %get-tuple-element.85.refs_2_, ...), custom_call_target="tpu_custom_call" | custom-call | flops 1000000 | bytes 100000 | tf_op jit(solution)/shard_map/pallas_call | solution.py:223
  471.8 4.4 all-to-all-start.9
  476.5 20.4 %shard_map.295 = (bf16[1536,128]{1,0:T(8,128)(2,1)S(1)}, bf16[1536,256]{1,0:T(8,128)(2,1)}) custom-call(s32[2]{0:T(128)S(1)} %copy-done.71, bf16[2,1536,128]{2,1,0:T(8,128)(2,1)} %copy-done.25, bf16[8,576,128]{2,1,0:T(8,128)(2,1)} %copy-done.72, bf16[1536,128]{1,0:T(8,128)(2,1)S(1)} %get-tuple-element.88.refs_2_, ...), custom_call_target="tpu_custom_call" | custom-call | flops 1000000 | bytes 100000 | tf_op jit(solution)/shard_map/pallas_call | solution.py:223
  496.8 19.4 %shard_map.296 = (bf16[1536,128]{1,0:T(8,128)(2,1)S(1)}, bf16[1536,256]{1,0:T(8,128)(2,1)S(1)}) custom-call(s32[2]{0:T(128)S(1)} %copy-done.71, bf16[2,1536,128]{2,1,0:T(8,128)(2,1)} %copy-done.25, bf16[8,576,128]{2,1,0:T(8,128)(2,1)} %copy-done.72, bf16[1536,128]{1,0:T(8,128)(2,1)S(1)} %get-tuple-element.88.refs_2_, bf16[8,192,384]{2,1,0:T(8,128)(2,1)} %copy-done.8, ...), custom_call_target="tpu_custom_call" | custom-call | flops 1000000 | bytes 100000 | tf_op jit(solution)/shard_map/pallas_call | solution.py:223
  522.1 12.5 %shard_map.297 = (f32[384,1024]{1,0:T(8,128)S(1)}, bf16[384,1024]{1,0:T(8,128)(2,1)S(1)}, bf16[8,384,128]{2,1,0:T(8,128)(2,1)}, f32[2,1024]{1,0:T(2,128)S(1)}) custom-call(bf16[8,384,384]{2,1,0:T(8,128)(2,1)} %all-to-all-done.9.t_ref.refs_4_, f32[384,1024]{1,0:T(8,128)S(1)} %copy-done.18, f32[576,1024]{1,0:T(8,128)S(1)} %copy-done.12, ...), custom_call_target="tpu_custom_call" | custom-call | flops 1000000 | bytes 100000 | tf_op jit(solution)/shard_map/pallas_call | solution.py:509
  535.8 19.5 %reduce-scatter.7.cloned.1.call-done.refs_0_ = bf16[128,9728]{1,0:T(8,128)(2,1)} async-done(((bf16[1024,9728]{1,0:T(8,128)(2,1)}), bf16[128,9728]{1,0:T(8,128)(2,1)}) %reduce-scatter.7.cloned.1.call-update) | async-done | bytes 2490384 | tf_op jit(solution)/shard_map/reduce_scatter | solution.py:932
  555.2 4.3 copy.139
  564.7 38.6 %collective-permute-done.16 = bf16[1536,256]{1,0:T(8,128)(2,1)} collective-permute-done((bf16[1536,256]{1,0:T(8,128)(2,1)}, bf16[1536,256]{1,0:T(8,128)(2,1)}, u32[]{:S(2)}, u32[]{:S(2)}) %collective-permute-start.16) | collective-permute-done | bytes 786464 | tf_op jit(solution)/shard_map/ppermute | solution.py:909
  613.6 4.9 collective-permute-start.12
  623.4 25.5 %shard_map.299 = (bf16[3072,128]{1,0:T(8,128)(2,1)S(1)}, bf16[1536,256]{1,0:T(8,128)(2,1)S(1)}) custom-call(s32[2]{0:T(128)S(1)} %pad_add_fusion.1.n_ref, bf16[2,3072,128]{2,1,0:T(8,128)(2,1)} %copy-done.39, bf16[8,384,128]{2,1,0:T(8,128)(2,1)} %copy-done.73, bf16[3072,128]{1,0:T(8,128)(2,1)} %copy-done.24, ...), custom_call_target="tpu_custom_call" | custom-call | flops 1000000 | bytes 100000 | tf_op jit(solution)/shard_map/pallas_call | solution.py:223
  653.0 9.0 shard_map.301
  667.2 11.6 %shard_map.304.refs_4_ = bf16[1024,4096]{1,0:T(8,128)(2,1)} custom-call(bf16[384,1024]{1,0:T(8,128)(2,1)} %copy-done.49, bf16[192,1024]{1,0:T(8,128)(2,1)} %copy-done.57, bf16[384,1024]{1,0:T(8,128)(2,1)} %copy-done.51, bf16[192,1024]{1,0:T(8,128)(2,1)} %copy-done.59, bf16[8,384,384]{2,1,0:T(8,128)(2,1)} %all-to-all-done.9.t_ref.refs_4_, ...), custom_call_target="tpu_custom_call" | custom-call | flops 1000000 | bytes 100000 | tf_op jit(solution)/shard_map/pallas_call | solution.py:567
  679.8 12.3 %all_to_all.91.refs_1_ = bf16[8,192,128]{2,1,0:T(8,128)(2,1)} all-to-all(bf16[8,192,128]{2,1,0:T(8,128)(2,1)S(1)} %copy-done.56), channel_id=1, replica_groups=mesh['seq'=8,'mp'=4] {'seq'}, dimensions={0} | all-to-all | bytes 786432 | tf_op jit(solution)/shard_map/all_to_all | solution.py:896
  696.5 11.6 %all-to-all-done.14.qa_ref = bf16[8,384,128]{2,1,0:T(8,128)(2,1)S(1)} async-done(((bf16[8,384,128]{2,1,0:T(8,128)(2,1)}), bf16[8,384,128]{2,1,0:T(8,128)(2,1)S(1)}, u32[]{:S(2)}, u32[]{:S(2)}) %all-to-all-start.14) | async-done | bytes 786464 | tf_op jit(solution)/shard_map/all_to_all | solution.py:896
  708.2 4.2 all-to-all-start.16
  712.4 19.4 %shard_map.305 = (bf16[1536,128]{1,0:T(8,128)(2,1)S(1)}, bf16[1536,256]{1,0:T(8,128)(2,1)S(1)}) custom-call(s32[2]{0:T(128)S(1)} %pad_add_fusion.n_ref, bf16[2,1536,128]{2,1,0:T(8,128)(2,1)} %copy-done.52, bf16[8,192,128]{2,1,0:T(8,128)(2,1)S(1)} %copy-done.15, bf16[1536,128]{1,0:T(8,128)(2,1)} %get-tuple-element.86.refs_2_, ...), custom_call_target="tpu_custom_call" | custom-call | flops 1000000 | bytes 100000 | tf_op jit(solution)/shard_map/pallas_call | solution.py:223
  733.5 4.5 all-to-all-start.15
  746.9 12.0 %all-to-all-done.15.b_ref = bf16[8,192,384]{2,1,0:T(8,128)(2,1)} async-done(((bf16[8,192,384]{2,1,0:T(8,128)(2,1)}), bf16[8,192,384]{2,1,0:T(8,128)(2,1)}, u32[]{:S(2)}, u32[]{:S(2)}) %all-to-all-start.15) | async-done | bytes 1179680 | tf_op jit(solution)/shard_map/all_to_all | solution.py:896
  758.9 12.2 %shard_map.308 = (bf16[96,1024]{1,0:T(8,128)(2,1)}, bf16[96,1024]{1,0:T(8,128)(2,1)}, bf16[96,1024]{1,0:T(8,128)(2,1)}, bf16[96,1024]{1,0:T(8,128)(2,1)}, bf16[9...) custom-call(s32[2]{0:T(128)} %pad_add_fusion.2.at_ref, ...), custom_call_target="tpu_custom_call" | custom-call | flops 1000000 | bytes 100000 | tf_op jit(solution)/shard_map/pallas_call | solution.py:719
  771.1 4.4 all-to-all-start.17
  784.2 15.2 %collective-permute-done.19 = bf16[18,1,128]{2,1,0:T(2,128)(2,1)S(1)} collective-permute-done((bf16[18,1,128]{2,1,0:T(2,128)(2,1)S(1)}, bf16[18,1,128]{2,1,0:T(2,128)(2,1)S(1)}, u32[]{:S(2)}, u32[]{:S(2)}) %collective-permute-start.19) | collective-permute-done | bytes 4640 | tf_op jit(solution)/shard_map/ppermute | solution.py:1277
  800.2 4.0 concatenate.43.refs_0_
  804.2 6.9 collective-permute-start.26
  817.5 60.5 %collective-permute-done.21.refs_2_ = bf16[96,1024]{1,0:T(8,128)(2,1)S(1)} collective-permute-done((bf16[96,1024]{1,0:T(8,128)(2,1)}, bf16[96,1024]{1,0:T(8,128)(2,1)S(1)}, u32[]{:S(2)}, u32[]{:S(2)}) %collective-permute-start.21) | collective-permute-done | bytes 196640 | tf_op jit(solution)/shard_map/ppermute | solution.py:937
  879.4 4.1 collective-permute-start.24
  899.0 11.7 %shard_map.311 = bf16[18,32,256]{2,1,0:T(8,128)(2,1)S(1)} custom-call(bf16[18,160,128]{2,1,0:T(8,128)(2,1)S(1)} %copy-done.14, bf16[18,561,256]{2,1,0:T(8,128)(2,1)S(1)} %bitcast.131), custom_call_target="tpu_custom_call" | custom-call | flops 1000000 | bytes 100000 | tf_op jit(solution)/shard_map/pallas_call | solution.py:883
  (382 shorter events, 199.8 us)
Async XLA Ops:
  7.2 81.4 %all-gather.7.cloned.1.call-start = ((), (), s32[]{:S(2)}) async-start(), calls=%async_computation.25 | async-start | bytes 6488064 | tf_op jit(solution)/shard_map/all_gather | solution.py:913
  11.8 169.0 %all-gather.9.cloned.1.call-start = ((), (), s32[]{:S(2)}) async-start(), calls=%async_computation.26 | async-start | bytes 8650752 | tf_op jit(solution)/shard_map/all_gather | solution.py:913
  22.8 307.8 %all-gather.11.cloned.1.call-start = ((), (), s32[]{:S(2)}) async-start(), calls=%async_computation.27 | async-start | bytes 20545536 | tf_op jit(solution)/shard_map/all_gather | solution.py:913
  27.2 38.9 %collective-permute-start.1 = (bf16[384,768]{1,0:T(8,128)(2,1)S(1)}, bf16[384,768]{1,0:T(8,128)(2,1)S(1)}, u32[]{:S(2)}, u32[]{:S(2)}) collective-permute-start(bf16[384,768]{1,0:T(8,128)(2,1)S(1)} %pad_maximum_fusion.4.refs_0_), channel_id=1, source_target_pairs={{0,8},{4,12},{8,0},{12,4},{16,24},{20,28},{24,16},{28,20},{1,9},{5... | collective-permute-start | bytes 1769480 | tf_op jit(solution)/shard_map/ppermute | solution.py:958
  30.2 41.6 %collective-permute-start.3 = (bf16[384,768]{1,0:T(8,128)(2,1)S(1)}, bf16[384,768]{1,0:T(8,128)(2,1)S(1)}, u32[]{:S(2)}, u32[]{:S(2)}) collective-permute-start(bf16[384,768]{1,0:T(8,128)(2,1)S(1)} %pad_maximum_fusion.4.refs_0_), channel_id=1, source_target_pairs={{0,16},{4,20},{8,24},{12,28},{16,0},{20,4},{24,8},{28,12},{1,17},{... | collective-permute-start | bytes 1769480 | tf_op jit(solution)/shard_map/ppermute | solution.py:958
  31.6 40.3 %collective-permute-start.5 = (bf16[384,768]{1,0:T(8,128)(2,1)S(1)}, bf16[384,768]{1,0:T(8,128)(2,1)}, u32[]{:S(2)}, u32[]{:S(2)}) collective-permute-start(bf16[384,768]{1,0:T(8,128)(2,1)S(1)} %pad_maximum_fusion.4.refs_0_), channel_id=1, source_target_pairs={{0,24},{4,28},{8,16},{12,20},{16,8},{20,12},{24,0},{28,4},{1,25},{... | collective-permute-start | bytes 1769480 | tf_op jit(solution)/shard_map/ppermute | solution.py:958
  49.5 12.8 %collective-permute-start.8 = (f32[18,8,128]{2,1,0:T(8,128)S(1)}, f32[18,8,128]{2,1,0:T(8,128)S(1)}, u32[]{:S(2)}, u32[]{:S(2)}) collective-permute-start(f32[18,8,128]{2,1,0:T(8,128)S(1)} %slice.159), channel_id=1, source_target_pairs={{0,16},{4,20},{8,24},{12,28},{1,17},{5,21},{9,25},{13,29},{2,18},{... | collective-permute-start | bytes 221192 | tf_op jit(solution)/shard_map/ppermute | solution.py:1067
  62.3 11.4 %collective-permute-start = (bf16[384,768]{1,0:T(8,128)(2,1)S(1)}, bf16[384,768]{1,0:T(8,128)(2,1)S(1)}, u32[]{:S(2)}, u32[]{:S(2)}) collective-permute-start(bf16[384,768]{1,0:T(8,128)(2,1)S(1)} %pad_maximum_fusion.4.refs_0_), channel_id=1, source_target_pairs={{0,4},{4,0},{8,12},{12,8},{16,20},{20,16},{24,28},{28,24},{1,5},{5... | collective-permute-start | bytes 1769480 | tf_op jit(solution)/shard_map/ppermute | solution.py:960
  122.6 23.7 %all-to-all-start.1 = ((bf16[32,72,128]{2,1,0:T(8,128)(2,1)}), bf16[32,72,128]{2,1,0:T(8,128)(2,1)}, u32[]{:S(2)}, u32[]{:S(2)}) async-start(bf16[32,72,128]{2,1,0:T(8,128)(2,1)} %shard_map.282), calls=%async_computation.1 | async-start | bytes 1179648 | tf_op jit(solution)/shard_map/all_to_all | solution.py:904
  146.2 26.7 %all-to-all-start.5 = ((bf16[8,192,128]{2,1,0:T(8,128)(2,1)}), bf16[8,192,128]{2,1,0:T(8,128)(2,1)S(1)}, u32[]{:S(2)}, u32[]{:S(2)}) async-start(bf16[8,192,128]{2,1,0:T(8,128)(2,1)} %bitcast.27), calls=%async_computation.5 | async-start | bytes 786432 | tf_op jit(solution)/shard_map/all_to_all | solution.py:896
  172.9 19.9 %all-to-all-start.2 = ((bf16[8,384,128]{2,1,0:T(8,128)(2,1)}), bf16[8,384,128]{2,1,0:T(8,128)(2,1)S(1)}, u32[]{:S(2)}, u32[]{:S(2)}) async-start(bf16[8,384,128]{2,1,0:T(8,128)(2,1)} %bitcast.139), calls=%async_computation.2 | async-start | bytes 1572864 | tf_op jit(solution)/shard_map/all_to_all | solution.py:896
  193.7 20.3 %all-to-all-start.6 = ((bf16[8,192,384]{2,1,0:T(8,128)(2,1)}), bf16[8,192,384]{2,1,0:T(8,128)(2,1)S(1)}, u32[]{:S(2)}, u32[]{:S(2)}) async-start(bf16[8,192,384]{2,1,0:T(8,128)(2,1)} %copy-done.44), calls=%async_computation.6 | async-start | bytes 2359296 | tf_op jit(solution)/shard_map/all_to_all | solution.py:896
  214.0 45.3 %all-to-all-start.3 = ((bf16[8,384,384]{2,1,0:T(8,128)(2,1)}), bf16[8,384,384]{2,1,0:T(8,128)(2,1)}, u32[]{:S(2)}, u32[]{:S(2)}) async-start(bf16[8,384,384]{2,1,0:T(8,128)(2,1)} %copy-done.37), calls=%async_computation.3 | async-start | bytes 4718592 | tf_op jit(solution)/shard_map/all_to_all | solution.py:896
  219.3 76.1 %collective-permute-start.10 = (bf16[8,192,256]{2,1,0:T(8,128)(2,1)}, bf16[8,192,256]{2,1,0:T(8,128)(2,1)}, u32[]{:S(2)}, u32[]{:S(2)}) collective-permute-start(bf16[8,192,256]{2,1,0:T(8,128)(2,1)} %slice.166), channel_id=1, source_target_pairs={{0,1},{1,0},{2,3},{3,2},{4,5},{5,4},{6,7},{7,6},{8,9},{9,8},{10,11... | collective-permute-start | bytes 2359304 | tf_op jit(solution)/shard_map/ppermute | solution.py:909
  291.0 23.4 %all-to-all-start.4 = ((bf16[8,384,128]{2,1,0:T(8,128)(2,1)}), bf16[8,384,128]{2,1,0:T(8,128)(2,1)}, u32[]{:S(2)}, u32[]{:S(2)}) async-start(bf16[8,384,128]{2,1,0:T(8,128)(2,1)} %bitcast.26), calls=%async_computation.4 | async-start | bytes 1572864 | tf_op jit(solution)/shard_map/all_to_all | solution.py:896
  314.4 12.5 %all-to-all-start.7 = ((bf16[8,192,128]{2,1,0:T(8,128)(2,1)}), bf16[8,192,128]{2,1,0:T(8,128)(2,1)S(1)}, u32[]{:S(2)}, u32[]{:S(2)}) async-start(bf16[8,192,128]{2,1,0:T(8,128)(2,1)} %shard_map.289), calls=%async_computation.7 | async-start | bytes 786432 | tf_op jit(solution)/shard_map/all_to_all | solution.py:896
  367.5 30.6 %all-to-all-start.8 = ((bf16[8,576,128]{2,1,0:T(8,128)(2,1)}), bf16[8,576,128]{2,1,0:T(8,128)(2,1)S(1)}, u32[]{:S(2)}, u32[]{:S(2)}) async-start(bf16[8,576,128]{2,1,0:T(8,128)(2,1)} %get-tuple-element.93), calls=%async_computation.8 | async-start | bytes 2359296 | tf_op jit(solution)/shard_map/all_to_all | solution.py:896
  373.5 181.7 %reduce-scatter.7.cloned.1.call-start = ((), (), s32[]{:S(2)}) async-start(), calls=%async_computation.22 | async-start | bytes 22413312 | tf_op jit(solution)/shard_map/reduce_scatter | solution.py:932
  401.2 70.6 %all-to-all-start.10 = ((bf16[32,72,128]{2,1,0:T(8,128)(2,1)}), bf16[32,72,128]{2,1,0:T(8,128)(2,1)S(1)}, u32[]{:S(2)}, u32[]{:S(2)}) async-start(bf16[32,72,128]{2,1,0:T(8,128)(2,1)} %bitcast.42), calls=%async_computation.10 | async-start | bytes 1179648 | tf_op jit(solution)/shard_map/all_to_all | solution.py:904
  471.8 47.2 %all-to-all-start.9 = ((bf16[8,384,384]{2,1,0:T(8,128)(2,1)}), bf16[8,384,384]{2,1,0:T(8,128)(2,1)}, u32[]{:S(2)}, u32[]{:S(2)}) async-start(bf16[8,384,384]{2,1,0:T(8,128)(2,1)} %bitcast.156), calls=%async_computation.9 | async-start | bytes 4718592 | tf_op jit(solution)/shard_map/all_to_all | solution.py:896
  476.2 187.5 %reduce-scatter.13.cloned.1.call-start = ((), (), s32[]{:S(2)}) async-start(), calls=%async_computation.28 | async-start | bytes 3112960
  559.6 43.8 %collective-permute-start.16 = (bf16[1536,256]{1,0:T(8,128)(2,1)}, bf16[1536,256]{1,0:T(8,128)(2,1)}, u32[]{:S(2)}, u32[]{:S(2)}) collective-permute-start(bf16[1536,256]{1,0:T(8,128)(2,1)} %get-tuple-element.112), channel_id=1, source_target_pairs={{0,1},{1,0},{2,3},{3,2},{4,5},{5,4},{6,7},{7,6},{8,9},{9,8},{10,11... | collective-permute-start | bytes 2359304 | tf_op jit(solution)/shard_map/ppermute | solution.py:909
  561.2 44.7 %all-to-all-start.11 = ((bf16[8,384,128]{2,1,0:T(8,128)(2,1)}), bf16[8,384,128]{2,1,0:T(8,128)(2,1)S(1)}, u32[]{:S(2)}, u32[]{:S(2)}) async-start(bf16[8,384,128]{2,1,0:T(8,128)(2,1)} %get-tuple-element.109), calls=%async_computation.11 | async-start | bytes 1572864 | tf_op jit(solution)/shard_map/all_to_all | solution.py:896
  606.8 43.0 %all-to-all-start.12 = ((bf16[8,192,384]{2,1,0:T(8,128)(2,1)}), bf16[8,192,384]{2,1,0:T(8,128)(2,1)S(1)}, u32[]{:S(2)}, u32[]{:S(2)}) async-start(bf16[8,192,384]{2,1,0:T(8,128)(2,1)} %shard_map.300), calls=%async_computation.12 | async-start | bytes 2359296 | tf_op jit(solution)/shard_map/all_to_all | solution.py:896
  610.4 167.4 %reduce-scatter.9.cloned.1.call-start = ((), (), s32[]{:S(2)}) async-start(), calls=%async_computation.23 | async-start | bytes 9437184 | tf_op jit(solution)/shard_map/reduce_scatter | solution.py:932
  613.6 52.9 %collective-permute-start.11 = (bf16[96,1024]{1,0:T(8,128)(2,1)}, bf16[96,1024]{1,0:T(8,128)(2,1)S(1)}, u32[]{:S(2)}, u32[]{:S(2)}) collective-permute-start(bf16[96,1024]{1,0:T(8,128)(2,1)} %get-tuple-element.211), channel_id=1, source_target_pairs={{0,1},{1,0},{2,3},{3,2},{4,5},{5,4},{6,7},{7,6},{8,9},{9,8},{10,11... | collective-permute-start | bytes 589832 | tf_op jit(solution)/shard_map/ppermute | solution.py:937
  613.6 52.9 %collective-permute-start.12 = (bf16[96,1024]{1,0:T(8,128)(2,1)}, bf16[96,1024]{1,0:T(8,128)(2,1)S(1)}, u32[]{:S(2)}, u32[]{:S(2)}) collective-permute-start(bf16[96,1024]{1,0:T(8,128)(2,1)} %get-tuple-element.210), channel_id=1, source_target_pairs={{0,2},{1,3},{2,0},{3,1},{4,6},{5,7},{6,4},{7,5},{8,10},{9,11},{10,... | collective-permute-start | bytes 589832 | tf_op jit(solution)/shard_map/ppermute | solution.py:937
  618.4 48.0 %collective-permute-start.13 = (bf16[96,1024]{1,0:T(8,128)(2,1)}, bf16[96,1024]{1,0:T(8,128)(2,1)}, u32[]{:S(2)}, u32[]{:S(2)}) collective-permute-start(bf16[96,1024]{1,0:T(8,128)(2,1)} %get-tuple-element.209), channel_id=1, source_target_pairs={{0,3},{1,2},{2,1},{3,0},{4,7},{5,6},{6,5},{7,4},{8,11},{9,10},{10,... | collective-permute-start | bytes 589832 | tf_op jit(solution)/shard_map/ppermute | solution.py:937
  619.2 47.3 %collective-permute-start.14 = (bf16[96,1024]{1,0:T(8,128)(2,1)}, bf16[96,1024]{1,0:T(8,128)(2,1)}, u32[]{:S(2)}, u32[]{:S(2)}) collective-permute-start(bf16[96,1024]{1,0:T(8,128)(2,1)} %get-tuple-element.219), channel_id=1, source_target_pairs={{0,0},{1,2},{2,1},{3,3},{4,4},{5,6},{6,5},{7,7},{8,8},{9,10},{10,9... | collective-permute-start | bytes 589832 | tf_op jit(solution)/shard_map/ppermute | solution.py:945
  622.2 44.3 %collective-permute-start.15 = (bf16[96,1024]{1,0:T(8,128)(2,1)}, bf16[96,1024]{1,0:T(8,128)(2,1)}, u32[]{:S(2)}, u32[]{:S(2)}) collective-permute-start(bf16[96,1024]{1,0:T(8,128)(2,1)} %get-tuple-element.218), channel_id=1, source_target_pairs={{0,1},{1,3},{2,0},{3,2},{4,5},{5,7},{6,4},{7,6},{8,9},{9,11},{10,8... | collective-permute-start | bytes 589832 | tf_op jit(solution)/shard_map/ppermute | solution.py:945
  692.1 16.1 %all-to-all-start.14 = ((bf16[8,384,128]{2,1,0:T(8,128)(2,1)}), bf16[8,384,128]{2,1,0:T(8,128)(2,1)S(1)}, u32[]{:S(2)}, u32[]{:S(2)}) async-start(bf16[8,384,128]{2,1,0:T(8,128)(2,1)} %shard_map.302), calls=%async_computation.14 | async-start | bytes 1572864 | tf_op jit(solution)/shard_map/all_to_all | solution.py:896
  708.2 25.4 %all-to-all-start.16 = ((bf16[8,192,256]{2,1,0:T(8,128)(2,1)}), bf16[8,192,256]{2,1,0:T(8,128)(2,1)}, u32[]{:S(2)}, u32[]{:S(2)}) async-start(bf16[8,192,256]{2,1,0:T(8,128)(2,1)} %shard_map.306), calls=%async_computation.17 | async-start | bytes 1572864 | tf_op jit(solution)/shard_map/all_to_all | solution.py:896
  733.5 25.4 %all-to-all-start.15 = ((bf16[8,192,384]{2,1,0:T(8,128)(2,1)}), bf16[8,192,384]{2,1,0:T(8,128)(2,1)}, u32[]{:S(2)}, u32[]{:S(2)}) async-start(bf16[8,192,384]{2,1,0:T(8,128)(2,1)} %pad_maximum_fusion.2), calls=%async_computation.16 | async-start | bytes 2359296 | tf_op jit(solution)/shard_map/all_to_all | solution.py:896
  771.1 114.6 %all-to-all-start.17 = ((bf16[8,1232,128]{2,1,0:T(8,128)(2,1)}), bf16[8,1232,128]{2,1,0:T(8,128)(2,1)}, u32[]{:S(2)}, u32[]{:S(2)}) async-start(bf16[8,1232,128]{2,1,0:T(8,128)(2,1)} %get-tuple-element.131.refs_6_.refs_1_), calls=%async_computation.18 | async-start | bytes 5046272 | tf_op jit(solution)/shard_map/all_to_all | solution.py:896
  775.5 148.3 %reduce-scatter.11.cloned.1.call-start = ((), (), s32[]{:S(2)}) async-start(), calls=%async_computation.24 | async-start | bytes 1310720 | tf_op jit(solution)/shard_map/reduce_scatter | solution.py:950
  778.0 22.1 %collective-permute-start.17 = (bf16[18,16,128]{2,1,0:T(8,128)(2,1)S(1)}, bf16[18,16,128]{2,1,0:T(8,128)(2,1)S(1)}, u32[]{:S(2)}, u32[]{:S(2)}) collective-permute-start(bf16[18,16,128]{2,1,0:T(8,128)(2,1)S(1)} %bitcast.185), channel_id=1, source_target_pairs={{4,0},{8,4},{12,8},{20,16},{24,20},{28,24},{5,1},{9,5},{13,9},{21,... | collective-permute-start | bytes 221192 | tf_op jit(solution)/shard_map/ppermute | solution.py:1275
  779.5 20.7 %collective-permute-start.18 = (bf16[18,8,128]{2,1,0:T(8,128)(2,1)S(1)}, bf16[18,8,128]{2,1,0:T(8,128)(2,1)S(1)}, u32[]{:S(2)}, u32[]{:S(2)}) collective-permute-start(bf16[18,8,128]{2,1,0:T(8,128)(2,1)S(1)} %slice_bitcast_fusion.7), channel_id=1, source_target_pairs={{16,0},{20,4},{24,8},{28,12},{17,1},{21,5},{25,9},{29,13},{18,2},{... | collective-permute-start | bytes 110600 | tf_op jit(solution)/shard_map/ppermute | solution.py:1276
  780.8 30.4 %collective-permute-start.20 = (bf16[96,1024]{1,0:T(8,128)(2,1)}, bf16[96,1024]{1,0:T(8,128)(2,1)S(1)}, u32[]{:S(2)}, u32[]{:S(2)}) collective-permute-start(bf16[96,1024]{1,0:T(8,128)(2,1)} %get-tuple-element.133), channel_id=1, source_target_pairs={{0,1},{1,0},{2,3},{3,2},{4,5},{5,4},{6,7},{7,6},{8,9},{9,8},{10,11... | collective-permute-start | bytes 589832 | tf_op jit(solution)/shard_map/ppermute | solution.py:937
  782.3 109.2 %collective-permute-start.25 = (bf16[2,192,768]{2,1,0:T(8,128)(2,1)S(1)}, bf16[2,192,768]{2,1,0:T(8,128)(2,1)S(1)}, u32[]{:S(2)}, u32[]{:S(2)}) collective-permute-start(bf16[2,192,768]{2,1,0:T(8,128)(2,1)S(1)} %copy-done.54), channel_id=1, source_target_pairs={{0,1},{1,0},{2,3},{3,2},{4,5},{5,4},{6,7},{7,6},{8,9},{9,8},{10,11... | collective-permute-start | bytes 1769480 | tf_op jit(solution)/shard_map/ppermute | solution.py:937
  782.9 16.5 %collective-permute-start.19 = (bf16[18,1,128]{2,1,0:T(2,128)(2,1)S(1)}, bf16[18,1,128]{2,1,0:T(2,128)(2,1)S(1)}, u32[]{:S(2)}, u32[]{:S(2)}) collective-permute-start(bf16[18,1,128]{2,1,0:T(2,128)(2,1)S(1)} %slice_bitcast_fusion.8), channel_id=1, source_target_pairs={{20,0},{24,4},{28,8},{21,1},{25,5},{29,9},{22,2},{26,6},{30,10},{2... | collective-permute-start | bytes 13832 | tf_op jit(solution)/shard_map/ppermute | solution.py:1277
  804.2 111.7 %collective-permute-start.26 = (bf16[2,192,768]{2,1,0:T(8,128)(2,1)S(1)}, bf16[2,192,768]{2,1,0:T(8,128)(2,1)}, u32[]{:S(2)}, u32[]{:S(2)}) collective-permute-start(bf16[2,192,768]{2,1,0:T(8,128)(2,1)S(1)} %copy-done.54), channel_id=1, source_target_pairs={{0,2},{1,3},{2,0},{3,1},{4,6},{5,7},{6,4},{7,5},{8,10},{9,11},{10,... | collective-permute-start | bytes 1769480 | tf_op jit(solution)/shard_map/ppermute | solution.py:937
  811.2 104.8 %collective-permute-start.27 = (bf16[2,192,768]{2,1,0:T(8,128)(2,1)S(1)}, bf16[2,192,768]{2,1,0:T(8,128)(2,1)}, u32[]{:S(2)}, u32[]{:S(2)}) collective-permute-start(bf16[2,192,768]{2,1,0:T(8,128)(2,1)S(1)} %copy-done.54), channel_id=1, source_target_pairs={{0,3},{1,2},{2,1},{3,0},{4,7},{5,6},{6,5},{7,4},{8,11},{9,10},{10,... | collective-permute-start | bytes 1769480 | tf_op jit(solution)/shard_map/ppermute | solution.py:937
  811.2 66.9 %collective-permute-start.21 = (bf16[96,1024]{1,0:T(8,128)(2,1)}, bf16[96,1024]{1,0:T(8,128)(2,1)S(1)}, u32[]{:S(2)}, u32[]{:S(2)}) collective-permute-start(bf16[96,1024]{1,0:T(8,128)(2,1)} %get-tuple-element.134), channel_id=1, source_target_pairs={{0,2},{1,3},{2,0},{3,1},{4,6},{5,7},{6,4},{7,5},{8,10},{9,11},{10,... | collective-permute-start | bytes 589832 | tf_op jit(solution)/shard_map/ppermute | solution.py:937
  811.2 67.5 %collective-permute-start.22 = (bf16[96,1024]{1,0:T(8,128)(2,1)}, bf16[96,1024]{1,0:T(8,128)(2,1)S(1)}, u32[]{:S(2)}, u32[]{:S(2)}) collective-permute-start(bf16[96,1024]{1,0:T(8,128)(2,1)} %get-tuple-element.135), channel_id=1, source_target_pairs={{0,3},{1,2},{2,1},{3,0},{4,7},{5,6},{6,5},{7,4},{8,11},{9,10},{10,... | collective-permute-start | bytes 589832 | tf_op jit(solution)/shard_map/ppermute | solution.py:937
  879.4 11.3 %collective-permute-start.24 = (bf16[96,1024]{1,0:T(8,128)(2,1)S(1)}, bf16[96,1024]{1,0:T(8,128)(2,1)S(1)}, u32[]{:S(2)}, u32[]{:S(2)}) collective-permute-start(bf16[96,1024]{1,0:T(8,128)(2,1)S(1)} %copy-done.86), channel_id=1, source_target_pairs={{0,1},{1,3},{2,0},{3,2},{4,5},{5,7},{6,4},{7,6},{8,9},{9,11},{10,8... | collective-permute-start | bytes 589832 | tf_op jit(solution)/shard_map/ppermute | solution.py:945
  889.7 29.8 %collective-permute-start.28 = (bf16[656,128]{1,0:T(8,128)(2,1)}, bf16[656,128]{1,0:T(8,128)(2,1)}, u32[]{:S(2)}, u32[]{:S(2)}) collective-permute-start(bf16[656,128]{1,0:T(8,128)(2,1)} %get-tuple-element.140), channel_id=1, source_target_pairs={{0,1},{1,0},{2,3},{3,2},{4,5},{5,4},{6,7},{7,6},{8,9},{9,8},{10,11... | collective-permute-start | bytes 503816 | tf_op jit(solution)/shard_map/ppermute | solution.py:937
  891.4 28.1 %collective-permute-start.29 = (bf16[656,128]{1,0:T(8,128)(2,1)}, bf16[656,128]{1,0:T(8,128)(2,1)}, u32[]{:S(2)}, u32[]{:S(2)}) collective-permute-start(bf16[656,128]{1,0:T(8,128)(2,1)} %get-tuple-element.141), channel_id=1, source_target_pairs={{0,2},{1,3},{2,0},{3,1},{4,6},{5,7},{6,4},{7,5},{8,10},{9,11},{10,... | collective-permute-start | bytes 503816 | tf_op jit(solution)/shard_map/ppermute | solution.py:937
  891.5 28.0 %collective-permute-start.30 = (bf16[656,128]{1,0:T(8,128)(2,1)}, bf16[656,128]{1,0:T(8,128)(2,1)}, u32[]{:S(2)}, u32[]{:S(2)}) collective-permute-start(bf16[656,128]{1,0:T(8,128)(2,1)} %get-tuple-element.142), channel_id=1, source_target_pairs={{0,3},{1,2},{2,1},{3,0},{4,7},{5,6},{6,5},{7,4},{8,11},{9,10},{10,... | collective-permute-start | bytes 503816 | tf_op jit(solution)/shard_map/ppermute | solution.py:937
  (94 other events, 805.1 us)
Sparse Core Ops, SparseCore 0:
  11.9 76.7 all-gather.6
  91.5 89.1 all-gather.8
  183.6 146.9 all-gather.10
  399.2 155.9 reduce-scatter.6
  559.7 64.8 reduce-scatter.12
  679.0 98.7 reduce-scatter.8
  780.2 46.7 reduce-scatter.10

commit v7 on v6

--- a/solution.py
+++ b/solution.py
@@ -113,8 +113,8 @@
     lax.fori_loop(0, qa_ref.shape[1] // bq, block, 0)
 
 
-def bwd_kernel(n_ref, *refs, n_in, blocks, do_spec, kv_specs, hpd, bq, kc, fixed):
-    ins, (dq_ref, dkv_ref, ka, va, da, dk, dv) = refs[:n_in], refs[-7:]
+def bwd_kernel(n_ref, *refs, n_in, n_dep, blocks, do_spec, kv_specs, hpd, bq, kc, fixed, form):
+    ins, (*outs, ka, va, da, dk, dv, dq) = refs[:n_in], refs[n_in + n_dep :]
     qa_ref, do_ref, o_ref = ins[:3]
     load_keys(n_ref, kv_specs, ins, ka, va, hpd, blocks)
     rows_q, do_off = do_spec
@@ -151,8 +151,8 @@
             return tuple(out)
 
         dqs = lax.fori_loop(0, steps, chunk, (jnp.zeros((LANES, bq), f32),) * hpd)
-        dq = jnp.concatenate([v[:HD, :] for v in dqs], axis=0).T
-        dq_ref[rows, :] = (dq * (1.0 / math.sqrt(HD))).astype(bf16)
+        grad = jnp.concatenate([v[:HD, :] for v in dqs], axis=0).T
+        dq[rows, :] = (grad * (1.0 / math.sqrt(HD))).astype(bf16)
         return 0
 
     lax.fori_loop(0, qa_ref.shape[1] // bq, block, 0)
@@ -160,8 +160,20 @@
 
     def finish(i, _):
         rows = pl.ds(pl.multiple_of(i * step, 16), step)
-        parts = [dk[h, rows, :HD] for h in range(hpd)] + [dv[h, rows, :HD] for h in range(hpd)]
-        dkv_ref[rows, :] = jnp.concatenate(parts, axis=1).astype(bf16)
+        q_rows = pl.ds(pl.multiple_of(i * rows_q, 16), rows_q)
+        k, v = [
+            jnp.concatenate([d[h, rows, :HD] for h in range(hpd)], axis=1).astype(bf16)
+            for d in (dk, dv)
+        ]
+        if form == "split":
+            outs[0][q_rows, :] = dq[q_rows, :]
+            outs[1][rows, :] = jnp.concatenate([k, v], axis=1)
+        elif form == "lanes":
+            outs[0][i] = jnp.concatenate([dq[q_rows, :], k, v], axis=1)
+        else:
+            outs[0][i, :rows_q, :] = dq[q_rows, :]
+            outs[0][i, rows_q : rows_q + step, :] = k
+            outs[0][i, rows_q + step :, :] = v
         return 0
 
     lax.fori_loop(0, blocks, finish, 0)
@@ -206,11 +218,18 @@
     )(limits, *ins, *deps)
 
 
-def attend_back(limits, ins, blocks, do_spec, kv_specs, total, hpd, fixed, deps=()):
+def attend_back(limits, ins, blocks, do_spec, kv_specs, total, hpd, fixed, deps=(), form="split"):
     queries = blocks * do_spec[0]
+    W, step = hpd * HD, total // blocks
+    shapes = {
+        "split": [(queries, W), (total, 2 * W)],
+        "lanes": [(blocks, step, 3 * W)],
+        "rows": [(blocks, do_spec[0] + 2 * step, W)],
+    }[form]
     body = functools.partial(
         bwd_kernel,
         n_in=len(ins),
+        n_dep=len(deps),
         blocks=blocks,
         do_spec=do_spec,
         kv_specs=kv_specs,
@@ -218,22 +237,21 @@
         bq=fit(queries, 512),
         kc=fit(total, 512),
         fixed=fixed,
-    )
-    work = hpd * queries * total
-    return pl.pallas_call(
+        form=form,
+    )
+    out = pl.pallas_call(
         body,
-        out_shape=(
-            jax.ShapeDtypeStruct((queries, hpd * HD), bf16),
-            jax.ShapeDtypeStruct((total, 2 * hpd * HD), bf16),
-        ),
+        out_shape=tuple(jax.ShapeDtypeStruct(v, bf16) for v in shapes),
         in_specs=[SM] + [VM] * len(ins) + [AN] * len(deps),
-        out_specs=(VM, VM),
+        out_specs=(VM,) * len(shapes),
         scratch_shapes=[pltpu.VMEM((hpd, total, LANES), bf16)] * 2
         + [pltpu.VMEM((hpd, queries, LANES), bf16)]
-        + [pltpu.VMEM((hpd, total, LANES), f32)] * 2,
+        + [pltpu.VMEM((hpd, total, LANES), f32)] * 2
+        + [pltpu.VMEM((queries, W), bf16)],
         compiler_params=pltpu.CompilerParams(vmem_limit_bytes=52 * 2**20),
         cost_estimate=BRIEF,
     )(limits, *ins, *deps)
+    return out if len(out) > 1 else out[0]
 
 
 def norm_parts(values):
@@ -275,7 +293,9 @@
     return pl.BlockSpec(shape, lambda i: (0,) * len(shape))
 
 
-def mid_kernel(a_ref, x_ref, norm_ref, wo_ref, wt_ref, x1_ref, n_ref, ac_ref, t_ref):
+def mid_kernel(a_ref, x_ref, norm_ref, wo_ref, wt_ref, *refs):
+    x1_ref, n_ref, ac_ref, t_ref = refs[-4:]
+
     @pl.when(pl.program_id(0) == 0)
     def _():
         a = joined(a_ref)
@@ -287,7 +307,7 @@
     t_ref[0] = dot(n_ref[...], flat(wt_ref), NT).astype(bf16)
 
 
-def middle(a, x, norm, w_out, w_triple):
+def middle(a, x, norm, w_out, w_triple, deps=()):
     S, rows, W = a.shape
     D = S * W
     return pl.pallas_call(
@@ -305,7 +325,8 @@
             once((2, D)),
             once(*w_out[1]),
             w_triple[1],
-        ],
+        ]
+        + [AN] * len(deps),
         out_specs=(
             held((rows, D)),
             held((rows, D)),
@@ -314,7 +335,7 @@
         ),
         compiler_params=pltpu.CompilerParams(vmem_limit_bytes=40 * 2**20),
         cost_estimate=BRIEF,
-    )(a, x, norm, w_out[0], w_triple[0])
+    )(a, x, norm, w_out[0], w_triple[0], *deps)
 
 
 def mlp_kernel(
@@ -620,114 +641,116 @@
     )(at, *x0, norm, w_kv[0], w_query[0], *patch_pieces, *deps)
 
 
-def finish_kernel(at_ref, ka_ref, kb_ref, *refs, pieces):
+def finish_kernel(at_ref, a_ref, b_ref, *refs, pieces, rows):
     p_in, out_ref = refs[:pieces], refs[-1]
     seq = at_ref[0]
-    slots, W = ka_ref.shape[1], ka_ref.shape[2] // 2
-    by_kv = 0.0
+    W = a_ref.shape[2]
+    slots = (a_ref.shape[1] - rows[0]) // 2
+    sums = [0.0, 0.0]
     for i in range(pieces):
-        j = seq ^ i
-        by_kv += dot(ka_ref[j], p_in[i][:slots, :], TN) + dot(kb_ref[j], p_in[i][slots:, :], TN)
-    wide = by_kv.shape[1] // pieces
-    grad_k, grad_v = by_kv[:W].T.astype(bf16), by_kv[W:].T.astype(bf16)
-    for i in range(pieces):
-        out_ref[i, :wide, :] = grad_k[i * wide : (i + 1) * wide, :]
-        out_ref[i, wide:, :] = grad_v[i * wide : (i + 1) * wide, :]
-
-
-def finish(at, dkv, patch_pieces):
-    S, W = dkv[0].shape[0], dkv[0].shape[2] // 2
-    rows = 2 * patch_pieces[0].shape[1] // S
+        for j, (ref, at) in enumerate(((a_ref, rows[0]), (b_ref, rows[1]))):
+            p = p_in[i][j * slots : (j + 1) * slots, :]
+            for k in range(2):
+                sums[k] += dot(ref[seq ^ i, at + k * slots : at + (k + 1) * slots, :], p, TN)
+    wide = sums[0].shape[1] // pieces
+    for k in range(2):
+        grad = sums[k].T.astype(bf16)
+        for i in range(pieces):
+            out_ref[i, k * wide : (k + 1) * wide, :] = grad[i * wide : (i + 1) * wide, :]
+
+
+def finish(at, cross, rows, patch_pieces, deps):
+    S, _, W = cross[0].shape
+    out = (S, 2 * patch_pieces[0].shape[1] // S, W)
     return pl.pallas_call(
-        functools.partial(finish_kernel, pieces=S),
-        out_shape=jax.ShapeDtypeStruct((S, rows, W), bf16),
-        in_specs=[SM] + [VM] * (2 + S),
+        functools.partial(finish_kernel, pieces=S, rows=rows),
+        out_shape=jax.ShapeDtypeStruct(out, bf16),
+        in_specs=[SM] + [VM] * (2 + S) + [AN] * len(deps),
         out_specs=VM,
         compiler_params=pltpu.CompilerParams(vmem_limit_bytes=32 * 2**20),
         cost_estimate=BRIEF,
-    )(at, *dkv, *patch_pieces)
+    )(at, *cross, *patch_pieces, *deps)
 
 
 def end_kernel(
-    at_ref,
-    qa_ref,
-    b_ref,
-    ka_ref,
-    wq_ref,
-    wkv_ref,
-    xa_ref,
-    xb_ref,
-    n_ref,
-    da_ref,
-    db_ref,
-    small_ref,
-    gain_ref,
-    head_ref,
-    *refs,
-    ranks,
+    at_ref, g_ref, wq_ref, wkv_ref, x_ref, n_ref, d_ref, gain_ref, *refs, blocks, more, n_dep
 ):
-    outs_a, outs_b = refs[:ranks], refs[ranks : ranks + ranks // 2]
-    part_ref, pay_ref, n_t, dq = refs[ranks + ranks // 2 :]
-    S, R, W = qa_ref.shape
-    own = R // ranks
-    dq[:R, :] = joined(qa_ref)
-    dq[R:, :] = jnp.concatenate([b_ref[i, :, :W] for i in range(S)], axis=1)
+    extra, refs = refs[:more], refs[more + n_dep :]
+    outs, part_ref, refs = refs[:blocks], refs[blocks], refs[blocks + 1 :]
+    outs_more, (n_t, dq, total) = refs[:-3], refs[-3:]
+    S, _, W = g_ref.shape
+    rows = x_ref.shape[0]
+    slots = (g_ref.shape[1] - rows) // 2
+    own = rows // blocks
+    dq[...] = jnp.concatenate([g_ref[i, :rows, :] for i in range(S)], axis=1)
     n_t[...] = n_ref[...].T
-    back = dot(dq[...], wq_ref[...], NN)
-    gain = gain_ref[...]
-    got_a = norm_back(xa_ref[...].astype(f32), gain, back[:R])
-    got_b = norm_back(xb_ref[...].astype(f32), gain, back[R:])
-    da_ref[...] += got_a[0]
-    db_ref[...] += got_b[0]
-    for i in range(ranks):
-        rows = pl.ds(pl.multiple_of((at_ref[1] ^ i) * own, 8), own)
-        outs_a[i][...] = da_ref[rows, :].astype(bf16)
-    for i in range(ranks // 2):
-        rows = pl.ds(pl.multiple_of((at_ref[1] // 2 ^ i) * own, 8), own)
-        outs_b[i][...] = db_ref[rows, :].astype(bf16)
-    for i, keys in enumerate((joined(ka_ref), None)):
-        if keys is None:
-            keys = jnp.concatenate([b_ref[j, :, W:] for j in range(S)], axis=1)
-        part_ref[i] = dot(keys, wkv_ref[...], NN).astype(bf16)
-    rows = n_t.shape[0] // S
+    grad, gain, shift = norm_back(
+        x_ref[...].astype(f32), gain_ref[...], dot(dq[...], wq_ref[...], NN)
+    )
+    total[...] = d_ref[...] + grad
+    place = at_ref[1] // 2 if more else at_ref[1]
+    for i in range(blocks):
+        outs[i][...] = total[pl.ds(pl.multiple_of((place ^ i) * own, 8), own), :].astype(bf16)
+    keys = []
+    for i in range(S):
+        keys += [g_ref[i, rows : rows + slots, :], g_ref[i, rows + slots :, :]]
+    part_ref[...] = dot(jnp.concatenate(keys, axis=1), wkv_ref[...], NN).astype(bf16)
+    lift = jnp.concatenate([gain, shift], axis=0)
+    tall = n_t.shape[0] // S
     for i in range(0, S, 2):
-        pair = dot(n_t[...], dq[:, i * W : (i + 2) * W], NN).astype(bf16)
-        for j in range(S):
-            block = pair[j * rows : (j + 1) * rows, :]
-            pay_ref[j, i * rows : (i + 1) * rows, :] = block[:, :W]
-            pay_ref[j, (i + 1) * rows : (i + 2) * rows, :] = block[:, W:]
-    at = S * rows
-    heads = head_ref.shape[1]
-    lift = jnp.concatenate([got_a[1] + got_b[1], got_a[2] + got_b[2]], axis=0)
-    sums = jnp.concatenate([lift, small_ref[...], jnp.zeros((2, n_t.shape[0]), f32)], axis=0)
+        pair = dot(n_t[...], dq[:, i * W : (i + 2) * W], NN)
+        if more:
+            pair += extra[0][i // 2]
+            for j in range(S):
+                block = pair[j * tall : (j + 1) * tall, :].astype(bf16)
+                outs_more[0][j, i * tall : (i + 1) * tall, :] = block[:, :W]
+                outs_more[0][j, (i + 1) * tall : (i + 2) * tall, :] = block[:, W:]
+        else:
+            outs_more[0][i // 2] = pair
+    if not more:
+        outs_more[1][...] = lift
+        return
+    at = S * tall
+    heads = extra[3].shape[1]
+    zero = jnp.zeros((2, n_t.shape[0]), f32)
+    sums = jnp.concatenate([lift + extra[1][...], extra[2][...], zero], axis=0)
     hi = sums.astype(bf16).astype(f32)
     both = jnp.concatenate([hi, sums - hi], axis=0).astype(bf16)
     for j in range(S):
-        pay_ref[j, at : at + heads, :] = head_ref[j]
-        pay_ref[j, at + heads :, :] = both[:, j * W : (j + 1) * W]
-
-
-def end(at, dq_a, both_b, dkv_a, w_query, w_kv, x0, n1, d1, small, gain, by_head, ranks):
-    S, R, W = dq_a.shape
-    RB = both_b.shape[1]
-    D, total = S * W, R + RB
-    own = R // ranks
-    slots, width = dkv_a.shape[1], w_kv.shape[1]
-    rows = D + by_head.shape[1] + 16
-    outs = [(own, D)] * (ranks + ranks // 2) + [(2, slots, width), (S, rows, W)]
-    whole = [dq_a, both_b, dkv_a, w_query, w_kv, *x0, n1, *d1, small, gain, by_head]
+        outs_more[0][j, at : at + heads, :] = extra[3][j]
+        outs_more[0][j, at + heads :, :] = both[:, j * W : (j + 1) * W]
+
+
+def end(at, got, place, w_query, w_kv, x0, n1, d1, gain, blocks, deps, more=()):
+    S, _, W = got.shape
+    rows, D = x0.shape
+    slots, width = (got.shape[1] - rows) // 2, w_kv.shape[1]
+    outs = [((rows // blocks, D), bf16)] * blocks + [((slots, width), bf16)]
+    if more:
+        outs += [((S, D + more[3].shape[1] + 16, W), bf16)]
+    else:
+        outs += [((S // 2, D, 2 * W), f32), ((2, D), f32)]
+    whole = [got, w_query, w_kv, x0, n1, d1, gain, *more]
+    specs = [once(v.shape) for v in whole]
+    specs[4] = once((rows, D), (place, 0))
     return pl.pallas_call(
-        functools.partial(end_kernel, ranks=ranks),
-        out_shape=tuple(jax.ShapeDtypeStruct(v, bf16) for v in outs),
-        in_specs=[SM] + [VM] * len(whole),
-        out_specs=(VM,) * len(outs),
-        scratch_shapes=[pltpu.VMEM((D, total), bf16), pltpu.VMEM((total, D), bf16)],
+        functools.partial(end_kernel, blocks=blocks, more=len(more), n_dep=len(deps)),
+        grid=(1,),
+        out_shape=tuple(jax.ShapeDtypeStruct(*v) for v in outs),
+        in_specs=[SM] + specs + [AN] * len(deps),
+        out_specs=tuple(held(v[0]) for v in outs),
+        scratch_shapes=[
+            pltpu.VMEM((D, rows), bf16),
+            pltpu.VMEM((rows, D), bf16),
+            pltpu.VMEM((rows, D), f32),
+        ],
         compiler_params=pltpu.CompilerParams(vmem_limit_bytes=56 * 2**20),
         cost_estimate=BRIEF,
-    )(at, *whole)
-
-
-def mix_kernel(at_ref, x_ref, *outs, heads):
+    )(at, *whole, *deps)
+
+
+def mix_kernel(at_ref, x_ref, *refs, heads, ranks):
+    outs = refs[-ranks:]
     S, rows, W = x_ref.shape
     blocks = rows - heads - 16
     pair = blocks // len(outs)
@@ -745,17 +768,17 @@
         outs[i][pair + 2 * heads :, :] = jnp.concatenate([hi, total - hi], axis=0).astype(bf16)
 
 
-def mix(at, got, ranks, heads):
+def mix(at, got, ranks, heads, deps):
     S, rows, W = got.shape
     shape = ((rows - heads - 16) // ranks + 2 * heads + 16, W)
     return pl.pallas_call(
-        functools.partial(mix_kernel, heads=heads),
+        functools.partial(mix_kernel, heads=heads, ranks=ranks),
         out_shape=(jax.ShapeDtypeStruct(shape, bf16),) * ranks,
-        in_specs=[SM, VM],
+        in_specs=[SM, VM] + [AN] * len(deps),
         out_specs=(VM,) * ranks,
         compiler_params=pltpu.CompilerParams(vmem_limit_bytes=24 * 2**20),
         cost_estimate=BRIEF,
-    )(at, got)
+    )(at, got, *deps)
 
 
 def last_kernel(*refs, heads):
@@ -812,25 +835,25 @@
 
 def patches_kernel(at_ref, *refs):
     ins, out_ref = refs[:-1], refs[-1]
-    pairs = len(ins) // 2
-    for i in range(pairs):
+    ranks = len(ins) // 2
+    for i in range(ranks // 2):
         out_ref[3 * i + 1] = jnp.zeros(out_ref.shape[1:], f32)
-    for i in range(len(ins)):
+    for i in range(ranks):
         src = at_ref[1] ^ i
-        out_ref[3 * (src // 2) + 2 * (src % 2)] = ins[i][0].astype(f32)
-        out_ref[3 * (src // 2) + 1] += ins[i][1].astype(f32)
-
-
-def place_patches(at, parts):
-    shape = (3 * len(parts) // 2,) + parts[0].shape[1:]
+        out_ref[3 * (src // 2) + 2 * (src % 2)] = ins[i][...].astype(f32)
+        out_ref[3 * (src // 2) + 1] += ins[ranks + i][...].astype(f32)
+
+
+def place_patches(at, parts_a, parts_b):
+    shape = (3 * len(parts_a) // 2,) + parts_a[0].shape
     return pl.pallas_call(
         patches_kernel,
         out_shape=jax.ShapeDtypeStruct(shape, f32),
-        in_specs=[SM] + [VM] * len(parts),
+        in_specs=[SM] + [VM] * (2 * len(parts_a)),
         out_specs=VM,
         compiler_params=pltpu.CompilerParams(vmem_limit_bytes=24 * 2**20),
         cost_estimate=BRIEF,
-    )(at, *parts)
+    )(at, *parts_a, *parts_b)
 
 
 CP = 32
@@ -852,7 +875,9 @@
             perm[2 * a + b] = jnp.where(pixel == at, 1.0, 0.0).astype(bf16)
 
 
-def pixel_grad_kernel(cot_ref, w_ref, out_ref, perm, *, TR, TC):
+def pixel_grad_kernel(cot_ref, w_ref, *refs, TR, TC):
+    out_ref, perm = refs[-2:]
+
     @pl.when(pl.program_id(0) == 0)
     def _():
         place(perm, out_ref.shape[1], TR, TC)
@@ -864,7 +889,9 @@
     out_ref[0] = jnp.concatenate(parts, axis=1)
 
 
-def pixel_sample_kernel(x_ref, w_ref, out_ref, perm, *, TR, TC):
+def pixel_sample_kernel(x_ref, w_ref, *refs, TR, TC):
+    out_ref, perm = refs[-2:]
+
     @pl.when(pl.program_id(0) == 0)
     def _():
         place(perm, x_ref.shape[1], TR, TC)
@@ -874,7 +901,7 @@
     out_ref[0] = dot(window.astype(bf16), w_ref[0], NN).astype(bf16)
 
 
-def per_plane(body, first, weights, out_rows, out_lanes, out_type, toks, TR, TC):
+def per_plane(body, first, weights, out_rows, out_lanes, out_type, toks, TR, TC, deps=()):
     planes, ext, samples = weights.shape
 
     def whole(shape):
@@ -884,12 +911,12 @@
         functools.partial(body, TR=TR, TC=TC),
         grid=(planes,),
         out_shape=jax.ShapeDtypeStruct((planes, out_rows, out_lanes), out_type),
-        in_specs=[whole(first.shape[1:]), whole((ext, samples))],
+        in_specs=[whole(first.shape[1:]), whole((ext, samples))] + [AN] * len(deps),
         out_specs=whole((out_rows, out_lanes)),
         scratch_shapes=[pltpu.VMEM((4, toks, ext), bf16)],
         compiler_params=pltpu.CompilerParams(vmem_limit_bytes=24 * 2**20),
         cost_estimate=BRIEF,
-    )(first, weights)
+    )(first, weights, *deps)
 
 
 def swap_seq(value):
@@ -1008,7 +1035,9 @@
 
     channels = decoder.shape[1]
     local_dec = jnp.pad(decoder.transpose(2, 1, 0), ((0, 0), (0, CP - channels), (0, 0)))
-    local_qkv = self_qkv.reshape(D, 3, 2, W).transpose(2, 1, 3, 0).reshape(-1, D)
+    part = S // 2
+    qkv_piece = lax.dynamic_slice_in_dim(self_qkv, s // part * W, W, 2).reshape(D, 3 * W)
+    qkv_piece = lax.dynamic_slice_in_dim(qkv_piece, s % part * (3 * W // part), 3 * W // part, 1)
     per = D // (S * M)
     dec_rows = 4 * CP // S
     kv_rows = 2 * per
@@ -1021,7 +1050,7 @@
     w_kv, w_query = bundle_part(lead, 0, kv_rows), bundle_part(lead, kv_rows, per)
     first = gather_rows(
         jnp.concatenate(
-            [mine(local_qkv, 0), mine(cross_out, 0)], axis=0
+            [qkv_piece.T, mine(cross_out, 0)], axis=0
         )
     )
     up_rows = mlp_up.shape[1] // S
@@ -1153,7 +1182,7 @@
     grads_one = weight_grads([[(n3, du)], [(e3, g)], [(e2, a2)], [(x3b, d_pix)]], M)
     grads_one = hold(grads_one, [da2])
     pix = hold(pix, [grads_one])
-    dq_a2, dkv_a2 = attend_back(
+    dt2_a = attend_back(
         wide,
         [res_a2, da2, o_a2, heads_two[0]],
         S,
@@ -1163,6 +1192,7 @@
         hpd,
         True,
         [grads_one],
+        "lanes",
     )
     grads_one = reduce_rows(grads_one)
     pix = pix.reshape(KA + KB, S, M, cu).transpose(1, 2, 0, 3)
@@ -1178,7 +1208,7 @@
         half_total,
         hpd,
         True,
-        [dq_a2, got],
+        [dt2_a, got],
     )
     given = swap_pair(dkv_p2)
     dq_b2, dkv_b2 = attend_back(
@@ -1195,7 +1225,7 @@
     dq_b2 = (dq_b2.astype(f32) + dq_p2.astype(f32)).astype(bf16)
     dkv_b2 = (dkv_b2.astype(f32) + given.astype(f32)).astype(bf16)
     dt2 = [
-        swap_seq(jnp.concatenate([dq_a2, dkv_a2], axis=1).reshape(S, R, 3 * W)),
+        swap_seq(dt2_a),
         jnp.concatenate([dq_b2, dkv_b2], axis=1).reshape(S, RB, 3 * W),
     ]
 
@@ -1205,7 +1235,7 @@
         )
 
     def cross_back(i, da1, deps):
-        dq, dkv = attend_back(
+        return attend_back(
             limits[i],
             [res1[i], da1, o1[i], keys_one],
             S,
@@ -1215,10 +1245,10 @@
             hpd,
             False,
             deps,
+            "rows",
         )
-        return dq.reshape(S, rows[i], W), dkv.reshape(S, slots, 2 * W)
-
-    low_a = below(0, [dq_b2])
+
+    low_a = below(0, [dq_b2, given])
     x3b = hold(x3b, [low_a[0]])
     blocks_a, blocks_b = x3b[:R].reshape(M, R // M, D), x3b[R:].reshape(pairs, R // M, D)
     blocks_a = [lax.dynamic_index_in_dim(blocks_a, m ^ i, 0, keepdims=False) for i in range(M)]
@@ -1228,47 +1258,45 @@
     blocks_a, blocks_b = to_ranks(blocks_a), to_halves(blocks_b)
     da1_a = swap_seq(low_a[2])
     dt2[1] = swap_seq(hold(dt2[1], [da1_a]))
-    dq1_a, dkv1_a = cross_back(0, da1_a, [])
-    grads_one = sum_ranks(hold(grads_one, [low_a[0]]))
-    low_b = below(1, [dkv1_a])
-    da1_b = swap_seq(low_b[2])
-    dq1_a = swap_seq(hold(dq1_a, [da1_b]))
-    dkv1_a_rows = swap_seq(hold(dkv1_a, [da1_b]))
+    cross_a = cross_back(0, da1_a, [])
+    grads_one = sum_ranks(hold(grads_one, [da1_a]))
+    low_b = below(1, [cross_a])
+    got_a = swap_seq(cross_a)
+    da1_b = swap_seq(hold(low_b[2], [got_a]))
     d1, e1, da1, sums_two = zip(low_a, low_b)
 
     grads_two = weight_grads(
-        [[(n2[i], dt2[i]) for i in range(2)], [(e1[i], a1[i]) for i in range(2)]], M, [grads_one] + blocks_a + blocks_b
-    )
-    dq1_b, dkv1_b = cross_back(1, da1_b, [grads_two])
-    dkv1 = (dkv1_a, dkv1_b)
+        [[(n2[i], dt2[i]) for i in range(2)], [(e1[i], a1[i]) for i in range(2)]], M, [grads_one, got_a] + blocks_a + blocks_b
+    )
+    *sent_a, part_a, share, lift = end(
+        at, got_a, 0, w_query, w_kv, x0[0], n1, d1[0], norm_gains[:1], M, [grads_two]
+    )
+    cross_b = cross_back(1, da1_b, [grads_two, part_a])
     grads_two = reduce_rows(grads_two)
-    both_b = swap_seq(jnp.concatenate([dq1_b, dkv1_b], axis=2))
+    got_b = swap_seq(cross_b)
+
     two = sums_two[0] + sums_two[1]
     small = jnp.concatenate([two, sums_three], axis=0)
-    by_head = finish(at, dkv1, patch_pieces)
-    done = end(
+    sent_a, part_a = to_ranks(sent_a), to_ranks([part_a] * M)
+    by_head = finish(at, [cross_a, cross_b], rows, patch_pieces, [cross_b])
+    heads = by_head.shape[1]
+    *sent_b, part_b, final = end(
         at,
-        dq1_a,
-        both_b,
-        dkv1_a_rows,
+        got_b,
+        R // RB,
         w_query,
         w_kv,
-        x0,
+        x0[1],
         n1,
-        d1,
-        small,
+        d1[1],
         norm_gains[:1],
-        by_head,
-        M,
-    )
-    got_last = swap_seq(done[-1])
-    grad_tokens = place_rows(at, to_ranks(done[:M]), to_halves(done[M : M + pairs]), f32)
-    patch_grad = place_patches(at, to_ranks([done[-2]] * M))
-    heads = by_head.shape[1]
-    final = last(to_ranks(mix(at, got_last, M, heads)), heads)
-    grad_cross_query, grad_keys, grad_values, small = final
-    grad_cross_kv = jnp.stack([grad_keys, grad_values], axis=1)
-
+        pairs,
+        [],
+        [share, lift, small, by_head],
+    )
+    got_last = swap_seq(final)
+    grad_tokens = place_rows(at, sent_a, to_halves(sent_b), f32)
+    patch_grad = place_patches(at, part_a, to_ranks([part_b] * M))
     px_a = got[:, :, :, :KA].transpose(1, 2, 0, 3, 4).reshape(pairs, 2, S * KA, cu)
     px_b = got[:, :, :, KA:].transpose(1, 0, 2, 3, 4).reshape(pairs, S * KA, cu)
     tile = jnp.stack([px_a[:, 0], px_b, px_a[:, 1]], axis=1).reshape(planes, TR, TC, cu)
@@ -1277,12 +1305,16 @@
     corner = lax.ppermute(tile[:, 0, :1], "seq", [(i + 5, i) for i in ways[5]])
     fill = jnp.zeros((planes, toks - rim - TC - 1, cu), bf16)
     ext = jnp.concatenate([tile.reshape(planes, own, cu), rights, belows, corner, fill], axis=1)
-    ext = hold(ext, [done[-1]])
-    tokens_out = place_rows(at, blocks_a, blocks_b, bf16, [done[-1]])
+    ext = hold(ext, [final])
+    tokens_out = place_rows(at, blocks_a, blocks_b, bf16, [final])
     sampled = per_plane(
         pixel_sample_kernel, ext, weights_in, CP, weights_in.shape[2], bf16, toks, TR, TC
     )
     sampled = sampled[:, :channels].reshape(objects, 3, channels, 1, -1)
+
+    final = last(to_ranks(mix(at, got_last, M, heads, [sampled, tokens_out])), heads)
+    grad_cross_query, grad_keys, grad_values, small = final
+    grad_cross_kv = jnp.stack([grad_keys, grad_values], axis=1)
 
     grads_two = sum_ranks(grads_two)
     ff = hidden // M

time: 950 us -> 900 us (0.947)
  waiting for transfers between devices: 235 us -> 159 us
  starting transfers between devices: 123 us -> 147 us
  blocking collectives: 34.3 us -> 47.6 us
    ppermute x2, waiting for transfers between devices: 38.6 us -> 0.01 us  [swap_pair(): return lax.ppermute(value, 'mp', [(i, i ^ 1) for i in range(count)])]
    ppermute x12 -> x15, waiting for transfers between devices: 60.6 us -> 32.2 us  [to_ranks(): lax.ppermute(v, 'mp', moves[i])]
    ppermute x12 -> x15, starting transfers between devices: 21.1 us -> 41.5 us  [to_ranks(): lax.ppermute(v, 'mp', moves[i])]
    all_to_all x14 -> x13, waiting for transfers between devices: 69.1 us -> 49.5 us  [swap_seq(): return lax.all_to_all(value, 'seq', split_axis=0, concat_axis=0, tiled=True)]
    all_gather x3, waiting for transfers between devices: 19.8 us -> 36.9 us  [gather_rows(): return lax.all_gather(piece, ('mp', 'seq'), axis=0, tiled=False)]
    ppermute x2, starting transfers between devices: 3.11 us -> 17.3 us  [swap_pair(): return lax.ppermute(value, 'mp', [(i, i ^ 1) for i in range(count)])]
    all_to_all x2, blocking collectives: 34.3 us -> 47.6 us  [swap_seq(): return lax.all_to_all(value, 'seq', split_axis=0, concat_axis=0, tiled=True)]
    ppermute x4, waiting for transfers between devices: 0.99 us -> 11.7 us  [to_halves(): arrived.append(lax.ppermute(blocks[step], 'mp', moves))]
  transfers between devices with their start and end apart: 54 -> 56, of which waited for: 21 -> 19; matrix products, arithmetic and copies ran while one was open for 7% -> 6% of each run, Pallas kernels for 38% -> 40%
where the time goes in v7:
time: 900 us; the launch traced here: 882 us
  Pallas kernels  404 us (45%)
  waiting for transfers between devices  159 us (18%)
  starting transfers between devices  147 us (16%)
  local copies, waits for them, and re-layouts  96.6 us (11%)
  blocking collectives  47.6 us (5%)
  between operations  16.1 us (2%)
  other arithmetic  11.5 us (1%)
    pallas_call x5, Pallas kernels, attend_back(): pl.pallas_call(body, out_shape=tuple((jax.ShapeDtypeStruct(v, bf16) for v...  144 us
    pallas_call x4, Pallas kernels, attend(): pl.pallas_call(body, out_shape=(jax.ShapeDtypeStruct((queries, hpd * HD),...  80.2 us
    unnamed x219, local copies, waits for them, and re-layouts  59.4 us
    all_to_all x13, starting transfers between devices, swap_seq(): return lax.all_to_all(value, 'seq', split_axis=0, concat_axis=0, tiled=True)  54.2 us
    all_to_all x13, waiting for transfers between devices, swap_seq(): return lax.all_to_all(value, 'seq', split_axis=0, concat_axis=0, tiled=True)  49.5 us
    all_to_all x2, blocking collectives, swap_seq(): return lax.all_to_all(value, 'seq', split_axis=0, concat_axis=0, tiled=True)  47.6 us
    ppermute x15, starting transfers between devices, to_ranks(): lax.ppermute(v, 'mp', moves[i])  41.5 us
    pallas_call x1, Pallas kernels, feed_forward(): pl.pallas_call(functools.partial(mlp_kernel, steps=steps), grid=(steps,),...  36.9 us
  transfers between devices with their start and end apart: 56, of which 19 were waited for; matrix products, arithmetic and copies ran while one was open for 6% of the time, Pallas kernels for 40%

profile of v7, /device:TPU:0, one launch (start us, length us, event | category | flops | bytes accessed | tf_op | source)
XLA Modules:
  0.0 881.8 jit_solution(248427925715956929)
XLA Ops:
  28.2 15.2 %shard_map.280 = f32[18,160,128]{2,1,0:T(8,128)S(1)} custom-call(bf16[18,32,256]{2,1,0:T(8,128)(2,1)S(1)} %pad.21.cot_ref, bf16[18,561,256]{2,1,0:T(8,128)(2,1)S(1)} %bitcast.124), custom_call_target="tpu_custom_call" | custom-call | flops 1000000 | bytes 100000 | tf_op jit(solution)/shard_map/pallas_call | solution.py:910
  64.4 25.2 %all-gather.7.cloned.1.call-done = bf16[3072,1024]{1,0:T(8,128)(2,1)} async-done(((bf16[96,1024]{1,0:T(8,128)(2,1)}), bf16[3072,1024]{1,0:T(8,128)(2,1)}) %all-gather.7.cloned.1.call-update) | async-done | bytes 6291472 | tf_op jit(solution)/shard_map/all_gather | solution.py:940
  89.6 11.8 %shard_map.281 = (bf16[8,576,128]{2,1,0:T(8,128)(2,1)}, bf16[8,384,256]{2,1,0:T(8,128)(2,1)}, bf16[576,1024]{1,0:T(8,128)(2,1)}, bf16[1024,1024]{1,0:T(8,128)(2,1)}, bf16[2048,768]{1,0:T(8,128)(2,1)}) custom-call(s32[2]{0:T(128)} %pad_add_fusion.2.at_ref, bf16[384,1024]{1,0:T(8,128)(2,1)} %dynamic-slice_bitcast_fusion.1.xa_ref.x_ref, ...), custom_call_target="tpu_custom_call" | custom-call | flops 1000000 | bytes 100000 | tf_op jit(solution)/shard_map/pallas_call | solution.py:629
  101.4 23.2 %all_to_all.85.refs_1_.refs_0_ = bf16[8,576,128]{2,1,0:T(8,128)(2,1)} all-to-all(bf16[8,576,128]{2,1,0:T(8,128)(2,1)} %get-tuple-element.78), channel_id=1, replica_groups=mesh['seq'=8,'mp'=4] {'seq'}, dimensions={0} | all-to-all | bytes 2359296 | tf_op jit(solution)/shard_map/all_to_all | solution.py:923
  129.5 11.9 %shard_map.286 = (bf16[1536,128]{1,0:T(8,128)(2,1)}, bf16[2,1536,128]{2,1,0:T(8,128)(2,1)S(1)}) custom-call(s32[2]{0:T(128)S(1)} %pad_add_fusion.n_ref, bf16[8,576,128]{2,1,0:T(8,128)(2,1)S(1)} %copy-done.12, bf16[8,384,256]{2,1,0:T(8,128)(2,1)S(1)} %copy-done.5), custom_call_target="tpu_custom_call" | custom-call | flops 1000000 | bytes 100000 | tf_op jit(solution)/shard_map/pallas_call | solution.py:207
  142.3 5.3 all-to-all-done.1.refs_2_
  152.2 20.0 %shard_map.283 = (bf16[3072,128]{1,0:T(8,128)(2,1)S(1)}, bf16[2,3072,128]{2,1,0:T(8,128)(2,1)S(1)}) custom-call(s32[2]{0:T(128)S(1)} %pad_add_fusion.1.n_ref, bf16[8,576,128]{2,1,0:T(8,128)(2,1)S(1)} %copy-done.12, bf16[8,384,256]{2,1,0:T(8,128)(2,1)S(1)} %copy-done.5, bf16[32,72,128]{2,1,0:T(8,128)(2,1)} %all-to-all-done.1.refs_2_), custom_call_target="tpu_custom_call" | custom-call | flops 1000000 | bytes 100000 | tf_op jit(solution)/shard_map/pallas_call | solution.py:207
  174.3 4.3 all-to-all-start.2
  185.3 5.1 shard_map.287
  198.5 10.0 %shard_map.284 = (f32[384,1024]{1,0:T(8,128)S(1)}, bf16[384,1024]{1,0:T(8,128)(2,1)S(1)}, bf16[384,1024]{1,0:T(8,128)(2,1)S(1)}, bf16[8,384,384]{2,1,0:T(8,128)(2,1)S(1)}) custom-call(bf16[8,384,128]{2,1,0:T(8,128)(2,1)S(1)} %all-to-all-done.2.a_ref, bf16[384,1024]{1,0:T(8,128)(2,1)S(1)} %copy-done.14, f32[2,1024]{1,0:T(2,128)S(1)} %pad_maximum_fusion.9.norm_ref, ...), custom_call_target="tpu_custom_call" | custom-call | flops 1000000 | bytes 100000 | tf_op jit(solution)/shard_map/pallas_call | solution.py:313
  214.1 4.4 all-to-all-start.3
  219.4 15.3 %collective-permute-start.10 = (bf16[8,192,256]{2,1,0:T(8,128)(2,1)}, bf16[8,192,256]{2,1,0:T(8,128)(2,1)S(1)}, u32[]{:S(2)}, u32[]{:S(2)}) collective-permute-start(bf16[8,192,256]{2,1,0:T(8,128)(2,1)} %slice.167), channel_id=1, source_target_pairs={{0,1},{1,0},{2,3},{3,2},{4,5},{5,4},{6,7},{7,6},{8,9},{9,8},{10,11... | collective-permute-start | bytes 2359304 | tf_op jit(solution)/shard_map/ppermute | solution.py:936
  234.7 25.4 %all-to-all-done.3.refs_0_.refs_3_ = bf16[8,384,384]{2,1,0:T(8,128)(2,1)} async-done(((bf16[8,384,384]{2,1,0:T(8,128)(2,1)}), bf16[8,384,384]{2,1,0:T(8,128)(2,1)}, u32[]{:S(2)}, u32[]{:S(2)}) %all-to-all-start.3) | async-done | bytes 2359328 | tf_op jit(solution)/shard_map/all_to_all | solution.py:923
  260.1 31.7 %shard_map.285 = (bf16[3072,128]{1,0:T(8,128)(2,1)}, bf16[2,3072,128]{2,1,0:T(8,128)(2,1)S(1)}) custom-call(s32[2]{0:T(128)S(1)} %copy-done.86, bf16[8,384,384]{2,1,0:T(8,128)(2,1)} %all-to-all-done.3.refs_0_.refs_3_), custom_call_target="tpu_custom_call" | custom-call | flops 1000000 | bytes 100000 | tf_op jit(solution)/shard_map/pallas_call | solution.py:207
  292.9 4.4 all-to-all-start.4
  297.4 16.6 %shard_map.288 = (bf16[1536,128]{1,0:T(8,128)(2,1)S(1)}, bf16[2,1536,128]{2,1,0:T(8,128)(2,1)S(1)}) custom-call(s32[2]{0:T(128)S(1)} %copy-done.86, bf16[8,192,384]{2,1,0:T(8,128)(2,1)S(1)} %all-to-all-done.6.refs_0_.refs_3_, bf16[8,192,256]{2,1,0:T(8,128)(2,1)S(1)} %collective-permute-done.10.refs_1_.refs_3_, bf16[3072,128]{1,0:T(8,128)(2,1)} %get-tuple-element.82.refs_2_), custom_call_target="tpu_custom_call" | custom-call | flops 1000000 | bytes 100000 | tf_op jit(solution)/shard_map/pallas_call | solution.py:207
  328.2 9.4 %all-gather.11.cloned.1.call-done = bf16[9728,1024]{1,0:T(8,128)(2,1)} async-done(((bf16[304,1024]{1,0:T(8,128)(2,1)}), bf16[9728,1024]{1,0:T(8,128)(2,1)}) %all-gather.11.cloned.1.call-update) | async-done | bytes 19922960 | tf_op jit(solution)/shard_map/all_gather | solution.py:940
  337.6 36.9 %shard_map.290 = (bf16[576,1024]{1,0:T(8,128)(2,1)}, bf16[576,1024]{1,0:T(8,128)(2,1)}, bf16[576,4096]{1,0:T(8,128)(2,1)}, bf16[576,4096]{1,0:T(8,128)(2,1)}, bf...) custom-call(bf16[8,384,128]{2,1,0:T(8,128)(2,1)} %all-to-all-done.4., ...), custom_call_target="tpu_custom_call" | custom-call | flops 1000000 | bytes 100000 | tf_op jit(solution)/shard_map/pallas_call | solution.py:433
  374.5 4.8 all-to-all-start.8
  379.8 24.0 %shard_map.291.refs_0_ = bf16[1024,9728]{1,0:T(8,128)(2,1)} custom-call(bf16[576,1024]{1,0:T(8,128)(2,1)} %get-tuple-element.91.refs_0_, bf16[576,1024]{1,0:T(8,128)(2,1)} %get-tuple-element.92.refs_1_, bf16[576,1024]{1,0:T(8,128)(2,1)} %get-tuple-element.93.refs_2_, bf16[576,1024]{1,0:T(8,128)(2,1)} %get-tuple-element.88.refs_3_.refs_0_, ...), custom_call_target="tpu_custom_call" | custom-call | flops 1000000 | bytes 100000 | tf_op jit(solution)/shard_map/pallas_call | solution.py:588
  407.1 4.2 all-to-all-start.10
  411.3 62.2 %shard_map.293.refs_4_ = bf16[8,384,384]{2,1,0:T(8,128)(2,1)} custom-call(s32[2]{0:T(128)S(1)} %copy-done.86, bf16[2,3072,128]{2,1,0:T(8,128)(2,1)} %copy-done.51, bf16[8,576,128]{2,1,0:T(8,128)(2,1)S(1)} %copy-done.4, bf16[3072,128]{1,0:T(8,128)(2,1)} %get-tuple-element.82.refs_2_, bf16[8,384,384]{2,1,0:T(8,128)(2,1)} %all-to-all-done.3.refs_0_.refs_3_, ...), custom_call_target="tpu_custom_call" | custom-call | flops 1000000 | bytes 100000 | tf_op jit(solution)/shard_map/pallas_call | solution.py:242
  473.5 4.4 all-to-all-start.9
  478.1 20.2 %shard_map.295 = (bf16[1536,128]{1,0:T(8,128)(2,1)S(1)}, bf16[1536,256]{1,0:T(8,128)(2,1)}) custom-call(s32[2]{0:T(128)S(1)} %copy-done.86, bf16[2,1536,128]{2,1,0:T(8,128)(2,1)} %copy-done.35, bf16[8,576,128]{2,1,0:T(8,128)(2,1)} %copy-done.3, bf16[1536,128]{1,0:T(8,128)(2,1)S(1)} %get-tuple-element.85.refs_2_, bf16[8,192,256]{2,1,0:T(8,128)(2,1)} %copy-done.34, ...), custom_call_target="tpu_custom_call" | custom-call | flops 1000000 | bytes 100000 | tf_op jit(solution)/shard_map/pallas_call | solution.py:242
  500.3 19.4 %shard_map.296 = (bf16[1536,128]{1,0:T(8,128)(2,1)S(1)}, bf16[1536,256]{1,0:T(8,128)(2,1)S(1)}) custom-call(s32[2]{0:T(128)S(1)} %copy-done.86, bf16[2,1536,128]{2,1,0:T(8,128)(2,1)} %copy-done.35, bf16[8,576,128]{2,1,0:T(8,128)(2,1)} %copy-done.3, bf16[1536,128]{1,0:T(8,128)(2,1)S(1)} %get-tuple-element.85.refs_2_, bf16[8,192,384]{2,1,0:T(8,128)(2,1)} %copy-done.13, ...), custom_call_target="tpu_custom_call" | custom-call | flops 1000000 | bytes 100000 | tf_op jit(solution)/shard_map/pallas_call | solution.py:242
  528.5 11.7 %shard_map.297 = (f32[384,1024]{1,0:T(8,128)S(1)}, bf16[384,1024]{1,0:T(8,128)(2,1)S(1)}, bf16[8,384,128]{2,1,0:T(8,128)(2,1)S(1)}, f32[2,1024]{1,0:T(2,128)S(1)}) custom-call(bf16[8,384,384]{2,1,0:T(8,128)(2,1)} %all-to-all-done.9.t_ref.refs_4_, f32[384,1024]{1,0:T(8,128)S(1)} %copy-done.23, f32[576,1024]{1,0:T(8,128)S(1)} %copy-done.17, ...), custom_call_target="tpu_custom_call" | custom-call | flops 1000000 | bytes 100000 | tf_op jit(solution)/shard_map/pallas_call | solution.py:530
  542.4 24.4 %all_to_all.86.refs_1_ = bf16[8,384,128]{2,1,0:T(8,128)(2,1)} all-to-all(bf16[8,384,128]{2,1,0:T(8,128)(2,1)S(1)} %get-tuple-element.106), channel_id=1, replica_groups=mesh['seq'=8,'mp'=4] {'seq'}, dimensions={0} | all-to-all | bytes 1572864 | tf_op jit(solution)/shard_map/all_to_all | solution.py:923
  569.0 4.3 copy.140
  581.0 26.2 %shard_map.300.refs_0_.a_ref = bf16[8,768,128]{2,1,0:T(8,128)(2,1)} custom-call(s32[2]{0:T(128)S(1)} %pad_add_fusion.1.n_ref, bf16[2,3072,128]{2,1,0:T(8,128)(2,1)} %copy-done.48, bf16[8,384,128]{2,1,0:T(8,128)(2,1)S(1)} %copy-done.15, bf16[3072,128]{1,0:T(8,128)(2,1)S(1)} %copy-done.33, bf16[8,384,256]{2,1,0:T(8,128)(2,1)} %get-tuple-element.79.refs_1_.refs_3_), custom_call_target="tpu_custom_call" | custom-call | flops 1000000 | bytes 100000 | tf_op jit(solution)/shard_map/pallas_call | solution.py:242
  607.2 4.3 all-to-all-start.13
  615.0 9.9 %collective-permute-start.12 = (bf16[96,1024]{1,0:T(8,128)(2,1)}, bf16[96,1024]{1,0:T(8,128)(2,1)S(1)}, u32[]{:S(2)}, u32[]{:S(2)}) collective-permute-start(bf16[96,1024]{1,0:T(8,128)(2,1)} %get-tuple-element.205), channel_id=1, source_target_pairs={{0,1},{1,0},{2,3},{3,2},{4,5},{5,4},{6,7},{7,6},{8,9},{9,8},{10,11... | collective-permute-start | bytes 589832 | tf_op jit(solution)/shard_map/ppermute | solution.py:964
  631.3 9.0 %shard_map.301 = (f32[192,1024]{1,0:T(8,128)S(1)}, bf16[192,1024]{1,0:T(8,128)(2,1)S(1)}, bf16[8,192,128]{2,1,0:T(8,128)(2,1)S(1)}, f32[2,1024]{1,0:T(2,128)S(1)}) custom-call(bf16[8,192,384]{2,1,0:T(8,128)(2,1)S(1)} %all-to-all-done.12.t_ref.refs_5_, f32[192,1024]{1,0:T(8,128)S(1)} %copy-done.28, f32[576,1024]{1,0:T(8,128)S(1)} %copy-done.18, ...), custom_call_target="tpu_custom_call" | custom-call | flops 1000000 | bytes 100000 | tf_op jit(solution)/shard_map/pallas_call | solution.py:530
  645.5 8.3 collective-permute-done.16.refs_15_.refs_5_
  653.8 11.6 %shard_map.304.refs_0_.refs_4_ = bf16[1024,4096]{1,0:T(8,128)(2,1)} custom-call(bf16[384,1024]{1,0:T(8,128)(2,1)} %copy-done.63, bf16[192,1024]{1,0:T(8,128)(2,1)} %copy-done.71, bf16[384,1024]{1,0:T(8,128)(2,1)} %copy-done.65, bf16[192,1024]{1,0:T(8,128)(2,1)} %copy-done.73, bf16[8,384,384]{2,1,0:T(8,128)(2,1)} %all-to-all-done.9.t_ref.refs_4_, ...), custom_call_target="tpu_custom_call" | custom-call | flops 1000000 | bytes 100000 | tf_op jit(solution)/shard_map/pallas_call | solution.py:588
  665.4 3.9 all-to-all-start.14
  669.3 10.5 %shard_map.305 = (bf16[96,1024]{1,0:T(8,128)(2,1)}, bf16[96,1024]{1,0:T(8,128)(2,1)}, bf16[96,1024]{1,0:T(8,128)(2,1)}, bf16[96,1024]{1,0:T(8,128)(2,1)}, bf16[1...) custom-call(s32[2]{0:T(128)} %pad_add_fusion.2.at_ref, ...), custom_call_target="tpu_custom_call" | custom-call | flops 1000000 | bytes 100000 | tf_op jit(solution)/shard_map/pallas_call | solution.py:736
  680.8 16.0 %shard_map.306.b_ref.refs_8_ = bf16[8,576,128]{2,1,0:T(8,128)(2,1)} custom-call(s32[2]{0:T(128)S(1)} %pad_add_fusion.n_ref, bf16[2,1536,128]{2,1,0:T(8,128)(2,1)S(1)} %copy-done.67, bf16[8,192,128]{2,1,0:T(8,128)(2,1)S(1)} %all-to-all-done.14.refs_1_, bf16[1536,128]{1,0:T(8,128)(2,1)} %get-tuple-element.83.refs_2_, ...), custom_call_target="tpu_custom_call" | custom-call | flops 1000000 | bytes 100000 | tf_op jit(solution)/shard_map/pallas_call | solution.py:242
  696.8 4.8 all-to-all-start.15
  712.0 15.2 %all-to-all-done.15.g_ref = bf16[8,576,128]{2,1,0:T(8,128)(2,1)} async-done(((bf16[8,576,128]{2,1,0:T(8,128)(2,1)}), bf16[8,576,128]{2,1,0:T(8,128)(2,1)}, u32[]{:S(2)}, u32[]{:S(2)}) %all-to-all-start.15) | async-done | bytes 1179680 | tf_op jit(solution)/shard_map/all_to_all | solution.py:923
  727.2 8.3 shard_map.308
  735.5 4.4 all-to-all-start.16
  740.1 10.9 %reduce-scatter.9.cloned.1.call-done = bf16[128,4096]{1,0:T(8,128)(2,1)} async-done(((bf16[1024,4096]{1,0:T(8,128)(2,1)}), bf16[128,4096]{1,0:T(8,128)(2,1)}) %reduce-scatter.9.cloned.1.call-update) | async-done | bytes 1048592 | tf_op jit(solution)/shard_map/reduce_scatter | solution.py:959
  759.3 8.0 collective-permute-done.19
  771.7 5.4 concatenate.35.refs_0_
  781.4 26.4 %collective-permute-done.22.refs_3_ = bf16[96,1024]{1,0:T(8,128)(2,1)S(1)} collective-permute-done((bf16[96,1024]{1,0:T(8,128)(2,1)}, bf16[96,1024]{1,0:T(8,128)(2,1)S(1)}, u32[]{:S(2)}, u32[]{:S(2)}) %collective-permute-start.22) | collective-permute-done | bytes 196640 | tf_op jit(solution)/shard_map/ppermute | solution.py:964
  807.9 11.3 %collective-permute-start.29 = (bf16[192,768]{1,0:T(8,128)(2,1)S(1)}, bf16[192,768]{1,0:T(8,128)(2,1)}, u32[]{:S(2)}, u32[]{:S(2)}) collective-permute-start(bf16[192,768]{1,0:T(8,128)(2,1)S(1)} %copy-done.74), channel_id=1, source_target_pairs={{0,2},{1,3},{2,0},{3,1},{4,6},{5,7},{6,4},{7,5},{8,10},{9,11},{10,... | collective-permute-start | bytes 884744 | tf_op jit(solution)/shard_map/ppermute | solution.py:964
  830.5 11.7 %shard_map.311 = bf16[18,32,256]{2,1,0:T(8,128)(2,1)S(1)} custom-call(bf16[18,160,128]{2,1,0:T(8,128)(2,1)S(1)} %copy-done.19, bf16[18,561,256]{2,1,0:T(8,128)(2,1)S(1)} %bitcast.125), custom_call_target="tpu_custom_call" | custom-call | flops 1000000 | bytes 100000 | tf_op jit(solution)/shard_map/pallas_call | solution.py:910
  862.6 5.7 collective-permute-done.32.refs_2_
  (412 shorter events, 198.1 us)
Async XLA Ops:
  7.2 82.4 %all-gather.7.cloned.1.call-start = ((), (), s32[]{:S(2)}) async-start(), calls=%async_computation.24 | async-start | bytes 6488064 | tf_op jit(solution)/shard_map/all_gather | solution.py:940
  11.8 169.2 %all-gather.9.cloned.1.call-start = ((), (), s32[]{:S(2)}) async-start(), calls=%async_computation.25 | async-start | bytes 8650752 | tf_op jit(solution)/shard_map/all_gather | solution.py:940
  16.7 320.9 %all-gather.11.cloned.1.call-start = ((), (), s32[]{:S(2)}) async-start(), calls=%async_computation.26 | async-start | bytes 20545536 | tf_op jit(solution)/shard_map/all_gather | solution.py:940
  21.1 37.7 %collective-permute-start.1 = (bf16[384,768]{1,0:T(8,128)(2,1)S(1)}, bf16[384,768]{1,0:T(8,128)(2,1)S(1)}, u32[]{:S(2)}, u32[]{:S(2)}) collective-permute-start(bf16[384,768]{1,0:T(8,128)(2,1)S(1)} %pad_maximum_fusion.2.refs_0_), channel_id=1, source_target_pairs={{0,8},{4,12},{8,0},{12,4},{16,24},{20,28},{24,16},{28,20},{1,9},{5... | collective-permute-start | bytes 1769480 | tf_op jit(solution)/shard_map/ppermute | solution.py:985
  24.1 35.9 %collective-permute-start.3 = (bf16[384,768]{1,0:T(8,128)(2,1)S(1)}, bf16[384,768]{1,0:T(8,128)(2,1)}, u32[]{:S(2)}, u32[]{:S(2)}) collective-permute-start(bf16[384,768]{1,0:T(8,128)(2,1)S(1)} %pad_maximum_fusion.2.refs_0_), channel_id=1, source_target_pairs={{0,16},{4,20},{8,24},{12,28},{16,0},{20,4},{24,8},{28,12},{1,17},{... | collective-permute-start | bytes 1769480 | tf_op jit(solution)/shard_map/ppermute | solution.py:985
  25.5 34.6 %collective-permute-start.5 = (bf16[384,768]{1,0:T(8,128)(2,1)S(1)}, bf16[384,768]{1,0:T(8,128)(2,1)}, u32[]{:S(2)}, u32[]{:S(2)}) collective-permute-start(bf16[384,768]{1,0:T(8,128)(2,1)S(1)} %pad_maximum_fusion.2.refs_0_), channel_id=1, source_target_pairs={{0,24},{4,28},{8,16},{12,20},{16,8},{20,12},{24,0},{28,4},{1,25},{... | collective-permute-start | bytes 1769480 | tf_op jit(solution)/shard_map/ppermute | solution.py:985
  43.4 12.3 %collective-permute-start.8 = (f32[18,8,128]{2,1,0:T(8,128)S(1)}, f32[18,8,128]{2,1,0:T(8,128)S(1)}, u32[]{:S(2)}, u32[]{:S(2)}) collective-permute-start(f32[18,8,128]{2,1,0:T(8,128)S(1)} %slice.160), channel_id=1, source_target_pairs={{0,16},{4,20},{8,24},{12,28},{1,17},{5,21},{9,25},{13,29},{2,18},{... | collective-permute-start | bytes 221192 | tf_op jit(solution)/shard_map/ppermute | solution.py:1096
  124.6 23.0 %all-to-all-start.1 = ((bf16[32,72,128]{2,1,0:T(8,128)(2,1)}), bf16[32,72,128]{2,1,0:T(8,128)(2,1)}, u32[]{:S(2)}, u32[]{:S(2)}) async-start(bf16[32,72,128]{2,1,0:T(8,128)(2,1)} %shard_map.282), calls=%async_computation.1 | async-start | bytes 1179648 | tf_op jit(solution)/shard_map/all_to_all | solution.py:931
  147.6 26.7 %all-to-all-start.5 = ((bf16[8,192,128]{2,1,0:T(8,128)(2,1)}), bf16[8,192,128]{2,1,0:T(8,128)(2,1)S(1)}, u32[]{:S(2)}, u32[]{:S(2)}) async-start(bf16[8,192,128]{2,1,0:T(8,128)(2,1)} %bitcast.27), calls=%async_computation.5 | async-start | bytes 786432 | tf_op jit(solution)/shard_map/all_to_all | solution.py:923
  174.3 18.7 %all-to-all-start.2 = ((bf16[8,384,128]{2,1,0:T(8,128)(2,1)}), bf16[8,384,128]{2,1,0:T(8,128)(2,1)S(1)}, u32[]{:S(2)}, u32[]{:S(2)}) async-start(bf16[8,384,128]{2,1,0:T(8,128)(2,1)} %bitcast.130), calls=%async_computation.2 | async-start | bytes 1572864 | tf_op jit(solution)/shard_map/all_to_all | solution.py:923
  193.8 20.3 %all-to-all-start.6 = ((bf16[8,192,384]{2,1,0:T(8,128)(2,1)}), bf16[8,192,384]{2,1,0:T(8,128)(2,1)S(1)}, u32[]{:S(2)}, u32[]{:S(2)}) async-start(bf16[8,192,384]{2,1,0:T(8,128)(2,1)} %copy-done.54), calls=%async_computation.6 | async-start | bytes 2359296 | tf_op jit(solution)/shard_map/all_to_all | solution.py:923
  214.1 46.0 %all-to-all-start.3 = ((bf16[8,384,384]{2,1,0:T(8,128)(2,1)}), bf16[8,384,384]{2,1,0:T(8,128)(2,1)}, u32[]{:S(2)}, u32[]{:S(2)}) async-start(bf16[8,384,384]{2,1,0:T(8,128)(2,1)} %copy-done.44), calls=%async_computation.3 | async-start | bytes 4718592 | tf_op jit(solution)/shard_map/all_to_all | solution.py:923
  219.4 77.9 %collective-permute-start.10 = (bf16[8,192,256]{2,1,0:T(8,128)(2,1)}, bf16[8,192,256]{2,1,0:T(8,128)(2,1)S(1)}, u32[]{:S(2)}, u32[]{:S(2)}) collective-permute-start(bf16[8,192,256]{2,1,0:T(8,128)(2,1)} %slice.167), channel_id=1, source_target_pairs={{0,1},{1,0},{2,3},{3,2},{4,5},{5,4},{6,7},{7,6},{8,9},{9,8},{10,11... | collective-permute-start | bytes 2359304 | tf_op jit(solution)/shard_map/ppermute | solution.py:936
  292.9 23.6 %all-to-all-start.4 = ((bf16[8,384,128]{2,1,0:T(8,128)(2,1)}), bf16[8,384,128]{2,1,0:T(8,128)(2,1)}, u32[]{:S(2)}, u32[]{:S(2)}) async-start(bf16[8,384,128]{2,1,0:T(8,128)(2,1)} %bitcast.26), calls=%async_computation.4 | async-start | bytes 1572864 | tf_op jit(solution)/shard_map/all_to_all | solution.py:923
  374.5 29.3 %all-to-all-start.8 = ((bf16[8,576,128]{2,1,0:T(8,128)(2,1)}), bf16[8,576,128]{2,1,0:T(8,128)(2,1)S(1)}, u32[]{:S(2)}, u32[]{:S(2)}) async-start(bf16[8,576,128]{2,1,0:T(8,128)(2,1)} %get-tuple-element.90), calls=%async_computation.8 | async-start | bytes 2359296 | tf_op jit(solution)/shard_map/all_to_all | solution.py:923
  379.3 189.7 %reduce-scatter.7.cloned.1.call-start = ((), (), s32[]{:S(2)}) async-start(), calls=%async_computation.21 | async-start | bytes 22413312 | tf_op jit(solution)/shard_map/reduce_scatter | solution.py:959
  407.1 66.4 %all-to-all-start.10 = ((bf16[32,72,128]{2,1,0:T(8,128)(2,1)}), bf16[32,72,128]{2,1,0:T(8,128)(2,1)S(1)}, u32[]{:S(2)}, u32[]{:S(2)}) async-start(bf16[32,72,128]{2,1,0:T(8,128)(2,1)} %bitcast.41), calls=%async_computation.10 | async-start | bytes 1179648 | tf_op jit(solution)/shard_map/all_to_all | solution.py:931
  473.5 50.8 %all-to-all-start.9 = ((bf16[8,384,384]{2,1,0:T(8,128)(2,1)}), bf16[8,384,384]{2,1,0:T(8,128)(2,1)}, u32[]{:S(2)}, u32[]{:S(2)}) async-start(bf16[8,384,384]{2,1,0:T(8,128)(2,1)} %shard_map.293.refs_4_), calls=%async_computation.9 | async-start | bytes 4718592 | tf_op jit(solution)/shard_map/all_to_all | solution.py:923
  477.9 164.9 %reduce-scatter.13.cloned.1.call-start = ((), (), s32[]{:S(2)}) async-start(), calls=%async_computation.27 | async-start | bytes 3112960
  498.3 21.5 %collective-permute-start.11 = (bf16[1536,256]{1,0:T(8,128)(2,1)}, bf16[1536,256]{1,0:T(8,128)(2,1)S(1)}, u32[]{:S(2)}, u32[]{:S(2)}) collective-permute-start(bf16[1536,256]{1,0:T(8,128)(2,1)} %get-tuple-element.102), channel_id=1, source_target_pairs={{0,1},{1,0},{2,3},{3,2},{4,5},{5,4},{6,7},{7,6},{8,9},{9,8},{10,11... | collective-permute-start | bytes 2359304 | tf_op jit(solution)/shard_map/ppermute | solution.py:936
  576.1 31.0 %all-to-all-start.12 = ((bf16[8,192,384]{2,1,0:T(8,128)(2,1)}), bf16[8,192,384]{2,1,0:T(8,128)(2,1)S(1)}, u32[]{:S(2)}, u32[]{:S(2)}) async-start(bf16[8,192,384]{2,1,0:T(8,128)(2,1)} %shard_map.299), calls=%async_computation.12 | async-start | bytes 2359296 | tf_op jit(solution)/shard_map/all_to_all | solution.py:923
  607.2 46.6 %all-to-all-start.13 = ((bf16[8,768,128]{2,1,0:T(8,128)(2,1)}), bf16[8,768,128]{2,1,0:T(8,128)(2,1)}, u32[]{:S(2)}, u32[]{:S(2)}) async-start(bf16[8,768,128]{2,1,0:T(8,128)(2,1)} %shard_map.300.refs_0_.a_ref), calls=%async_computation.13 | async-start | bytes 3145728 | tf_op jit(solution)/shard_map/all_to_all | solution.py:923
  611.5 139.6 %reduce-scatter.9.cloned.1.call-start = ((), (), s32[]{:S(2)}) async-start(), calls=%async_computation.22 | async-start | bytes 9437184 | tf_op jit(solution)/shard_map/reduce_scatter | solution.py:959
  615.0 30.4 %collective-permute-start.12 = (bf16[96,1024]{1,0:T(8,128)(2,1)}, bf16[96,1024]{1,0:T(8,128)(2,1)S(1)}, u32[]{:S(2)}, u32[]{:S(2)}) collective-permute-start(bf16[96,1024]{1,0:T(8,128)(2,1)} %get-tuple-element.205), channel_id=1, source_target_pairs={{0,1},{1,0},{2,3},{3,2},{4,5},{5,4},{6,7},{7,6},{8,9},{9,8},{10,11... | collective-permute-start | bytes 589832 | tf_op jit(solution)/shard_map/ppermute | solution.py:964
  624.9 20.5 %collective-permute-start.13 = (bf16[96,1024]{1,0:T(8,128)(2,1)}, bf16[96,1024]{1,0:T(8,128)(2,1)S(1)}, u32[]{:S(2)}, u32[]{:S(2)}) collective-permute-start(bf16[96,1024]{1,0:T(8,128)(2,1)} %get-tuple-element.204), channel_id=1, source_target_pairs={{0,2},{1,3},{2,0},{3,1},{4,6},{5,7},{6,4},{7,5},{8,10},{9,11},{10,... | collective-permute-start | bytes 589832 | tf_op jit(solution)/shard_map/ppermute | solution.py:964
  624.9 20.5 %collective-permute-start.14 = (bf16[96,1024]{1,0:T(8,128)(2,1)}, bf16[96,1024]{1,0:T(8,128)(2,1)S(1)}, u32[]{:S(2)}, u32[]{:S(2)}) collective-permute-start(bf16[96,1024]{1,0:T(8,128)(2,1)} %get-tuple-element.203), channel_id=1, source_target_pairs={{0,3},{1,2},{2,1},{3,0},{4,7},{5,6},{6,5},{7,4},{8,11},{9,10},{10,... | collective-permute-start | bytes 589832 | tf_op jit(solution)/shard_map/ppermute | solution.py:964
  628.0 17.4 %collective-permute-start.15 = (bf16[96,1024]{1,0:T(8,128)(2,1)}, bf16[96,1024]{1,0:T(8,128)(2,1)S(1)}, u32[]{:S(2)}, u32[]{:S(2)}) collective-permute-start(bf16[96,1024]{1,0:T(8,128)(2,1)} %get-tuple-element.213), channel_id=1, source_target_pairs={{0,0},{1,2},{2,1},{3,3},{4,4},{5,6},{6,5},{7,7},{8,8},{9,10},{10,9... | collective-permute-start | bytes 589832 | tf_op jit(solution)/shard_map/ppermute | solution.py:972
  629.6 24.2 %collective-permute-start.16 = (bf16[96,1024]{1,0:T(8,128)(2,1)}, bf16[96,1024]{1,0:T(8,128)(2,1)}, u32[]{:S(2)}, u32[]{:S(2)}) collective-permute-start(bf16[96,1024]{1,0:T(8,128)(2,1)} %get-tuple-element.212), channel_id=1, source_target_pairs={{0,1},{1,3},{2,0},{3,2},{4,5},{5,7},{6,4},{7,6},{8,9},{9,11},{10,8... | collective-permute-start | bytes 589832 | tf_op jit(solution)/shard_map/ppermute | solution.py:972
  665.4 14.4 %all-to-all-start.14 = ((bf16[8,192,128]{2,1,0:T(8,128)(2,1)}), bf16[8,192,128]{2,1,0:T(8,128)(2,1)S(1)}, u32[]{:S(2)}, u32[]{:S(2)}) async-start(bf16[8,192,128]{2,1,0:T(8,128)(2,1)} %shard_map.302), calls=%async_computation.14 | async-start | bytes 786432 | tf_op jit(solution)/shard_map/all_to_all | solution.py:923
  696.8 30.4 %all-to-all-start.15 = ((bf16[8,576,128]{2,1,0:T(8,128)(2,1)}), bf16[8,576,128]{2,1,0:T(8,128)(2,1)}, u32[]{:S(2)}, u32[]{:S(2)}) async-start(bf16[8,576,128]{2,1,0:T(8,128)(2,1)} %shard_map.306.b_ref.refs_8_), calls=%async_computation.16 | async-start | bytes 2359296 | tf_op jit(solution)/shard_map/all_to_all | solution.py:923
  735.5 109.2 %all-to-all-start.16 = ((bf16[8,1232,128]{2,1,0:T(8,128)(2,1)}), bf16[8,1232,128]{2,1,0:T(8,128)(2,1)}, u32[]{:S(2)}, u32[]{:S(2)}) async-start(bf16[8,1232,128]{2,1,0:T(8,128)(2,1)} %get-tuple-element.125.refs_6_.refs_1_), calls=%async_computation.17 | async-start | bytes 5046272 | tf_op jit(solution)/shard_map/all_to_all | solution.py:923
  739.9 131.6 %reduce-scatter.11.cloned.1.call-start = ((), (), s32[]{:S(2)}) async-start(), calls=%async_computation.23 | async-start | bytes 1310720 | tf_op jit(solution)/shard_map/reduce_scatter | solution.py:977
  751.3 19.9 %collective-permute-start.17 = (bf16[18,16,128]{2,1,0:T(8,128)(2,1)S(1)}, bf16[18,16,128]{2,1,0:T(8,128)(2,1)S(1)}, u32[]{:S(2)}, u32[]{:S(2)}) collective-permute-start(bf16[18,16,128]{2,1,0:T(8,128)(2,1)S(1)} %bitcast.171), channel_id=1, source_target_pairs={{4,0},{8,4},{12,8},{20,16},{24,20},{28,24},{5,1},{9,5},{13,9},{21,... | collective-permute-start | bytes 221192 | tf_op jit(solution)/shard_map/ppermute | solution.py:1303
  752.8 16.0 %collective-permute-start.18 = (bf16[18,8,128]{2,1,0:T(8,128)(2,1)S(1)}, bf16[18,8,128]{2,1,0:T(8,128)(2,1)S(1)}, u32[]{:S(2)}, u32[]{:S(2)}) collective-permute-start(bf16[18,8,128]{2,1,0:T(8,128)(2,1)S(1)} %slice_bitcast_fusion.7), channel_id=1, source_target_pairs={{16,0},{20,4},{24,8},{28,12},{17,1},{21,5},{25,9},{29,13},{18,2},{... | collective-permute-start | bytes 110600 | tf_op jit(solution)/shard_map/ppermute | solution.py:1304
  754.1 23.1 %collective-permute-start.20 = (bf16[96,1024]{1,0:T(8,128)(2,1)}, bf16[96,1024]{1,0:T(8,128)(2,1)S(1)}, u32[]{:S(2)}, u32[]{:S(2)}) collective-permute-start(bf16[96,1024]{1,0:T(8,128)(2,1)} %get-tuple-element.127), channel_id=1, source_target_pairs={{0,1},{1,0},{2,3},{3,2},{4,5},{5,4},{6,7},{7,6},{8,9},{9,8},{10,11... | collective-permute-start | bytes 589832 | tf_op jit(solution)/shard_map/ppermute | solution.py:964
  756.0 24.5 %collective-permute-start.21 = (bf16[96,1024]{1,0:T(8,128)(2,1)}, bf16[96,1024]{1,0:T(8,128)(2,1)S(1)}, u32[]{:S(2)}, u32[]{:S(2)}) collective-permute-start(bf16[96,1024]{1,0:T(8,128)(2,1)} %get-tuple-element.128), channel_id=1, source_target_pairs={{0,2},{1,3},{2,0},{3,1},{4,6},{5,7},{6,4},{7,5},{8,10},{9,11},{10,... | collective-permute-start | bytes 589832 | tf_op jit(solution)/shard_map/ppermute | solution.py:964
  767.3 51.8 %collective-permute-start.25 = (bf16[192,768]{1,0:T(8,128)(2,1)S(1)}, bf16[192,768]{1,0:T(8,128)(2,1)S(1)}, u32[]{:S(2)}, u32[]{:S(2)}) collective-permute-start(bf16[192,768]{1,0:T(8,128)(2,1)S(1)} %copy-done.53), channel_id=1, source_target_pairs={{0,1},{1,0},{2,3},{3,2},{4,5},{5,4},{6,7},{7,6},{8,9},{9,8},{10,11... | collective-permute-start | bytes 884744 | tf_op jit(solution)/shard_map/ppermute | solution.py:964
  768.8 52.3 %collective-permute-start.26 = (bf16[192,768]{1,0:T(8,128)(2,1)S(1)}, bf16[192,768]{1,0:T(8,128)(2,1)S(1)}, u32[]{:S(2)}, u32[]{:S(2)}) collective-permute-start(bf16[192,768]{1,0:T(8,128)(2,1)S(1)} %copy-done.53), channel_id=1, source_target_pairs={{0,2},{1,3},{2,0},{3,1},{4,6},{5,7},{6,4},{7,5},{8,10},{9,11},{10,... | collective-permute-start | bytes 884744 | tf_op jit(solution)/shard_map/ppermute | solution.py:964
  771.2 52.8 %collective-permute-start.27 = (bf16[192,768]{1,0:T(8,128)(2,1)S(1)}, bf16[192,768]{1,0:T(8,128)(2,1)S(1)}, u32[]{:S(2)}, u32[]{:S(2)}) collective-permute-start(bf16[192,768]{1,0:T(8,128)(2,1)S(1)} %copy-done.53), channel_id=1, source_target_pairs={{0,3},{1,2},{2,1},{3,0},{4,7},{5,6},{6,5},{7,4},{8,11},{9,10},{10,... | collective-permute-start | bytes 884744 | tf_op jit(solution)/shard_map/ppermute | solution.py:964
  777.2 30.7 %collective-permute-start.22 = (bf16[96,1024]{1,0:T(8,128)(2,1)}, bf16[96,1024]{1,0:T(8,128)(2,1)S(1)}, u32[]{:S(2)}, u32[]{:S(2)}) collective-permute-start(bf16[96,1024]{1,0:T(8,128)(2,1)} %get-tuple-element.129), channel_id=1, source_target_pairs={{0,3},{1,2},{2,1},{3,0},{4,7},{5,6},{6,5},{7,4},{8,11},{9,10},{10,... | collective-permute-start | bytes 589832 | tf_op jit(solution)/shard_map/ppermute | solution.py:964
  780.5 73.4 %collective-permute-start.28 = (bf16[192,768]{1,0:T(8,128)(2,1)S(1)}, bf16[192,768]{1,0:T(8,128)(2,1)}, u32[]{:S(2)}, u32[]{:S(2)}) collective-permute-start(bf16[192,768]{1,0:T(8,128)(2,1)S(1)} %copy-done.74), channel_id=1, source_target_pairs={{0,1},{1,0},{2,3},{3,2},{4,5},{5,4},{6,7},{7,6},{8,9},{9,8},{10,11... | collective-permute-start | bytes 884744 | tf_op jit(solution)/shard_map/ppermute | solution.py:964
  807.9 51.3 %collective-permute-start.29 = (bf16[192,768]{1,0:T(8,128)(2,1)S(1)}, bf16[192,768]{1,0:T(8,128)(2,1)}, u32[]{:S(2)}, u32[]{:S(2)}) collective-permute-start(bf16[192,768]{1,0:T(8,128)(2,1)S(1)} %copy-done.74), channel_id=1, source_target_pairs={{0,2},{1,3},{2,0},{3,1},{4,6},{5,7},{6,4},{7,5},{8,10},{9,11},{10,... | collective-permute-start | bytes 884744 | tf_op jit(solution)/shard_map/ppermute | solution.py:964
  819.1 40.0 %collective-permute-start.30 = (bf16[192,768]{1,0:T(8,128)(2,1)S(1)}, bf16[192,768]{1,0:T(8,128)(2,1)}, u32[]{:S(2)}, u32[]{:S(2)}) collective-permute-start(bf16[192,768]{1,0:T(8,128)(2,1)S(1)} %copy-done.74), channel_id=1, source_target_pairs={{0,3},{1,2},{2,1},{3,0},{4,7},{5,6},{6,5},{7,4},{8,11},{9,10},{10,... | collective-permute-start | bytes 884744 | tf_op jit(solution)/shard_map/ppermute | solution.py:964
  821.1 26.9 %collective-permute-start.23 = (bf16[96,1024]{1,0:T(8,128)(2,1)}, bf16[96,1024]{1,0:T(8,128)(2,1)}, u32[]{:S(2)}, u32[]{:S(2)}) collective-permute-start(bf16[96,1024]{1,0:T(8,128)(2,1)} %get-tuple-element.130), channel_id=1, source_target_pairs={{0,0},{1,2},{2,1},{3,3},{4,4},{5,6},{6,5},{7,7},{8,8},{9,10},{10,9... | collective-permute-start | bytes 589832 | tf_op jit(solution)/shard_map/ppermute | solution.py:972
  824.1 29.9 %collective-permute-start.24 = (bf16[96,1024]{1,0:T(8,128)(2,1)}, bf16[96,1024]{1,0:T(8,128)(2,1)}, u32[]{:S(2)}, u32[]{:S(2)}) collective-permute-start(bf16[96,1024]{1,0:T(8,128)(2,1)} %get-tuple-element.131), channel_id=1, source_target_pairs={{0,1},{1,3},{2,0},{3,2},{4,5},{5,7},{6,4},{7,6},{8,9},{9,11},{10,8... | collective-permute-start | bytes 589832 | tf_op jit(solution)/shard_map/ppermute | solution.py:972
  848.0 14.5 %collective-permute-start.31 = (bf16[656,128]{1,0:T(8,128)(2,1)S(1)}, bf16[656,128]{1,0:T(8,128)(2,1)S(1)}, u32[]{:S(2)}, u32[]{:S(2)}) collective-permute-start(bf16[656,128]{1,0:T(8,128)(2,1)S(1)} %get-tuple-element.134), channel_id=1, source_target_pairs={{0,1},{1,0},{2,3},{3,2},{4,5},{5,4},{6,7},{7,6},{8,9},{9,8},{10,11... | collective-permute-start | bytes 503816 | tf_op jit(solution)/shard_map/ppermute | solution.py:964
  853.9 14.4 %collective-permute-start.32 = (bf16[656,128]{1,0:T(8,128)(2,1)S(1)}, bf16[656,128]{1,0:T(8,128)(2,1)S(1)}, u32[]{:S(2)}, u32[]{:S(2)}) collective-permute-start(bf16[656,128]{1,0:T(8,128)(2,1)S(1)} %get-tuple-element.135), channel_id=1, source_target_pairs={{0,2},{1,3},{2,0},{3,1},{4,6},{5,7},{6,4},{7,5},{8,10},{9,11},{10,... | collective-permute-start | bytes 503816 | tf_op jit(solution)/shard_map/ppermute | solution.py:964
  853.9 14.4 %collective-permute-start.33 = (bf16[656,128]{1,0:T(8,128)(2,1)S(1)}, bf16[656,128]{1,0:T(8,128)(2,1)S(1)}, u32[]{:S(2)}, u32[]{:S(2)}) collective-permute-start(bf16[656,128]{1,0:T(8,128)(2,1)S(1)} %get-tuple-element.136), channel_id=1, source_target_pairs={{0,3},{1,2},{2,1},{3,0},{4,7},{5,6},{6,5},{7,4},{8,11},{9,10},{10,... | collective-permute-start | bytes 503816 | tf_op jit(solution)/shard_map/ppermute | solution.py:964
  (110 other events, 943.1 us)
Sparse Core Ops, SparseCore 0:
  11.9 77.6 all-gather.6
  92.5 88.4 all-gather.8
  183.8 153.8 all-gather.10
  405.0 164.0 reduce-scatter.6
  573.5 52.0 reduce-scatter.12
  665.6 85.4 reduce-scatter.8
  753.4 45.9 reduce-scatter.10

commit v8 on v7

--- a/solution.py
+++ b/solution.py
@@ -672,11 +672,24 @@
     )(at, *cross, *patch_pieces, *deps)
 
 
+def pack_lanes(ref, at, value):
+    rows = value.shape[0]
+    for i in range(value.shape[1] // LANES):
+        ref[at + i * rows : at + (i + 1) * rows, :] = value[:, i * LANES : (i + 1) * LANES]
+
+
+def unpack_lanes(ref, at, rows, columns):
+    parts = [ref[at + i * rows : at + (i + 1) * rows, :] for i in range(columns // LANES)]
+    return jnp.concatenate(parts, axis=1)
+
+
 def end_kernel(
     at_ref, g_ref, wq_ref, wkv_ref, x_ref, n_ref, d_ref, gain_ref, *refs, blocks, more, n_dep
 ):
     extra, refs = refs[:more], refs[more + n_dep :]
-    outs, part_ref, refs = refs[:blocks], refs[blocks], refs[blocks + 1 :]
+    outs, refs = refs[:blocks], refs[blocks:]
+    if more:
+        part_ref, refs = refs[0], refs[1:]
     outs_more, (n_t, dq, total) = refs[:-3], refs[-3:]
     S, _, W = g_ref.shape
     rows = x_ref.shape[0]
@@ -689,12 +702,19 @@
     )
     total[...] = d_ref[...] + grad
     place = at_ref[1] // 2 if more else at_ref[1]
-    for i in range(blocks):
-        outs[i][...] = total[pl.ds(pl.multiple_of((place ^ i) * own, 8), own), :].astype(bf16)
     keys = []
     for i in range(S):
         keys += [g_ref[i, rows : rows + slots, :], g_ref[i, rows + slots :, :]]
-    part_ref[...] = dot(jnp.concatenate(keys, axis=1), wkv_ref[...], NN).astype(bf16)
+    part = dot(jnp.concatenate(keys, axis=1), wkv_ref[...], NN).astype(bf16)
+    for i in range(blocks):
+        block = total[pl.ds(pl.multiple_of((place ^ i) * own, 8), own), :].astype(bf16)
+        if more:
+            outs[i][...] = block
+        else:
+            pack_lanes(outs[i], 0, block)
+            pack_lanes(outs[i], own * block.shape[1] // LANES, part)
+    if more:
+        part_ref[...] = part
     lift = jnp.concatenate([gain, shift], axis=0)
     tall = n_t.shape[0] // S
     for i in range(0, S, 2):
@@ -725,10 +745,12 @@
     S, _, W = got.shape
     rows, D = x0.shape
     slots, width = (got.shape[1] - rows) // 2, w_kv.shape[1]
-    outs = [((rows // blocks, D), bf16)] * blocks + [((slots, width), bf16)]
+    own = rows // blocks
     if more:
+        outs = [((own, D), bf16)] * blocks + [((slots, width), bf16)]
         outs += [((S, D + more[3].shape[1] + 16, W), bf16)]
     else:
+        outs = [(((own * D + slots * width) // LANES, LANES), bf16)] * blocks
         outs += [((S // 2, D, 2 * W), f32), ((2, D), f32)]
     whole = [got, w_query, w_kv, x0, n1, d1, gain, *more]
     specs = [once(v.shape) for v in whole]
@@ -806,25 +828,23 @@
     )(*parts)
 
 
-def place_kernel(at_ref, *refs, ranks):
-    whole, halves, out_ref = refs[:ranks], refs[ranks:-1], refs[-1]
+def place_kernel(at_ref, *refs, ranks, packed):
+    whole, halves, out_ref = refs[:ranks], refs[ranks : ranks + ranks // 2], refs[-1]
+    _, own, D = out_ref.shape
     for i in range(ranks):
         src = at_ref[1] ^ i
-        out_ref[3 * (src // 2) + 2 * (src % 2)] = whole[i][...].astype(out_ref.dtype)
+        block = unpack_lanes(whole[i], 0, own, D) if packed else whole[i][...]
+        out_ref[3 * (src // 2) + 2 * (src % 2)] = block.astype(out_ref.dtype)
     for i in range(ranks // 2):
         src = at_ref[1] % (ranks // 2) ^ i
         out_ref[3 * src + 1] = halves[i][...].astype(out_ref.dtype)
 
 
-def place_rows(at, whole, halves, kind, deps=()):
+def place_rows(at, whole, halves, kind, deps=(), packed=False):
     ranks = len(whole)
-    shape = (3 * ranks // 2,) + whole[0].shape
-
-    def kernel(at_ref, *refs):
-        place_kernel(at_ref, *refs[: ranks + ranks // 2], refs[-1], ranks=ranks)
-
+    shape = (3 * ranks // 2,) + halves[0].shape
     return pl.pallas_call(
-        kernel,
+        functools.partial(place_kernel, ranks=ranks, packed=packed),
         out_shape=jax.ShapeDtypeStruct(shape, kind),
         in_specs=[SM] + [VM] * (ranks + ranks // 2) + [AN] * len(deps),
         out_specs=VM,
@@ -836,16 +856,19 @@
 def patches_kernel(at_ref, *refs):
     ins, out_ref = refs[:-1], refs[-1]
     ranks = len(ins) // 2
+    _, slots, width = out_ref.shape
+    at = ins[0].shape[0] - slots * width // LANES
     for i in range(ranks // 2):
         out_ref[3 * i + 1] = jnp.zeros(out_ref.shape[1:], f32)
     for i in range(ranks):
         src = at_ref[1] ^ i
-        out_ref[3 * (src // 2) + 2 * (src % 2)] = ins[i][...].astype(f32)
+        block = unpack_lanes(ins[i], at, slots, width)
+        out_ref[3 * (src // 2) + 2 * (src % 2)] = block.astype(f32)
         out_ref[3 * (src // 2) + 1] += ins[ranks + i][...].astype(f32)
 
 
 def place_patches(at, parts_a, parts_b):
-    shape = (3 * len(parts_a) // 2,) + parts_a[0].shape
+    shape = (3 * len(parts_a) // 2,) + parts_b[0].shape
     return pl.pallas_call(
         patches_kernel,
         out_shape=jax.ShapeDtypeStruct(shape, f32),
@@ -1268,17 +1291,25 @@
     grads_two = weight_grads(
         [[(n2[i], dt2[i]) for i in range(2)], [(e1[i], a1[i]) for i in range(2)]], M, [grads_one, got_a] + blocks_a + blocks_b
     )
-    *sent_a, part_a, share, lift = end(
+    *sent_a, share, lift = end(
         at, got_a, 0, w_query, w_kv, x0[0], n1, d1[0], norm_gains[:1], M, [grads_two]
     )
-    cross_b = cross_back(1, da1_b, [grads_two, part_a])
+    cross_b = cross_back(1, da1_b, [grads_two, lift])
     grads_two = reduce_rows(grads_two)
     got_b = swap_seq(cross_b)
 
     two = sums_two[0] + sums_two[1]
     small = jnp.concatenate([two, sums_three], axis=0)
-    sent_a, part_a = to_ranks(sent_a), to_ranks([part_a] * M)
-    by_head = finish(at, [cross_a, cross_b], rows, patch_pieces, [cross_b])
+    px_a = got[:, :, :, :KA].transpose(1, 2, 0, 3, 4).reshape(pairs, 2, S * KA, cu)
+    px_b = got[:, :, :, KA:].transpose(1, 0, 2, 3, 4).reshape(pairs, S * KA, cu)
+    tile = jnp.stack([px_a[:, 0], px_b, px_a[:, 1]], axis=1).reshape(planes, TR, TC, cu)
+    rights = lax.ppermute(tile[:, :, 0], "seq", [(i + 1, i) for i in ways[1]])
+    belows = lax.ppermute(tile[:, 0], "seq", [(i + 4, i) for i in ways[4]])
+    corner = lax.ppermute(tile[:, 0, :1], "seq", [(i + 5, i) for i in ways[5]])
+    fill = jnp.zeros((planes, toks - rim - TC - 1, cu), bf16)
+    ext = jnp.concatenate([tile.reshape(planes, own, cu), rights, belows, corner, fill], axis=1)
+    sent_a = to_ranks(sent_a)
+    by_head = finish(at, [cross_a, cross_b], rows, patch_pieces, [*sent_a, ext])
     heads = by_head.shape[1]
     *sent_b, part_b, final = end(
         at,
@@ -1295,16 +1326,8 @@
         [share, lift, small, by_head],
     )
     got_last = swap_seq(final)
-    grad_tokens = place_rows(at, sent_a, to_halves(sent_b), f32)
-    patch_grad = place_patches(at, part_a, to_ranks([part_b] * M))
-    px_a = got[:, :, :, :KA].transpose(1, 2, 0, 3, 4).reshape(pairs, 2, S * KA, cu)
-    px_b = got[:, :, :, KA:].transpose(1, 0, 2, 3, 4).reshape(pairs, S * KA, cu)
-    tile = jnp.stack([px_a[:, 0], px_b, px_a[:, 1]], axis=1).reshape(planes, TR, TC, cu)
-    rights = lax.ppermute(tile[:, :, 0], "seq", [(i + 1, i) for i in ways[1]])
-    belows = lax.ppermute(tile[:, 0], "seq", [(i + 4, i) for i in ways[4]])
-    corner = lax.ppermute(tile[:, 0, :1], "seq", [(i + 5, i) for i in ways[5]])
-    fill = jnp.zeros((planes, toks - rim - TC - 1, cu), bf16)
-    ext = jnp.concatenate([tile.reshape(planes, own, cu), rights, belows, corner, fill], axis=1)
+    grad_tokens = place_rows(at, sent_a, to_halves(sent_b), f32, [], True)
+    patch_grad = place_patches(at, sent_a, to_ranks([part_b] * M))
     ext = hold(ext, [final])
     tokens_out = place_rows(at, blocks_a, blocks_b, bf16, [final])
     sampled = per_plane(

time: 900 us -> 866 us (0.962)
  waiting for transfers between devices: 159 us -> 129 us
  Pallas kernels: 404 us -> 413 us
    ppermute x15 -> x12, waiting for transfers between devices: 32.2 us -> 13 us  [to_ranks(): lax.ppermute(v, 'mp', moves[i])]
    ppermute x2, starting transfers between devices: 17.3 us -> 3.59 us  [swap_pair(): return lax.ppermute(value, 'mp', [(i, i ^ 1) for i in range(count)])]
    reduce_scatter x2, waiting for transfers between devices: 13.2 us -> 3.15 us  [reduce_rows(): return lax.psum_scatter(value, 'seq', scatter_dimension=0, tiled=True)]
    ppermute x15 -> x12, starting transfers between devices: 41.5 us -> 44.9 us  [to_ranks(): lax.ppermute(v, 'mp', moves[i])]
    unnamed x219 -> x209, local copies, waits for them, and re-layouts: 59.4 us -> 59.3 us
  transfers between devices with their start and end apart: 56 -> 53, of which waited for: 19 -> 17; matrix products, arithmetic and copies ran while one was open for 6% -> 6% of each run, Pallas kernels for 40% -> 43%
where the time goes in v8:
time: 866 us; the launch traced here: 852 us
  Pallas kernels  413 us (48%)
  starting transfers between devices  140 us (16%)
  waiting for transfers between devices  129 us (15%)
  local copies, waits for them, and re-layouts  94.7 us (11%)
  blocking collectives  47.1 us (5%)
  between operations  16.2 us (2%)
  other arithmetic  11.6 us (1%)
    pallas_call x5, Pallas kernels, attend_back(): pl.pallas_call(body, out_shape=tuple((jax.ShapeDtypeStruct(v, bf16) for v...  148 us
    pallas_call x4, Pallas kernels, attend(): pl.pallas_call(body, out_shape=(jax.ShapeDtypeStruct((queries, hpd * HD),...  84 us
    unnamed x209, local copies, waits for them, and re-layouts  59.3 us
    all_to_all x13, starting transfers between devices, swap_seq(): return lax.all_to_all(value, 'seq', split_axis=0, concat_axis=0, tiled=True)  55.6 us
    all_to_all x2, blocking collectives, swap_seq(): return lax.all_to_all(value, 'seq', split_axis=0, concat_axis=0, tiled=True)  47.1 us
    all_to_all x13, waiting for transfers between devices, swap_seq(): return lax.all_to_all(value, 'seq', split_axis=0, concat_axis=0, tiled=True)  47 us
    ppermute x12, starting transfers between devices, to_ranks(): lax.ppermute(v, 'mp', moves[i])  44.9 us
    pallas_call x1, Pallas kernels, feed_forward(): pl.pallas_call(functools.partial(mlp_kernel, steps=steps), grid=(steps,),...  36.9 us
  transfers between devices with their start and end apart: 53, of which 17 were waited for; matrix products, arithmetic and copies ran while one was open for 6% of the time, Pallas kernels for 43%

profile of v8, /device:TPU:0, one launch (start us, length us, event | category | flops | bytes accessed | tf_op | source)
XLA Modules:
  0.0 851.8 jit_solution(17320414126913018556)
XLA Ops:
  28.2 15.2 %shard_map.280 = f32[18,160,128]{2,1,0:T(8,128)S(1)} custom-call(bf16[18,32,256]{2,1,0:T(8,128)(2,1)S(1)} %pad.21.cot_ref, bf16[18,561,256]{2,1,0:T(8,128)(2,1)S(1)} %bitcast.124), custom_call_target="tpu_custom_call" | custom-call | flops 1000000 | bytes 100000 | tf_op jit(solution)/shard_map/pallas_call | solution.py:933
  43.5 3.7 collective-permute-start.8
  64.2 25.6 %all-gather.7.cloned.1.call-done = bf16[3072,1024]{1,0:T(8,128)(2,1)} async-done(((bf16[96,1024]{1,0:T(8,128)(2,1)}), bf16[3072,1024]{1,0:T(8,128)(2,1)}) %all-gather.7.cloned.1.call-update) | async-done | bytes 6291472 | tf_op jit(solution)/shard_map/all_gather | solution.py:963
  89.8 11.8 %shard_map.281 = (bf16[8,576,128]{2,1,0:T(8,128)(2,1)}, bf16[8,384,256]{2,1,0:T(8,128)(2,1)}, bf16[576,1024]{1,0:T(8,128)(2,1)}, bf16[1024,1024]{1,0:T(8,128)(2,1)}, bf16[2048,768]{1,0:T(8,128)(2,1)}) custom-call(s32[2]{0:T(128)} %pad_add_fusion.2.at_ref, bf16[384,1024]{1,0:T(8,128)(2,1)} %dynamic-slice_bitcast_fusion.1.xa_ref.x_ref, ...), custom_call_target="tpu_custom_call" | custom-call | flops 1000000 | bytes 100000 | tf_op jit(solution)/shard_map/pallas_call | solution.py:629
  101.6 22.7 %all_to_all.85.refs_1_.refs_0_ = bf16[8,576,128]{2,1,0:T(8,128)(2,1)} all-to-all(bf16[8,576,128]{2,1,0:T(8,128)(2,1)} %get-tuple-element.77), channel_id=1, replica_groups=mesh['seq'=8,'mp'=4] {'seq'}, dimensions={0} | all-to-all | bytes 2359296 | tf_op jit(solution)/shard_map/all_to_all | solution.py:946
  129.2 15.0 %shard_map.286 = (bf16[1536,128]{1,0:T(8,128)(2,1)}, bf16[2,1536,128]{2,1,0:T(8,128)(2,1)S(1)}) custom-call(s32[2]{0:T(128)S(1)} %pad_add_fusion.n_ref, bf16[8,576,128]{2,1,0:T(8,128)(2,1)S(1)} %copy-done.11, bf16[8,384,256]{2,1,0:T(8,128)(2,1)S(1)} %copy-done.5), custom_call_target="tpu_custom_call" | custom-call | flops 1000000 | bytes 100000 | tf_op jit(solution)/shard_map/pallas_call | solution.py:207
  147.4 3.9 all-to-all-start.5
  152.1 20.0 %shard_map.283 = (bf16[3072,128]{1,0:T(8,128)(2,1)S(1)}, bf16[2,3072,128]{2,1,0:T(8,128)(2,1)S(1)}) custom-call(s32[2]{0:T(128)S(1)} %pad_add_fusion.1.n_ref, bf16[8,576,128]{2,1,0:T(8,128)(2,1)S(1)} %copy-done.11, bf16[8,384,256]{2,1,0:T(8,128)(2,1)S(1)} %copy-done.5, bf16[32,72,128]{2,1,0:T(8,128)(2,1)} %all-to-all-done.1.refs_2_), custom_call_target="tpu_custom_call" | custom-call | flops 1000000 | bytes 100000 | tf_op jit(solution)/shard_map/pallas_call | solution.py:207
  174.2 4.4 all-to-all-start.2
  185.3 5.1 shard_map.287
  197.9 10.2 %shard_map.284 = (f32[384,1024]{1,0:T(8,128)S(1)}, bf16[384,1024]{1,0:T(8,128)(2,1)S(1)}, bf16[384,1024]{1,0:T(8,128)(2,1)S(1)}, bf16[8,384,384]{2,1,0:T(8,128)(2,1)S(1)}) custom-call(bf16[8,384,128]{2,1,0:T(8,128)(2,1)} %all-to-all-done.2.a_ref, bf16[384,1024]{1,0:T(8,128)(2,1)S(1)} %copy-done.13, f32[2,1024]{1,0:T(2,128)S(1)} %pad_maximum_fusion.9.norm_ref, ...), custom_call_target="tpu_custom_call" | custom-call | flops 1000000 | bytes 100000 | tf_op jit(solution)/shard_map/pallas_call | solution.py:313
  213.5 4.4 all-to-all-start.3
  220.5 40.8 %all-to-all-done.3.refs_0_.refs_3_ = bf16[8,384,384]{2,1,0:T(8,128)(2,1)} async-done(((bf16[8,384,384]{2,1,0:T(8,128)(2,1)}), bf16[8,384,384]{2,1,0:T(8,128)(2,1)}, u32[]{:S(2)}, u32[]{:S(2)}) %all-to-all-start.3) | async-done | bytes 2359328 | tf_op jit(solution)/shard_map/all_to_all | solution.py:946
  261.3 31.7 %shard_map.285 = (bf16[3072,128]{1,0:T(8,128)(2,1)}, bf16[2,3072,128]{2,1,0:T(8,128)(2,1)S(1)}) custom-call(s32[2]{0:T(128)S(1)} %copy-done.80, bf16[8,384,384]{2,1,0:T(8,128)(2,1)} %all-to-all-done.3.refs_0_.refs_3_), custom_call_target="tpu_custom_call" | custom-call | flops 1000000 | bytes 100000 | tf_op jit(solution)/shard_map/pallas_call | solution.py:207
  293.0 4.4 all-to-all-start.4
  297.5 17.2 %shard_map.288 = (bf16[1536,128]{1,0:T(8,128)(2,1)S(1)}, bf16[2,1536,128]{2,1,0:T(8,128)(2,1)S(1)}) custom-call(s32[2]{0:T(128)S(1)} %copy-done.80, bf16[8,192,384]{2,1,0:T(8,128)(2,1)S(1)} %all-to-all-done.6.refs_0_.refs_3_, bf16[8,192,256]{2,1,0:T(8,128)(2,1)} %collective-permute-done.10.refs_1_.refs_3_, bf16[3072,128]{1,0:T(8,128)(2,1)} %get-tuple-element.81.refs_2_), custom_call_target="tpu_custom_call" | custom-call | flops 1000000 | bytes 100000 | tf_op jit(solution)/shard_map/pallas_call | solution.py:207
  316.4 4.2 all-to-all-start.7
  328.9 5.2 all-gather.11.cloned.1.call-done
  334.1 36.9 %shard_map.290 = (bf16[576,1024]{1,0:T(8,128)(2,1)}, bf16[576,1024]{1,0:T(8,128)(2,1)}, bf16[576,4096]{1,0:T(8,128)(2,1)}, bf16[576,4096]{1,0:T(8,128)(2,1)}, bf...) custom-call(bf16[8,384,128]{2,1,0:T(8,128)(2,1)} %all-to-all-done.4., ...), custom_call_target="tpu_custom_call" | custom-call | flops 1000000 | bytes 100000 | tf_op jit(solution)/shard_map/pallas_call | solution.py:433
  371.0 5.2 all-to-all-start.8
  376.6 24.0 %shard_map.291.refs_0_ = bf16[1024,9728]{1,0:T(8,128)(2,1)} custom-call(bf16[576,1024]{1,0:T(8,128)(2,1)} %get-tuple-element.90.refs_0_, bf16[576,1024]{1,0:T(8,128)(2,1)} %get-tuple-element.91.refs_1_, bf16[576,1024]{1,0:T(8,128)(2,1)} %get-tuple-element.92.refs_2_, bf16[576,1024]{1,0:T(8,128)(2,1)} %get-tuple-element.87.refs_3_.refs_0_, ...), custom_call_target="tpu_custom_call" | custom-call | flops 1000000 | bytes 100000 | tf_op jit(solution)/shard_map/pallas_call | solution.py:588
  403.9 4.2 all-to-all-start.10
  408.0 62.2 %shard_map.293.refs_4_ = bf16[8,384,384]{2,1,0:T(8,128)(2,1)} custom-call(s32[2]{0:T(128)S(1)} %copy-done.80, bf16[2,3072,128]{2,1,0:T(8,128)(2,1)} %copy-done.55, bf16[8,576,128]{2,1,0:T(8,128)(2,1)S(1)} %copy-done.4, bf16[3072,128]{1,0:T(8,128)(2,1)} %get-tuple-element.81.refs_2_, bf16[8,384,384]{2,1,0:T(8,128)(2,1)} %all-to-all-done.3.refs_0_.refs_3_, ...), custom_call_target="tpu_custom_call" | custom-call | flops 1000000 | bytes 100000 | tf_op jit(solution)/shard_map/pallas_call | solution.py:242
  470.3 4.4 all-to-all-start.9
  474.9 20.2 %shard_map.295 = (bf16[1536,128]{1,0:T(8,128)(2,1)S(1)}, bf16[1536,256]{1,0:T(8,128)(2,1)}) custom-call(s32[2]{0:T(128)S(1)} %copy-done.80, bf16[2,1536,128]{2,1,0:T(8,128)(2,1)} %copy-done.37, bf16[8,576,128]{2,1,0:T(8,128)(2,1)} %copy-done.3, bf16[1536,128]{1,0:T(8,128)(2,1)S(1)} %get-tuple-element.84.refs_2_, ...), custom_call_target="tpu_custom_call" | custom-call | flops 1000000 | bytes 100000 | tf_op jit(solution)/shard_map/pallas_call | solution.py:242
  497.0 19.4 %shard_map.296 = (bf16[1536,128]{1,0:T(8,128)(2,1)S(1)}, bf16[1536,256]{1,0:T(8,128)(2,1)S(1)}) custom-call(s32[2]{0:T(128)S(1)} %copy-done.80, bf16[2,1536,128]{2,1,0:T(8,128)(2,1)} %copy-done.37, bf16[8,576,128]{2,1,0:T(8,128)(2,1)} %copy-done.3, bf16[1536,128]{1,0:T(8,128)(2,1)S(1)} %get-tuple-element.84.refs_2_, bf16[8,192,384]{2,1,0:T(8,128)(2,1)} %copy-done.12, ...), custom_call_target="tpu_custom_call" | custom-call | flops 1000000 | bytes 100000 | tf_op jit(solution)/shard_map/pallas_call | solution.py:242
  525.3 11.7 %shard_map.297 = (f32[384,1024]{1,0:T(8,128)S(1)}, bf16[384,1024]{1,0:T(8,128)(2,1)S(1)}, bf16[8,384,128]{2,1,0:T(8,128)(2,1)S(1)}, f32[2,1024]{1,0:T(2,128)S(1)}) custom-call(bf16[8,384,384]{2,1,0:T(8,128)(2,1)} %all-to-all-done.9.t_ref.refs_4_, f32[384,1024]{1,0:T(8,128)S(1)} %copy-done.24, f32[576,1024]{1,0:T(8,128)S(1)} %copy-done.19, ...), custom_call_target="tpu_custom_call" | custom-call | flops 1000000 | bytes 100000 | tf_op jit(solution)/shard_map/pallas_call | solution.py:530
  538.2 24.4 %all_to_all.86.refs_1_ = bf16[8,384,128]{2,1,0:T(8,128)(2,1)} all-to-all(bf16[8,384,128]{2,1,0:T(8,128)(2,1)S(1)} %get-tuple-element.105), channel_id=1, replica_groups=mesh['seq'=8,'mp'=4] {'seq'}, dimensions={0} | all-to-all | bytes 1572864 | tf_op jit(solution)/shard_map/all_to_all | solution.py:946
  565.8 4.4 copy.140
  572.6 3.7 all-to-all-start.12
  577.5 26.2 %shard_map.300.refs_0_.a_ref = bf16[8,768,128]{2,1,0:T(8,128)(2,1)} custom-call(s32[2]{0:T(128)S(1)} %pad_add_fusion.1.n_ref, bf16[2,3072,128]{2,1,0:T(8,128)(2,1)} %copy-done.52, bf16[8,384,128]{2,1,0:T(8,128)(2,1)S(1)} %copy-done.14, bf16[3072,128]{1,0:T(8,128)(2,1)S(1)} %copy-done.36, bf16[8,384,256]{2,1,0:T(8,128)(2,1)} %get-tuple-element.78.refs_1_.refs_3_), custom_call_target="tpu_custom_call" | custom-call | flops 1000000 | bytes 100000 | tf_op jit(solution)/shard_map/pallas_call | solution.py:242
  603.7 4.3 all-to-all-start.13
  620.8 9.1 %shard_map.301 = (f32[192,1024]{1,0:T(8,128)S(1)}, bf16[192,1024]{1,0:T(8,128)(2,1)S(1)}, bf16[8,192,128]{2,1,0:T(8,128)(2,1)S(1)}, f32[2,1024]{1,0:T(2,128)S(1)}) custom-call(bf16[8,192,384]{2,1,0:T(8,128)(2,1)S(1)} %all-to-all-done.12.t_ref.refs_5_, f32[192,1024]{1,0:T(8,128)S(1)} %copy-done.31, f32[576,1024]{1,0:T(8,128)S(1)} %copy-done.20, ...), custom_call_target="tpu_custom_call" | custom-call | flops 1000000 | bytes 100000 | tf_op jit(solution)/shard_map/pallas_call | solution.py:530
  635.0 9.5 %collective-permute-done.16.refs_15_.refs_5_ = bf16[96,1024]{1,0:T(8,128)(2,1)S(1)} collective-permute-done((bf16[96,1024]{1,0:T(8,128)(2,1)}, bf16[96,1024]{1,0:T(8,128)(2,1)S(1)}, u32[]{:S(2)}, u32[]{:S(2)}) %collective-permute-start.16) | collective-permute-done | bytes 196640 | tf_op jit(solution)/shard_map/ppermute | solution.py:995
  645.1 11.6 %shard_map.304.refs_0_.refs_4_ = bf16[1024,4096]{1,0:T(8,128)(2,1)} custom-call(bf16[384,1024]{1,0:T(8,128)(2,1)} %copy-done.67, bf16[192,1024]{1,0:T(8,128)(2,1)} %copy-done.73, bf16[384,1024]{1,0:T(8,128)(2,1)} %copy-done.69, bf16[192,1024]{1,0:T(8,128)(2,1)} %copy-done.75, bf16[8,384,384]{2,1,0:T(8,128)(2,1)} %all-to-all-done.9.t_ref.refs_4_, ...), custom_call_target="tpu_custom_call" | custom-call | flops 1000000 | bytes 100000 | tf_op jit(solution)/shard_map/pallas_call | solution.py:588
  660.5 11.0 %shard_map.305 = (bf16[1920,128]{1,0:T(8,128)(2,1)}, bf16[1920,128]{1,0:T(8,128)(2,1)}, bf16[1920,128]{1,0:T(8,128)(2,1)}, bf16[1920,128]{1,0:T(8,128)(2,1)}, f3...) custom-call(s32[2]{0:T(128)} %pad_add_fusion.2.at_ref, bf16[8,768,128]{2,1,0:T(8,128)(2,1)} %all-to-all-done.13.refs_1_.refs_9_.g_ref, ...), custom_call_target="tpu_custom_call" | custom-call | flops 1000000 | bytes 100000 | tf_op jit(solution)/shard_map/pallas_call | solution.py:758
  672.2 20.3 %shard_map.306.b_ref = bf16[8,576,128]{2,1,0:T(8,128)(2,1)} custom-call(s32[2]{0:T(128)S(1)} %pad_add_fusion.n_ref, bf16[2,1536,128]{2,1,0:T(8,128)(2,1)S(1)} %copy-done.71, bf16[8,192,128]{2,1,0:T(8,128)(2,1)S(1)} %all-to-all-done.14.refs_1_, bf16[1536,128]{1,0:T(8,128)(2,1)} %get-tuple-element.82.refs_2_, ...), custom_call_target="tpu_custom_call" | custom-call | flops 1000000 | bytes 100000 | tf_op jit(solution)/shard_map/pallas_call | solution.py:242
  692.5 4.3 all-to-all-start.15
  698.8 4.3 collective-permute-start.19
  704.5 10.7 %collective-permute-done.22 = bf16[18,1,128]{2,1,0:T(2,128)(2,1)S(1)} collective-permute-done((bf16[18,1,128]{2,1,0:T(2,128)(2,1)S(1)}, bf16[18,1,128]{2,1,0:T(2,128)(2,1)S(1)}, u32[]{:S(2)}, u32[]{:S(2)}) %collective-permute-start.22) | collective-permute-done | bytes 4640 | tf_op jit(solution)/shard_map/ppermute | solution.py:1308
  716.7 4.3 collective-permute-done.21
  726.0 9.1 %collective-permute-done.18.refs_10_.refs_2_ = bf16[1920,128]{1,0:T(8,128)(2,1)} collective-permute-done((bf16[1920,128]{1,0:T(8,128)(2,1)}, bf16[1920,128]{1,0:T(8,128)(2,1)}, u32[]{:S(2)}, u32[]{:S(2)}) %collective-permute-start.18) | collective-permute-done | bytes 491552 | tf_op jit(solution)/shard_map/ppermute | solution.py:987
  745.7 8.3 shard_map.308
  754.0 5.3 all-to-all-start.16
  760.1 10.4 %collective-permute-start.25 = (bf16[192,768]{1,0:T(8,128)(2,1)S(1)}, bf16[192,768]{1,0:T(8,128)(2,1)S(1)}, u32[]{:S(2)}, u32[]{:S(2)}) collective-permute-start(bf16[192,768]{1,0:T(8,128)(2,1)S(1)} %copy-done.76), channel_id=1, source_target_pairs={{0,1},{1,0},{2,3},{3,2},{4,5},{5,4},{6,7},{7,6},{8,9},{9,8},{10,11... | collective-permute-start | bytes 884744 | tf_op jit(solution)/shard_map/ppermute | solution.py:987
  783.7 11.7 %shard_map.311 = bf16[18,32,256]{2,1,0:T(8,128)(2,1)S(1)} custom-call(bf16[18,160,128]{2,1,0:T(8,128)(2,1)S(1)} %copy-done.16, bf16[18,561,256]{2,1,0:T(8,128)(2,1)S(1)} %bitcast.125), custom_call_target="tpu_custom_call" | custom-call | flops 1000000 | bytes 100000 | tf_op jit(solution)/shard_map/pallas_call | solution.py:933
  800.8 21.9 %collective-permute-start.28 = (bf16[656,128]{1,0:T(8,128)(2,1)S(1)}, bf16[656,128]{1,0:T(8,128)(2,1)S(1)}, u32[]{:S(2)}, u32[]{:S(2)}) collective-permute-start(bf16[656,128]{1,0:T(8,128)(2,1)S(1)} %get-tuple-element.132), channel_id=1, source_target_pairs={{0,1},{1,0},{2,3},{3,2},{4,5},{5,4},{6,7},{7,6},{8,9},{9,8},{10,11... | collective-permute-start | bytes 503816 | tf_op jit(solution)/shard_map/ppermute | solution.py:987
  834.4 3.9 collective-permute-done.29.refs_2_
  (396 shorter events, 183.4 us)
Async XLA Ops:
  7.2 82.6 %all-gather.7.cloned.1.call-start = ((), (), s32[]{:S(2)}) async-start(), calls=%async_computation.24 | async-start | bytes 6488064 | tf_op jit(solution)/shard_map/all_gather | solution.py:963
  11.8 169.1 %all-gather.9.cloned.1.call-start = ((), (), s32[]{:S(2)}) async-start(), calls=%async_computation.25 | async-start | bytes 8650752 | tf_op jit(solution)/shard_map/all_gather | solution.py:963
  16.7 317.4 %all-gather.11.cloned.1.call-start = ((), (), s32[]{:S(2)}) async-start(), calls=%async_computation.26 | async-start | bytes 20545536 | tf_op jit(solution)/shard_map/all_gather | solution.py:963
  21.1 37.7 %collective-permute-start.1 = (bf16[384,768]{1,0:T(8,128)(2,1)S(1)}, bf16[384,768]{1,0:T(8,128)(2,1)S(1)}, u32[]{:S(2)}, u32[]{:S(2)}) collective-permute-start(bf16[384,768]{1,0:T(8,128)(2,1)S(1)} %pad_maximum_fusion.2.refs_0_), channel_id=1, source_target_pairs={{0,8},{4,12},{8,0},{12,4},{16,24},{20,28},{24,16},{28,20},{1,9},{5... | collective-permute-start | bytes 1769480 | tf_op jit(solution)/shard_map/ppermute | solution.py:1008
  24.1 35.9 %collective-permute-start.3 = (bf16[384,768]{1,0:T(8,128)(2,1)S(1)}, bf16[384,768]{1,0:T(8,128)(2,1)S(1)}, u32[]{:S(2)}, u32[]{:S(2)}) collective-permute-start(bf16[384,768]{1,0:T(8,128)(2,1)S(1)} %pad_maximum_fusion.2.refs_0_), channel_id=1, source_target_pairs={{0,16},{4,20},{8,24},{12,28},{16,0},{20,4},{24,8},{28,12},{1,17},{... | collective-permute-start | bytes 1769480 | tf_op jit(solution)/shard_map/ppermute | solution.py:1008
  25.5 34.6 %collective-permute-start.5 = (bf16[384,768]{1,0:T(8,128)(2,1)S(1)}, bf16[384,768]{1,0:T(8,128)(2,1)}, u32[]{:S(2)}, u32[]{:S(2)}) collective-permute-start(bf16[384,768]{1,0:T(8,128)(2,1)S(1)} %pad_maximum_fusion.2.refs_0_), channel_id=1, source_target_pairs={{0,24},{4,28},{8,16},{12,20},{16,8},{20,12},{24,0},{28,4},{1,25},{... | collective-permute-start | bytes 1769480 | tf_op jit(solution)/shard_map/ppermute | solution.py:1008
  43.5 12.3 %collective-permute-start.8 = (f32[18,8,128]{2,1,0:T(8,128)S(1)}, f32[18,8,128]{2,1,0:T(8,128)S(1)}, u32[]{:S(2)}, u32[]{:S(2)}) collective-permute-start(f32[18,8,128]{2,1,0:T(8,128)S(1)} %slice.160), channel_id=1, source_target_pairs={{0,16},{4,20},{8,24},{12,28},{1,17},{5,21},{9,25},{13,29},{2,18},{... | collective-permute-start | bytes 221192 | tf_op jit(solution)/shard_map/ppermute | solution.py:1119
  47.2 6.5 collective-permute-start.9
  53.8 8.1 collective-permute-start
  124.3 23.1 %all-to-all-start.1 = ((bf16[32,72,128]{2,1,0:T(8,128)(2,1)}), bf16[32,72,128]{2,1,0:T(8,128)(2,1)}, u32[]{:S(2)}, u32[]{:S(2)}) async-start(bf16[32,72,128]{2,1,0:T(8,128)(2,1)} %shard_map.282), calls=%async_computation.1 | async-start | bytes 1179648 | tf_op jit(solution)/shard_map/all_to_all | solution.py:954
  147.4 26.8 %all-to-all-start.5 = ((bf16[8,192,128]{2,1,0:T(8,128)(2,1)}), bf16[8,192,128]{2,1,0:T(8,128)(2,1)S(1)}, u32[]{:S(2)}, u32[]{:S(2)}) async-start(bf16[8,192,128]{2,1,0:T(8,128)(2,1)} %bitcast.27), calls=%async_computation.5 | async-start | bytes 786432 | tf_op jit(solution)/shard_map/all_to_all | solution.py:946
  174.2 17.9 %all-to-all-start.2 = ((bf16[8,384,128]{2,1,0:T(8,128)(2,1)}), bf16[8,384,128]{2,1,0:T(8,128)(2,1)}, u32[]{:S(2)}, u32[]{:S(2)}) async-start(bf16[8,384,128]{2,1,0:T(8,128)(2,1)} %bitcast.130), calls=%async_computation.2 | async-start | bytes 1572864 | tf_op jit(solution)/shard_map/all_to_all | solution.py:946
  193.2 20.3 %all-to-all-start.6 = ((bf16[8,192,384]{2,1,0:T(8,128)(2,1)}), bf16[8,192,384]{2,1,0:T(8,128)(2,1)S(1)}, u32[]{:S(2)}, u32[]{:S(2)}) async-start(bf16[8,192,384]{2,1,0:T(8,128)(2,1)} %copy-done.56), calls=%async_computation.6 | async-start | bytes 2359296 | tf_op jit(solution)/shard_map/all_to_all | solution.py:946
  213.5 47.8 %all-to-all-start.3 = ((bf16[8,384,384]{2,1,0:T(8,128)(2,1)}), bf16[8,384,384]{2,1,0:T(8,128)(2,1)}, u32[]{:S(2)}, u32[]{:S(2)}) async-start(bf16[8,384,384]{2,1,0:T(8,128)(2,1)} %copy-done.38), calls=%async_computation.3 | async-start | bytes 4718592 | tf_op jit(solution)/shard_map/all_to_all | solution.py:946
  218.9 78.6 %collective-permute-start.10 = (bf16[8,192,256]{2,1,0:T(8,128)(2,1)}, bf16[8,192,256]{2,1,0:T(8,128)(2,1)}, u32[]{:S(2)}, u32[]{:S(2)}) collective-permute-start(bf16[8,192,256]{2,1,0:T(8,128)(2,1)} %slice.167), channel_id=1, source_target_pairs={{0,1},{1,0},{2,3},{3,2},{4,5},{5,4},{6,7},{7,6},{8,9},{9,8},{10,11... | collective-permute-start | bytes 2359304 | tf_op jit(solution)/shard_map/ppermute | solution.py:959
  293.0 23.4 %all-to-all-start.4 = ((bf16[8,384,128]{2,1,0:T(8,128)(2,1)}), bf16[8,384,128]{2,1,0:T(8,128)(2,1)}, u32[]{:S(2)}, u32[]{:S(2)}) async-start(bf16[8,384,128]{2,1,0:T(8,128)(2,1)} %bitcast.26), calls=%async_computation.4 | async-start | bytes 1572864 | tf_op jit(solution)/shard_map/all_to_all | solution.py:946
  316.4 12.5 %all-to-all-start.7 = ((bf16[8,192,128]{2,1,0:T(8,128)(2,1)}), bf16[8,192,128]{2,1,0:T(8,128)(2,1)S(1)}, u32[]{:S(2)}, u32[]{:S(2)}) async-start(bf16[8,192,128]{2,1,0:T(8,128)(2,1)} %shard_map.289), calls=%async_computation.7 | async-start | bytes 786432 | tf_op jit(solution)/shard_map/all_to_all | solution.py:946
  371.0 29.6 %all-to-all-start.8 = ((bf16[8,576,128]{2,1,0:T(8,128)(2,1)}), bf16[8,576,128]{2,1,0:T(8,128)(2,1)S(1)}, u32[]{:S(2)}, u32[]{:S(2)}) async-start(bf16[8,576,128]{2,1,0:T(8,128)(2,1)} %get-tuple-element.89), calls=%async_computation.8 | async-start | bytes 2359296 | tf_op jit(solution)/shard_map/all_to_all | solution.py:946
  376.1 189.6 %reduce-scatter.7.cloned.1.call-start = ((), (), s32[]{:S(2)}) async-start(), calls=%async_computation.21 | async-start | bytes 22413312 | tf_op jit(solution)/shard_map/reduce_scatter | solution.py:982
  403.9 66.4 %all-to-all-start.10 = ((bf16[32,72,128]{2,1,0:T(8,128)(2,1)}), bf16[32,72,128]{2,1,0:T(8,128)(2,1)S(1)}, u32[]{:S(2)}, u32[]{:S(2)}) async-start(bf16[32,72,128]{2,1,0:T(8,128)(2,1)} %bitcast.41), calls=%async_computation.10 | async-start | bytes 1179648 | tf_op jit(solution)/shard_map/all_to_all | solution.py:954
  470.3 50.8 %all-to-all-start.9 = ((bf16[8,384,384]{2,1,0:T(8,128)(2,1)}), bf16[8,384,384]{2,1,0:T(8,128)(2,1)}, u32[]{:S(2)}, u32[]{:S(2)}) async-start(bf16[8,384,384]{2,1,0:T(8,128)(2,1)} %shard_map.293.refs_4_), calls=%async_computation.9 | async-start | bytes 4718592 | tf_op jit(solution)/shard_map/all_to_all | solution.py:946
  474.6 157.7 %reduce-scatter.13.cloned.1.call-start = ((), (), s32[]{:S(2)}) async-start(), calls=%async_computation.27 | async-start | bytes 3112960
  495.1 21.5 %collective-permute-start.11 = (bf16[1536,256]{1,0:T(8,128)(2,1)}, bf16[1536,256]{1,0:T(8,128)(2,1)S(1)}, u32[]{:S(2)}, u32[]{:S(2)}) collective-permute-start(bf16[1536,256]{1,0:T(8,128)(2,1)} %get-tuple-element.101), channel_id=1, source_target_pairs={{0,1},{1,0},{2,3},{3,2},{4,5},{5,4},{6,7},{7,6},{8,9},{9,8},{10,11... | collective-permute-start | bytes 2359304 | tf_op jit(solution)/shard_map/ppermute | solution.py:959
  572.6 31.0 %all-to-all-start.12 = ((bf16[8,192,384]{2,1,0:T(8,128)(2,1)}), bf16[8,192,384]{2,1,0:T(8,128)(2,1)S(1)}, u32[]{:S(2)}, u32[]{:S(2)}) async-start(bf16[8,192,384]{2,1,0:T(8,128)(2,1)} %shard_map.299), calls=%async_computation.12 | async-start | bytes 2359296 | tf_op jit(solution)/shard_map/all_to_all | solution.py:946
  603.7 40.8 %all-to-all-start.13 = ((bf16[8,768,128]{2,1,0:T(8,128)(2,1)}), bf16[8,768,128]{2,1,0:T(8,128)(2,1)}, u32[]{:S(2)}, u32[]{:S(2)}) async-start(bf16[8,768,128]{2,1,0:T(8,128)(2,1)} %shard_map.300.refs_0_.a_ref), calls=%async_computation.13 | async-start | bytes 3145728 | tf_op jit(solution)/shard_map/all_to_all | solution.py:946
  608.0 151.4 %reduce-scatter.9.cloned.1.call-start = ((), (), s32[]{:S(2)}) async-start(), calls=%async_computation.22 | async-start | bytes 9437184 | tf_op jit(solution)/shard_map/reduce_scatter | solution.py:982
  611.4 23.5 %collective-permute-start.12 = (bf16[96,1024]{1,0:T(8,128)(2,1)S(1)}, bf16[96,1024]{1,0:T(8,128)(2,1)S(1)}, u32[]{:S(2)}, u32[]{:S(2)}) collective-permute-start(bf16[96,1024]{1,0:T(8,128)(2,1)S(1)} %get-tuple-element.203), channel_id=1, source_target_pairs={{0,1},{1,0},{2,3},{3,2},{4,5},{5,4},{6,7},{7,6},{8,9},{9,8},{10,11... | collective-permute-start | bytes 589832 | tf_op jit(solution)/shard_map/ppermute | solution.py:987
  612.9 22.0 %collective-permute-start.13 = (bf16[96,1024]{1,0:T(8,128)(2,1)S(1)}, bf16[96,1024]{1,0:T(8,128)(2,1)S(1)}, u32[]{:S(2)}, u32[]{:S(2)}) collective-permute-start(bf16[96,1024]{1,0:T(8,128)(2,1)S(1)} %get-tuple-element.202), channel_id=1, source_target_pairs={{0,2},{1,3},{2,0},{3,1},{4,6},{5,7},{6,4},{7,5},{8,10},{9,11},{10,... | collective-permute-start | bytes 589832 | tf_op jit(solution)/shard_map/ppermute | solution.py:987
  615.3 19.6 %collective-permute-start.14 = (bf16[96,1024]{1,0:T(8,128)(2,1)S(1)}, bf16[96,1024]{1,0:T(8,128)(2,1)S(1)}, u32[]{:S(2)}, u32[]{:S(2)}) collective-permute-start(bf16[96,1024]{1,0:T(8,128)(2,1)S(1)} %get-tuple-element.201), channel_id=1, source_target_pairs={{0,3},{1,2},{2,1},{3,0},{4,7},{5,6},{6,5},{7,4},{8,11},{9,10},{10,... | collective-permute-start | bytes 589832 | tf_op jit(solution)/shard_map/ppermute | solution.py:987
  616.5 18.4 %collective-permute-start.15 = (bf16[96,1024]{1,0:T(8,128)(2,1)}, bf16[96,1024]{1,0:T(8,128)(2,1)S(1)}, u32[]{:S(2)}, u32[]{:S(2)}) collective-permute-start(bf16[96,1024]{1,0:T(8,128)(2,1)} %get-tuple-element.211), channel_id=1, source_target_pairs={{0,0},{1,2},{2,1},{3,3},{4,4},{5,6},{6,5},{7,7},{8,8},{9,10},{10,9... | collective-permute-start | bytes 589832 | tf_op jit(solution)/shard_map/ppermute | solution.py:995
  618.1 26.3 %collective-permute-start.16 = (bf16[96,1024]{1,0:T(8,128)(2,1)}, bf16[96,1024]{1,0:T(8,128)(2,1)S(1)}, u32[]{:S(2)}, u32[]{:S(2)}) collective-permute-start(bf16[96,1024]{1,0:T(8,128)(2,1)} %get-tuple-element.210), channel_id=1, source_target_pairs={{0,1},{1,3},{2,0},{3,2},{4,5},{5,7},{6,4},{7,6},{8,9},{9,11},{10,8... | collective-permute-start | bytes 589832 | tf_op jit(solution)/shard_map/ppermute | solution.py:995
  656.7 14.8 %all-to-all-start.14 = ((bf16[8,192,128]{2,1,0:T(8,128)(2,1)}), bf16[8,192,128]{2,1,0:T(8,128)(2,1)S(1)}, u32[]{:S(2)}, u32[]{:S(2)}) async-start(bf16[8,192,128]{2,1,0:T(8,128)(2,1)} %shard_map.302), calls=%async_computation.14 | async-start | bytes 786432 | tf_op jit(solution)/shard_map/all_to_all | solution.py:946
  692.5 53.2 %all-to-all-start.15 = ((bf16[8,576,128]{2,1,0:T(8,128)(2,1)}), bf16[8,576,128]{2,1,0:T(8,128)(2,1)}, u32[]{:S(2)}, u32[]{:S(2)}) async-start(bf16[8,576,128]{2,1,0:T(8,128)(2,1)} %shard_map.306.b_ref), calls=%async_computation.16 | async-start | bytes 2359296 | tf_op jit(solution)/shard_map/all_to_all | solution.py:946
  697.1 23.9 %collective-permute-start.20 = (bf16[18,16,128]{2,1,0:T(8,128)(2,1)S(1)}, bf16[18,16,128]{2,1,0:T(8,128)(2,1)S(1)}, u32[]{:S(2)}, u32[]{:S(2)}) collective-permute-start(bf16[18,16,128]{2,1,0:T(8,128)(2,1)S(1)} %bitcast.171), channel_id=1, source_target_pairs={{4,0},{8,4},{12,8},{20,16},{24,20},{28,24},{5,1},{9,5},{13,9},{21,... | collective-permute-start | bytes 221192 | tf_op jit(solution)/shard_map/ppermute | solution.py:1306
  698.7 27.3 %collective-permute-start.17 = (bf16[1920,128]{1,0:T(8,128)(2,1)}, bf16[1920,128]{1,0:T(8,128)(2,1)}, u32[]{:S(2)}, u32[]{:S(2)}) collective-permute-start(bf16[1920,128]{1,0:T(8,128)(2,1)} %get-tuple-element.124), channel_id=1, source_target_pairs={{0,1},{1,0},{2,3},{3,2},{4,5},{5,4},{6,7},{7,6},{8,9},{9,8},{10,11... | collective-permute-start | bytes 1474568 | tf_op jit(solution)/shard_map/ppermute | solution.py:987
  698.8 36.3 %collective-permute-start.18 = (bf16[1920,128]{1,0:T(8,128)(2,1)}, bf16[1920,128]{1,0:T(8,128)(2,1)}, u32[]{:S(2)}, u32[]{:S(2)}) collective-permute-start(bf16[1920,128]{1,0:T(8,128)(2,1)} %get-tuple-element.125), channel_id=1, source_target_pairs={{0,2},{1,3},{2,0},{3,1},{4,6},{5,7},{6,4},{7,5},{8,10},{9,11},{10,... | collective-permute-start | bytes 1474568 | tf_op jit(solution)/shard_map/ppermute | solution.py:987
  698.8 36.3 %collective-permute-start.19 = (bf16[1920,128]{1,0:T(8,128)(2,1)}, bf16[1920,128]{1,0:T(8,128)(2,1)}, u32[]{:S(2)}, u32[]{:S(2)}) collective-permute-start(bf16[1920,128]{1,0:T(8,128)(2,1)} %get-tuple-element.126), channel_id=1, source_target_pairs={{0,3},{1,2},{2,1},{3,0},{4,7},{5,6},{6,5},{7,4},{8,11},{9,10},{10,... | collective-permute-start | bytes 1474568 | tf_op jit(solution)/shard_map/ppermute | solution.py:987
  703.2 12.0 %collective-permute-start.22 = (bf16[18,1,128]{2,1,0:T(2,128)(2,1)S(1)}, bf16[18,1,128]{2,1,0:T(2,128)(2,1)S(1)}, u32[]{:S(2)}, u32[]{:S(2)}) collective-permute-start(bf16[18,1,128]{2,1,0:T(2,128)(2,1)S(1)} %slice_bitcast_fusion.8), channel_id=1, source_target_pairs={{20,0},{24,4},{28,8},{21,1},{25,5},{29,9},{22,2},{26,6},{30,10},{2... | collective-permute-start | bytes 13832 | tf_op jit(solution)/shard_map/ppermute | solution.py:1308
  754.0 43.4 %all-to-all-start.16 = ((bf16[8,1232,128]{2,1,0:T(8,128)(2,1)}), bf16[8,1232,128]{2,1,0:T(8,128)(2,1)}, u32[]{:S(2)}, u32[]{:S(2)}) async-start(bf16[8,1232,128]{2,1,0:T(8,128)(2,1)} %get-tuple-element.127.refs_6_.refs_1_), calls=%async_computation.17 | async-start | bytes 5046272 | tf_op jit(solution)/shard_map/all_to_all | solution.py:946
  759.3 82.2 %reduce-scatter.11.cloned.1.call-start = ((), (), s32[]{:S(2)}) async-start(), calls=%async_computation.23 | async-start | bytes 1310720 | tf_op jit(solution)/shard_map/reduce_scatter | solution.py:1000
  760.1 65.7 %collective-permute-start.25 = (bf16[192,768]{1,0:T(8,128)(2,1)S(1)}, bf16[192,768]{1,0:T(8,128)(2,1)S(1)}, u32[]{:S(2)}, u32[]{:S(2)}) collective-permute-start(bf16[192,768]{1,0:T(8,128)(2,1)S(1)} %copy-done.76), channel_id=1, source_target_pairs={{0,1},{1,0},{2,3},{3,2},{4,5},{5,4},{6,7},{7,6},{8,9},{9,8},{10,11... | collective-permute-start | bytes 884744 | tf_op jit(solution)/shard_map/ppermute | solution.py:987
  771.3 59.5 %collective-permute-start.26 = (bf16[192,768]{1,0:T(8,128)(2,1)S(1)}, bf16[192,768]{1,0:T(8,128)(2,1)S(1)}, u32[]{:S(2)}, u32[]{:S(2)}) collective-permute-start(bf16[192,768]{1,0:T(8,128)(2,1)S(1)} %copy-done.76), channel_id=1, source_target_pairs={{0,2},{1,3},{2,0},{3,1},{4,6},{5,7},{6,4},{7,5},{8,10},{9,11},{10,... | collective-permute-start | bytes 884744 | tf_op jit(solution)/shard_map/ppermute | solution.py:987
  771.3 59.5 %collective-permute-start.27 = (bf16[192,768]{1,0:T(8,128)(2,1)S(1)}, bf16[192,768]{1,0:T(8,128)(2,1)S(1)}, u32[]{:S(2)}, u32[]{:S(2)}) collective-permute-start(bf16[192,768]{1,0:T(8,128)(2,1)S(1)} %copy-done.76), channel_id=1, source_target_pairs={{0,3},{1,2},{2,1},{3,0},{4,7},{5,6},{6,5},{7,4},{8,11},{9,10},{10,... | collective-permute-start | bytes 884744 | tf_op jit(solution)/shard_map/ppermute | solution.py:987
  773.7 27.1 %collective-permute-start.23 = (bf16[96,1024]{1,0:T(8,128)(2,1)}, bf16[96,1024]{1,0:T(8,128)(2,1)S(1)}, u32[]{:S(2)}, u32[]{:S(2)}) collective-permute-start(bf16[96,1024]{1,0:T(8,128)(2,1)} %get-tuple-element.128), channel_id=1, source_target_pairs={{0,0},{1,2},{2,1},{3,3},{4,4},{5,6},{6,5},{7,7},{8,8},{9,10},{10,9... | collective-permute-start | bytes 589832 | tf_op jit(solution)/shard_map/ppermute | solution.py:995
  775.3 50.6 %collective-permute-start.24 = (bf16[96,1024]{1,0:T(8,128)(2,1)}, bf16[96,1024]{1,0:T(8,128)(2,1)}, u32[]{:S(2)}, u32[]{:S(2)}) collective-permute-start(bf16[96,1024]{1,0:T(8,128)(2,1)} %get-tuple-element.129), channel_id=1, source_target_pairs={{0,1},{1,3},{2,0},{3,2},{4,5},{5,7},{6,4},{7,6},{8,9},{9,11},{10,8... | collective-permute-start | bytes 589832 | tf_op jit(solution)/shard_map/ppermute | solution.py:995
  800.8 33.6 %collective-permute-start.28 = (bf16[656,128]{1,0:T(8,128)(2,1)S(1)}, bf16[656,128]{1,0:T(8,128)(2,1)S(1)}, u32[]{:S(2)}, u32[]{:S(2)}) collective-permute-start(bf16[656,128]{1,0:T(8,128)(2,1)S(1)} %get-tuple-element.132), channel_id=1, source_target_pairs={{0,1},{1,0},{2,3},{3,2},{4,5},{5,4},{6,7},{7,6},{8,9},{9,8},{10,11... | collective-permute-start | bytes 503816 | tf_op jit(solution)/shard_map/ppermute | solution.py:987
  825.8 12.5 %collective-permute-start.29 = (bf16[656,128]{1,0:T(8,128)(2,1)S(1)}, bf16[656,128]{1,0:T(8,128)(2,1)S(1)}, u32[]{:S(2)}, u32[]{:S(2)}) collective-permute-start(bf16[656,128]{1,0:T(8,128)(2,1)S(1)} %get-tuple-element.133), channel_id=1, source_target_pairs={{0,2},{1,3},{2,0},{3,1},{4,6},{5,7},{6,4},{7,5},{8,10},{9,11},{10,... | collective-permute-start | bytes 503816 | tf_op jit(solution)/shard_map/ppermute | solution.py:987
  825.8 12.5 %collective-permute-start.30 = (bf16[656,128]{1,0:T(8,128)(2,1)S(1)}, bf16[656,128]{1,0:T(8,128)(2,1)S(1)}, u32[]{:S(2)}, u32[]{:S(2)}) collective-permute-start(bf16[656,128]{1,0:T(8,128)(2,1)S(1)} %get-tuple-element.134), channel_id=1, source_target_pairs={{0,3},{1,2},{2,1},{3,0},{4,7},{5,6},{6,5},{7,4},{8,11},{9,10},{10,... | collective-permute-start | bytes 503816 | tf_op jit(solution)/shard_map/ppermute | solution.py:987
  (102 other events, 903.5 us)
Sparse Core Ops, SparseCore 0:
  11.9 77.8 all-gather.6
  93.2 87.5 all-gather.8
  183.7 150.3 all-gather.10
  401.8 163.9 reduce-scatter.6
  570.3 54.0 reduce-scatter.12
  656.9 83.4 reduce-scatter.8
  762.6 51.9 reduce-scatter.10

commit v9 on v8

--- a/solution.py
+++ b/solution.py
@@ -235,7 +235,7 @@
         kv_specs=kv_specs,
         hpd=hpd,
         bq=fit(queries, 512),
-        kc=fit(total, 512),
+        kc=fit(total, 1024 if fixed else 512),
         fixed=fixed,
         form=form,
     )
@@ -604,13 +604,21 @@
     )(*lefts, *rights, *deps)
 
 
-def start_kernel(at_ref, xa_ref, xb_ref, norm_ref, wk_ref, wq_in, *refs, pieces, width):
+def start_kernel(at_ref, xa_ref, xb_ref, norm_ref, wk_ref, *refs, pieces, width):
     p_in, (q_ref, k_ref, n_ref, wq_ref, wkv_ref) = refs[:pieces], refs[-5:]
     seq = at_ref[0]
     R = xa_ref.shape[0]
     W = q_ref.shape[2]
-    wq_ref[...] = flat(wq_in)
-    wkv_ref[...] = flat(wk_ref)[:, :width]
+    groups, per = wk_ref.shape[0], wq_ref.shape[0] // wk_ref.shape[0]
+    size = wkv_ref.shape[0] // groups
+    for i in range(groups):
+        wq_ref[i * per : (i + 1) * per, :] = wk_ref[i, :per, :]
+        kept = wk_ref.shape[1] - per
+        wkv_ref[i * size : i * size + kept, :] = wk_ref[i, per:, :width]
+        if kept < size:
+            tall = size - kept
+            tail = [wk_ref[i, at : at + tall, width:] for at in range(per, per + kept, tall)]
+            wkv_ref[i * size + kept : (i + 1) * size, :] = jnp.concatenate(tail, axis=1)
     for block, x_ref in ((slice(0, R), xa_ref), (slice(R, n_ref.shape[0]), xb_ref)):
         n_ref[block, :] = layer_norm(x_ref[...].astype(f32), norm_ref[0:1, :], norm_ref[1:2, :])
     for i in range(pieces):
@@ -620,7 +628,7 @@
         k_ref[seq ^ i] = dot(p_in[i][...], own, NT).astype(bf16)
 
 
-def start(at, x0, norm, w_kv, w_query, patch_pieces, W, deps):
+def start(at, x0, norm, lead, patch_pieces, W, deps):
     S, D = len(patch_pieces), x0[0].shape[1]
     total = x0[0].shape[0] + x0[1].shape[0]
     slots, width = patch_pieces[0].shape
@@ -632,13 +640,13 @@
         out_shape=tuple(jax.ShapeDtypeStruct(v, bf16) for v in outs),
         in_specs=[SM]
         + [once(v) for v in whole]
-        + [once(*w_kv[1]), once(*w_query[1])]
+        + [once(lead.shape)]
         + [once((slots, width))] * S
         + [AN] * len(deps),
         out_specs=tuple(held(v) for v in outs),
         compiler_params=pltpu.CompilerParams(vmem_limit_bytes=56 * 2**20),
         cost_estimate=BRIEF,
-    )(at, *x0, norm, w_kv[0], w_query[0], *patch_pieces, *deps)
+    )(at, *x0, norm, lead, *patch_pieces, *deps)
 
 
 def finish_kernel(at_ref, a_ref, b_ref, *refs, pieces, rows):
@@ -1068,9 +1076,17 @@
     kv_piece = lax.dynamic_slice(
         cross_kv, (0, (at // W) % 2, at // (2 * W) * W + at % W), (width, 1, kv_rows)
     )
-    kv_piece = jnp.pad(kv_piece[:, 0].T, ((0, 0), (0, D - width)))
-    lead = gather_rows(jnp.concatenate([kv_piece, mine(cross_query, 1).T], axis=0))
-    w_kv, w_query = bundle_part(lead, 0, kv_rows), bundle_part(lead, kv_rows, per)
+    kv_piece = kv_piece[:, 0].T
+    tail_rows = kv_rows - kv_rows * width // D
+    if (kv_rows - tail_rows) % tail_rows == 0 and tail_rows % 16 == 0 and width % 128 == 0:
+        folds = (kv_rows - tail_rows) // tail_rows
+        tail = jnp.split(kv_piece[-tail_rows:], folds, axis=1)
+        kv_piece = jnp.concatenate([kv_piece[:-tail_rows], jnp.concatenate(tail)], axis=1)
+    else:
+        kv_piece = jnp.pad(kv_piece, ((0, 0), (0, D - width)))
+    kv_rows = kv_piece.shape[0]
+    lead = [mine(cross_query, 1).T, kv_piece]
+    lead = gather_rows(jnp.concatenate(lead, axis=0))
     first = gather_rows(
         jnp.concatenate(
             [qkv_piece.T, mine(cross_out, 0)], axis=0
@@ -1130,7 +1146,7 @@
     sent = jnp.concatenate([gp_a, gp_b], axis=3).reshape(S * M, KA + KB, cu)
 
     q1, keys_one, n1, w_query, w_kv = start(
-        at, x0, norms[0], w_kv, w_query, patch_pieces, W, [sent]
+        at, x0, norms[0], lead, patch_pieces, W, [sent]
     )
     heads_one = swap_seq(q1)
     back = swap_all(hold(sent, [heads_one]))

time: 866 us -> 864 us (level)
  Pallas kernels: 413 us -> 424 us
  waiting for transfers between devices: 129 us -> 119 us
    all_gather x3, waiting for transfers between devices: 33.1 us -> 21.2 us  [gather_rows(): return lax.all_gather(piece, ('mp', 'seq'), axis=0, tiled=False)]
    unnamed x209 -> x211, local copies, waits for them, and re-layouts: 59.3 us -> 58.4 us
  transfers between devices with their start and end apart: 53 -> 53, of which waited for: 17 -> 17; matrix products, arithmetic and copies ran while one was open for 6% -> 6% of each run, Pallas kernels for 43% -> 44%
where the time goes in v9:
time: 864 us; the launch traced here: 851 us
  Pallas kernels  424 us (49%)
  starting transfers between devices  141 us (16%)
  waiting for transfers between devices  119 us (14%)
  local copies, waits for them, and re-layouts  92.8 us (11%)
  blocking collectives  46.4 us (5%)
  between operations  16.2 us (2%)
  other arithmetic  11.5 us (1%)
    pallas_call x5, Pallas kernels, attend_back(): pl.pallas_call(body, out_shape=tuple((jax.ShapeDtypeStruct(v, bf16) for v...  154 us
    pallas_call x4, Pallas kernels, attend(): pl.pallas_call(body, out_shape=(jax.ShapeDtypeStruct((queries, hpd * HD),...  90.3 us
    unnamed x211, local copies, waits for them, and re-layouts  58.4 us
    all_to_all x13, starting transfers between devices, swap_seq(): return lax.all_to_all(value, 'seq', split_axis=0, concat_axis=0, tiled=True)  56.5 us
    all_to_all x13, waiting for transfers between devices, swap_seq(): return lax.all_to_all(value, 'seq', split_axis=0, concat_axis=0, tiled=True)  50.5 us
    all_to_all x2, blocking collectives, swap_seq(): return lax.all_to_all(value, 'seq', split_axis=0, concat_axis=0, tiled=True)  46.4 us
    ppermute x12, starting transfers between devices, to_ranks(): lax.ppermute(v, 'mp', moves[i])  45 us
    pallas_call x1, Pallas kernels, feed_forward(): pl.pallas_call(functools.partial(mlp_kernel, steps=steps), grid=(steps,),...  37 us
  transfers between devices with their start and end apart: 53, of which 17 were waited for; matrix products, arithmetic and copies ran while one was open for 6% of the time, Pallas kernels for 44%

profile of v9, /device:TPU:0, one launch (start us, length us, event | category | flops | bytes accessed | tf_op | source)
XLA Modules:
  0.0 850.8 jit_solution(4452408193319930154)
XLA Ops:
  27.3 15.2 %shard_map.280 = f32[18,160,128]{2,1,0:T(8,128)S(1)} custom-call(bf16[18,32,256]{2,1,0:T(8,128)(2,1)S(1)} %pad.16.cot_ref, bf16[18,561,256]{2,1,0:T(8,128)(2,1)S(1)} %bitcast.124), custom_call_target="tpu_custom_call" | custom-call | flops 1000000 | bytes 100000 | tf_op jit(solution)/shard_map/pallas_call | solution.py:941
  42.6 3.8 collective-permute-start.8
  63.0 20.5 %all-gather.7.cloned.1.call-done = bf16[2560,1024]{1,0:T(8,128)(2,1)} async-done(((bf16[80,1024]{1,0:T(8,128)(2,1)}), bf16[2560,1024]{1,0:T(8,128)(2,1)}) %all-gather.7.cloned.1.call-update) | async-done | bytes 5242896 | tf_op jit(solution)/shard_map/all_gather | solution.py:971
  83.6 11.5 %shard_map.281 = (bf16[8,576,128]{2,1,0:T(8,128)(2,1)}, bf16[8,384,256]{2,1,0:T(8,128)(2,1)}, bf16[576,1024]{1,0:T(8,128)(2,1)}, bf16[1024,1024]{1,0:T(8,128)(2,1)}, bf16[2048,768]{1,0:T(8,128)(2,1)}) custom-call(s32[2]{0:T(128)} %pad_add_fusion.2.at_ref, bf16[384,1024]{1,0:T(8,128)(2,1)} %dynamic-slice_bitcast_fusion.1.xa_ref.x_ref, ...), custom_call_target="tpu_custom_call" | custom-call | flops 1000000 | bytes 100000 | tf_op jit(solution)/shard_map/pallas_call | solution.py:637
  95.1 22.0 %all_to_all.85.refs_1_.refs_0_ = bf16[8,576,128]{2,1,0:T(8,128)(2,1)} all-to-all(bf16[8,576,128]{2,1,0:T(8,128)(2,1)} %get-tuple-element.77), channel_id=1, replica_groups=mesh['seq'=8,'mp'=4] {'seq'}, dimensions={0} | all-to-all | bytes 2359296 | tf_op jit(solution)/shard_map/all_to_all | solution.py:954
  121.9 15.0 %shard_map.286 = (bf16[1536,128]{1,0:T(8,128)(2,1)}, bf16[2,1536,128]{2,1,0:T(8,128)(2,1)S(1)}) custom-call(s32[2]{0:T(128)S(1)} %pad_add_fusion.n_ref, bf16[8,576,128]{2,1,0:T(8,128)(2,1)S(1)} %copy-done.11, bf16[8,384,256]{2,1,0:T(8,128)(2,1)S(1)} %copy-done.5), custom_call_target="tpu_custom_call" | custom-call | flops 1000000 | bytes 100000 | tf_op jit(solution)/shard_map/pallas_call | solution.py:207
  145.5 26.3 %shard_map.283 = (bf16[3072,128]{1,0:T(8,128)(2,1)S(1)}, bf16[2,3072,128]{2,1,0:T(8,128)(2,1)S(1)}) custom-call(s32[2]{0:T(128)S(1)} %pad_add_fusion.1.n_ref, bf16[8,576,128]{2,1,0:T(8,128)(2,1)S(1)} %copy-done.11, bf16[8,384,256]{2,1,0:T(8,128)(2,1)S(1)} %copy-done.5, bf16[32,72,128]{2,1,0:T(8,128)(2,1)} %all-to-all-done.1.refs_2_), custom_call_target="tpu_custom_call" | custom-call | flops 1000000 | bytes 100000 | tf_op jit(solution)/shard_map/pallas_call | solution.py:207
  174.0 4.3 all-to-all-start.2
  182.8 5.1 shard_map.287
  197.9 10.2 %shard_map.284 = (f32[384,1024]{1,0:T(8,128)S(1)}, bf16[384,1024]{1,0:T(8,128)(2,1)S(1)}, bf16[384,1024]{1,0:T(8,128)(2,1)S(1)}, bf16[8,384,384]{2,1,0:T(8,128)(2,1)S(1)}) custom-call(bf16[8,384,128]{2,1,0:T(8,128)(2,1)} %all-to-all-done.2.a_ref, bf16[384,1024]{1,0:T(8,128)(2,1)S(1)} %copy-done.13, f32[2,1024]{1,0:T(2,128)S(1)} %pad_maximum_fusion.9.norm_ref, ...), custom_call_target="tpu_custom_call" | custom-call | flops 1000000 | bytes 100000 | tf_op jit(solution)/shard_map/pallas_call | solution.py:313
  212.5 4.2 all-to-all-done.6.refs_0_.refs_3_
  216.7 4.4 all-to-all-start.3
  222.0 34.7 %all-to-all-done.3.refs_0_.refs_3_ = bf16[8,384,384]{2,1,0:T(8,128)(2,1)} async-done(((bf16[8,384,384]{2,1,0:T(8,128)(2,1)}), bf16[8,384,384]{2,1,0:T(8,128)(2,1)}, u32[]{:S(2)}, u32[]{:S(2)}) %all-to-all-start.3) | async-done | bytes 2359328 | tf_op jit(solution)/shard_map/all_to_all | solution.py:954
  256.6 31.7 %shard_map.285 = (bf16[3072,128]{1,0:T(8,128)(2,1)}, bf16[2,3072,128]{2,1,0:T(8,128)(2,1)S(1)}) custom-call(s32[2]{0:T(128)S(1)} %copy-done.80, bf16[8,384,384]{2,1,0:T(8,128)(2,1)} %all-to-all-done.3.refs_0_.refs_3_), custom_call_target="tpu_custom_call" | custom-call | flops 1000000 | bytes 100000 | tf_op jit(solution)/shard_map/pallas_call | solution.py:207
  288.4 4.4 all-to-all-start.4
  292.8 17.2 %shard_map.288 = (bf16[1536,128]{1,0:T(8,128)(2,1)S(1)}, bf16[2,1536,128]{2,1,0:T(8,128)(2,1)S(1)}) custom-call(s32[2]{0:T(128)S(1)} %copy-done.80, bf16[8,192,384]{2,1,0:T(8,128)(2,1)S(1)} %all-to-all-done.6.refs_0_.refs_3_, bf16[8,192,256]{2,1,0:T(8,128)(2,1)} %collective-permute-done.10.refs_1_.refs_3_, bf16[3072,128]{1,0:T(8,128)(2,1)} %get-tuple-element.81.refs_2_), custom_call_target="tpu_custom_call" | custom-call | flops 1000000 | bytes 100000 | tf_op jit(solution)/shard_map/pallas_call | solution.py:207
  311.7 4.2 all-to-all-start.7
  325.0 37.0 %shard_map.290 = (bf16[576,1024]{1,0:T(8,128)(2,1)}, bf16[576,1024]{1,0:T(8,128)(2,1)}, bf16[576,4096]{1,0:T(8,128)(2,1)}, bf16[576,4096]{1,0:T(8,128)(2,1)}, bf...) custom-call(bf16[8,384,128]{2,1,0:T(8,128)(2,1)} %all-to-all-done.4., ...), custom_call_target="tpu_custom_call" | custom-call | flops 1000000 | bytes 100000 | tf_op jit(solution)/shard_map/pallas_call | solution.py:433
  361.9 6.1 all-to-all-start.8
  368.4 24.0 %shard_map.291.refs_0_ = bf16[1024,9728]{1,0:T(8,128)(2,1)} custom-call(bf16[576,1024]{1,0:T(8,128)(2,1)} %get-tuple-element.90.refs_0_, bf16[576,1024]{1,0:T(8,128)(2,1)} %get-tuple-element.91.refs_1_, bf16[576,1024]{1,0:T(8,128)(2,1)} %get-tuple-element.92.refs_2_, bf16[576,1024]{1,0:T(8,128)(2,1)} %get-tuple-element.87.refs_3_.refs_0_, ...), custom_call_target="tpu_custom_call" | custom-call | flops 1000000 | bytes 100000 | tf_op jit(solution)/shard_map/pallas_call | solution.py:588
  395.8 4.8 all-to-all-start.10
  400.6 59.3 %shard_map.293.refs_4_ = bf16[8,384,384]{2,1,0:T(8,128)(2,1)} custom-call(s32[2]{0:T(128)S(1)} %copy-done.80, bf16[2,3072,128]{2,1,0:T(8,128)(2,1)} %copy-done.55, bf16[8,576,128]{2,1,0:T(8,128)(2,1)S(1)} %copy-done.4, bf16[3072,128]{1,0:T(8,128)(2,1)} %get-tuple-element.81.refs_2_, bf16[8,384,384]{2,1,0:T(8,128)(2,1)} %all-to-all-done.3.refs_0_.refs_3_, ...), custom_call_target="tpu_custom_call" | custom-call | flops 1000000 | bytes 100000 | tf_op jit(solution)/shard_map/pallas_call | solution.py:242
  460.0 4.4 all-to-all-start.9
  464.6 20.4 %shard_map.295 = (bf16[1536,128]{1,0:T(8,128)(2,1)S(1)}, bf16[1536,256]{1,0:T(8,128)(2,1)}) custom-call(s32[2]{0:T(128)S(1)} %copy-done.80, bf16[2,1536,128]{2,1,0:T(8,128)(2,1)} %copy-done.37, bf16[8,576,128]{2,1,0:T(8,128)(2,1)} %copy-done.3, bf16[1536,128]{1,0:T(8,128)(2,1)S(1)} %get-tuple-element.84.refs_2_, ...), custom_call_target="tpu_custom_call" | custom-call | flops 1000000 | bytes 100000 | tf_op jit(solution)/shard_map/pallas_call | solution.py:242
  486.9 19.4 %shard_map.296 = (bf16[1536,128]{1,0:T(8,128)(2,1)S(1)}, bf16[1536,256]{1,0:T(8,128)(2,1)S(1)}) custom-call(s32[2]{0:T(128)S(1)} %copy-done.80, bf16[2,1536,128]{2,1,0:T(8,128)(2,1)} %copy-done.37, bf16[8,576,128]{2,1,0:T(8,128)(2,1)} %copy-done.3, bf16[1536,128]{1,0:T(8,128)(2,1)S(1)} %get-tuple-element.84.refs_2_, bf16[8,192,384]{2,1,0:T(8,128)(2,1)} %copy-done.12, ...), custom_call_target="tpu_custom_call" | custom-call | flops 1000000 | bytes 100000 | tf_op jit(solution)/shard_map/pallas_call | solution.py:242
  507.3 6.4 all-to-all-done.9.t_ref.refs_4_
  517.8 11.8 %shard_map.297 = (f32[384,1024]{1,0:T(8,128)S(1)}, bf16[384,1024]{1,0:T(8,128)(2,1)S(1)}, bf16[8,384,128]{2,1,0:T(8,128)(2,1)S(1)}, f32[2,1024]{1,0:T(2,128)S(1)}) custom-call(bf16[8,384,384]{2,1,0:T(8,128)(2,1)} %all-to-all-done.9.t_ref.refs_4_, f32[384,1024]{1,0:T(8,128)S(1)} %copy-done.24, f32[576,1024]{1,0:T(8,128)S(1)} %copy-done.19, ...), custom_call_target="tpu_custom_call" | custom-call | flops 1000000 | bytes 100000 | tf_op jit(solution)/shard_map/pallas_call | solution.py:530
  530.8 24.4 %all_to_all.86.refs_1_ = bf16[8,384,128]{2,1,0:T(8,128)(2,1)} all-to-all(bf16[8,384,128]{2,1,0:T(8,128)(2,1)S(1)} %get-tuple-element.105), channel_id=1, replica_groups=mesh['seq'=8,'mp'=4] {'seq'}, dimensions={0} | all-to-all | bytes 1572864 | tf_op jit(solution)/shard_map/all_to_all | solution.py:954
  558.3 4.4 copy.140
  565.1 3.7 all-to-all-start.12
  570.0 34.6 %shard_map.300.refs_0_.a_ref = bf16[8,768,128]{2,1,0:T(8,128)(2,1)} custom-call(s32[2]{0:T(128)S(1)} %pad_add_fusion.1.n_ref, bf16[2,3072,128]{2,1,0:T(8,128)(2,1)} %copy-done.52, bf16[8,384,128]{2,1,0:T(8,128)(2,1)S(1)} %copy-done.14, bf16[3072,128]{1,0:T(8,128)(2,1)S(1)} %copy-done.36, bf16[8,384,256]{2,1,0:T(8,128)(2,1)} %get-tuple-element.78.refs_1_.refs_3_), custom_call_target="tpu_custom_call" | custom-call | flops 1000000 | bytes 100000 | tf_op jit(solution)/shard_map/pallas_call | solution.py:242
  604.6 4.3 all-to-all-start.13
  621.8 9.0 %shard_map.301 = (f32[192,1024]{1,0:T(8,128)S(1)}, bf16[192,1024]{1,0:T(8,128)(2,1)S(1)}, bf16[8,192,128]{2,1,0:T(8,128)(2,1)S(1)}, f32[2,1024]{1,0:T(2,128)S(1)}) custom-call(bf16[8,192,384]{2,1,0:T(8,128)(2,1)S(1)} %all-to-all-done.12.t_ref.refs_5_, f32[192,1024]{1,0:T(8,128)S(1)} %copy-done.31, f32[576,1024]{1,0:T(8,128)S(1)} %copy-done.20, ...), custom_call_target="tpu_custom_call" | custom-call | flops 1000000 | bytes 100000 | tf_op jit(solution)/shard_map/pallas_call | solution.py:530
  635.9 5.5 collective-permute-done.16.refs_15_.refs_5_
  642.1 11.6 %shard_map.304.refs_0_.refs_4_ = bf16[1024,4096]{1,0:T(8,128)(2,1)} custom-call(bf16[384,1024]{1,0:T(8,128)(2,1)} %copy-done.67, bf16[192,1024]{1,0:T(8,128)(2,1)} %copy-done.73, bf16[384,1024]{1,0:T(8,128)(2,1)} %copy-done.69, bf16[192,1024]{1,0:T(8,128)(2,1)} %copy-done.75, bf16[8,384,384]{2,1,0:T(8,128)(2,1)} %all-to-all-done.9.t_ref.refs_4_, ...), custom_call_target="tpu_custom_call" | custom-call | flops 1000000 | bytes 100000 | tf_op jit(solution)/shard_map/pallas_call | solution.py:588
  653.7 3.9 all-to-all-start.14
  657.7 10.4 %shard_map.305 = (bf16[1920,128]{1,0:T(8,128)(2,1)}, bf16[1920,128]{1,0:T(8,128)(2,1)}, bf16[1920,128]{1,0:T(8,128)(2,1)}, bf16[1920,128]{1,0:T(8,128)(2,1)}, f3...) custom-call(s32[2]{0:T(128)} %pad_add_fusion.2.at_ref, bf16[8,768,128]{2,1,0:T(8,128)(2,1)} %all-to-all-done.13.refs_1_.refs_9_.g_ref, ...), custom_call_target="tpu_custom_call" | custom-call | flops 1000000 | bytes 100000 | tf_op jit(solution)/shard_map/pallas_call | solution.py:766
  668.8 20.5 %shard_map.306.b_ref = bf16[8,576,128]{2,1,0:T(8,128)(2,1)} custom-call(s32[2]{0:T(128)S(1)} %pad_add_fusion.n_ref, bf16[2,1536,128]{2,1,0:T(8,128)(2,1)S(1)} %copy-done.71, bf16[8,192,128]{2,1,0:T(8,128)(2,1)S(1)} %all-to-all-done.14.refs_1_, bf16[1536,128]{1,0:T(8,128)(2,1)} %get-tuple-element.82.refs_2_, ...), custom_call_target="tpu_custom_call" | custom-call | flops 1000000 | bytes 100000 | tf_op jit(solution)/shard_map/pallas_call | solution.py:242
  689.3 4.3 all-to-all-start.15
  701.3 11.5 %collective-permute-done.22 = bf16[18,1,128]{2,1,0:T(2,128)(2,1)S(1)} collective-permute-done((bf16[18,1,128]{2,1,0:T(2,128)(2,1)S(1)}, bf16[18,1,128]{2,1,0:T(2,128)(2,1)S(1)}, u32[]{:S(2)}, u32[]{:S(2)}) %collective-permute-start.22) | collective-permute-done | bytes 4640 | tf_op jit(solution)/shard_map/ppermute | solution.py:1324
  714.3 4.5 collective-permute-done.21
  723.9 9.1 %collective-permute-done.18.refs_10_.refs_2_ = bf16[1920,128]{1,0:T(8,128)(2,1)} collective-permute-done((bf16[1920,128]{1,0:T(8,128)(2,1)}, bf16[1920,128]{1,0:T(8,128)(2,1)}, u32[]{:S(2)}, u32[]{:S(2)}) %collective-permute-start.18) | collective-permute-done | bytes 491552 | tf_op jit(solution)/shard_map/ppermute | solution.py:995
  743.6 8.3 shard_map.308
  751.9 5.4 all-to-all-start.16
  758.0 10.4 %collective-permute-start.25 = (bf16[192,768]{1,0:T(8,128)(2,1)S(1)}, bf16[192,768]{1,0:T(8,128)(2,1)S(1)}, u32[]{:S(2)}, u32[]{:S(2)}) collective-permute-start(bf16[192,768]{1,0:T(8,128)(2,1)S(1)} %copy-done.76), channel_id=1, source_target_pairs={{0,1},{1,0},{2,3},{3,2},{4,5},{5,4},{6,7},{7,6},{8,9},{9,8},{10,11... | collective-permute-start | bytes 884744 | tf_op jit(solution)/shard_map/ppermute | solution.py:995
  782.6 11.7 %shard_map.311 = bf16[18,32,256]{2,1,0:T(8,128)(2,1)S(1)} custom-call(bf16[18,160,128]{2,1,0:T(8,128)(2,1)S(1)} %copy-done.16, bf16[18,561,256]{2,1,0:T(8,128)(2,1)S(1)} %bitcast.125), custom_call_target="tpu_custom_call" | custom-call | flops 1000000 | bytes 100000 | tf_op jit(solution)/shard_map/pallas_call | solution.py:941
  799.8 20.9 %collective-permute-start.28 = (bf16[656,128]{1,0:T(8,128)(2,1)S(1)}, bf16[656,128]{1,0:T(8,128)(2,1)S(1)}, u32[]{:S(2)}, u32[]{:S(2)}) collective-permute-start(bf16[656,128]{1,0:T(8,128)(2,1)S(1)} %get-tuple-element.132), channel_id=1, source_target_pairs={{0,1},{1,0},{2,3},{3,2},{4,5},{5,4},{6,7},{7,6},{8,9},{9,8},{10,11... | collective-permute-start | bytes 503816 | tf_op jit(solution)/shard_map/ppermute | solution.py:995
  833.4 3.9 collective-permute-done.29.refs_2_
  (400 shorter events, 184.1 us)
Async XLA Ops:
  7.2 76.3 %all-gather.7.cloned.1.call-start = ((), (), s32[]{:S(2)}) async-start(), calls=%async_computation.24 | async-start | bytes 5406720 | tf_op jit(solution)/shard_map/all_gather | solution.py:971
  10.9 167.5 %all-gather.9.cloned.1.call-start = ((), (), s32[]{:S(2)}) async-start(), calls=%async_computation.25 | async-start | bytes 8650752 | tf_op jit(solution)/shard_map/all_gather | solution.py:971
  15.9 309.0 %all-gather.11.cloned.1.call-start = ((), (), s32[]{:S(2)}) async-start(), calls=%async_computation.26 | async-start | bytes 20545536 | tf_op jit(solution)/shard_map/all_gather | solution.py:971
  20.3 37.3 %collective-permute-start.1 = (bf16[384,768]{1,0:T(8,128)(2,1)S(1)}, bf16[384,768]{1,0:T(8,128)(2,1)S(1)}, u32[]{:S(2)}, u32[]{:S(2)}) collective-permute-start(bf16[384,768]{1,0:T(8,128)(2,1)S(1)} %pad_maximum_fusion.2.refs_0_), channel_id=1, source_target_pairs={{0,8},{4,12},{8,0},{12,4},{16,24},{20,28},{24,16},{28,20},{1,9},{5... | collective-permute-start | bytes 1769480 | tf_op jit(solution)/shard_map/ppermute | solution.py:1016
  23.3 35.6 %collective-permute-start.3 = (bf16[384,768]{1,0:T(8,128)(2,1)S(1)}, bf16[384,768]{1,0:T(8,128)(2,1)S(1)}, u32[]{:S(2)}, u32[]{:S(2)}) collective-permute-start(bf16[384,768]{1,0:T(8,128)(2,1)S(1)} %pad_maximum_fusion.2.refs_0_), channel_id=1, source_target_pairs={{0,16},{4,20},{8,24},{12,28},{16,0},{20,4},{24,8},{28,12},{1,17},{... | collective-permute-start | bytes 1769480 | tf_op jit(solution)/shard_map/ppermute | solution.py:1016
  24.6 34.3 %collective-permute-start.5 = (bf16[384,768]{1,0:T(8,128)(2,1)S(1)}, bf16[384,768]{1,0:T(8,128)(2,1)}, u32[]{:S(2)}, u32[]{:S(2)}) collective-permute-start(bf16[384,768]{1,0:T(8,128)(2,1)S(1)} %pad_maximum_fusion.2.refs_0_), channel_id=1, source_target_pairs={{0,24},{4,28},{8,16},{12,20},{16,8},{20,12},{24,0},{28,4},{1,25},{... | collective-permute-start | bytes 1769480 | tf_op jit(solution)/shard_map/ppermute | solution.py:1016
  42.6 11.9 %collective-permute-start.8 = (f32[18,8,128]{2,1,0:T(8,128)S(1)}, f32[18,8,128]{2,1,0:T(8,128)S(1)}, u32[]{:S(2)}, u32[]{:S(2)}) collective-permute-start(f32[18,8,128]{2,1,0:T(8,128)S(1)} %slice.169), channel_id=1, source_target_pairs={{0,16},{4,20},{8,24},{12,28},{1,17},{5,21},{9,25},{13,29},{2,18},{... | collective-permute-start | bytes 221192 | tf_op jit(solution)/shard_map/ppermute | solution.py:1135
  46.4 6.6 collective-permute-start.9
  52.9 7.8 collective-permute-start
  117.0 24.1 %all-to-all-start.1 = ((bf16[32,72,128]{2,1,0:T(8,128)(2,1)}), bf16[32,72,128]{2,1,0:T(8,128)(2,1)}, u32[]{:S(2)}, u32[]{:S(2)}) async-start(bf16[32,72,128]{2,1,0:T(8,128)(2,1)} %shard_map.282), calls=%async_computation.1 | async-start | bytes 1179648 | tf_op jit(solution)/shard_map/all_to_all | solution.py:962
  141.2 32.8 %all-to-all-start.5 = ((bf16[8,192,128]{2,1,0:T(8,128)(2,1)}), bf16[8,192,128]{2,1,0:T(8,128)(2,1)S(1)}, u32[]{:S(2)}, u32[]{:S(2)}) async-start(bf16[8,192,128]{2,1,0:T(8,128)(2,1)} %bitcast.28), calls=%async_computation.5 | async-start | bytes 786432 | tf_op jit(solution)/shard_map/all_to_all | solution.py:954
  174.0 19.2 %all-to-all-start.2 = ((bf16[8,384,128]{2,1,0:T(8,128)(2,1)}), bf16[8,384,128]{2,1,0:T(8,128)(2,1)}, u32[]{:S(2)}, u32[]{:S(2)}) async-start(bf16[8,384,128]{2,1,0:T(8,128)(2,1)} %bitcast.130), calls=%async_computation.2 | async-start | bytes 1572864 | tf_op jit(solution)/shard_map/all_to_all | solution.py:954
  193.2 23.4 %all-to-all-start.6 = ((bf16[8,192,384]{2,1,0:T(8,128)(2,1)}), bf16[8,192,384]{2,1,0:T(8,128)(2,1)S(1)}, u32[]{:S(2)}, u32[]{:S(2)}) async-start(bf16[8,192,384]{2,1,0:T(8,128)(2,1)} %copy-done.56), calls=%async_computation.6 | async-start | bytes 2359296 | tf_op jit(solution)/shard_map/all_to_all | solution.py:954
  216.7 40.0 %all-to-all-start.3 = ((bf16[8,384,384]{2,1,0:T(8,128)(2,1)}), bf16[8,384,384]{2,1,0:T(8,128)(2,1)}, u32[]{:S(2)}, u32[]{:S(2)}) async-start(bf16[8,384,384]{2,1,0:T(8,128)(2,1)} %copy-done.38), calls=%async_computation.3 | async-start | bytes 4718592 | tf_op jit(solution)/shard_map/all_to_all | solution.py:954
  222.0 70.8 %collective-permute-start.10 = (bf16[8,192,256]{2,1,0:T(8,128)(2,1)}, bf16[8,192,256]{2,1,0:T(8,128)(2,1)}, u32[]{:S(2)}, u32[]{:S(2)}) collective-permute-start(bf16[8,192,256]{2,1,0:T(8,128)(2,1)} %slice.176), channel_id=1, source_target_pairs={{0,1},{1,0},{2,3},{3,2},{4,5},{5,4},{6,7},{7,6},{8,9},{9,8},{10,11... | collective-permute-start | bytes 2359304 | tf_op jit(solution)/shard_map/ppermute | solution.py:967
  288.4 23.3 %all-to-all-start.4 = ((bf16[8,384,128]{2,1,0:T(8,128)(2,1)}), bf16[8,384,128]{2,1,0:T(8,128)(2,1)}, u32[]{:S(2)}, u32[]{:S(2)}) async-start(bf16[8,384,128]{2,1,0:T(8,128)(2,1)} %bitcast.27), calls=%async_computation.4 | async-start | bytes 1572864 | tf_op jit(solution)/shard_map/all_to_all | solution.py:954
  311.7 12.5 %all-to-all-start.7 = ((bf16[8,192,128]{2,1,0:T(8,128)(2,1)}), bf16[8,192,128]{2,1,0:T(8,128)(2,1)S(1)}, u32[]{:S(2)}, u32[]{:S(2)}) async-start(bf16[8,192,128]{2,1,0:T(8,128)(2,1)} %shard_map.289), calls=%async_computation.7 | async-start | bytes 786432 | tf_op jit(solution)/shard_map/all_to_all | solution.py:954
  361.9 30.5 %all-to-all-start.8 = ((bf16[8,576,128]{2,1,0:T(8,128)(2,1)}), bf16[8,576,128]{2,1,0:T(8,128)(2,1)S(1)}, u32[]{:S(2)}, u32[]{:S(2)}) async-start(bf16[8,576,128]{2,1,0:T(8,128)(2,1)} %get-tuple-element.89), calls=%async_computation.8 | async-start | bytes 2359296 | tf_op jit(solution)/shard_map/all_to_all | solution.py:954
  368.0 190.3 %reduce-scatter.7.cloned.1.call-start = ((), (), s32[]{:S(2)}) async-start(), calls=%async_computation.21 | async-start | bytes 22413312 | tf_op jit(solution)/shard_map/reduce_scatter | solution.py:990
  395.8 64.2 %all-to-all-start.10 = ((bf16[32,72,128]{2,1,0:T(8,128)(2,1)}), bf16[32,72,128]{2,1,0:T(8,128)(2,1)S(1)}, u32[]{:S(2)}, u32[]{:S(2)}) async-start(bf16[32,72,128]{2,1,0:T(8,128)(2,1)} %bitcast.42), calls=%async_computation.10 | async-start | bytes 1179648 | tf_op jit(solution)/shard_map/all_to_all | solution.py:962
  460.0 53.7 %all-to-all-start.9 = ((bf16[8,384,384]{2,1,0:T(8,128)(2,1)}), bf16[8,384,384]{2,1,0:T(8,128)(2,1)}, u32[]{:S(2)}, u32[]{:S(2)}) async-start(bf16[8,384,384]{2,1,0:T(8,128)(2,1)} %shard_map.293.refs_4_), calls=%async_computation.9 | async-start | bytes 4718592 | tf_op jit(solution)/shard_map/all_to_all | solution.py:954
  464.4 168.8 %reduce-scatter.13.cloned.1.call-start = ((), (), s32[]{:S(2)}) async-start(), calls=%async_computation.27 | async-start | bytes 3112960
  485.1 21.3 %collective-permute-start.11 = (bf16[1536,256]{1,0:T(8,128)(2,1)}, bf16[1536,256]{1,0:T(8,128)(2,1)S(1)}, u32[]{:S(2)}, u32[]{:S(2)}) collective-permute-start(bf16[1536,256]{1,0:T(8,128)(2,1)} %get-tuple-element.101), channel_id=1, source_target_pairs={{0,1},{1,0},{2,3},{3,2},{4,5},{5,4},{6,7},{7,6},{8,9},{9,8},{10,11... | collective-permute-start | bytes 2359304 | tf_op jit(solution)/shard_map/ppermute | solution.py:967
  565.1 39.4 %all-to-all-start.12 = ((bf16[8,192,384]{2,1,0:T(8,128)(2,1)}), bf16[8,192,384]{2,1,0:T(8,128)(2,1)S(1)}, u32[]{:S(2)}, u32[]{:S(2)}) async-start(bf16[8,192,384]{2,1,0:T(8,128)(2,1)} %shard_map.299), calls=%async_computation.12 | async-start | bytes 2359296 | tf_op jit(solution)/shard_map/all_to_all | solution.py:954
  604.6 36.8 %all-to-all-start.13 = ((bf16[8,768,128]{2,1,0:T(8,128)(2,1)}), bf16[8,768,128]{2,1,0:T(8,128)(2,1)}, u32[]{:S(2)}, u32[]{:S(2)}) async-start(bf16[8,768,128]{2,1,0:T(8,128)(2,1)} %shard_map.300.refs_0_.a_ref), calls=%async_computation.13 | async-start | bytes 3145728 | tf_op jit(solution)/shard_map/all_to_all | solution.py:954
  608.9 148.4 %reduce-scatter.9.cloned.1.call-start = ((), (), s32[]{:S(2)}) async-start(), calls=%async_computation.22 | async-start | bytes 9437184 | tf_op jit(solution)/shard_map/reduce_scatter | solution.py:990
  612.3 23.5 %collective-permute-start.12 = (bf16[96,1024]{1,0:T(8,128)(2,1)S(1)}, bf16[96,1024]{1,0:T(8,128)(2,1)S(1)}, u32[]{:S(2)}, u32[]{:S(2)}) collective-permute-start(bf16[96,1024]{1,0:T(8,128)(2,1)S(1)} %get-tuple-element.203), channel_id=1, source_target_pairs={{0,1},{1,0},{2,3},{3,2},{4,5},{5,4},{6,7},{7,6},{8,9},{9,8},{10,11... | collective-permute-start | bytes 589832 | tf_op jit(solution)/shard_map/ppermute | solution.py:995
  612.3 23.5 %collective-permute-start.13 = (bf16[96,1024]{1,0:T(8,128)(2,1)S(1)}, bf16[96,1024]{1,0:T(8,128)(2,1)S(1)}, u32[]{:S(2)}, u32[]{:S(2)}) collective-permute-start(bf16[96,1024]{1,0:T(8,128)(2,1)S(1)} %get-tuple-element.202), channel_id=1, source_target_pairs={{0,2},{1,3},{2,0},{3,1},{4,6},{5,7},{6,4},{7,5},{8,10},{9,11},{10,... | collective-permute-start | bytes 589832 | tf_op jit(solution)/shard_map/ppermute | solution.py:995
  614.8 21.1 %collective-permute-start.14 = (bf16[96,1024]{1,0:T(8,128)(2,1)S(1)}, bf16[96,1024]{1,0:T(8,128)(2,1)S(1)}, u32[]{:S(2)}, u32[]{:S(2)}) collective-permute-start(bf16[96,1024]{1,0:T(8,128)(2,1)S(1)} %get-tuple-element.201), channel_id=1, source_target_pairs={{0,3},{1,2},{2,1},{3,0},{4,7},{5,6},{6,5},{7,4},{8,11},{9,10},{10,... | collective-permute-start | bytes 589832 | tf_op jit(solution)/shard_map/ppermute | solution.py:995
  617.4 18.4 %collective-permute-start.15 = (bf16[96,1024]{1,0:T(8,128)(2,1)}, bf16[96,1024]{1,0:T(8,128)(2,1)S(1)}, u32[]{:S(2)}, u32[]{:S(2)}) collective-permute-start(bf16[96,1024]{1,0:T(8,128)(2,1)} %get-tuple-element.211), channel_id=1, source_target_pairs={{0,0},{1,2},{2,1},{3,3},{4,4},{5,6},{6,5},{7,7},{8,8},{9,10},{10,9... | collective-permute-start | bytes 589832 | tf_op jit(solution)/shard_map/ppermute | solution.py:1003
  619.0 22.4 %collective-permute-start.16 = (bf16[96,1024]{1,0:T(8,128)(2,1)}, bf16[96,1024]{1,0:T(8,128)(2,1)S(1)}, u32[]{:S(2)}, u32[]{:S(2)}) collective-permute-start(bf16[96,1024]{1,0:T(8,128)(2,1)} %get-tuple-element.210), channel_id=1, source_target_pairs={{0,1},{1,3},{2,0},{3,2},{4,5},{5,7},{6,4},{7,6},{8,9},{9,11},{10,8... | collective-permute-start | bytes 589832 | tf_op jit(solution)/shard_map/ppermute | solution.py:1003
  653.7 14.4 %all-to-all-start.14 = ((bf16[8,192,128]{2,1,0:T(8,128)(2,1)}), bf16[8,192,128]{2,1,0:T(8,128)(2,1)S(1)}, u32[]{:S(2)}, u32[]{:S(2)}) async-start(bf16[8,192,128]{2,1,0:T(8,128)(2,1)} %shard_map.302), calls=%async_computation.14 | async-start | bytes 786432 | tf_op jit(solution)/shard_map/all_to_all | solution.py:954
  689.3 54.3 %all-to-all-start.15 = ((bf16[8,576,128]{2,1,0:T(8,128)(2,1)}), bf16[8,576,128]{2,1,0:T(8,128)(2,1)}, u32[]{:S(2)}, u32[]{:S(2)}) async-start(bf16[8,576,128]{2,1,0:T(8,128)(2,1)} %shard_map.306.b_ref), calls=%async_computation.16 | async-start | bytes 2359296 | tf_op jit(solution)/shard_map/all_to_all | solution.py:954
  693.9 24.9 %collective-permute-start.20 = (bf16[18,16,128]{2,1,0:T(8,128)(2,1)S(1)}, bf16[18,16,128]{2,1,0:T(8,128)(2,1)S(1)}, u32[]{:S(2)}, u32[]{:S(2)}) collective-permute-start(bf16[18,16,128]{2,1,0:T(8,128)(2,1)S(1)} %bitcast.171), channel_id=1, source_target_pairs={{4,0},{8,4},{12,8},{20,16},{24,20},{28,24},{5,1},{9,5},{13,9},{21,... | collective-permute-start | bytes 221192 | tf_op jit(solution)/shard_map/ppermute | solution.py:1322
  695.5 28.4 %collective-permute-start.17 = (bf16[1920,128]{1,0:T(8,128)(2,1)}, bf16[1920,128]{1,0:T(8,128)(2,1)}, u32[]{:S(2)}, u32[]{:S(2)}) collective-permute-start(bf16[1920,128]{1,0:T(8,128)(2,1)} %get-tuple-element.124), channel_id=1, source_target_pairs={{0,1},{1,0},{2,3},{3,2},{4,5},{5,4},{6,7},{7,6},{8,9},{9,8},{10,11... | collective-permute-start | bytes 1474568 | tf_op jit(solution)/shard_map/ppermute | solution.py:995
  696.3 36.7 %collective-permute-start.18 = (bf16[1920,128]{1,0:T(8,128)(2,1)}, bf16[1920,128]{1,0:T(8,128)(2,1)}, u32[]{:S(2)}, u32[]{:S(2)}) collective-permute-start(bf16[1920,128]{1,0:T(8,128)(2,1)} %get-tuple-element.125), channel_id=1, source_target_pairs={{0,2},{1,3},{2,0},{3,1},{4,6},{5,7},{6,4},{7,5},{8,10},{9,11},{10,... | collective-permute-start | bytes 1474568 | tf_op jit(solution)/shard_map/ppermute | solution.py:995
  699.7 33.3 %collective-permute-start.19 = (bf16[1920,128]{1,0:T(8,128)(2,1)}, bf16[1920,128]{1,0:T(8,128)(2,1)}, u32[]{:S(2)}, u32[]{:S(2)}) collective-permute-start(bf16[1920,128]{1,0:T(8,128)(2,1)} %get-tuple-element.126), channel_id=1, source_target_pairs={{0,3},{1,2},{2,1},{3,0},{4,7},{5,6},{6,5},{7,4},{8,11},{9,10},{10,... | collective-permute-start | bytes 1474568 | tf_op jit(solution)/shard_map/ppermute | solution.py:995
  700.0 12.8 %collective-permute-start.22 = (bf16[18,1,128]{2,1,0:T(2,128)(2,1)S(1)}, bf16[18,1,128]{2,1,0:T(2,128)(2,1)S(1)}, u32[]{:S(2)}, u32[]{:S(2)}) collective-permute-start(bf16[18,1,128]{2,1,0:T(2,128)(2,1)S(1)} %slice_bitcast_fusion.8), channel_id=1, source_target_pairs={{20,0},{24,4},{28,8},{21,1},{25,5},{29,9},{22,2},{26,6},{30,10},{2... | collective-permute-start | bytes 13832 | tf_op jit(solution)/shard_map/ppermute | solution.py:1324
  751.9 44.5 %all-to-all-start.16 = ((bf16[8,1232,128]{2,1,0:T(8,128)(2,1)}), bf16[8,1232,128]{2,1,0:T(8,128)(2,1)}, u32[]{:S(2)}, u32[]{:S(2)}) async-start(bf16[8,1232,128]{2,1,0:T(8,128)(2,1)} %get-tuple-element.127.refs_6_.refs_1_), calls=%async_computation.17 | async-start | bytes 5046272 | tf_op jit(solution)/shard_map/all_to_all | solution.py:954
  757.3 83.3 %reduce-scatter.11.cloned.1.call-start = ((), (), s32[]{:S(2)}) async-start(), calls=%async_computation.23 | async-start | bytes 1310720 | tf_op jit(solution)/shard_map/reduce_scatter | solution.py:1008
  758.0 65.8 %collective-permute-start.25 = (bf16[192,768]{1,0:T(8,128)(2,1)S(1)}, bf16[192,768]{1,0:T(8,128)(2,1)S(1)}, u32[]{:S(2)}, u32[]{:S(2)}) collective-permute-start(bf16[192,768]{1,0:T(8,128)(2,1)S(1)} %copy-done.76), channel_id=1, source_target_pairs={{0,1},{1,0},{2,3},{3,2},{4,5},{5,4},{6,7},{7,6},{8,9},{9,8},{10,11... | collective-permute-start | bytes 884744 | tf_op jit(solution)/shard_map/ppermute | solution.py:995
  769.3 60.5 %collective-permute-start.26 = (bf16[192,768]{1,0:T(8,128)(2,1)S(1)}, bf16[192,768]{1,0:T(8,128)(2,1)S(1)}, u32[]{:S(2)}, u32[]{:S(2)}) collective-permute-start(bf16[192,768]{1,0:T(8,128)(2,1)S(1)} %copy-done.76), channel_id=1, source_target_pairs={{0,2},{1,3},{2,0},{3,1},{4,6},{5,7},{6,4},{7,5},{8,10},{9,11},{10,... | collective-permute-start | bytes 884744 | tf_op jit(solution)/shard_map/ppermute | solution.py:995
  770.3 59.6 %collective-permute-start.27 = (bf16[192,768]{1,0:T(8,128)(2,1)S(1)}, bf16[192,768]{1,0:T(8,128)(2,1)S(1)}, u32[]{:S(2)}, u32[]{:S(2)}) collective-permute-start(bf16[192,768]{1,0:T(8,128)(2,1)S(1)} %copy-done.76), channel_id=1, source_target_pairs={{0,3},{1,2},{2,1},{3,0},{4,7},{5,6},{6,5},{7,4},{8,11},{9,10},{10,... | collective-permute-start | bytes 884744 | tf_op jit(solution)/shard_map/ppermute | solution.py:995
  771.7 28.1 %collective-permute-start.23 = (bf16[96,1024]{1,0:T(8,128)(2,1)}, bf16[96,1024]{1,0:T(8,128)(2,1)S(1)}, u32[]{:S(2)}, u32[]{:S(2)}) collective-permute-start(bf16[96,1024]{1,0:T(8,128)(2,1)} %get-tuple-element.128), channel_id=1, source_target_pairs={{0,0},{1,2},{2,1},{3,3},{4,4},{5,6},{6,5},{7,7},{8,8},{9,10},{10,9... | collective-permute-start | bytes 589832 | tf_op jit(solution)/shard_map/ppermute | solution.py:1003
  773.3 50.5 %collective-permute-start.24 = (bf16[96,1024]{1,0:T(8,128)(2,1)}, bf16[96,1024]{1,0:T(8,128)(2,1)}, u32[]{:S(2)}, u32[]{:S(2)}) collective-permute-start(bf16[96,1024]{1,0:T(8,128)(2,1)} %get-tuple-element.129), channel_id=1, source_target_pairs={{0,1},{1,3},{2,0},{3,2},{4,5},{5,7},{6,4},{7,6},{8,9},{9,11},{10,8... | collective-permute-start | bytes 589832 | tf_op jit(solution)/shard_map/ppermute | solution.py:1003
  799.8 33.6 %collective-permute-start.28 = (bf16[656,128]{1,0:T(8,128)(2,1)S(1)}, bf16[656,128]{1,0:T(8,128)(2,1)S(1)}, u32[]{:S(2)}, u32[]{:S(2)}) collective-permute-start(bf16[656,128]{1,0:T(8,128)(2,1)S(1)} %get-tuple-element.132), channel_id=1, source_target_pairs={{0,1},{1,0},{2,3},{3,2},{4,5},{5,4},{6,7},{7,6},{8,9},{9,8},{10,11... | collective-permute-start | bytes 503816 | tf_op jit(solution)/shard_map/ppermute | solution.py:995
  823.8 13.5 %collective-permute-start.29 = (bf16[656,128]{1,0:T(8,128)(2,1)S(1)}, bf16[656,128]{1,0:T(8,128)(2,1)S(1)}, u32[]{:S(2)}, u32[]{:S(2)}) collective-permute-start(bf16[656,128]{1,0:T(8,128)(2,1)S(1)} %get-tuple-element.133), channel_id=1, source_target_pairs={{0,2},{1,3},{2,0},{3,1},{4,6},{5,7},{6,4},{7,5},{8,10},{9,11},{10,... | collective-permute-start | bytes 503816 | tf_op jit(solution)/shard_map/ppermute | solution.py:995
  823.8 13.5 %collective-permute-start.30 = (bf16[656,128]{1,0:T(8,128)(2,1)S(1)}, bf16[656,128]{1,0:T(8,128)(2,1)S(1)}, u32[]{:S(2)}, u32[]{:S(2)}) collective-permute-start(bf16[656,128]{1,0:T(8,128)(2,1)S(1)} %get-tuple-element.134), channel_id=1, source_target_pairs={{0,3},{1,2},{2,1},{3,0},{4,7},{5,6},{6,5},{7,4},{8,11},{9,10},{10,... | collective-permute-start | bytes 503816 | tf_op jit(solution)/shard_map/ppermute | solution.py:995
  (103 other events, 874.7 us)
Sparse Core Ops, SparseCore 0:
  11.5 72.0 all-gather.6
  87.0 88.2 all-gather.8
  178.1 146.6 all-gather.10
  393.6 164.5 reduce-scatter.6
  562.8 50.0 reduce-scatter.12
  653.8 85.3 reduce-scatter.8
  760.5 53.0 reduce-scatter.10

commit v10 on v9

--- a/solution.py
+++ b/solution.py
@@ -1325,7 +1325,7 @@
     fill = jnp.zeros((planes, toks - rim - TC - 1, cu), bf16)
     ext = jnp.concatenate([tile.reshape(planes, own, cu), rights, belows, corner, fill], axis=1)
     sent_a = to_ranks(sent_a)
-    by_head = finish(at, [cross_a, cross_b], rows, patch_pieces, [*sent_a, ext])
+    by_head = finish(at, [cross_a, cross_b], rows, patch_pieces, [ext])
     heads = by_head.shape[1]
     *sent_b, part_b, final = end(
         at,
@@ -1338,7 +1338,7 @@
         d1[1],
         norm_gains[:1],
         pairs,
-        [],
+        sent_a,
         [share, lift, small, by_head],
     )
     got_last = swap_seq(final)

time: 864 us -> 850 us (0.984)
  Pallas kernels: 424 us -> 403 us
    pallas_call x5, Pallas kernels: 154 us -> 141 us  [attend_back(): pl.pallas_call(body, out_shape=tuple((jax.ShapeDtypeStruct(v, bf16) for v...]
    pallas_call x4, Pallas kernels: 90.3 us -> 80.8 us  [attend(): pl.pallas_call(body, out_shape=(jax.ShapeDtypeStruct((queries, hpd * HD),...]
    ppermute x12, waiting for transfers between devices: 13 us -> 4.08 us  [to_ranks(): lax.ppermute(v, 'mp', moves[i])]
    unnamed x211 -> x207, local copies, waits for them, and re-layouts: 58.4 us -> 58.9 us
  transfers between devices with their start and end apart: 53 -> 53, of which waited for: 17 -> 16; matrix products, arithmetic and copies ran while one was open for 6% -> 6% of each run, Pallas kernels for 44% -> 42%
where the time goes in v10:
time: 850 us; the launch traced here: 835 us
  Pallas kernels  403 us (47%)
  starting transfers between devices  142 us (17%)
  waiting for transfers between devices  124 us (15%)
  local copies, waits for them, and re-layouts  92.5 us (11%)
  blocking collectives  46.4 us (5%)
  between operations  16.2 us (2%)
  other arithmetic  11.6 us (1%)
    pallas_call x5, Pallas kernels, attend_back(): pl.pallas_call(body, out_shape=tuple((jax.ShapeDtypeStruct(v, bf16) for v...  141 us
    pallas_call x4, Pallas kernels, attend(): pl.pallas_call(body, out_shape=(jax.ShapeDtypeStruct((queries, hpd * HD),...  80.8 us
    unnamed x207, local copies, waits for them, and re-layouts  58.9 us
    all_to_all x13, starting transfers between devices, swap_seq(): return lax.all_to_all(value, 'seq', split_axis=0, concat_axis=0, tiled=True)  57.3 us
    all_to_all x13, waiting for transfers between devices, swap_seq(): return lax.all_to_all(value, 'seq', split_axis=0, concat_axis=0, tiled=True)  49.5 us
    all_to_all x2, blocking collectives, swap_seq(): return lax.all_to_all(value, 'seq', split_axis=0, concat_axis=0, tiled=True)  46.4 us
    ppermute x12, starting transfers between devices, to_ranks(): lax.ppermute(v, 'mp', moves[i])  44.5 us
    pallas_call x1, Pallas kernels, feed_forward(): pl.pallas_call(functools.partial(mlp_kernel, steps=steps), grid=(steps,),...  36.9 us
  transfers between devices with their start and end apart: 53, of which 16 were waited for; matrix products, arithmetic and copies ran while one was open for 6% of the time, Pallas kernels for 42%

profile of v10, /device:TPU:0, one launch (start us, length us, event | category | flops | bytes accessed | tf_op | source)
XLA Modules:
  0.0 834.8 jit_solution(12702811501758745924)
XLA Ops:
  27.3 15.2 %shard_map.280 = f32[18,160,128]{2,1,0:T(8,128)S(1)} custom-call(bf16[18,32,256]{2,1,0:T(8,128)(2,1)S(1)} %pad.16.cot_ref, bf16[18,561,256]{2,1,0:T(8,128)(2,1)S(1)} %bitcast.124), custom_call_target="tpu_custom_call" | custom-call | flops 1000000 | bytes 100000 | tf_op jit(solution)/shard_map/pallas_call | solution.py:941
  42.6 3.7 collective-permute-start.8
  63.0 20.4 %all-gather.7.cloned.1.call-done = bf16[2560,1024]{1,0:T(8,128)(2,1)} async-done(((bf16[80,1024]{1,0:T(8,128)(2,1)}), bf16[2560,1024]{1,0:T(8,128)(2,1)}) %all-gather.7.cloned.1.call-update) | async-done | bytes 5242896 | tf_op jit(solution)/shard_map/all_gather | solution.py:971
  83.4 11.5 %shard_map.281 = (bf16[8,576,128]{2,1,0:T(8,128)(2,1)}, bf16[8,384,256]{2,1,0:T(8,128)(2,1)}, bf16[576,1024]{1,0:T(8,128)(2,1)}, bf16[1024,1024]{1,0:T(8,128)(2,1)}, bf16[2048,768]{1,0:T(8,128)(2,1)}) custom-call(s32[2]{0:T(128)} %pad_add_fusion.2.at_ref, bf16[384,1024]{1,0:T(8,128)(2,1)} %dynamic-slice_bitcast_fusion.1.xa_ref.x_ref, ...), custom_call_target="tpu_custom_call" | custom-call | flops 1000000 | bytes 100000 | tf_op jit(solution)/shard_map/pallas_call | solution.py:637
  94.9 22.0 %all_to_all.85.refs_1_.refs_0_ = bf16[8,576,128]{2,1,0:T(8,128)(2,1)} all-to-all(bf16[8,576,128]{2,1,0:T(8,128)(2,1)} %get-tuple-element.77), channel_id=1, replica_groups=mesh['seq'=8,'mp'=4] {'seq'}, dimensions={0} | all-to-all | bytes 2359296 | tf_op jit(solution)/shard_map/all_to_all | solution.py:954
  121.8 11.9 %shard_map.286 = (bf16[1536,128]{1,0:T(8,128)(2,1)}, bf16[2,1536,128]{2,1,0:T(8,128)(2,1)S(1)}) custom-call(s32[2]{0:T(128)S(1)} %pad_add_fusion.n_ref, bf16[8,576,128]{2,1,0:T(8,128)(2,1)S(1)} %copy-done.11, bf16[8,384,256]{2,1,0:T(8,128)(2,1)S(1)} %copy-done.7), custom_call_target="tpu_custom_call" | custom-call | flops 1000000 | bytes 100000 | tf_op jit(solution)/shard_map/pallas_call | solution.py:207
  134.5 6.5 all-to-all-done.1.refs_2_
  145.4 20.0 %shard_map.283 = (bf16[3072,128]{1,0:T(8,128)(2,1)S(1)}, bf16[2,3072,128]{2,1,0:T(8,128)(2,1)S(1)}) custom-call(s32[2]{0:T(128)S(1)} %pad_add_fusion.1.n_ref, bf16[8,576,128]{2,1,0:T(8,128)(2,1)S(1)} %copy-done.11, bf16[8,384,256]{2,1,0:T(8,128)(2,1)S(1)} %copy-done.7, bf16[32,72,128]{2,1,0:T(8,128)(2,1)} %all-to-all-done.1.refs_2_), custom_call_target="tpu_custom_call" | custom-call | flops 1000000 | bytes 100000 | tf_op jit(solution)/shard_map/pallas_call | solution.py:207
  167.5 4.4 all-to-all-start.2
  179.5 5.1 shard_map.287
  192.1 10.2 %shard_map.284 = (f32[384,1024]{1,0:T(8,128)S(1)}, bf16[384,1024]{1,0:T(8,128)(2,1)S(1)}, bf16[384,1024]{1,0:T(8,128)(2,1)S(1)}, bf16[8,384,384]{2,1,0:T(8,128)(2,1)S(1)}) custom-call(bf16[8,384,128]{2,1,0:T(8,128)(2,1)} %all-to-all-done.2.a_ref, bf16[384,1024]{1,0:T(8,128)(2,1)S(1)} %copy-done.13, f32[2,1024]{1,0:T(2,128)S(1)} %pad_maximum_fusion.9.norm_ref, ...), custom_call_target="tpu_custom_call" | custom-call | flops 1000000 | bytes 100000 | tf_op jit(solution)/shard_map/pallas_call | solution.py:313
  207.8 4.4 all-to-all-start.3
  214.6 40.5 %all-to-all-done.3.refs_0_.refs_3_ = bf16[8,384,384]{2,1,0:T(8,128)(2,1)} async-done(((bf16[8,384,384]{2,1,0:T(8,128)(2,1)}), bf16[8,384,384]{2,1,0:T(8,128)(2,1)}, u32[]{:S(2)}, u32[]{:S(2)}) %all-to-all-start.3) | async-done | bytes 2359328 | tf_op jit(solution)/shard_map/all_to_all | solution.py:954
  255.1 31.7 %shard_map.285 = (bf16[3072,128]{1,0:T(8,128)(2,1)}, bf16[2,3072,128]{2,1,0:T(8,128)(2,1)S(1)}) custom-call(s32[2]{0:T(128)S(1)} %copy-done.79, bf16[8,384,384]{2,1,0:T(8,128)(2,1)} %all-to-all-done.3.refs_0_.refs_3_), custom_call_target="tpu_custom_call" | custom-call | flops 1000000 | bytes 100000 | tf_op jit(solution)/shard_map/pallas_call | solution.py:207
  286.8 4.4 all-to-all-start.4
  291.3 17.2 %shard_map.288 = (bf16[1536,128]{1,0:T(8,128)(2,1)S(1)}, bf16[2,1536,128]{2,1,0:T(8,128)(2,1)S(1)}) custom-call(s32[2]{0:T(128)S(1)} %copy-done.79, bf16[8,192,384]{2,1,0:T(8,128)(2,1)S(1)} %all-to-all-done.6.refs_0_.refs_3_, bf16[8,192,256]{2,1,0:T(8,128)(2,1)} %collective-permute-done.10.refs_1_.refs_3_, bf16[3072,128]{1,0:T(8,128)(2,1)} %get-tuple-element.81.refs_2_), custom_call_target="tpu_custom_call" | custom-call | flops 1000000 | bytes 100000 | tf_op jit(solution)/shard_map/pallas_call | solution.py:207
  310.2 4.2 all-to-all-start.7
  322.7 5.0 all-gather.11.cloned.1.call-done
  327.7 36.9 %shard_map.290 = (bf16[576,1024]{1,0:T(8,128)(2,1)}, bf16[576,1024]{1,0:T(8,128)(2,1)}, bf16[576,4096]{1,0:T(8,128)(2,1)}, bf16[576,4096]{1,0:T(8,128)(2,1)}, bf...) custom-call(bf16[8,384,128]{2,1,0:T(8,128)(2,1)} %all-to-all-done.4., ...), custom_call_target="tpu_custom_call" | custom-call | flops 1000000 | bytes 100000 | tf_op jit(solution)/shard_map/pallas_call | solution.py:433
  364.6 5.2 all-to-all-start.8
  370.3 24.0 %shard_map.291.refs_0_ = bf16[1024,9728]{1,0:T(8,128)(2,1)} custom-call(bf16[576,1024]{1,0:T(8,128)(2,1)} %get-tuple-element.90.refs_0_, bf16[576,1024]{1,0:T(8,128)(2,1)} %get-tuple-element.91.refs_1_, bf16[576,1024]{1,0:T(8,128)(2,1)} %get-tuple-element.92.refs_2_, bf16[576,1024]{1,0:T(8,128)(2,1)} %get-tuple-element.87.refs_3_.refs_0_, ...), custom_call_target="tpu_custom_call" | custom-call | flops 1000000 | bytes 100000 | tf_op jit(solution)/shard_map/pallas_call | solution.py:588
  397.6 4.2 all-to-all-start.10
  401.8 59.4 %shard_map.293.refs_4_ = bf16[8,384,384]{2,1,0:T(8,128)(2,1)} custom-call(s32[2]{0:T(128)S(1)} %copy-done.79, bf16[2,3072,128]{2,1,0:T(8,128)(2,1)} %copy-done.54, bf16[8,576,128]{2,1,0:T(8,128)(2,1)S(1)} %copy-done.4, bf16[3072,128]{1,0:T(8,128)(2,1)} %get-tuple-element.81.refs_2_, bf16[8,384,384]{2,1,0:T(8,128)(2,1)} %all-to-all-done.3.refs_0_.refs_3_, ...), custom_call_target="tpu_custom_call" | custom-call | flops 1000000 | bytes 100000 | tf_op jit(solution)/shard_map/pallas_call | solution.py:242
  461.1 4.4 all-to-all-start.9
  465.8 20.4 %shard_map.295 = (bf16[1536,128]{1,0:T(8,128)(2,1)S(1)}, bf16[1536,256]{1,0:T(8,128)(2,1)}) custom-call(s32[2]{0:T(128)S(1)} %copy-done.79, bf16[2,1536,128]{2,1,0:T(8,128)(2,1)} %copy-done.36, bf16[8,576,128]{2,1,0:T(8,128)(2,1)} %copy-done.3, bf16[1536,128]{1,0:T(8,128)(2,1)S(1)} %get-tuple-element.84.refs_2_, ...), custom_call_target="tpu_custom_call" | custom-call | flops 1000000 | bytes 100000 | tf_op jit(solution)/shard_map/pallas_call | solution.py:242
  488.0 19.4 %shard_map.296 = (bf16[1536,128]{1,0:T(8,128)(2,1)S(1)}, bf16[1536,256]{1,0:T(8,128)(2,1)S(1)}) custom-call(s32[2]{0:T(128)S(1)} %copy-done.79, bf16[2,1536,128]{2,1,0:T(8,128)(2,1)} %copy-done.36, bf16[8,576,128]{2,1,0:T(8,128)(2,1)} %copy-done.3, bf16[1536,128]{1,0:T(8,128)(2,1)S(1)} %get-tuple-element.84.refs_2_, bf16[8,192,384]{2,1,0:T(8,128)(2,1)} %copy-done.12, ...), custom_call_target="tpu_custom_call" | custom-call | flops 1000000 | bytes 100000 | tf_op jit(solution)/shard_map/pallas_call | solution.py:242
  508.4 6.3 all-to-all-done.9.t_ref.refs_4_
  519.0 11.8 %shard_map.297 = (f32[384,1024]{1,0:T(8,128)S(1)}, bf16[384,1024]{1,0:T(8,128)(2,1)S(1)}, bf16[8,384,128]{2,1,0:T(8,128)(2,1)S(1)}, f32[2,1024]{1,0:T(2,128)S(1)}) custom-call(bf16[8,384,384]{2,1,0:T(8,128)(2,1)} %all-to-all-done.9.t_ref.refs_4_, f32[384,1024]{1,0:T(8,128)S(1)} %copy-done.24, f32[576,1024]{1,0:T(8,128)S(1)} %copy-done.19, ...), custom_call_target="tpu_custom_call" | custom-call | flops 1000000 | bytes 100000 | tf_op jit(solution)/shard_map/pallas_call | solution.py:530
  532.0 24.4 %all_to_all.86.refs_1_ = bf16[8,384,128]{2,1,0:T(8,128)(2,1)} all-to-all(bf16[8,384,128]{2,1,0:T(8,128)(2,1)S(1)} %get-tuple-element.105), channel_id=1, replica_groups=mesh['seq'=8,'mp'=4] {'seq'}, dimensions={0} | all-to-all | bytes 1572864 | tf_op jit(solution)/shard_map/all_to_all | solution.py:954
  559.4 4.4 copy.140
  566.3 3.7 all-to-all-start.12
  571.2 26.2 %shard_map.300.refs_0_.a_ref = bf16[8,768,128]{2,1,0:T(8,128)(2,1)} custom-call(s32[2]{0:T(128)S(1)} %pad_add_fusion.1.n_ref, bf16[2,3072,128]{2,1,0:T(8,128)(2,1)} %copy-done.51, bf16[8,384,128]{2,1,0:T(8,128)(2,1)S(1)} %copy-done.14, bf16[3072,128]{1,0:T(8,128)(2,1)S(1)} %copy-done.35, bf16[8,384,256]{2,1,0:T(8,128)(2,1)} %get-tuple-element.78.refs_1_.refs_3_), custom_call_target="tpu_custom_call" | custom-call | flops 1000000 | bytes 100000 | tf_op jit(solution)/shard_map/pallas_call | solution.py:242
  597.4 4.3 all-to-all-start.13
  614.6 9.1 %shard_map.301 = (f32[192,1024]{1,0:T(8,128)S(1)}, bf16[192,1024]{1,0:T(8,128)(2,1)S(1)}, bf16[8,192,128]{2,1,0:T(8,128)(2,1)S(1)}, f32[2,1024]{1,0:T(2,128)S(1)}) custom-call(bf16[8,192,384]{2,1,0:T(8,128)(2,1)S(1)} %all-to-all-done.12.t_ref.refs_5_, f32[192,1024]{1,0:T(8,128)S(1)} %copy-done.30, f32[576,1024]{1,0:T(8,128)S(1)} %copy-done.20, ...), custom_call_target="tpu_custom_call" | custom-call | flops 1000000 | bytes 100000 | tf_op jit(solution)/shard_map/pallas_call | solution.py:530
  628.7 9.5 %collective-permute-done.16.refs_15_.refs_5_ = bf16[96,1024]{1,0:T(8,128)(2,1)S(1)} collective-permute-done((bf16[96,1024]{1,0:T(8,128)(2,1)}, bf16[96,1024]{1,0:T(8,128)(2,1)S(1)}, u32[]{:S(2)}, u32[]{:S(2)}) %collective-permute-start.16) | collective-permute-done | bytes 196640 | tf_op jit(solution)/shard_map/ppermute | solution.py:1003
  638.8 11.6 %shard_map.304.refs_0_.refs_4_ = bf16[1024,4096]{1,0:T(8,128)(2,1)} custom-call(bf16[384,1024]{1,0:T(8,128)(2,1)} %copy-done.66, bf16[192,1024]{1,0:T(8,128)(2,1)} %copy-done.72, bf16[384,1024]{1,0:T(8,128)(2,1)} %copy-done.69, bf16[192,1024]{1,0:T(8,128)(2,1)} %copy-done.74, bf16[8,384,384]{2,1,0:T(8,128)(2,1)} %all-to-all-done.9.t_ref.refs_4_, ...), custom_call_target="tpu_custom_call" | custom-call | flops 1000000 | bytes 100000 | tf_op jit(solution)/shard_map/pallas_call | solution.py:588
  654.2 11.0 %shard_map.305 = (bf16[1920,128]{1,0:T(8,128)(2,1)}, bf16[1920,128]{1,0:T(8,128)(2,1)}, bf16[1920,128]{1,0:T(8,128)(2,1)}, bf16[1920,128]{1,0:T(8,128)(2,1)}, f3...) custom-call(s32[2]{0:T(128)} %pad_add_fusion.2.at_ref, bf16[8,768,128]{2,1,0:T(8,128)(2,1)} %all-to-all-done.13.refs_1_.refs_9_.g_ref, ...), custom_call_target="tpu_custom_call" | custom-call | flops 1000000 | bytes 100000 | tf_op jit(solution)/shard_map/pallas_call | solution.py:766
  665.9 16.1 %shard_map.306.b_ref = bf16[8,576,128]{2,1,0:T(8,128)(2,1)} custom-call(s32[2]{0:T(128)S(1)} %pad_add_fusion.n_ref, bf16[2,1536,128]{2,1,0:T(8,128)(2,1)S(1)} %copy-done.71, bf16[8,192,128]{2,1,0:T(8,128)(2,1)S(1)} %all-to-all-done.14.refs_1_, bf16[1536,128]{1,0:T(8,128)(2,1)} %get-tuple-element.82.refs_2_, ...), custom_call_target="tpu_custom_call" | custom-call | flops 1000000 | bytes 100000 | tf_op jit(solution)/shard_map/pallas_call | solution.py:242
  682.0 4.3 all-to-all-start.15
  688.3 5.9 collective-permute-start.21
  695.5 9.9 %collective-permute-done.19 = bf16[18,1,128]{2,1,0:T(2,128)(2,1)S(1)} collective-permute-done((bf16[18,1,128]{2,1,0:T(2,128)(2,1)S(1)}, bf16[18,1,128]{2,1,0:T(2,128)(2,1)S(1)}, u32[]{:S(2)}, u32[]{:S(2)}) %collective-permute-start.19) | collective-permute-done | bytes 4640 | tf_op jit(solution)/shard_map/ppermute | solution.py:1324
  707.0 6.3 collective-permute-done.18
  727.7 8.4 %shard_map.308 = (bf16[96,1024]{1,0:T(8,128)(2,1)}, bf16[96,1024]{1,0:T(8,128)(2,1)}, bf16[192,768]{1,0:T(8,128)(2,1)}, bf16[8,1232,128]{2,1,0:T(8,128)(2,1)}) custom-call(s32[2]{0:T(128)} %pad_add_fusion.2.at_ref, bf16[8,576,128]{2,1,0:T(8,128)(2,1)} %all-to-all-done.15.g_ref, bf16[1024,1024]{1,0:T(8,128)(2,1)} %get-tuple-element.114.wq_ref, ...), custom_call_target="tpu_custom_call" | custom-call | flops 1000000 | bytes 100000 | tf_op jit(solution)/shard_map/pallas_call | solution.py:766
  736.1 7.2 all-to-all-start.16
  744.0 8.4 %collective-permute-start.25 = (bf16[192,768]{1,0:T(8,128)(2,1)S(1)}, bf16[192,768]{1,0:T(8,128)(2,1)S(1)}, u32[]{:S(2)}, u32[]{:S(2)}) collective-permute-start(bf16[192,768]{1,0:T(8,128)(2,1)S(1)} %copy-done.75), channel_id=1, source_target_pairs={{0,1},{1,0},{2,3},{3,2},{4,5},{5,4},{6,7},{7,6},{8,9},{9,8},{10,11... | collective-permute-start | bytes 884744 | tf_op jit(solution)/shard_map/ppermute | solution.py:995
  766.6 11.7 %shard_map.311 = bf16[18,32,256]{2,1,0:T(8,128)(2,1)S(1)} custom-call(bf16[18,160,128]{2,1,0:T(8,128)(2,1)S(1)} %copy-done.16, bf16[18,561,256]{2,1,0:T(8,128)(2,1)S(1)} %bitcast.125), custom_call_target="tpu_custom_call" | custom-call | flops 1000000 | bytes 100000 | tf_op jit(solution)/shard_map/pallas_call | solution.py:941
  783.8 20.9 %collective-permute-start.28 = (bf16[656,128]{1,0:T(8,128)(2,1)S(1)}, bf16[656,128]{1,0:T(8,128)(2,1)S(1)}, u32[]{:S(2)}, u32[]{:S(2)}) collective-permute-start(bf16[656,128]{1,0:T(8,128)(2,1)S(1)} %get-tuple-element.132), channel_id=1, source_target_pairs={{0,1},{1,0},{2,3},{3,2},{4,5},{5,4},{6,7},{7,6},{8,9},{9,8},{10,11... | collective-permute-start | bytes 503816 | tf_op jit(solution)/shard_map/ppermute | solution.py:995
  817.3 4.1 collective-permute-done.29.refs_2_
  (396 shorter events, 181.2 us)
Async XLA Ops:
  7.2 76.2 %all-gather.7.cloned.1.call-start = ((), (), s32[]{:S(2)}) async-start(), calls=%async_computation.24 | async-start | bytes 5406720 | tf_op jit(solution)/shard_map/all_gather | solution.py:971
  10.9 164.2 %all-gather.9.cloned.1.call-start = ((), (), s32[]{:S(2)}) async-start(), calls=%async_computation.25 | async-start | bytes 8650752 | tf_op jit(solution)/shard_map/all_gather | solution.py:971
  15.9 311.9 %all-gather.11.cloned.1.call-start = ((), (), s32[]{:S(2)}) async-start(), calls=%async_computation.26 | async-start | bytes 20545536 | tf_op jit(solution)/shard_map/all_gather | solution.py:971
  20.3 37.3 %collective-permute-start.1 = (bf16[384,768]{1,0:T(8,128)(2,1)S(1)}, bf16[384,768]{1,0:T(8,128)(2,1)S(1)}, u32[]{:S(2)}, u32[]{:S(2)}) collective-permute-start(bf16[384,768]{1,0:T(8,128)(2,1)S(1)} %pad_maximum_fusion.2.refs_0_), channel_id=1, source_target_pairs={{0,8},{4,12},{8,0},{12,4},{16,24},{20,28},{24,16},{28,20},{1,9},{5... | collective-permute-start | bytes 1769480 | tf_op jit(solution)/shard_map/ppermute | solution.py:1016
  23.3 35.6 %collective-permute-start.3 = (bf16[384,768]{1,0:T(8,128)(2,1)S(1)}, bf16[384,768]{1,0:T(8,128)(2,1)S(1)}, u32[]{:S(2)}, u32[]{:S(2)}) collective-permute-start(bf16[384,768]{1,0:T(8,128)(2,1)S(1)} %pad_maximum_fusion.2.refs_0_), channel_id=1, source_target_pairs={{0,16},{4,20},{8,24},{12,28},{16,0},{20,4},{24,8},{28,12},{1,17},{... | collective-permute-start | bytes 1769480 | tf_op jit(solution)/shard_map/ppermute | solution.py:1016
  24.6 34.3 %collective-permute-start.5 = (bf16[384,768]{1,0:T(8,128)(2,1)S(1)}, bf16[384,768]{1,0:T(8,128)(2,1)}, u32[]{:S(2)}, u32[]{:S(2)}) collective-permute-start(bf16[384,768]{1,0:T(8,128)(2,1)S(1)} %pad_maximum_fusion.2.refs_0_), channel_id=1, source_target_pairs={{0,24},{4,28},{8,16},{12,20},{16,8},{20,12},{24,0},{28,4},{1,25},{... | collective-permute-start | bytes 1769480 | tf_op jit(solution)/shard_map/ppermute | solution.py:1016
  42.6 11.9 %collective-permute-start.8 = (f32[18,8,128]{2,1,0:T(8,128)S(1)}, f32[18,8,128]{2,1,0:T(8,128)S(1)}, u32[]{:S(2)}, u32[]{:S(2)}) collective-permute-start(f32[18,8,128]{2,1,0:T(8,128)S(1)} %slice.169), channel_id=1, source_target_pairs={{0,16},{4,20},{8,24},{12,28},{1,17},{5,21},{9,25},{13,29},{2,18},{... | collective-permute-start | bytes 221192 | tf_op jit(solution)/shard_map/ppermute | solution.py:1135
  52.9 7.8 collective-permute-start
  116.9 24.1 %all-to-all-start.1 = ((bf16[32,72,128]{2,1,0:T(8,128)(2,1)}), bf16[32,72,128]{2,1,0:T(8,128)(2,1)}, u32[]{:S(2)}, u32[]{:S(2)}) async-start(bf16[32,72,128]{2,1,0:T(8,128)(2,1)} %shard_map.282), calls=%async_computation.1 | async-start | bytes 1179648 | tf_op jit(solution)/shard_map/all_to_all | solution.py:962
  141.0 26.5 %all-to-all-start.5 = ((bf16[8,192,128]{2,1,0:T(8,128)(2,1)}), bf16[8,192,128]{2,1,0:T(8,128)(2,1)S(1)}, u32[]{:S(2)}, u32[]{:S(2)}) async-start(bf16[8,192,128]{2,1,0:T(8,128)(2,1)} %bitcast.28), calls=%async_computation.5 | async-start | bytes 786432 | tf_op jit(solution)/shard_map/all_to_all | solution.py:954
  167.5 18.9 %all-to-all-start.2 = ((bf16[8,384,128]{2,1,0:T(8,128)(2,1)}), bf16[8,384,128]{2,1,0:T(8,128)(2,1)}, u32[]{:S(2)}, u32[]{:S(2)}) async-start(bf16[8,384,128]{2,1,0:T(8,128)(2,1)} %bitcast.130), calls=%async_computation.2 | async-start | bytes 1572864 | tf_op jit(solution)/shard_map/all_to_all | solution.py:954
  187.4 20.3 %all-to-all-start.6 = ((bf16[8,192,384]{2,1,0:T(8,128)(2,1)}), bf16[8,192,384]{2,1,0:T(8,128)(2,1)S(1)}, u32[]{:S(2)}, u32[]{:S(2)}) async-start(bf16[8,192,384]{2,1,0:T(8,128)(2,1)} %copy-done.55), calls=%async_computation.6 | async-start | bytes 2359296 | tf_op jit(solution)/shard_map/all_to_all | solution.py:954
  207.8 47.4 %all-to-all-start.3 = ((bf16[8,384,384]{2,1,0:T(8,128)(2,1)}), bf16[8,384,384]{2,1,0:T(8,128)(2,1)}, u32[]{:S(2)}, u32[]{:S(2)}) async-start(bf16[8,384,384]{2,1,0:T(8,128)(2,1)} %copy-done.47), calls=%async_computation.3 | async-start | bytes 4718592 | tf_op jit(solution)/shard_map/all_to_all | solution.py:954
  213.1 78.2 %collective-permute-start.10 = (bf16[8,192,256]{2,1,0:T(8,128)(2,1)}, bf16[8,192,256]{2,1,0:T(8,128)(2,1)}, u32[]{:S(2)}, u32[]{:S(2)}) collective-permute-start(bf16[8,192,256]{2,1,0:T(8,128)(2,1)} %slice.176), channel_id=1, source_target_pairs={{0,1},{1,0},{2,3},{3,2},{4,5},{5,4},{6,7},{7,6},{8,9},{9,8},{10,11... | collective-permute-start | bytes 2359304 | tf_op jit(solution)/shard_map/ppermute | solution.py:967
  286.8 23.4 %all-to-all-start.4 = ((bf16[8,384,128]{2,1,0:T(8,128)(2,1)}), bf16[8,384,128]{2,1,0:T(8,128)(2,1)}, u32[]{:S(2)}, u32[]{:S(2)}) async-start(bf16[8,384,128]{2,1,0:T(8,128)(2,1)} %bitcast.27), calls=%async_computation.4 | async-start | bytes 1572864 | tf_op jit(solution)/shard_map/all_to_all | solution.py:954
  310.2 12.5 %all-to-all-start.7 = ((bf16[8,192,128]{2,1,0:T(8,128)(2,1)}), bf16[8,192,128]{2,1,0:T(8,128)(2,1)S(1)}, u32[]{:S(2)}, u32[]{:S(2)}) async-start(bf16[8,192,128]{2,1,0:T(8,128)(2,1)} %shard_map.289), calls=%async_computation.7 | async-start | bytes 786432 | tf_op jit(solution)/shard_map/all_to_all | solution.py:954
  364.6 29.7 %all-to-all-start.8 = ((bf16[8,576,128]{2,1,0:T(8,128)(2,1)}), bf16[8,576,128]{2,1,0:T(8,128)(2,1)S(1)}, u32[]{:S(2)}, u32[]{:S(2)}) async-start(bf16[8,576,128]{2,1,0:T(8,128)(2,1)} %get-tuple-element.89), calls=%async_computation.8 | async-start | bytes 2359296 | tf_op jit(solution)/shard_map/all_to_all | solution.py:954
  369.9 189.6 %reduce-scatter.7.cloned.1.call-start = ((), (), s32[]{:S(2)}) async-start(), calls=%async_computation.21 | async-start | bytes 22413312 | tf_op jit(solution)/shard_map/reduce_scatter | solution.py:990
  397.6 63.6 %all-to-all-start.10 = ((bf16[32,72,128]{2,1,0:T(8,128)(2,1)}), bf16[32,72,128]{2,1,0:T(8,128)(2,1)S(1)}, u32[]{:S(2)}, u32[]{:S(2)}) async-start(bf16[32,72,128]{2,1,0:T(8,128)(2,1)} %bitcast.42), calls=%async_computation.10 | async-start | bytes 1179648 | tf_op jit(solution)/shard_map/all_to_all | solution.py:962
  461.1 53.7 %all-to-all-start.9 = ((bf16[8,384,384]{2,1,0:T(8,128)(2,1)}), bf16[8,384,384]{2,1,0:T(8,128)(2,1)}, u32[]{:S(2)}, u32[]{:S(2)}) async-start(bf16[8,384,384]{2,1,0:T(8,128)(2,1)} %shard_map.293.refs_4_), calls=%async_computation.9 | async-start | bytes 4718592 | tf_op jit(solution)/shard_map/all_to_all | solution.py:954
  465.6 160.4 %reduce-scatter.13.cloned.1.call-start = ((), (), s32[]{:S(2)}) async-start(), calls=%async_computation.27 | async-start | bytes 3112960
  486.2 21.3 %collective-permute-start.11 = (bf16[1536,256]{1,0:T(8,128)(2,1)}, bf16[1536,256]{1,0:T(8,128)(2,1)S(1)}, u32[]{:S(2)}, u32[]{:S(2)}) collective-permute-start(bf16[1536,256]{1,0:T(8,128)(2,1)} %get-tuple-element.101), channel_id=1, source_target_pairs={{0,1},{1,0},{2,3},{3,2},{4,5},{5,4},{6,7},{7,6},{8,9},{9,8},{10,11... | collective-permute-start | bytes 2359304 | tf_op jit(solution)/shard_map/ppermute | solution.py:967
  566.3 31.0 %all-to-all-start.12 = ((bf16[8,192,384]{2,1,0:T(8,128)(2,1)}), bf16[8,192,384]{2,1,0:T(8,128)(2,1)S(1)}, u32[]{:S(2)}, u32[]{:S(2)}) async-start(bf16[8,192,384]{2,1,0:T(8,128)(2,1)} %shard_map.299), calls=%async_computation.12 | async-start | bytes 2359296 | tf_op jit(solution)/shard_map/all_to_all | solution.py:954
  597.4 40.8 %all-to-all-start.13 = ((bf16[8,768,128]{2,1,0:T(8,128)(2,1)}), bf16[8,768,128]{2,1,0:T(8,128)(2,1)}, u32[]{:S(2)}, u32[]{:S(2)}) async-start(bf16[8,768,128]{2,1,0:T(8,128)(2,1)} %shard_map.300.refs_0_.a_ref), calls=%async_computation.13 | async-start | bytes 3145728 | tf_op jit(solution)/shard_map/all_to_all | solution.py:954
  601.7 141.7 %reduce-scatter.9.cloned.1.call-start = ((), (), s32[]{:S(2)}) async-start(), calls=%async_computation.22 | async-start | bytes 9437184 | tf_op jit(solution)/shard_map/reduce_scatter | solution.py:990
  605.1 23.6 %collective-permute-start.12 = (bf16[96,1024]{1,0:T(8,128)(2,1)S(1)}, bf16[96,1024]{1,0:T(8,128)(2,1)S(1)}, u32[]{:S(2)}, u32[]{:S(2)}) collective-permute-start(bf16[96,1024]{1,0:T(8,128)(2,1)S(1)} %get-tuple-element.203), channel_id=1, source_target_pairs={{0,1},{1,0},{2,3},{3,2},{4,5},{5,4},{6,7},{7,6},{8,9},{9,8},{10,11... | collective-permute-start | bytes 589832 | tf_op jit(solution)/shard_map/ppermute | solution.py:995
  606.6 22.0 %collective-permute-start.13 = (bf16[96,1024]{1,0:T(8,128)(2,1)S(1)}, bf16[96,1024]{1,0:T(8,128)(2,1)S(1)}, u32[]{:S(2)}, u32[]{:S(2)}) collective-permute-start(bf16[96,1024]{1,0:T(8,128)(2,1)S(1)} %get-tuple-element.202), channel_id=1, source_target_pairs={{0,2},{1,3},{2,0},{3,1},{4,6},{5,7},{6,4},{7,5},{8,10},{9,11},{10,... | collective-permute-start | bytes 589832 | tf_op jit(solution)/shard_map/ppermute | solution.py:995
  609.1 19.6 %collective-permute-start.14 = (bf16[96,1024]{1,0:T(8,128)(2,1)S(1)}, bf16[96,1024]{1,0:T(8,128)(2,1)S(1)}, u32[]{:S(2)}, u32[]{:S(2)}) collective-permute-start(bf16[96,1024]{1,0:T(8,128)(2,1)S(1)} %get-tuple-element.201), channel_id=1, source_target_pairs={{0,3},{1,2},{2,1},{3,0},{4,7},{5,6},{6,5},{7,4},{8,11},{9,10},{10,... | collective-permute-start | bytes 589832 | tf_op jit(solution)/shard_map/ppermute | solution.py:995
  610.2 18.5 %collective-permute-start.15 = (bf16[96,1024]{1,0:T(8,128)(2,1)}, bf16[96,1024]{1,0:T(8,128)(2,1)S(1)}, u32[]{:S(2)}, u32[]{:S(2)}) collective-permute-start(bf16[96,1024]{1,0:T(8,128)(2,1)} %get-tuple-element.211), channel_id=1, source_target_pairs={{0,0},{1,2},{2,1},{3,3},{4,4},{5,6},{6,5},{7,7},{8,8},{9,10},{10,9... | collective-permute-start | bytes 589832 | tf_op jit(solution)/shard_map/ppermute | solution.py:1003
  611.8 26.4 %collective-permute-start.16 = (bf16[96,1024]{1,0:T(8,128)(2,1)}, bf16[96,1024]{1,0:T(8,128)(2,1)S(1)}, u32[]{:S(2)}, u32[]{:S(2)}) collective-permute-start(bf16[96,1024]{1,0:T(8,128)(2,1)} %get-tuple-element.210), channel_id=1, source_target_pairs={{0,1},{1,3},{2,0},{3,2},{4,5},{5,7},{6,4},{7,6},{8,9},{9,11},{10,8... | collective-permute-start | bytes 589832 | tf_op jit(solution)/shard_map/ppermute | solution.py:1003
  650.5 14.8 %all-to-all-start.14 = ((bf16[8,192,128]{2,1,0:T(8,128)(2,1)}), bf16[8,192,128]{2,1,0:T(8,128)(2,1)S(1)}, u32[]{:S(2)}, u32[]{:S(2)}) async-start(bf16[8,192,128]{2,1,0:T(8,128)(2,1)} %shard_map.302), calls=%async_computation.14 | async-start | bytes 786432 | tf_op jit(solution)/shard_map/all_to_all | solution.py:954
  682.0 45.7 %all-to-all-start.15 = ((bf16[8,576,128]{2,1,0:T(8,128)(2,1)}), bf16[8,576,128]{2,1,0:T(8,128)(2,1)}, u32[]{:S(2)}, u32[]{:S(2)}) async-start(bf16[8,576,128]{2,1,0:T(8,128)(2,1)} %shard_map.306.b_ref), calls=%async_computation.16 | async-start | bytes 2359296 | tf_op jit(solution)/shard_map/all_to_all | solution.py:954
  686.7 26.6 %collective-permute-start.17 = (bf16[18,16,128]{2,1,0:T(8,128)(2,1)S(1)}, bf16[18,16,128]{2,1,0:T(8,128)(2,1)S(1)}, u32[]{:S(2)}, u32[]{:S(2)}) collective-permute-start(bf16[18,16,128]{2,1,0:T(8,128)(2,1)S(1)} %bitcast.171), channel_id=1, source_target_pairs={{4,0},{8,4},{12,8},{20,16},{24,20},{28,24},{5,1},{9,5},{13,9},{21,... | collective-permute-start | bytes 221192 | tf_op jit(solution)/shard_map/ppermute | solution.py:1322
  688.2 39.4 %collective-permute-start.20 = (bf16[1920,128]{1,0:T(8,128)(2,1)}, bf16[1920,128]{1,0:T(8,128)(2,1)}, u32[]{:S(2)}, u32[]{:S(2)}) collective-permute-start(bf16[1920,128]{1,0:T(8,128)(2,1)} %get-tuple-element.124), channel_id=1, source_target_pairs={{0,1},{1,0},{2,3},{3,2},{4,5},{5,4},{6,7},{7,6},{8,9},{9,8},{10,11... | collective-permute-start | bytes 1474568 | tf_op jit(solution)/shard_map/ppermute | solution.py:995
  688.3 39.3 %collective-permute-start.21 = (bf16[1920,128]{1,0:T(8,128)(2,1)}, bf16[1920,128]{1,0:T(8,128)(2,1)}, u32[]{:S(2)}, u32[]{:S(2)}) collective-permute-start(bf16[1920,128]{1,0:T(8,128)(2,1)} %get-tuple-element.125), channel_id=1, source_target_pairs={{0,2},{1,3},{2,0},{3,1},{4,6},{5,7},{6,4},{7,5},{8,10},{9,11},{10,... | collective-permute-start | bytes 1474568 | tf_op jit(solution)/shard_map/ppermute | solution.py:995
  694.2 33.5 %collective-permute-start.22 = (bf16[1920,128]{1,0:T(8,128)(2,1)}, bf16[1920,128]{1,0:T(8,128)(2,1)}, u32[]{:S(2)}, u32[]{:S(2)}) collective-permute-start(bf16[1920,128]{1,0:T(8,128)(2,1)} %get-tuple-element.126), channel_id=1, source_target_pairs={{0,3},{1,2},{2,1},{3,0},{4,7},{5,6},{6,5},{7,4},{8,11},{9,10},{10,... | collective-permute-start | bytes 1474568 | tf_op jit(solution)/shard_map/ppermute | solution.py:995
  694.2 11.2 %collective-permute-start.19 = (bf16[18,1,128]{2,1,0:T(2,128)(2,1)S(1)}, bf16[18,1,128]{2,1,0:T(2,128)(2,1)S(1)}, u32[]{:S(2)}, u32[]{:S(2)}) collective-permute-start(bf16[18,1,128]{2,1,0:T(2,128)(2,1)S(1)} %slice_bitcast_fusion.8), channel_id=1, source_target_pairs={{20,0},{24,4},{28,8},{21,1},{25,5},{29,9},{22,2},{26,6},{30,10},{2... | collective-permute-start | bytes 13832 | tf_op jit(solution)/shard_map/ppermute | solution.py:1324
  705.4 7.9 collective-permute-start.18
  736.1 44.3 %all-to-all-start.16 = ((bf16[8,1232,128]{2,1,0:T(8,128)(2,1)}), bf16[8,1232,128]{2,1,0:T(8,128)(2,1)}, u32[]{:S(2)}, u32[]{:S(2)}) async-start(bf16[8,1232,128]{2,1,0:T(8,128)(2,1)} %get-tuple-element.127.refs_6_.refs_1_), calls=%async_computation.17 | async-start | bytes 5046272 | tf_op jit(solution)/shard_map/all_to_all | solution.py:954
  743.3 81.3 %reduce-scatter.11.cloned.1.call-start = ((), (), s32[]{:S(2)}) async-start(), calls=%async_computation.23 | async-start | bytes 1310720 | tf_op jit(solution)/shard_map/reduce_scatter | solution.py:1008
  744.0 63.6 %collective-permute-start.25 = (bf16[192,768]{1,0:T(8,128)(2,1)S(1)}, bf16[192,768]{1,0:T(8,128)(2,1)S(1)}, u32[]{:S(2)}, u32[]{:S(2)}) collective-permute-start(bf16[192,768]{1,0:T(8,128)(2,1)S(1)} %copy-done.75), channel_id=1, source_target_pairs={{0,1},{1,0},{2,3},{3,2},{4,5},{5,4},{6,7},{7,6},{8,9},{9,8},{10,11... | collective-permute-start | bytes 884744 | tf_op jit(solution)/shard_map/ppermute | solution.py:995
  753.3 60.4 %collective-permute-start.26 = (bf16[192,768]{1,0:T(8,128)(2,1)S(1)}, bf16[192,768]{1,0:T(8,128)(2,1)S(1)}, u32[]{:S(2)}, u32[]{:S(2)}) collective-permute-start(bf16[192,768]{1,0:T(8,128)(2,1)S(1)} %copy-done.75), channel_id=1, source_target_pairs={{0,2},{1,3},{2,0},{3,1},{4,6},{5,7},{6,4},{7,5},{8,10},{9,11},{10,... | collective-permute-start | bytes 884744 | tf_op jit(solution)/shard_map/ppermute | solution.py:995
  754.3 59.4 %collective-permute-start.27 = (bf16[192,768]{1,0:T(8,128)(2,1)S(1)}, bf16[192,768]{1,0:T(8,128)(2,1)S(1)}, u32[]{:S(2)}, u32[]{:S(2)}) collective-permute-start(bf16[192,768]{1,0:T(8,128)(2,1)S(1)} %copy-done.75), channel_id=1, source_target_pairs={{0,3},{1,2},{2,1},{3,0},{4,7},{5,6},{6,5},{7,4},{8,11},{9,10},{10,... | collective-permute-start | bytes 884744 | tf_op jit(solution)/shard_map/ppermute | solution.py:995
  755.7 28.1 %collective-permute-start.23 = (bf16[96,1024]{1,0:T(8,128)(2,1)}, bf16[96,1024]{1,0:T(8,128)(2,1)S(1)}, u32[]{:S(2)}, u32[]{:S(2)}) collective-permute-start(bf16[96,1024]{1,0:T(8,128)(2,1)} %get-tuple-element.128), channel_id=1, source_target_pairs={{0,0},{1,2},{2,1},{3,3},{4,4},{5,6},{6,5},{7,7},{8,8},{9,10},{10,9... | collective-permute-start | bytes 589832 | tf_op jit(solution)/shard_map/ppermute | solution.py:1003
  757.3 50.4 %collective-permute-start.24 = (bf16[96,1024]{1,0:T(8,128)(2,1)}, bf16[96,1024]{1,0:T(8,128)(2,1)}, u32[]{:S(2)}, u32[]{:S(2)}) collective-permute-start(bf16[96,1024]{1,0:T(8,128)(2,1)} %get-tuple-element.129), channel_id=1, source_target_pairs={{0,1},{1,3},{2,0},{3,2},{4,5},{5,7},{6,4},{7,6},{8,9},{9,11},{10,8... | collective-permute-start | bytes 589832 | tf_op jit(solution)/shard_map/ppermute | solution.py:1003
  783.8 33.5 %collective-permute-start.28 = (bf16[656,128]{1,0:T(8,128)(2,1)S(1)}, bf16[656,128]{1,0:T(8,128)(2,1)S(1)}, u32[]{:S(2)}, u32[]{:S(2)}) collective-permute-start(bf16[656,128]{1,0:T(8,128)(2,1)S(1)} %get-tuple-element.132), channel_id=1, source_target_pairs={{0,1},{1,0},{2,3},{3,2},{4,5},{5,4},{6,7},{7,6},{8,9},{9,8},{10,11... | collective-permute-start | bytes 503816 | tf_op jit(solution)/shard_map/ppermute | solution.py:995
  807.7 13.7 %collective-permute-start.29 = (bf16[656,128]{1,0:T(8,128)(2,1)S(1)}, bf16[656,128]{1,0:T(8,128)(2,1)S(1)}, u32[]{:S(2)}, u32[]{:S(2)}) collective-permute-start(bf16[656,128]{1,0:T(8,128)(2,1)S(1)} %get-tuple-element.133), channel_id=1, source_target_pairs={{0,2},{1,3},{2,0},{3,1},{4,6},{5,7},{6,4},{7,5},{8,10},{9,11},{10,... | collective-permute-start | bytes 503816 | tf_op jit(solution)/shard_map/ppermute | solution.py:995
  807.7 13.7 %collective-permute-start.30 = (bf16[656,128]{1,0:T(8,128)(2,1)S(1)}, bf16[656,128]{1,0:T(8,128)(2,1)S(1)}, u32[]{:S(2)}, u32[]{:S(2)}) collective-permute-start(bf16[656,128]{1,0:T(8,128)(2,1)S(1)} %get-tuple-element.134), channel_id=1, source_target_pairs={{0,3},{1,2},{2,1},{3,0},{4,7},{5,6},{6,5},{7,4},{8,11},{9,10},{10,... | collective-permute-start | bytes 503816 | tf_op jit(solution)/shard_map/ppermute | solution.py:995
  (101 other events, 841.2 us)
Sparse Core Ops, SparseCore 0:
  11.5 71.8 all-gather.6
  86.8 88.2 all-gather.8
  178.0 149.7 all-gather.10
  395.5 163.9 reduce-scatter.6
  563.9 54.1 reduce-scatter.12
  650.6 83.0 reduce-scatter.8
  746.5 50.9 reduce-scatter.10
